TPU v7x, 512 devices: a whole 4x8x8 slice. The times are simulated.
512 devices in a mesh: ens: 32 (over x, z_lo, core), node: 16 (over z_hi, y).
Axes of the slice: x: 4, y: 8, z: 8 (z_hi: 2, z_lo: 4; z = z_hi * 4 + z_lo), core: 2. Of those that a mesh axis runs over, the one named last changes fastest.
Arguments:
- hidden: bfloat16 [32, 2048, 1024], P('ens', 'node'), may hold values from -30 to 30
- forcing: bfloat16 [2048, 1024], P('node'), may hold values from -3 to 3
- norm_gain: float32 [1024], replicated, may hold values from 0.1 to 1.9
- w_query: bfloat16 [1024, 1024], P('ens'), may hold values from -0.375 to 0.375
- w_key: bfloat16 [1024, 1024], P('ens'), may hold values from -0.375 to 0.375
- w_value: bfloat16 [1024, 1024], P('ens'), may hold values from -0.1875 to 0.1875
- w_out: bfloat16 [1024, 1024], P('ens'), may hold values from -0.1875 to 0.1875
- w_decode: bfloat16 [1024, 100], replicated, may hold values from -0.1875 to 0.1875
- targets: bfloat16 [100, 2048], P(None, 'node'), may hold values from -6 to 6
- area_weight: float32 [2048], P('node'), may hold values from 0.4 to 14, as said below
Outputs:
- grad_hidden: bfloat16 [32, 2048, 1024], P('ens', 'node')
- grad_out_proj: float32 [1024, 1024], P('ens')
- loss: float32 [], replicated
Inputs may be any that keep to these rules, and one draw needn't show every extreme that they name: `area_weight`: positive.
All inputs are finite; a program needn't handle non-finite values.
Results may differ from a plain program's by a relative error of at most 0.035.
Values may be sent and summed in bfloat16 or wider, within the bound.
No kernel may reach another device: no remote copies, remote signals or barrier semaphores. Data moves between devices by JAX's collectives and lax.ppermute only.
A program may use at most 128 MiB of HBM per device.

v0:
```python
import math

import jax
import jax.numpy as jnp
from jax import lax
from jax.sharding import PartitionSpec as P

HEADS = 16
HALO = 128


ALPHA = 0.95
KAPPA = 0.25
EPS_NORM = 1e-05


def extended_2(block, sides, width):
    for axis, dim in sides:
        count = lax.axis_size(axis)
        forward = [(i, i + 1) for i in range(count - 1)]
        forward.append((count - 1, 0))
        backward = [(target, source) for source, target in forward]
        low = lax.ppermute(
            lax.slice_in_dim(block, block.shape[dim] - width, None, axis=dim), axis, forward
        )
        high = lax.ppermute(lax.slice_in_dim(block, 0, width, axis=dim), axis, backward)
        block = jnp.concatenate([low, block, high], axis=dim)
    return block


def shifted(value, axis, steps):
    count = lax.axis_size(axis)
    pairs = [(source, (source + steps) % count) for source in range(count)]
    return lax.ppermute(value, axis, pairs)


def smooth_abs(delta):
    return jnp.sqrt(delta * delta + KAPPA * KAPPA) - KAPPA


def smooth_slope(delta):
    return delta / jnp.sqrt(delta * delta + KAPPA * KAPPA)


def per_device(
    hidden, forcing, norm_gain, w_query, w_key, w_value, w_out, w_decode, targets, area_weight
):
    node_rows = hidden.shape[1]
    width = hidden.shape[2]
    head_size = width // HEADS
    span = node_rows + 2 * HALO
    scale = 1.0 / math.sqrt(head_size)
    members = lax.axis_size("ens")
    variables = w_decode.shape[1]
    full_query = lax.all_gather(w_query, "ens", axis=0, tiled=True)
    full_key = lax.all_gather(w_key, "ens", axis=0, tiled=True)
    full_value = lax.all_gather(w_value, "ens", axis=0, tiled=True)
    full_out = lax.all_gather(w_out, "ens", axis=0, tiled=True)
    xfield = hidden[0].astype(jnp.float32) + forcing.astype(jnp.float32)
    inverse_rms = lax.rsqrt(jnp.mean(xfield * xfield, -1, keepdims=True) + EPS_NORM)
    normed = (xfield * inverse_rms * norm_gain).astype(jnp.bfloat16)
    queries = jnp.dot(normed, full_query, preferred_element_type=jnp.float32).astype(jnp.bfloat16)
    keys_local = jnp.dot(normed, full_key, preferred_element_type=jnp.float32).astype(jnp.bfloat16)
    values_local = jnp.dot(normed, full_value, preferred_element_type=jnp.float32).astype(
        jnp.bfloat16
    )
    paired = jnp.concatenate([keys_local, values_local], 1)
    extended = extended_2(paired, (("node", 0),), HALO)
    query3 = queries.reshape(node_rows, HEADS, head_size)
    key3 = extended[:, :width].reshape(span, HEADS, head_size)
    value3 = extended[:, width:].reshape(span, HEADS, head_size)
    query_pos = lax.broadcasted_iota(jnp.int32, (node_rows, span), 0)
    key_pos = lax.broadcasted_iota(jnp.int32, (node_rows, span), 1)
    offset = key_pos - query_pos
    window = (offset >= 0) & (offset <= 2 * HALO)
    scores = jnp.einsum("qhd,khd->hqk", query3, key3, preferred_element_type=jnp.float32) * scale
    expo = jnp.where(window[None], jnp.exp(scores), jnp.float32(0.0))
    probs = expo / jnp.sum(expo, -1, keepdims=True)
    probs_b = probs.astype(jnp.bfloat16)
    attended = jnp.einsum("hqk,khd->qhd", probs_b, value3, preferred_element_type=jnp.float32)
    attended = attended.astype(jnp.bfloat16).reshape(node_rows, width)
    resid = xfield + jnp.dot(attended, full_out, preferred_element_type=jnp.float32)
    resid_b = resid.astype(jnp.bfloat16)
    pred_b = lax.dot_general(
        w_decode, resid_b, (((0,), (1,)), ((), ())), preferred_element_type=jnp.float32
    ).astype(jnp.bfloat16)
    eps = (1.0 - ALPHA) / members
    coeff = (1.0 - eps) / (2.0 * (members - 1))
    own = pred_b.astype(jnp.float32)
    delta = own[None] - lax.all_gather(pred_b[None], "ens", axis=0, tiled=True).astype(jnp.float32)
    pair_abs = jnp.sum(smooth_abs(delta), 0)
    pair_slope = jnp.sum(smooth_slope(delta), 0)
    truth = targets.astype(jnp.float32)
    weights = area_weight[None, :]
    entries = smooth_abs(own - truth) - coeff * pair_abs
    loss_part = jnp.sum(weights * entries)
    grad_pred = (weights * (smooth_slope(own - truth) - 2.0 * coeff * pair_slope)).astype(
        jnp.bfloat16
    )
    total_nodes = node_rows * lax.axis_size("node")
    loss = lax.psum(loss_part, ("ens", "node")) / (members * total_nodes * variables)
    grad_resid = lax.dot_general(
        grad_pred, w_decode, (((0,), (1,)), ((), ())), preferred_element_type=jnp.float32
    )
    grad_resid_b = grad_resid.astype(jnp.bfloat16)
    shard_grad = lax.psum_scatter(
        lax.dot_general(
            attended, grad_resid_b, (((0,), (0,)), ((), ())), preferred_element_type=jnp.float32
        ).astype(jnp.bfloat16),
        "ens",
        scatter_dimension=0,
        tiled=True,
    )
    grad_out_proj = lax.psum(shard_grad, "node").astype(jnp.float32)
    grad_attended = lax.dot_general(
        grad_resid_b, full_out, (((1,), (1,)), ((), ())), preferred_element_type=jnp.float32
    ).astype(jnp.bfloat16)
    grad3 = grad_attended.reshape(node_rows, HEADS, head_size)
    grad_probs = jnp.einsum("qhd,khd->hqk", grad3, value3, preferred_element_type=jnp.float32)
    delta_row = jnp.sum(probs * grad_probs, -1, keepdims=True)
    grad_scores = (probs * (grad_probs - delta_row) * scale).astype(jnp.bfloat16)
    grad_queries = jnp.einsum("hqk,khd->qhd", grad_scores, key3, preferred_element_type=jnp.float32)
    grad_queries = grad_queries.astype(jnp.bfloat16).reshape(node_rows, width)
    grad_key_ext = jnp.einsum(
        "hqk,qhd->khd", grad_scores, query3, preferred_element_type=jnp.float32
    ).reshape(span, width)
    grad_value_ext = jnp.einsum(
        "hqk,qhd->khd", probs_b, grad3, preferred_element_type=jnp.float32
    ).reshape(span, width)
    grad_ext = jnp.concatenate([grad_key_ext, grad_value_ext], 1)
    from_right = shifted(grad_ext[:HALO].astype(jnp.bfloat16), "node", -1).astype(jnp.float32)
    from_left = shifted(grad_ext[node_rows + HALO :].astype(jnp.bfloat16), "node", 1).astype(
        jnp.float32
    )
    inner = grad_ext[HALO : HALO + node_rows]
    inner = inner.at[:HALO].add(from_left)
    inner = inner.at[node_rows - HALO :].add(from_right)
    grad_keys = inner[:, :width].astype(jnp.bfloat16)
    grad_values = inner[:, width:].astype(jnp.bfloat16)
    contract = (((1,), (1,)), ((), ()))
    grad_normed = (
        lax.dot_general(grad_queries, full_query, contract, preferred_element_type=jnp.float32)
        + lax.dot_general(grad_keys, full_key, contract, preferred_element_type=jnp.float32)
        + lax.dot_general(grad_values, full_value, contract, preferred_element_type=jnp.float32)
    )
    scaled = norm_gain * grad_normed
    grad_x = inverse_rms * scaled - xfield * inverse_rms**3 * jnp.mean(
        xfield * scaled, -1, keepdims=True
    )
    grad_hidden = (grad_resid + grad_x).astype(jnp.bfloat16)[None]
    return (grad_hidden, grad_out_proj, loss)


def solution(mesh):
    placed = (
        P("ens", "node", None),
        P("node", None),
        P(),
        P("ens", None),
        P("ens", None),
        P("ens", None),
        P("ens", None),
        P(),
        P(None, "node"),
        P("node"),
    )
    return jax.shard_map(
        per_device,
        mesh=mesh,
        in_specs=placed,
        out_specs=(P("ens", "node", None), P("ens", None), P()),
        check_vma=False,
    )
```

profile of v0, /device:TPU:1, one launch (start us, length us, event | category | flops | bytes accessed | tf_op | source)
XLA Modules:
  0.0 686.0 jit_solution(10192387114882302418)
XLA Ops:
  12.4 66.9 %all-gather.9.cloned.1.call-done = bf16[1024,1024]{1,0:T(8,128)(2,1)} async-done(((bf16[32,1024]{1,0:T(8,128)(2,1)}), bf16[1024,1024]{1,0:T(8,128)(2,1)}) %all-gather.9.cloned.1.call-update) | async-done | bytes 2097168 | tf_op jit(solution)/shard_map/all_gather | solution.py:57
  79.3 2.0 convolution_convert_fusion.4
  81.4 62.0 %all-gather.7.cloned.1.call-done = bf16[1024,1024]{1,0:T(8,128)(2,1)} async-done(((bf16[32,1024]{1,0:T(8,128)(2,1)}), bf16[1024,1024]{1,0:T(8,128)(2,1)}) %all-gather.7.cloned.1.call-update) | async-done | bytes 2097168 | tf_op jit(solution)/shard_map/all_gather | solution.py:56
  143.4 2.0 convolution_convert_fusion.5
  145.4 8.2 %collective-permute-start.1 = (bf16[128,2048]{1,0:T(8,128)(2,1)S(1)}, bf16[128,2048]{1,0:T(8,128)(2,1)S(1)}, u32[]{:S(2)}, u32[]{:S(2)}) collective-permute-start(bf16[128,2048]{1,0:T(8,128)(2,1)S(1)} %pad_maximum_fusion.2), channel_id=1, source_target_pairs={{1,0},{2,1},{3,2},{4,3},{5,4},{6,5},{7,6},{8,7},{9,8},{10,9},{11,1... | collective-permute-start | bytes 1572872 | tf_op jit(solution)/shard_map/ppermute | solution.py:26
  153.7 1.9 collective-permute-start
  155.7 71.8 %all-gather.11.cloned.1.call-done = bf16[1024,1024]{1,0:T(8,128)(2,1)} async-done(((bf16[32,1024]{1,0:T(8,128)(2,1)}), bf16[1024,1024]{1,0:T(8,128)(2,1)}) %all-gather.11.cloned.1.call-update) | async-done | bytes 2097168 | tf_op jit(solution)/shard_map/all_gather | solution.py:55
  227.4 2.0 convolution_convert_fusion.3
  231.7 1.6 copy-done.18
  234.4 52.7 %all-gather.13.cloned.1.call-done = bf16[1024,1024]{1,0:T(8,128)(2,1)} async-done(((bf16[32,1024]{1,0:T(8,128)(2,1)}), bf16[1024,1024]{1,0:T(8,128)(2,1)}) %all-gather.13.cloned.1.call-update) | async-done | bytes 2097168 | tf_op jit(solution)/shard_map/all_gather | solution.py:58
  287.1 2.3 bitcast_convert_fusion
  289.4 44.6 %all-gather.1 = bf16[32,100,128]{2,1,0:T(8,128)(2,1)S(1)} all-gather(bf16[1,100,128]{2,1,0:T(8,128)(2,1)S(1)} %bitcast.75), channel_id=2, replica_groups=mesh['ens'=32,'node'=16] {'ens'}, dimensions={0}, use_global_device_ids=true | all-gather | bytes 844800 | tf_op jit(solution)/shard_map/all_gather | solution.py:90
  335.2 3.1 convolution_convert_fusion
  338.5 1.5 convolution_convert_fusion.1
  341.2 3.4 fusion.63
  344.6 15.9 %fusion.8 = f32[16,64,384]{2,1,0:T(8,128)S(1)} fusion(bf16[128,16,64]{0,2,1:T(8,128)(2,1)S(1)} %bitcast.77, f32[16,128,384]{2,1,0:T(8,128)} %fusion.63, f32[16,128,384]{2,1,0:T(8,128)} %copy-done.18, f32[16,128]{1,0:T(8,128)S(1)} %get-tuple-element.51, pred[128,384]{1,0:T(8,128)(4,1)S(1)} %fusion.42), kind=kOutput, calls=%fused_computation.11 | convolution fusion | flops 109316480 | bytes 8183808 | tf_op jit(solution)/shard_map/hqk,qhd->khd/dot_general | solution.py:124
  360.5 3.4 fusion.33
  365.4 8.3 %collective-permute-start.3 = (bf16[128,2048]{0,1:T(8,128)(2,1)}, bf16[128,2048]{0,1:T(8,128)(2,1)}, u32[]{:S(2)}, u32[]{:S(2)}) collective-permute-start(bf16[128,2048]{0,1:T(8,128)(2,1)} %get-tuple-element.46), channel_id=1, source_target_pairs={{0,15},{1,0},{2,1},{3,2},{4,3},{5,4},{6,5},{7,6},{8,7},{9,8},{10,9... | collective-permute-start | bytes 1572872 | tf_op jit(solution)/shard_map/ppermute | solution.py:34
  374.4 1.9 collective-permute-start.2
  376.3 112.1 %psum.15 = f32[]{:T(128)} all-reduce(f32[]{:T(128)} %multiply_reduce_fusion.3), channel_id=1, replica_groups=mesh['ens'=32,'node'=16] {'ens','node'}, use_global_device_ids=true, to_apply=%region_9.10 | all-reduce | flops 1 | bytes 8 | tf_op jit(solution)/shard_map/psum | solution.py:101
  489.1 17.2 %fusion.23 = bf16[16,64,128]{2,1,0:T(8,128)(2,1)} fusion(bf16[384,16,64]{0,2,1:T(8,128)(2,1)} %bitcast.74, f32[16,128,384]{2,1,0:T(8,128)} %fusion.63, f32[16,128,384]{2,1,0:T(8,128)} %copy-done.18, f32[16,128]{1,0:T(8,128)S(1)} %get-tuple-element.51, pred[128,384]{1,0:T(8,128)(4,1)S(1)} %fusion.42), kind=kOutput, calls=%fused_computation.29 | convolution fusion | flops 109447552 | bytes 7397376 | tf_op jit(solution)/shard_map/hqk,khd->qhd/dot_general | solution.py:122
  506.3 1.9 fusion.64
  508.2 1.7 fusion.32
  512.7 163.8 %all-reduce.2.cloned.1.call-done = bf16[32,1024]{1,0:T(8,128)(2,1)} async-done(((bf16[32,1024]{1,0:T(8,128)(2,1)}), bf16[32,1024]{1,0:T(8,128)(2,1)}) %all-reduce.2.cloned.1.call-update) | async-done | bytes 65552 | tf_op jit(solution)/shard_map/psum | solution.py:114
  (77 shorter events, 17.2 us)
Async XLA Ops:
  7.2 280.0 %copy-start = (bf16[1024,100]{0,1:T(8,128)(2,1)S(1)}, bf16[1024,100]{0,1:T(8,128)(2,1)}, u32[]{:S(2)}) copy-start(bf16[1024,100]{0,1:T(8,128)(2,1)} %param.25) | copy-start | bytes 614404
  7.2 72.1 %all-gather.9.cloned.1.call-start = ((), (), s32[]{:S(2)}) async-start(), calls=%async_computation.2 | async-start | bytes 2162688 | tf_op jit(solution)/shard_map/all_gather | solution.py:57
  7.9 135.4 %all-gather.7.cloned.1.call-start = ((), (), s32[]{:S(2)}) async-start(), calls=%async_computation.1 | async-start | bytes 2162688 | tf_op jit(solution)/shard_map/all_gather | solution.py:56
  8.7 218.7 %all-gather.11.cloned.1.call-start = ((), (), s32[]{:S(2)}) async-start(), calls=%async_computation.3 | async-start | bytes 2162688 | tf_op jit(solution)/shard_map/all_gather | solution.py:55
  9.4 277.7 %all-gather.13.cloned.1.call-start = ((), (), s32[]{:S(2)}) async-start(), calls=%async_computation.4 | async-start | bytes 2162688 | tf_op jit(solution)/shard_map/all_gather | solution.py:58
  10.0 501.8 %reduce-scatter.2.cloned.1.call-start = ((), (), s32[]{:S(2)}) async-start(), calls=%async_computation.5 | async-start | bytes 2162688 | tf_op jit(solution)/shard_map/reduce_scatter | solution.py:106
  145.4 84.2 %collective-permute-start.1 = (bf16[128,2048]{1,0:T(8,128)(2,1)S(1)}, bf16[128,2048]{1,0:T(8,128)(2,1)S(1)}, u32[]{:S(2)}, u32[]{:S(2)}) collective-permute-start(bf16[128,2048]{1,0:T(8,128)(2,1)S(1)} %pad_maximum_fusion.2), channel_id=1, source_target_pairs={{1,0},{2,1},{3,2},{4,3},{5,4},{6,5},{7,6},{8,7},{9,8},{10,9},{11,1... | collective-permute-start | bytes 1572872 | tf_op jit(solution)/shard_map/ppermute | solution.py:26
  153.7 76.0 %collective-permute-start = (bf16[128,2048]{1,0:T(8,128)(2,1)S(1)}, bf16[128,2048]{1,0:T(8,128)(2,1)S(1)}, u32[]{:S(2)}, u32[]{:S(2)}) collective-permute-start(bf16[128,2048]{1,0:T(8,128)(2,1)S(1)} %pad_maximum_fusion.2), channel_id=1, source_target_pairs={{0,1},{1,2},{2,3},{3,4},{4,5},{5,6},{6,7},{7,8},{8,9},{9,10},{10,1... | collective-permute-start | bytes 1572872 | tf_op jit(solution)/shard_map/ppermute | solution.py:23
  230.3 4.1 copy-start.10
  230.7 3.7 copy-start.12
  233.3 53.8 %copy-start.5 = (bf16[128,1024]{1,0:T(8,128)(2,1)S(1)}, bf16[128,1024]{1,0:T(8,128)(2,1)}, u32[]{:S(2)}) copy-start(bf16[128,1024]{1,0:T(8,128)(2,1)} %param.19) | copy-start | bytes 786436
  233.3 53.8 %copy-start.6 = (bf16[1,128,1024]{2,1,0:T(8,128)(2,1)S(1)}, bf16[1,128,1024]{2,1,0:T(8,128)(2,1)}, u32[]{:S(2)}) copy-start(bf16[1,128,1024]{2,1,0:T(8,128)(2,1)} %param.18) | copy-start | bytes 786436
  234.4 99.6 %copy-start.11 = (bf16[16,64,128]{2,1,0:T(8,128)(2,1)}, bf16[16,64,128]{2,1,0:T(8,128)(2,1)S(1)}, u32[]{:S(2)}) copy-start(bf16[16,64,128]{2,1,0:T(8,128)(2,1)S(1)} %convolution_convert_fusion.2) | copy-start | bytes 786436
  234.4 100.5 %copy-start.15 = (bf16[100,128]{1,0:T(8,128)(2,1)S(1)}, bf16[100,128]{1,0:T(8,128)(2,1)}, u32[]{:S(2)}) copy-start(bf16[100,128]{1,0:T(8,128)(2,1)} %param.26) | copy-start | bytes 76804
  234.4 100.5 %copy-start.17 = (f32[128]{0:T(128)S(1)}, f32[128]{0:T(128)}, u32[]{:S(2)}) copy-start(f32[128]{0:T(128)} %param.27) | copy-start | bytes 1540
  334.9 3.5 copy-start.4
  338.4 338.1 %all-reduce.2.cloned.1.call-start = ((), (), s32[]{:S(2)}) async-start(), calls=%async_computation.6 | async-start | bytes 131072 | tf_op jit(solution)/shard_map/psum | solution.py:114
  340.0 4.6 copy-start.14
  360.5 3.5 copy-start.7
  365.4 142.8 %collective-permute-start.3 = (bf16[128,2048]{0,1:T(8,128)(2,1)}, bf16[128,2048]{0,1:T(8,128)(2,1)}, u32[]{:S(2)}, u32[]{:S(2)}) collective-permute-start(bf16[128,2048]{0,1:T(8,128)(2,1)} %get-tuple-element.46), channel_id=1, source_target_pairs={{0,15},{1,0},{2,1},{3,2},{4,3},{5,4},{6,5},{7,6},{8,7},{9,8},{10,9... | collective-permute-start | bytes 1572872 | tf_op jit(solution)/shard_map/ppermute | solution.py:34
  374.4 133.9 %collective-permute-start.2 = (bf16[128,2048]{0,1:T(8,128)(2,1)}, bf16[128,2048]{0,1:T(8,128)(2,1)}, u32[]{:S(2)}, u32[]{:S(2)}) collective-permute-start(bf16[128,2048]{0,1:T(8,128)(2,1)} %get-tuple-element.45), channel_id=1, source_target_pairs={{0,1},{1,2},{2,3},{3,4},{4,5},{5,6},{6,7},{7,8},{8,9},{9,10},{10,1... | collective-permute-start | bytes 1572872 | tf_op jit(solution)/shard_map/ppermute | solution.py:34
  489.0 17.2 %copy-start.2 = (bf16[1024,1024]{1,0:T(8,128)(2,1)S(1)}, bf16[1024,1024]{1,0:T(8,128)(2,1)}, u32[]{:S(2)}) copy-start(bf16[1024,1024]{1,0:T(8,128)(2,1)} %all-gather.11.cloned.1.call-done) | copy-start | bytes 6291460
  506.3 3.7 copy-start.3
  508.2 2.6 copy-start.1
  (5 other events, 8.8 us)
Sparse Core Ops, SparseCore 0:
  10.2 69.1 all-gather.8
  81.5 61.8 all-gather.6
  145.5 81.8 all-gather.10
  229.4 57.6 all-gather.12
  338.5 162.0 reduce-scatter.1
  511.9 164.5 all-reduce.1
where the time goes:
time: 693 us; the launch traced here: 686 us
  waiting for transfers between devices  420 us (61%)
  blocking collectives  157 us (23%)
  matrix products  59 us (9%)
  starting transfers between devices  20.6 us (3%)
  between operations  16.3 us (2%)
  other arithmetic  8.38 us (1%)
    psum x1, waiting for transfers between devices, per_device(): grad_out_proj = lax.psum(shard_grad, 'node').astype(jnp.float32)  164 us
    psum x1, blocking collectives, per_device(): lax.psum(loss_part, ('ens', 'node')) / (members * total_nodes * variables)  112 us
    all_gather x1, waiting for transfers between devices, per_device(): full_query = lax.all_gather(w_query, 'ens', axis=0, tiled=True)  71.8 us
    all_gather x1, waiting for transfers between devices, per_device(): full_value = lax.all_gather(w_value, 'ens', axis=0, tiled=True)  66.9 us
    all_gather x1, waiting for transfers between devices, per_device(): full_key = lax.all_gather(w_key, 'ens', axis=0, tiled=True)  62 us
    all_gather x1, waiting for transfers between devices, per_device(): full_out = lax.all_gather(w_out, 'ens', axis=0, tiled=True)  52.7 us
    all_gather x1, blocking collectives, per_device(): lax.all_gather(pred_b[None], 'ens', axis=0, tiled=True).astype(jnp.float32)  44.6 us
    dot_general x1, matrix products, per_device(): jnp.einsum('hqk,khd->qhd', grad_scores, key3, preferred_element_type=jnp....  17.2 us
  transfers between devices with their start and end apart: 10, of which 5 were waited for; matrix products, arithmetic and copies ran while one was open for 9% of the time, Pallas kernels for 0%

commit v1 on v0

v1 whole, which is shorter than its diff:
```python
import math

import jax
import jax.numpy as jnp
from jax import lax
from jax.sharding import PartitionSpec as P

HEADS = 16
HALO = 128
LANES = 128


ALPHA = 0.95
KAPPA = 0.25
EPS_NORM = 1e-05


def extended_2(block, sides, width):
    for axis, dim in sides:
        count = lax.axis_size(axis)
        forward = [(i, i + 1) for i in range(count - 1)]
        forward.append((count - 1, 0))
        backward = [(target, source) for source, target in forward]
        low = lax.ppermute(
            lax.slice_in_dim(block, block.shape[dim] - width, None, axis=dim), axis, forward
        )
        high = lax.ppermute(lax.slice_in_dim(block, 0, width, axis=dim), axis, backward)
        block = jnp.concatenate([low, block, high], axis=dim)
    return block


def shifted(value, axis, steps):
    count = lax.axis_size(axis)
    pairs = [(source, (source + steps) % count) for source in range(count)]
    return lax.ppermute(value, axis, pairs)


def smooth_abs(delta):
    return jnp.sqrt(delta * delta + KAPPA * KAPPA) - KAPPA


def smooth_slope(delta):
    return delta / jnp.sqrt(delta * delta + KAPPA * KAPPA)


def per_device(
    hidden, forcing, norm_gain, w_query, w_key, w_value, w_out, w_decode, targets, area_weight
):
    f32, b16 = jnp.float32, jnp.bfloat16
    node_rows = hidden.shape[1]
    width = hidden.shape[2]
    head_size = width // HEADS
    span = node_rows + 2 * HALO
    scale = 1.0 / math.sqrt(head_size)
    members = lax.axis_size("ens")
    shards = lax.axis_size("node")
    rows = w_query.shape[0]
    variables = w_decode.shape[1]
    decode = jnp.pad(w_decode, ((0, 0), (0, LANES - variables)))
    mixed = jnp.dot(w_out, decode, preferred_element_type=f32).astype(b16)
    packed = jnp.concatenate([w_query, w_key, w_value, mixed], 1)
    full = lax.all_gather(packed, "ens", axis=0, tiled=True)
    full_query = full[:, :width]
    full_key = full[:, width : 2 * width]
    full_value = full[:, 2 * width : 3 * width]
    full_mixed = full[:, 3 * width :]
    xfield = hidden[0].astype(f32) + forcing.astype(f32)
    inverse_rms = lax.rsqrt(jnp.mean(xfield * xfield, -1, keepdims=True) + EPS_NORM)
    normed = (xfield * inverse_rms * norm_gain).astype(b16)
    queries = jnp.dot(normed, full_query, preferred_element_type=f32).astype(b16)
    keys_local = jnp.dot(normed, full_key, preferred_element_type=f32).astype(b16)
    values_local = jnp.dot(normed, full_value, preferred_element_type=f32).astype(b16)
    paired = jnp.concatenate([keys_local, values_local], 1)
    extended = extended_2(paired, (("node", 0),), HALO)
    query3 = queries.reshape(node_rows, HEADS, head_size)
    key3 = extended[:, :width].reshape(span, HEADS, head_size)
    value3 = extended[:, width:].reshape(span, HEADS, head_size)
    query_pos = lax.broadcasted_iota(jnp.int32, (node_rows, span), 0)
    key_pos = lax.broadcasted_iota(jnp.int32, (node_rows, span), 1)
    offset = key_pos - query_pos
    window = (offset >= 0) & (offset <= 2 * HALO)
    scores = jnp.einsum("qhd,khd->hqk", query3, key3, preferred_element_type=f32) * scale
    expo = jnp.where(window[None], jnp.exp(scores), f32(0.0))
    probs = expo / jnp.sum(expo, -1, keepdims=True)
    probs_b = probs.astype(b16)
    attended = jnp.einsum("hqk,khd->qhd", probs_b, value3, preferred_element_type=f32)
    attended = attended.astype(b16).reshape(node_rows, width)
    contract0 = (((0,), (1,)), ((), ()))
    pred_b = (
        lax.dot_general(decode, hidden[0], contract0, preferred_element_type=f32)
        + lax.dot_general(decode, forcing, contract0, preferred_element_type=f32)
        + lax.dot_general(full_mixed, attended, contract0, preferred_element_type=f32)
    )[:variables].astype(b16)
    eps = (1.0 - ALPHA) / members
    coeff = (1.0 - eps) / (2.0 * (members - 1))
    own = pred_b.astype(f32)
    others = lax.all_to_all(
        jnp.broadcast_to(pred_b[None], (members,) + pred_b.shape), "ens", 0, 0, tiled=True
    )
    delta = own[None] - others.astype(f32)
    pair_abs = jnp.sum(smooth_abs(delta), 0)
    pair_slope = jnp.sum(smooth_slope(delta), 0)
    truth = targets.astype(f32)
    weights = area_weight[None, :]
    entries = smooth_abs(own - truth) - coeff * pair_abs
    loss_part = jnp.sum(weights * entries)
    grad_pred = (weights * (smooth_slope(own - truth) - 2.0 * coeff * pair_slope)).astype(b16)
    grad_pred = jnp.pad(grad_pred, ((0, LANES - variables), (0, 0)))
    grad_resid = lax.dot_general(
        grad_pred, decode, (((0,), (1,)), ((), ())), preferred_element_type=f32
    )
    gram = lax.dot_general(
        attended, grad_pred, (((0,), (1,)), ((), ())), preferred_element_type=f32
    ).astype(b16)
    loss_high = loss_part.astype(b16)
    loss_rest = loss_part - loss_high.astype(f32)
    loss_mid = loss_rest.astype(b16)
    loss_low = (loss_rest - loss_mid.astype(f32)).astype(b16)
    column = lax.broadcasted_iota(jnp.int32, gram.shape, 1)
    gram = jnp.where(column == variables, loss_high, gram)
    gram = jnp.where(column == variables + 1, loss_mid, gram)
    gram = jnp.where(column == variables + 2, loss_low, gram)
    parts = lax.all_to_all(gram.reshape(members, rows, LANES), "ens", 0, 0, tiled=True)
    part = jnp.sum(parts.astype(f32), 0)
    parts = lax.all_to_all(
        jnp.broadcast_to(part[None], (shards,) + part.shape), "node", 0, 0, tiled=True
    )
    total = jnp.sum(parts, 0)
    grad_out_proj = lax.dot_general(
        total[:, :variables],
        w_decode.astype(f32),
        (((1,), (1,)), ((), ())),
        preferred_element_type=f32,
    )
    loss = jnp.sum(total[0, variables : variables + 3]) / (members * node_rows * shards * variables)
    grad_attended = lax.dot_general(
        grad_pred, full_mixed, (((0,), (1,)), ((), ())), preferred_element_type=f32
    ).astype(b16)
    grad3 = grad_attended.reshape(node_rows, HEADS, head_size)
    grad_probs = jnp.einsum("qhd,khd->hqk", grad3, value3, preferred_element_type=f32)
    delta_row = jnp.sum(probs * grad_probs, -1, keepdims=True)
    grad_scores = (probs * (grad_probs - delta_row) * scale).astype(b16)
    grad_queries = jnp.einsum("hqk,khd->qhd", grad_scores, key3, preferred_element_type=f32)
    grad_queries = grad_queries.astype(b16).reshape(node_rows, width)
    grad_key_ext = jnp.einsum(
        "hqk,qhd->khd", grad_scores, query3, preferred_element_type=f32
    ).reshape(span, width)
    grad_value_ext = jnp.einsum(
        "hqk,qhd->khd", probs_b, grad3, preferred_element_type=f32
    ).reshape(span, width)
    grad_ext = jnp.concatenate([grad_key_ext, grad_value_ext], 1)
    from_right = shifted(grad_ext[:HALO].astype(b16), "node", -1).astype(f32)
    from_left = shifted(grad_ext[node_rows + HALO :].astype(b16), "node", 1).astype(f32)
    inner = grad_ext[HALO : HALO + node_rows]
    inner = inner.at[:HALO].add(from_left)
    inner = inner.at[node_rows - HALO :].add(from_right)
    grad_keys = inner[:, :width].astype(b16)
    grad_values = inner[:, width:].astype(b16)
    contract = (((1,), (1,)), ((), ()))
    grad_normed = (
        lax.dot_general(grad_queries, full_query, contract, preferred_element_type=f32)
        + lax.dot_general(grad_keys, full_key, contract, preferred_element_type=f32)
        + lax.dot_general(grad_values, full_value, contract, preferred_element_type=f32)
    )
    scaled = norm_gain * grad_normed
    grad_x = inverse_rms * scaled - xfield * inverse_rms**3 * jnp.mean(
        xfield * scaled, -1, keepdims=True
    )
    grad_hidden = (grad_resid + grad_x).astype(b16)[None]
    return (grad_hidden, grad_out_proj, loss)


def solution(mesh):
    placed = (
        P("ens", "node", None),
        P("node", None),
        P(),
        P("ens", None),
        P("ens", None),
        P("ens", None),
        P("ens", None),
        P(),
        P(None, "node"),
        P("node"),
    )
    return jax.shard_map(
        per_device,
        mesh=mesh,
        in_specs=placed,
        out_specs=(P("ens", "node", None), P("ens", None), P()),
        check_vma=False,
    )
```

time: 693 us -> 266 us (0.38)
  waiting for transfers between devices: 420 us -> 127 us
  blocking collectives: 157 us -> 0 us
  starting transfers between devices: 20.6 us -> 36.2 us
    all_gather x4 -> x1, waiting for transfers between devices: 253 us -> 72.3 us  [per_device(): full = lax.all_gather(packed, 'ens', axis=0, tiled=True)]
    psum x1 -> x0, waiting for transfers between devices: 164 us -> none  [per_device(): grad_out_proj = lax.psum(shard_grad, 'node').astype(jnp.float32)]
    psum x1 -> x0, blocking collectives: 112 us -> none  [per_device(): lax.psum(loss_part, ('ens', 'node')) / (members * total_nodes * variables)]
    all_gather x1 -> x0, blocking collectives: 44.6 us -> none  [per_device(): lax.all_gather(pred_b[None], 'ens', axis=0, tiled=True).astype(jnp.float32)]
    all_to_all x0 -> x3, waiting for transfers between devices: none -> 28.7 us  [the longest x1 23.7 us: per_device(): lax.all_to_all(jnp.broadcast_to(pred_b[None], (members,) + pred_b.shape),...]
    all_to_all x0 -> x3, starting transfers between devices: none -> 15 us  [the longest x1 6.34 us: per_device(): lax.all_to_all(jnp.broadcast_to(pred_b[None], (members,) + pred_b.shape),...]
    ppermute x1, waiting for transfers between devices: 0.01 us -> 13.2 us  [extended_2(): lax.ppermute(lax.slice_in_dim(block, block.shape[dim] - width, None, axis...]
    ppermute x1, waiting for transfers between devices: 0.01 us -> 12.9 us  [extended_2(): lax.ppermute(lax.slice_in_dim(block, 0, width, axis=dim), axis, backward)]
  transfers between devices with their start and end apart: 10 -> 8, of which waited for: 5 -> 5; matrix products, arithmetic and copies ran while one was open for 9% -> 21% of each run, Pallas kernels for 0% -> 0%
where the time goes in v1:
time: 266 us; the launch traced here: 263 us
  waiting for transfers between devices  127 us (48%)
  matrix products  64.2 us (24%)
  starting transfers between devices  36.2 us (14%)
  between operations  17.6 us (7%)
  other arithmetic  11.2 us (4%)
  local copies, waits for them, and re-layouts  6.83 us (3%)
    all_gather x1, waiting for transfers between devices, per_device(): full = lax.all_gather(packed, 'ens', axis=0, tiled=True)  72.3 us
    all_to_all x1, waiting for transfers between devices, per_device(): lax.all_to_all(jnp.broadcast_to(pred_b[None], (members,) + pred_b.shape),...  23.7 us
    dot_general x1, matrix products, per_device(): jnp.einsum('hqk,khd->qhd', grad_scores, key3, preferred_element_type=f32)  17 us
    dot_general x1, matrix products, per_device(): jnp.einsum('hqk,qhd->khd', grad_scores, query3, preferred_element_type=f32)  16.2 us
    ppermute x1, waiting for transfers between devices, extended_2(): lax.ppermute(lax.slice_in_dim(block, block.shape[dim] - width, None, axis...  13.2 us
    ppermute x1, waiting for transfers between devices, extended_2(): lax.ppermute(lax.slice_in_dim(block, 0, width, axis=dim), axis, backward)  12.9 us
    ppermute x2, starting transfers between devices, shifted(): return lax.ppermute(value, axis, pairs)  11.3 us
    ppermute x1, starting transfers between devices, extended_2(): lax.ppermute(lax.slice_in_dim(block, 0, width, axis=dim), axis, backward)  7.99 us
  transfers between devices with their start and end apart: 8, of which 5 were waited for; matrix products, arithmetic and copies ran while one was open for 21% of the time, Pallas kernels for 0%

profile of v1, /device:TPU:1, one launch (start us, length us, event | category | flops | bytes accessed | tf_op | source)
XLA Modules:
  0.0 263.1 jit_solution(16411555913563230172)
XLA Ops:
  9.1 1.6 pad_maximum_fusion.3
  14.4 72.3 %all-gather.2.cloned.1.call-done = bf16[1024,3200]{1,0:T(8,128)(2,1)} async-done(((bf16[32,3200]{1,0:T(8,128)(2,1)}), bf16[1024,3200]{1,0:T(8,128)(2,1)}) %all-gather.2.cloned.1.call-update) | async-done | bytes 6553616 | tf_op jit(solution)/shard_map/all_gather | solution.py:62
  86.7 2.0 fusion.42
  88.8 2.0 fusion.39
  90.8 8.0 %collective-permute-start.1 = (bf16[128,2048]{1,0:T(8,128)(2,1)S(1)}, bf16[128,2048]{1,0:T(8,128)(2,1)S(1)}, u32[]{:S(2)}, u32[]{:S(2)}) collective-permute-start(bf16[128,2048]{1,0:T(8,128)(2,1)S(1)} %pad_maximum_fusion.2), channel_id=1, source_target_pairs={{1,0},{2,1},{3,2},{4,3},{5,4},{6,5},{7,6},{8,7},{9,8},{10,9},{11,1... | collective-permute-start | bytes 1572872 | tf_op jit(solution)/shard_map/ppermute | solution.py:27
  98.8 1.9 collective-permute-start
  102.3 2.0 fusion.45
  105.2 12.9 %collective-permute-done.1 = bf16[128,2048]{1,0:T(8,128)(2,1)S(1)} collective-permute-done((bf16[128,2048]{1,0:T(8,128)(2,1)S(1)}, bf16[128,2048]{1,0:T(8,128)(2,1)S(1)}, u32[]{:S(2)}, u32[]{:S(2)}) %collective-permute-start.1) | collective-permute-done | bytes 524320 | tf_op jit(solution)/shard_map/ppermute | solution.py:27
  118.1 13.2 %collective-permute-done = bf16[128,2048]{1,0:T(8,128)(2,1)S(1)} collective-permute-done((bf16[128,2048]{1,0:T(8,128)(2,1)S(1)}, bf16[128,2048]{1,0:T(8,128)(2,1)S(1)}, u32[]{:S(2)}, u32[]{:S(2)}) %collective-permute-start) | collective-permute-done | bytes 524320 | tf_op jit(solution)/shard_map/ppermute | solution.py:24
  132.3 1.9 fusion.4
  138.9 6.3 %all-to-all-start = ((bf16[32,100,128]{2,1,0:T(8,128)(2,1)}), bf16[32,100,128]{2,1,0:T(8,128)(2,1)S(1)}, u32[]{:S(2)}, u32[]{:S(2)}) async-start(bf16[32,100,128]{2,1,0:T(8,128)(2,1)} %broadcast_in_dim.48), calls=%async_computation | async-start | bytes 1703936 | tf_op jit(solution)/shard_map/all_to_all | solution.py:97
  145.3 23.7 %all-to-all-done = bf16[32,100,128]{2,1,0:T(8,128)(2,1)S(1)} async-done(((bf16[32,100,128]{2,1,0:T(8,128)(2,1)}), bf16[32,100,128]{2,1,0:T(8,128)(2,1)S(1)}, u32[]{:S(2)}, u32[]{:S(2)}) %all-to-all-start) | async-done | bytes 819232 | tf_op jit(solution)/shard_map/all_to_all | solution.py:97
  172.5 2.9 %fusion.60 = f32[16,64,384]{2,1,0:T(8,128)S(1)} fusion(bf16[128,16,64]{0,2,1:T(8,128)(2,1)S(1)} %bitcast.51, f32[16,128,384]{2,1,0:T(8,128)} %copy-done.15, f32[16,128]{1,0:T(8,128)S(1)} %get-tuple-element.55, pred[128,384]{1,0:T(8,128)(4,1)S(1)} %copy-done.11), kind=kOutput, calls=%fused_computation.55 | convolution fusion | flops 103809024 | bytes 5038080 | tf_op jit(solution)/shard_map/hqk,qhd->khd/dot_general | solution.py:148
  175.4 2.3 fusion.104
  179.9 4.4 %all-to-all-start.1 = ((bf16[32,32,128]{2,1,0:T(8,128)(2,1)}), bf16[32,32,128]{2,1,0:T(8,128)(2,1)}, u32[]{:S(2)}, u32[]{:S(2)}) async-start(bf16[32,32,128]{2,1,0:T(8,128)(2,1)} %bitcast.16), calls=%async_computation.1 | async-start | bytes 524288 | tf_op jit(solution)/shard_map/all_to_all | solution.py:123
  184.3 16.2 %fusion.8 = f32[16,64,384]{2,1,0:T(8,128)S(1)} fusion(bf16[128,16,64]{0,2,1:T(8,128)(2,1)} %bitcast.56, f32[16,128,384]{2,1,0:T(8,128)} %fusion.104, f32[16,128,384]{2,1,0:T(8,128)} %copy-done.15, f32[16,128]{1,0:T(8,128)S(1)} %get-tuple-element.55, pred[128,384]{1,0:T(8,128)(4,1)} %fusion.77), kind=kOutput, calls=%fused_computation.11 | convolution fusion | flops 109316480 | bytes 8183808 | tf_op jit(solution)/shard_map/hqk,qhd->khd/dot_general | solution.py:145
  201.8 1.9 collective-permute-start.2
  203.7 9.4 %collective-permute-start.3 = (bf16[128,2048]{0,1:T(8,128)(2,1)}, bf16[128,2048]{0,1:T(8,128)(2,1)}, u32[]{:S(2)}, u32[]{:S(2)}) collective-permute-start(bf16[128,2048]{0,1:T(8,128)(2,1)} %get-tuple-element.48), channel_id=1, source_target_pairs={{0,15},{1,0},{2,1},{3,2},{4,3},{5,4},{6,5},{7,6},{8,7},{9,8},{10,9... | collective-permute-start | bytes 1572872 | tf_op jit(solution)/shard_map/ppermute | solution.py:35
  213.1 17.0 %fusion.48 = bf16[16,64,128]{2,1,0:T(8,128)(2,1)} fusion(bf16[384,16,64]{0,2,1:T(8,128)(2,1)} %bitcast.54, f32[16,128,384]{2,1,0:T(8,128)} %fusion.104, f32[16,128,384]{2,1,0:T(8,128)} %copy-done.15, f32[16,128]{1,0:T(8,128)S(1)} %get-tuple-element.55, pred[128,384]{1,0:T(8,128)(4,1)} %fusion.77), kind=kOutput, calls=%fused_computation.41 | convolution fusion | flops 109447552 | bytes 7397376 | tf_op jit(solution)/shard_map/hqk,khd->qhd/dot_general | solution.py:143
  230.1 3.3 %fusion.13 = f32[128,1024]{1,0:T(8,128)} fusion(bf16[128,1024]{0,1:T(8,128)(2,1)} %bitcast.59, bf16[1024,3200]{1,0:T(8,128)(2,1)} %all-gather.2.cloned.1.call-done), kind=kOutput, calls=%fused_computation.13 | convolution fusion | flops 268435456 | bytes 2883584 | tf_op jit(solution)/shard_map/dot_general | solution.py:161
  235.2 4.2 %all-to-all-start.2 = ((f32[16,32,128]{2,1,0:T(8,128)}), f32[16,32,128]{2,1,0:T(8,128)}, u32[]{:S(2)}, u32[]{:S(2)}) async-start(f32[16,32,128]{2,1,0:T(8,128)} %broadcast_in_dim.53), calls=%async_computation.2 | async-start | bytes 524288 | tf_op jit(solution)/shard_map/all_to_all | solution.py:125
  240.9 2.5 fusion.17
  243.4 2.6 multiply_reduce_fusion.1
  246.9 5.0 %all-to-all-done.2 = f32[16,32,128]{2,1,0:T(8,128)} async-done(((f32[16,32,128]{2,1,0:T(8,128)}), f32[16,32,128]{2,1,0:T(8,128)}, u32[]{:S(2)}, u32[]{:S(2)}) %all-to-all-start.2) | async-done | bytes 262176 | tf_op jit(solution)/shard_map/all_to_all | solution.py:125
  (71 shorter events, 25.9 us)
Async XLA Ops:
  7.2 0.8 copy-start
  7.2 79.5 %all-gather.2.cloned.1.call-start = ((), (), s32[]{:S(2)}) async-start(), calls=%async_computation.3 | async-start | bytes 6758400 | tf_op jit(solution)/shard_map/all_gather | solution.py:62
  14.4 87.0 %copy-start.1 = (bf16[128,1024]{1,0:T(8,128)(2,1)S(1)}, bf16[128,1024]{1,0:T(8,128)(2,1)}, u32[]{:S(2)}) copy-start(bf16[128,1024]{1,0:T(8,128)(2,1)} %param.19) | copy-start | bytes 786436
  14.4 87.0 %copy-start.3 = (bf16[1024,100]{0,1:T(8,128)(2,1)S(1)}, bf16[1024,100]{0,1:T(8,128)(2,1)}, u32[]{:S(2)}) copy-start(bf16[1024,100]{0,1:T(8,128)(2,1)} %param.25) | copy-start | bytes 614404
  90.8 27.3 %collective-permute-start.1 = (bf16[128,2048]{1,0:T(8,128)(2,1)S(1)}, bf16[128,2048]{1,0:T(8,128)(2,1)S(1)}, u32[]{:S(2)}, u32[]{:S(2)}) collective-permute-start(bf16[128,2048]{1,0:T(8,128)(2,1)S(1)} %pad_maximum_fusion.2), channel_id=1, source_target_pairs={{1,0},{2,1},{3,2},{4,3},{5,4},{6,5},{7,6},{8,7},{9,8},{10,9},{11,1... | collective-permute-start | bytes 1572872 | tf_op jit(solution)/shard_map/ppermute | solution.py:27
  98.8 32.4 %collective-permute-start = (bf16[128,2048]{1,0:T(8,128)(2,1)S(1)}, bf16[128,2048]{1,0:T(8,128)(2,1)S(1)}, u32[]{:S(2)}, u32[]{:S(2)}) collective-permute-start(bf16[128,2048]{1,0:T(8,128)(2,1)S(1)} %pad_maximum_fusion.2), channel_id=1, source_target_pairs={{0,1},{1,2},{2,3},{3,4},{4,5},{5,6},{6,7},{7,8},{8,9},{9,10},{10,1... | collective-permute-start | bytes 1572872 | tf_op jit(solution)/shard_map/ppermute | solution.py:24
  131.9 3.4 %copy-start.5 = (bf16[384,1024]{0,1:T(8,128)(2,1)}, bf16[384,1024]{0,1:T(8,128)(2,1)S(1)}, u32[]{:S(2)}) copy-start(bf16[384,1024]{0,1:T(8,128)(2,1)S(1)} %copy.37) | copy-start | bytes 2359300
  131.9 2.3 copy-start.10
  134.2 1.7 copy-start.15
  134.2 3.6 %copy-start.9 = (f32[128,128]{1,0:T(8,128)S(1)}, f32[128,128]{1,0:T(8,128)}, u32[]{:S(2)}) copy-start(f32[128,128]{1,0:T(8,128)} %fusion.69) | copy-start | bytes 196612
  135.9 0.7 copy-start.7
  135.9 34.5 %copy-start.12 = (bf16[100,128]{1,0:T(8,128)(2,1)S(1)}, bf16[100,128]{1,0:T(8,128)(2,1)}, u32[]{:S(2)}) copy-start(bf16[100,128]{1,0:T(8,128)(2,1)} %param.26) | copy-start | bytes 76804
  135.9 34.5 %copy-start.14 = (f32[128]{0:T(128)S(1)}, f32[128]{0:T(128)}, u32[]{:S(2)}) copy-start(f32[128]{0:T(128)} %param.27) | copy-start | bytes 1540
  136.6 35.8 %copy-start.11 = (pred[128,384]{1,0:T(8,128)(4,1)S(1)}, pred[128,384]{1,0:T(8,128)(4,1)}, u32[]{:S(2)}) copy-start(pred[128,384]{1,0:T(8,128)(4,1)} %fusion.77) | copy-start | bytes 147460
  138.9 30.1 %all-to-all-start = ((bf16[32,100,128]{2,1,0:T(8,128)(2,1)}), bf16[32,100,128]{2,1,0:T(8,128)(2,1)S(1)}, u32[]{:S(2)}, u32[]{:S(2)}) async-start(bf16[32,100,128]{2,1,0:T(8,128)(2,1)} %broadcast_in_dim.48), calls=%async_computation | async-start | bytes 1703936 | tf_op jit(solution)/shard_map/all_to_all | solution.py:97
  175.4 3.6 %copy-start.8 = (bf16[16,64,128]{2,1,0:T(8,128)(2,1)S(1)}, bf16[16,64,128]{2,1,0:T(8,128)(2,1)}, u32[]{:S(2)}) copy-start(bf16[16,64,128]{2,1,0:T(8,128)(2,1)} %copy-done.7) | copy-start | bytes 786436
  179.9 53.5 %all-to-all-start.1 = ((bf16[32,32,128]{2,1,0:T(8,128)(2,1)}), bf16[32,32,128]{2,1,0:T(8,128)(2,1)}, u32[]{:S(2)}, u32[]{:S(2)}) async-start(bf16[32,32,128]{2,1,0:T(8,128)(2,1)} %bitcast.16), calls=%async_computation.1 | async-start | bytes 524288 | tf_op jit(solution)/shard_map/all_to_all | solution.py:123
  201.8 37.6 %collective-permute-start.2 = (bf16[128,2048]{0,1:T(8,128)(2,1)}, bf16[128,2048]{0,1:T(8,128)(2,1)}, u32[]{:S(2)}, u32[]{:S(2)}) collective-permute-start(bf16[128,2048]{0,1:T(8,128)(2,1)} %get-tuple-element.47), channel_id=1, source_target_pairs={{0,1},{1,2},{2,3},{3,4},{4,5},{5,6},{6,7},{7,8},{8,9},{9,10},{10,1... | collective-permute-start | bytes 1572872 | tf_op jit(solution)/shard_map/ppermute | solution.py:35
  203.7 35.7 %collective-permute-start.3 = (bf16[128,2048]{0,1:T(8,128)(2,1)}, bf16[128,2048]{0,1:T(8,128)(2,1)}, u32[]{:S(2)}, u32[]{:S(2)}) collective-permute-start(bf16[128,2048]{0,1:T(8,128)(2,1)} %get-tuple-element.48), channel_id=1, source_target_pairs={{0,15},{1,0},{2,1},{3,2},{4,3},{5,4},{6,5},{7,6},{8,7},{9,8},{10,9... | collective-permute-start | bytes 1572872 | tf_op jit(solution)/shard_map/ppermute | solution.py:35
  235.2 16.8 %all-to-all-start.2 = ((f32[16,32,128]{2,1,0:T(8,128)}), f32[16,32,128]{2,1,0:T(8,128)}, u32[]{:S(2)}, u32[]{:S(2)}) async-start(f32[16,32,128]{2,1,0:T(8,128)} %broadcast_in_dim.53), calls=%async_computation.2 | async-start | bytes 524288 | tf_op jit(solution)/shard_map/all_to_all | solution.py:125
  239.4 4.0 %copy-start.2 = (bf16[1,128,1024]{2,1,0:T(8,128)(2,1)S(1)}, bf16[1,128,1024]{2,1,0:T(8,128)(2,1)}, u32[]{:S(2)}) copy-start(bf16[1,128,1024]{2,1,0:T(8,128)(2,1)} %param.18) | copy-start | bytes 786436
  239.4 4.0 %copy-start.6 = (f32[128,1024]{1,0:T(8,128)S(1)}, f32[128,1024]{1,0:T(8,128)}, u32[]{:S(2)}) copy-start(f32[128,1024]{1,0:T(8,128)} %fusion.13) | copy-start | bytes 1572868
  239.4 4.0 %copy-start.13 = (f32[1024]{0:T(1024)S(1)}, f32[1024]{0:T(1024)}, u32[]{:S(2)}) copy-start(f32[1024]{0:T(1024)} %param.20) | copy-start | bytes 12292
  240.9 5.1 %copy-start.4 = (bf16[1024,100]{0,1:T(8,128)(2,1)S(1)}, bf16[1024,100]{0,1:T(8,128)(2,1)}, u32[]{:S(2)}) copy-start(bf16[1024,100]{0,1:T(8,128)(2,1)} %param.25) | copy-start | bytes 614404
Sparse Core Ops, SparseCore 0:
  10.9 75.7 all-gather.1

commit v2 on v1

v2 whole, which is shorter than its diff:
```python
import math

import jax
import jax.numpy as jnp
from jax import lax
from jax.experimental import pallas as pl
from jax.experimental.pallas import tpu as pltpu
from jax.sharding import PartitionSpec as P

HEADS = 16
HALO = 128
LANES = 128
STEP = 256
VROWS = 112


ALPHA = 0.95
KAPPA = 0.25
EPS_NORM = 1e-05
FAR = -1e30

f32 = jnp.float32
b16 = jnp.bfloat16


def nn(a, b):
    return lax.dot_general(a, b, (((1,), (0,)), ((), ())), preferred_element_type=f32)


def nt(a, b):
    return lax.dot_general(a, b, (((1,), (1,)), ((), ())), preferred_element_type=f32)


def tn(a, b):
    return lax.dot_general(a, b, (((0,), (0,)), ((), ())), preferred_element_type=f32)


def whole(shape):
    return pl.BlockSpec(shape, lambda i: (0,) * len(shape))


def head_masks(value):
    lane = lax.broadcasted_iota(jnp.int32, (1, LANES), 1)
    first = jnp.where(lane < LANES // 2, value, 0.0).astype(b16)
    second = jnp.where(lane < LANES // 2, 0.0, value).astype(b16)
    return first, second


def window_mask(rows, span):
    offset = lax.broadcasted_iota(jnp.int32, (rows, span), 1) - lax.broadcasted_iota(
        jnp.int32, (rows, span), 0
    )
    return (offset >= 0) & (offset <= 2 * HALO)


def split_bf16(value, pieces):
    out = []
    for _ in range(pieces):
        piece = value.astype(b16)
        out.append(piece)
        value = value - piece.astype(f32)
    return out


def forward_kernel(
    scale, variables, low, own, high, wq, wk, wv, mixed, hidden, forcing, decode,
    queries, keys, values, attended, lse, pred, normed, total,
):
    step = pl.program_id(0)
    rows = own.shape[0]
    span = rows + 2 * HALO

    @pl.when(step == 0)
    def _():
        normed[:HALO] = low[...]
        normed[HALO : HALO + rows] = own[...]
        normed[HALO + rows :] = high[...]
        total[...] = nn(hidden[0], decode[...]) + nn(forcing[...], decode[...])

    field = normed[...]
    queries[...] = nn(field, wq[...]).astype(b16)
    keys[...] = nn(field, wk[...]).astype(b16)
    values[...] = nn(field, wv[...]).astype(b16)
    window = window_mask(rows, span)
    masks = head_masks(scale)
    lower = lax.broadcasted_iota(jnp.int32, (rows, LANES), 1) < LANES // 2
    for pair in range(STEP // LANES):
        cols = slice(pair * LANES, (pair + 1) * LANES)
        query = queries[HALO : HALO + rows, cols]
        key = keys[:, cols]
        value = values[:, cols]
        outs, stats = [], []
        for mask in masks:
            scores = jnp.where(window, nt(query * mask, key), FAR)
            top = jnp.max(scores, -1, keepdims=True)
            expo = jnp.exp(scores - top)
            norm = jnp.sum(expo, -1, keepdims=True)
            probs = (expo * (1.0 / norm)).astype(b16)
            outs.append(nn(probs, value))
            stats.append(top + jnp.log(norm))
        attended[:, cols] = jnp.where(lower, outs[0], outs[1]).astype(b16)
        lse[:, cols] = jnp.where(lower, stats[0], stats[1])
    total[...] += nn(attended[...], mixed[...])

    @pl.when(step == pl.num_programs(0) - 1)
    def _():
        pred[...] = total[...].T[:VROWS].astype(b16)


def loss_kernel(
    coeff, variables, others, pred, targets, weight, attended, mixed, lse,
    gram, halo, grad_attended,
):
    own = pred[...].astype(f32)
    rows = attended.shape[0]
    width = attended.shape[1]

    def member(index, carry):
        pair_abs, pair_slope = carry
        delta = own - others[index].astype(f32)
        square = delta * delta + KAPPA * KAPPA
        inverse = lax.rsqrt(square)
        return pair_abs + (square * inverse - KAPPA), pair_slope + delta * inverse

    zero = jnp.zeros((VROWS, LANES), f32)
    pair_abs, pair_slope = lax.fori_loop(0, others.shape[0], member, (zero, zero), unroll=4)
    delta = own - targets[...].astype(f32)
    square = delta * delta + KAPPA * KAPPA
    inverse = lax.rsqrt(square)
    real = lax.broadcasted_iota(jnp.int32, (VROWS, LANES), 0) < variables
    scale = weight[...]
    entries = jnp.where(real, scale * (square * inverse - KAPPA - coeff * pair_abs), 0.0)
    loss = jnp.sum(jnp.sum(entries, 0, keepdims=True), 1, keepdims=True)
    grad = jnp.where(real, scale * (delta * inverse - 2.0 * coeff * pair_slope), 0.0)
    grad_b = grad.astype(b16)
    halo[:VROWS] = grad_b
    grad_full = jnp.concatenate([grad, jnp.zeros((LANES - VROWS, LANES), f32)], 0)
    grad_t = grad_full.T.astype(b16)
    parts = nn(grad_full.astype(b16), attended[...])
    parts = parts.T
    column = lax.broadcasted_iota(jnp.int32, (width, LANES), 1)
    for index, piece in enumerate(split_bf16(loss, 3)):
        parts = jnp.where(column == variables + index, piece.astype(f32), parts)
    gram[...] = parts.astype(b16)
    grad_att = nt(grad_t, mixed[...]).astype(b16)
    grad_attended[...] = grad_att
    size = width // HEADS
    head = lax.broadcasted_iota(jnp.int32, (HEADS, width), 0)
    feature = lax.broadcasted_iota(jnp.int32, (HEADS, width), 1)
    inside = jnp.where((feature >= head * size) & (feature < (head + 1) * size), 1.0, 0.0)
    chosen = jnp.where(feature == head * size, 1.0, 0.0).astype(b16)
    inside = inside.astype(b16)
    product = grad_att.astype(f32) * attended[...].astype(f32)
    row_delta = sum(nt(inside, piece) for piece in split_bf16(product, 2))
    row_lse = sum(nt(chosen, piece) for piece in split_bf16(lse[...], 3))
    at = VROWS
    for piece in split_bf16(row_delta, 2) + split_bf16(row_lse, 3):
        halo[at : at + HEADS] = piece
        at += HEADS


def own_kernel(scale, query, keys, values, grad_att, lse, grad_query, grad_key, grad_value):
    rows = query.shape[0]
    span = keys.shape[0]
    window = window_mask(rows, span)
    scaled = head_masks(scale)
    plain = head_masks(1.0)
    center = slice(HALO, HALO + rows)
    for pair in range(STEP // LANES):
        cols = slice(pair * LANES, (pair + 1) * LANES)
        q, k, v, g = query[:, cols], keys[:, cols], values[:, cols], grad_att[:, cols]
        stats = lse[:, cols]
        d_query = d_key = d_value = None
        for half in range(2):
            q_half = q * scaled[half]
            g_half = g * plain[half]
            at = half * (LANES // 2)
            probs = jnp.where(window, jnp.exp(nt(q_half, k) - stats[:, at : at + 1]), 0.0)
            d_probs = nt(g_half, v)
            delta = jnp.sum(probs * d_probs, -1, keepdims=True)
            d_scores = (probs * (d_probs - delta)).astype(b16)
            probs = probs.astype(b16)
            dq = nn(d_scores, k * scaled[half])
            dk = tn(d_scores[:, center], q_half)
            dv = tn(probs[:, center], g_half)
            d_query = dq if d_query is None else d_query + dq
            d_key = dk if d_key is None else d_key + dk
            d_value = dv if d_value is None else d_value + dv
        grad_query[:, cols] = d_query.astype(b16)
        grad_key[:, cols] = d_key
        grad_value[:, cols] = d_value


def halo_kernel(
    scale, low, high, query_low, query_high, keys, values, grad_query, key_part, value_part,
    wq, wk, wv, mixed, hidden, forcing, inverse_rms, gain, halo, decode,
    grad_hidden, grad_t, stats, total,
):
    step = pl.program_id(0)
    rows = keys.shape[0]

    @pl.when(step == 0)
    def _():
        zero = jnp.zeros((LANES - VROWS, LANES), b16)
        for side, part in enumerate((low, high)):
            grad = jnp.concatenate([part[:VROWS], zero], 0)
            grad_t[side * HALO : (side + 1) * HALO] = grad.astype(f32).T.astype(b16)
            at = slice(side * HALO, (side + 1) * HALO)
            pieces = [
                part[VROWS + HEADS * n : VROWS + HEADS * (n + 1)].astype(f32) for n in range(5)
            ]
            stats[0, :, at] = pieces[0] + pieces[1]
            stats[1, :, at] = pieces[2] + pieces[3] + pieces[4]
        total[...] = jnp.zeros_like(total)

    key_at = lax.broadcasted_iota(jnp.int32, (rows, 2 * HALO), 0)
    query_at = lax.broadcasted_iota(jnp.int32, (rows, 2 * HALO), 1)
    window = ((query_at < HALO) & (query_at >= key_at)) | (
        (query_at >= HALO) & (query_at - HALO <= key_at)
    )
    scaled = head_masks(scale)
    plain = head_masks(1.0)
    grad_att = nt(grad_t[...], mixed[...]).astype(b16)
    per_step = 2 * (STEP // LANES)
    d_keys, d_values = [], []
    for pair in range(STEP // LANES):
        cols = slice(pair * LANES, (pair + 1) * LANES)
        q = jnp.concatenate([query_low[:, cols], query_high[:, cols]], 0)
        k, v, g = keys[:, cols], values[:, cols], grad_att[:, cols]
        d_key = key_part[:, cols]
        d_value = value_part[:, cols]
        for half in range(2):
            row = step * per_step + 2 * pair + half
            delta = stats[0, pl.ds(row, 1), :]
            lse = stats[1, pl.ds(row, 1), :]
            probs = jnp.where(window, jnp.exp(nt(k * scaled[half], q) - lse), 0.0)
            d_probs = nt(v * plain[half], g)
            d_scores = (probs * (d_probs - delta)).astype(b16)
            d_key = d_key + nn(d_scores, q * scaled[half])
            d_value = d_value + nn(probs.astype(b16), g * plain[half])
        d_keys.append(d_key.astype(b16))
        d_values.append(d_value.astype(b16))
    total[...] += (
        nt(grad_query[...], wq[...])
        + nt(jnp.concatenate(d_keys, 1), wk[...])
        + nt(jnp.concatenate(d_values, 1), wv[...])
    )

    @pl.when(step == pl.num_programs(0) - 1)
    def _():
        zero = jnp.zeros((LANES - VROWS, LANES), b16)
        own = jnp.concatenate([halo[:VROWS], zero], 0).astype(f32).T.astype(b16)
        grad_resid = nt(own, decode[...])
        xfield = hidden[0].astype(f32) + forcing[...].astype(f32)
        inverse = inverse_rms[...]
        grad = gain[...] * total[...]
        mean = jnp.mean(xfield * grad, -1, keepdims=True)
        result = grad_resid + inverse * grad - xfield * (inverse * inverse * inverse * mean)
        grad_hidden[0] = result.astype(b16)


def shifted(value, axis, steps):
    count = lax.axis_size(axis)
    pairs = [(source, (source + steps) % count) for source in range(count)]
    return lax.ppermute(value, axis, pairs)


def per_device(
    hidden, forcing, norm_gain, w_query, w_key, w_value, w_out, w_decode, targets, area_weight
):
    node_rows = hidden.shape[1]
    width = hidden.shape[2]
    head_size = width // HEADS
    span = node_rows + 2 * HALO
    scale = 1.0 / math.sqrt(head_size)
    members = lax.axis_size("ens")
    shards = lax.axis_size("node")
    rows = w_query.shape[0]
    variables = w_decode.shape[1]
    steps = width // STEP
    shape = jax.ShapeDtypeStruct
    params = pltpu.CompilerParams(
        dimension_semantics=("arbitrary",), vmem_limit_bytes=48 * 1024 * 1024
    )
    decode = jnp.pad(w_decode, ((0, 0), (0, LANES - variables)))
    mixed = jnp.dot(w_out, decode, preferred_element_type=f32).astype(b16)
    packed = jnp.concatenate([w_query, w_key, w_value, mixed], 1)
    full = lax.all_gather(packed, "ens", axis=0, tiled=True)
    xfield = hidden[0].astype(f32) + forcing.astype(f32)
    inverse_rms = lax.rsqrt(jnp.mean(xfield * xfield, -1, keepdims=True) + EPS_NORM)
    normed = (xfield * inverse_rms * norm_gain).astype(b16)
    low = shifted(normed, "node", 1)
    high = shifted(normed, "node", -1)

    def columns(at):
        return pl.BlockSpec((width, STEP), lambda i: (0, at * steps + i))

    def blocks(height, at=0):
        return pl.BlockSpec((height, STEP), lambda i: (at, i))

    mixed_block = pl.BlockSpec((STEP, LANES), lambda i: (i, 3 * width // LANES))
    own_block = whole((1, node_rows, width))
    queries, keys, values, attended, lse, pred = pl.pallas_call(
        lambda *refs: forward_kernel(scale, variables, *refs),
        grid=(steps,),
        in_specs=[
            whole((HALO, width)),
            whole((node_rows, width)),
            whole((HALO, width)),
            columns(0),
            columns(1),
            columns(2),
            mixed_block,
            own_block,
            whole((node_rows, width)),
            whole((width, LANES)),
        ],
        out_specs=[
            blocks(span),
            blocks(span),
            blocks(span),
            blocks(node_rows),
            blocks(node_rows),
            whole((VROWS, node_rows)),
        ],
        out_shape=[
            shape((span, width), b16),
            shape((span, width), b16),
            shape((span, width), b16),
            shape((node_rows, width), b16),
            shape((node_rows, width), f32),
            shape((VROWS, node_rows), b16),
        ],
        scratch_shapes=[
            pltpu.VMEM((span, width), b16),
            pltpu.VMEM((node_rows, LANES), f32),
        ],
        compiler_params=params,
        name="forward",
    )(low, normed, high, full, full, full, full, hidden, forcing, decode)

    others = lax.all_to_all(
        jnp.broadcast_to(pred[None], (members,) + pred.shape), "ens", 0, 0, tiled=True
    )
    eps = (1.0 - ALPHA) / members
    coeff = (1.0 - eps) / (2.0 * (members - 1))
    truth = jnp.pad(targets, ((0, VROWS - variables), (0, 0)))
    payload = VROWS + 5 * HEADS
    gram, halo, grad_attended = pl.pallas_call(
        lambda *refs: loss_kernel(coeff, variables, *refs),
        grid=(1,),
        in_specs=[
            whole((members, VROWS, node_rows)),
            whole((VROWS, node_rows)),
            whole((VROWS, node_rows)),
            whole((1, node_rows)),
            whole((node_rows, width)),
            pl.BlockSpec((width, LANES), lambda i: (0, 3 * width // LANES)),
            whole((node_rows, width)),
        ],
        out_specs=[
            whole((width, LANES)),
            whole((payload, node_rows)),
            whole((node_rows, width)),
        ],
        out_shape=[
            shape((width, LANES), b16),
            shape((payload, node_rows), b16),
            shape((node_rows, width), b16),
        ],
        compiler_params=params,
        name="crps",
    )(others, pred, truth, area_weight[None], attended, full, lse)

    halo_low = shifted(halo, "node", 1)
    halo_high = shifted(halo, "node", -1)
    parts = lax.all_to_all(gram.reshape(members, rows, LANES), "ens", 0, 0, tiled=True)
    part = jnp.sum(parts.astype(f32), 0)
    parts = lax.all_to_all(
        jnp.broadcast_to(part[None], (shards,) + part.shape), "node", 0, 0, tiled=True
    )
    total = jnp.sum(parts, 0)
    grad_out_proj = lax.dot_general(
        total[:, :variables],
        w_decode.astype(f32),
        (((1,), (1,)), ((), ())),
        preferred_element_type=f32,
    )
    loss = jnp.sum(total[0, variables : variables + 3]) / (members * node_rows * shards * variables)

    grad_query, key_part, value_part = pl.pallas_call(
        lambda *refs: own_kernel(scale, *refs),
        grid=(steps,),
        in_specs=[
            blocks(node_rows, HALO // node_rows),
            blocks(span),
            blocks(span),
            blocks(node_rows),
            blocks(node_rows),
        ],
        out_specs=[blocks(node_rows)] * 3,
        out_shape=[
            shape((node_rows, width), b16),
            shape((node_rows, width), f32),
            shape((node_rows, width), f32),
        ],
        compiler_params=params,
        name="own_queries",
    )(queries, keys, values, grad_attended, lse)

    (grad_hidden,) = pl.pallas_call(
        lambda *refs: halo_kernel(scale, *refs),
        grid=(steps,),
        in_specs=[
            whole((payload, node_rows)),
            whole((payload, node_rows)),
            blocks(HALO, 0),
            blocks(HALO, 2),
            blocks(node_rows, 1),
            blocks(node_rows, 1),
            blocks(node_rows),
            blocks(node_rows),
            blocks(node_rows),
            columns(0),
            columns(1),
            columns(2),
            mixed_block,
            own_block,
            whole((node_rows, width)),
            whole((node_rows, 1)),
            whole((1, width)),
            whole((payload, node_rows)),
            whole((width, LANES)),
        ],
        out_specs=[own_block],
        out_shape=[shape((1, node_rows, width), b16)],
        scratch_shapes=[
            pltpu.VMEM((2 * HALO, LANES), b16),
            pltpu.VMEM((2, HEADS, 2 * HALO), f32),
            pltpu.VMEM((node_rows, width), f32),
        ],
        compiler_params=params,
        name="neighbour_queries",
    )(
        halo_low, halo_high, queries, queries, keys, values, grad_query, key_part, value_part,
        full, full, full, full, hidden, forcing, inverse_rms, norm_gain[None], halo, decode,
    )
    return (grad_hidden, grad_out_proj, loss)


def solution(mesh):
    placed = (
        P("ens", "node", None),
        P("node", None),
        P(),
        P("ens", None),
        P("ens", None),
        P("ens", None),
        P("ens", None),
        P(),
        P(None, "node"),
        P("node"),
    )
    return jax.shard_map(
        per_device,
        mesh=mesh,
        in_specs=placed,
        out_specs=(P("ens", "node", None), P("ens", None), P()),
        check_vma=False,
    )
```

time: 266 us -> 212 us (0.80)
  matrix products: 64.2 us -> 0.97 us
  waiting for transfers between devices: 127 us -> 88.2 us
  Pallas kernels: 0 us -> 29.5 us
  blocking collectives: 0 us -> 14.9 us
  local copies, waits for them, and re-layouts: 6.83 us -> 14.1 us
  starting transfers between devices: 36.2 us -> 42.9 us
  other arithmetic: 11.2 us -> 4.72 us
    dot_general x18 -> x0, matrix products: 62.3 us -> none  [the longest x1 17 us: per_device(): jnp.einsum('hqk,khd->qhd', grad_scores, key3, preferred_element_type=f32)]
    pallas_call x0 -> x4, Pallas kernels: none -> 29.5 us  [the longest x1 12.3 us: per_device(): pl.pallas_call(lambda *refs: forward_kernel(scale, variables, *refs), gri...]
    ppermute x2 -> x0, waiting for transfers between devices: 26.1 us -> none  [the longest x1 13.2 us: extended_2(): lax.ppermute(lax.slice_in_dim(block, block.shape[dim] - width, None, axis...]
    ppermute x2 -> x4, starting transfers between devices: 11.3 us -> 27.6 us  [shifted(): return lax.ppermute(value, axis, pairs)]
    all_to_all x0 -> x1, blocking collectives: none -> 14.9 us  [per_device(): lax.all_to_all(gram.reshape(members, rows, LANES), 'ens', 0, 0, tiled=True)]
    all_gather x1, waiting for transfers between devices: 72.3 us -> 57.6 us  [per_device(): full = lax.all_gather(packed, 'ens', axis=0, tiled=True)]
    ppermute x2 -> x0, starting transfers between devices: 9.91 us -> none  [the longest x1 7.99 us: extended_2(): lax.ppermute(lax.slice_in_dim(block, 0, width, axis=dim), axis, backward)]
    unnamed x32 -> x41, local copies, waits for them, and re-layouts: 2.19 us -> 12.1 us
  transfers between devices with their start and end apart: 8 -> 7, of which waited for: 5 -> 3; matrix products, arithmetic and copies ran while one was open for 21% -> 1% of each run, Pallas kernels for 0% -> 7%
where the time goes in v2:
time: 212 us; the launch traced here: 211 us
  waiting for transfers between devices  88.2 us (42%)
  starting transfers between devices  42.9 us (20%)
  Pallas kernels  29.5 us (14%)
  between operations  16 us (8%)
  blocking collectives  14.9 us (7%)
  local copies, waits for them, and re-layouts  14.1 us (7%)
  other arithmetic  4.72 us (2%)
    all_gather x1, waiting for transfers between devices, per_device(): full = lax.all_gather(packed, 'ens', axis=0, tiled=True)  57.6 us
    ppermute x4, starting transfers between devices, shifted(): return lax.ppermute(value, axis, pairs)  27.6 us
    all_to_all x1, waiting for transfers between devices, per_device(): lax.all_to_all(jnp.broadcast_to(pred[None], (members,) + pred.shape), 'en...  25.1 us
    all_to_all x1, blocking collectives, per_device(): lax.all_to_all(gram.reshape(members, rows, LANES), 'ens', 0, 0, tiled=True)  14.9 us
    pallas_call x1, Pallas kernels, per_device(): pl.pallas_call(lambda *refs: forward_kernel(scale, variables, *refs), gri...  12.3 us
    unnamed x41, local copies, waits for them, and re-layouts  12.1 us
    all_to_all x1, starting transfers between devices, per_device(): lax.all_to_all(jnp.broadcast_to(part[None], (shards,) + part.shape), 'nod...  11 us
    pallas_call x1, Pallas kernels, per_device(): pl.pallas_call(lambda *refs: halo_kernel(scale, *refs), grid=(steps,), in...  9.35 us
  transfers between devices with their start and end apart: 7, of which 3 were waited for; matrix products, arithmetic and copies ran while one was open for 1% of the time, Pallas kernels for 7%

profile of v2, /device:TPU:1, one launch (start us, length us, event | category | flops | bytes accessed | tf_op | source)
XLA Modules:
  0.0 211.3 jit_solution(961322413997626429)
XLA Ops:
  7.2 1.1 copy.15
  8.5 1.6 pad_maximum_fusion
  10.2 1.2 multiply_reduce_fusion
  11.4 1.1 multiply_convert_fusion.refs_1_
  12.5 4.0 %collective-permute-start = (bf16[128,1024]{1,0:T(8,128)(2,1)S(1)}, bf16[128,1024]{1,0:T(8,128)(2,1)S(1)}, u32[]{:S(2)}, u32[]{:S(2)}) collective-permute-start(bf16[128,1024]{1,0:T(8,128)(2,1)S(1)} %multiply_convert_fusion.refs_1_), channel_id=1, source_target_pairs={{0,1},{1,2},{2,3},{3,4},{4,5},{5,6},{6,7},{7,8},{8,9},{9,10},{10,1... | collective-permute-start | bytes 786440 | tf_op jit(solution)/shard_map/ppermute | solution.py:265
  16.6 12.3 %collective-permute-start.1 = (bf16[128,1024]{1,0:T(8,128)(2,1)S(1)}, bf16[128,1024]{1,0:T(8,128)(2,1)S(1)}, u32[]{:S(2)}, u32[]{:S(2)}) collective-permute-start(bf16[128,1024]{1,0:T(8,128)(2,1)S(1)} %multiply_convert_fusion.refs_1_), channel_id=1, source_target_pairs={{0,15},{1,0},{2,1},{3,2},{4,3},{5,4},{6,5},{7,6},{8,7},{9,8},{10,9... | collective-permute-start | bytes 786440 | tf_op jit(solution)/shard_map/ppermute | solution.py:265
  28.9 5.5 %collective-permute-done.refs_0_ = bf16[128,1024]{1,0:T(8,128)(2,1)S(1)} collective-permute-done((bf16[128,1024]{1,0:T(8,128)(2,1)S(1)}, bf16[128,1024]{1,0:T(8,128)(2,1)S(1)}, u32[]{:S(2)}, u32[]{:S(2)}) %collective-permute-start) | collective-permute-done | bytes 262176 | tf_op jit(solution)/shard_map/ppermute | solution.py:265
  35.1 57.6 %all-gather.2.cloned.1.call-done.refs_3_.refs_4_.refs_5_.refs_6_.refs_9_.refs_10_.refs_11_.refs_12_ = bf16[1024,3200]{1,0:T(8,128)(2,1)} async-done(((bf16[32,3200]{1,0:T(8,128)(2,1)}), bf16[1024,3200]{1,0:T(8,128)(2,1)}) %all-gather.2.cloned.1.call-update) | async-done | bytes 6553616 | tf_op jit(solution)/shard_map/all_gather | solution.py:288
  92.7 0.9 copy-done.1
  93.6 0.9 copy-done.3
  95.5 12.3 %forward.1 = (bf16[384,1024]{1,0:T(8,128)(2,1)S(1)}, bf16[384,1024]{1,0:T(8,128)(2,1)S(1)}, bf16[384,1024]{1,0:T(8,128)(2,1)S(1)}, bf16[128,1024]{1,0:T(8,128)(2...) custom-call(bf16[128,1024]{1,0:T(8,128)(2,1)S(1)} %collective-permute-done.refs_0_, ...), custom_call_target="tpu_custom_call" | custom-call | tf_op jit(solution)/shard_map/forward/pallas_call | solution.py:303
  109.4 1.1 broadcast_in_dim.8
  110.6 4.3 %all-to-all-start = ((bf16[32,112,128]{2,1,0:T(8,128)(2,1)}), bf16[32,112,128]{2,1,0:T(8,128)(2,1)S(1)}, u32[]{:S(2)}, u32[]{:S(2)}) async-start(bf16[32,112,128]{2,1,0:T(8,128)(2,1)} %broadcast_in_dim.8), calls=%async_computation | async-start | bytes 1835008 | tf_op jit(solution)/shard_map/all_to_all | solution.py:342
  114.9 25.1 %all-to-all-done.refs_0_ = bf16[32,112,128]{2,1,0:T(8,128)(2,1)S(1)} async-done(((bf16[32,112,128]{2,1,0:T(8,128)(2,1)}), bf16[32,112,128]{2,1,0:T(8,128)(2,1)S(1)}, u32[]{:S(2)}, u32[]{:S(2)}) %all-to-all-start) | async-done | bytes 917536 | tf_op jit(solution)/shard_map/all_to_all | solution.py:342
  140.0 1.0 copy-done.8
  142.0 2.4 %crps.1 = (bf16[1024,128]{1,0:T(8,128)(2,1)S(1)}, bf16[192,128]{1,0:T(8,128)(2,1)S(1)}, bf16[128,1024]{1,0:T(8,128)(2,1)S(1)}) custom-call(bf16[32,112,128]{2,1,0:T(8,128)(2,1)S(1)} %all-to-all-done.refs_0_, bf16[112,128]{1,0:T(8,128)(2,1)S(1)} %get-tuple-element.15.refs_1_, bf16[112,128]{1,0:T(8,128)(2,1)S(1)} %pad.9.refs_2_, f32[1,128]{1,0:T(1,128)S(1)} %bitcast.15, ...), custom_call_target="tpu_custom_call" | custom-call | tf_op jit(solution)/shard_map/crps/pallas_call | solution.py:349
  145.1 14.9 %all_to_all.15 = bf16[32,32,128]{2,1,0:T(8,128)(2,1)S(1)} all-to-all(bf16[32,32,128]{2,1,0:T(8,128)(2,1)S(1)} %bitcast.13), channel_id=1, replica_groups=mesh['ens'=32,'node'=16] {'ens'}, dimensions={0} | all-to-all | bytes 524288 | tf_op jit(solution)/shard_map/all_to_all | solution.py:377
  160.8 11.0 %all-to-all-start.2 = ((f32[16,32,128]{2,1,0:T(8,128)}), f32[16,32,128]{2,1,0:T(8,128)S(1)}, u32[]{:S(2)}, u32[]{:S(2)}) async-start(f32[16,32,128]{2,1,0:T(8,128)} %broadcast_in_dim.11), calls=%async_computation.2 | async-start | bytes 524288 | tf_op jit(solution)/shard_map/all_to_all | solution.py:379
  171.8 3.3 %collective-permute-start.2 = (bf16[192,128]{1,0:T(8,128)(2,1)S(1)}, bf16[192,128]{1,0:T(8,128)(2,1)S(1)}, u32[]{:S(2)}, u32[]{:S(2)}) collective-permute-start(bf16[192,128]{1,0:T(8,128)(2,1)S(1)} %get-tuple-element.18.refs_17_), channel_id=1, source_target_pairs={{0,1},{1,2},{2,3},{3,4},{4,5},{5,6},{6,7},{7,8},{8,9},{9,10},{10,1... | collective-permute-start | bytes 147464 | tf_op jit(solution)/shard_map/ppermute | solution.py:265
  175.0 8.0 %collective-permute-start.3 = (bf16[192,128]{1,0:T(8,128)(2,1)S(1)}, bf16[192,128]{1,0:T(8,128)(2,1)S(1)}, u32[]{:S(2)}, u32[]{:S(2)}) collective-permute-start(bf16[192,128]{1,0:T(8,128)(2,1)S(1)} %get-tuple-element.18.refs_17_), channel_id=1, source_target_pairs={{0,15},{1,0},{2,1},{3,2},{4,3},{5,4},{6,5},{7,6},{8,7},{9,8},{10,9... | collective-permute-start | bytes 147464 | tf_op jit(solution)/shard_map/ppermute | solution.py:265
  183.2 1.1 copy-done.6
  184.3 1.0 copy-done.9
  186.3 5.4 %own_queries.1 = (bf16[128,1024]{1,0:T(8,128)(2,1)S(1)}, f32[128,1024]{1,0:T(8,128)S(1)}, f32[128,1024]{1,0:T(8,128)S(1)}) custom-call(bf16[384,1024]{1,0:T(8,128)(2,1)S(1)} %get-tuple-element.19.refs_0_.refs_2_.refs_3_, bf16[384,1024]{1,0:T(8,128)(2,1)S(1)} %get-tuple-element.20.refs_1_.refs_4_, bf16[384,1024]{1,0:T(8,128)(2,1)S(1)} %copy-done.6, ...), custom_call_target="tpu_custom_call" | custom-call | tf_op jit(solution)/shard_map/own_queries/pallas_call | solution.py:391
  191.8 9.4 %neighbour_queries.1 = bf16[1,128,1024]{2,1,0:T(8,128)(2,1)} custom-call(bf16[192,128]{1,0:T(8,128)(2,1)S(1)} %collective-permute-done.2.refs_0_, bf16[192,128]{1,0:T(8,128)(2,1)S(1)} %collective-permute-done.3.refs_1_, bf16[384,1024]{1,0:T(8,128)(2,1)S(1)} %get-tuple-element.19.refs_0_.refs_2_.refs_3_, ...), custom_call_target="tpu_custom_call" | custom-call | tf_op jit(solution)/shard_map/neighbour_queries/pallas_call | solution.py:411
  (51 shorter events, 8.6 us)
Async XLA Ops:
  7.2 1.2 copy-start
  7.2 85.5 %all-gather.2.cloned.1.call-start = ((), (), s32[]{:S(2)}) async-start(), calls=%async_computation.3 | async-start | bytes 6758400 | tf_op jit(solution)/shard_map/all_gather | solution.py:288
  12.5 21.9 %collective-permute-start = (bf16[128,1024]{1,0:T(8,128)(2,1)S(1)}, bf16[128,1024]{1,0:T(8,128)(2,1)S(1)}, u32[]{:S(2)}, u32[]{:S(2)}) collective-permute-start(bf16[128,1024]{1,0:T(8,128)(2,1)S(1)} %multiply_convert_fusion.refs_1_), channel_id=1, source_target_pairs={{0,1},{1,2},{2,3},{3,4},{4,5},{5,6},{6,7},{7,8},{8,9},{9,10},{10,1... | collective-permute-start | bytes 786440 | tf_op jit(solution)/shard_map/ppermute | solution.py:265
  16.6 17.8 %collective-permute-start.1 = (bf16[128,1024]{1,0:T(8,128)(2,1)S(1)}, bf16[128,1024]{1,0:T(8,128)(2,1)S(1)}, u32[]{:S(2)}, u32[]{:S(2)}) collective-permute-start(bf16[128,1024]{1,0:T(8,128)(2,1)S(1)} %multiply_convert_fusion.refs_1_), channel_id=1, source_target_pairs={{0,15},{1,0},{2,1},{3,2},{4,3},{5,4},{6,5},{7,6},{8,7},{9,8},{10,9... | collective-permute-start | bytes 786440 | tf_op jit(solution)/shard_map/ppermute | solution.py:265
  28.8 86.1 %copy-start.19 = (bf16[100,128]{1,0:T(8,128)(2,1)S(1)}, bf16[100,128]{1,0:T(8,128)(2,1)}, u32[]{:S(2)}) copy-start(bf16[100,128]{1,0:T(8,128)(2,1)} %param.18) | copy-start | bytes 76804
  28.8 111.2 %copy-start.17 = (f32[128]{0:T(128)S(1)}, f32[128]{0:T(128)}, u32[]{:S(2)}) copy-start(f32[128]{0:T(128)} %param.19) | copy-start | bytes 1540
  92.7 0.9 copy-start.1
  93.6 0.9 copy-start.3
  94.6 0.9 copy-start.11
  107.9 0.8 copy-start.7
  109.4 1.2 copy-start.5
  110.6 29.4 %all-to-all-start = ((bf16[32,112,128]{2,1,0:T(8,128)(2,1)}), bf16[32,112,128]{2,1,0:T(8,128)(2,1)S(1)}, u32[]{:S(2)}, u32[]{:S(2)}) async-start(bf16[32,112,128]{2,1,0:T(8,128)(2,1)} %broadcast_in_dim.8), calls=%async_computation | async-start | bytes 1835008 | tf_op jit(solution)/shard_map/all_to_all | solution.py:342
  140.0 1.0 copy-start.8
  141.1 0.9 copy-start.15
  142.0 49.7 %copy-start.2 = (bf16[128,1024]{1,0:T(8,128)(2,1)S(1)}, bf16[128,1024]{1,0:T(8,128)(2,1)}, u32[]{:S(2)}) copy-start(bf16[128,1024]{1,0:T(8,128)(2,1)} %refs_14_.1) | copy-start | bytes 786436
  142.0 49.7 %copy-start.4 = (bf16[1,128,1024]{2,1,0:T(8,128)(2,1)S(1)}, bf16[1,128,1024]{2,1,0:T(8,128)(2,1)}, u32[]{:S(2)}) copy-start(bf16[1,128,1024]{2,1,0:T(8,128)(2,1)} %refs_13_.1) | copy-start | bytes 786436
  142.0 49.8 %copy-start.16 = (f32[1024]{0:T(1024)S(1)}, f32[1024]{0:T(1024)}, u32[]{:S(2)}) copy-start(f32[1024]{0:T(1024)} %param.12) | copy-start | bytes 12292
  160.8 40.4 %all-to-all-start.2 = ((f32[16,32,128]{2,1,0:T(8,128)}), f32[16,32,128]{2,1,0:T(8,128)S(1)}, u32[]{:S(2)}, u32[]{:S(2)}) async-start(f32[16,32,128]{2,1,0:T(8,128)} %broadcast_in_dim.11), calls=%async_computation.2 | async-start | bytes 524288 | tf_op jit(solution)/shard_map/all_to_all | solution.py:379
  171.8 20.0 %collective-permute-start.2 = (bf16[192,128]{1,0:T(8,128)(2,1)S(1)}, bf16[192,128]{1,0:T(8,128)(2,1)S(1)}, u32[]{:S(2)}, u32[]{:S(2)}) collective-permute-start(bf16[192,128]{1,0:T(8,128)(2,1)S(1)} %get-tuple-element.18.refs_17_), channel_id=1, source_target_pairs={{0,1},{1,2},{2,3},{3,4},{4,5},{5,6},{6,7},{7,8},{8,9},{9,10},{10,1... | collective-permute-start | bytes 147464 | tf_op jit(solution)/shard_map/ppermute | solution.py:265
  175.0 16.7 %collective-permute-start.3 = (bf16[192,128]{1,0:T(8,128)(2,1)S(1)}, bf16[192,128]{1,0:T(8,128)(2,1)S(1)}, u32[]{:S(2)}, u32[]{:S(2)}) collective-permute-start(bf16[192,128]{1,0:T(8,128)(2,1)S(1)} %get-tuple-element.18.refs_17_), channel_id=1, source_target_pairs={{0,15},{1,0},{2,1},{3,2},{4,3},{5,4},{6,5},{7,6},{8,7},{9,8},{10,9... | collective-permute-start | bytes 147464 | tf_op jit(solution)/shard_map/ppermute | solution.py:265
  183.2 1.1 copy-start.6
  184.3 1.0 copy-start.9
  185.4 0.9 copy-start.13
  191.8 9.4 %copy-start.18 = (bf16[1024,100]{0,1:T(8,128)(2,1)S(1)}, bf16[1024,100]{0,1:T(8,128)(2,1)}, u32[]{:S(2)}) copy-start(bf16[1024,100]{0,1:T(8,128)(2,1)} %param.17) | copy-start | bytes 614404
  (3 other events, 2.1 us)
Sparse Core Ops, SparseCore 0:
  10.3 82.3 all-gather.1

commit v3 on v2

--- a/solution.py
+++ b/solution.py
@@ -12,6 +12,10 @@
 LANES = 128
 STEP = 256
 VROWS = 112
+SIDE = 4
+RING_Z = 8
+RING_Y = 8
+HOPS = (0, SIDE - 1, 1, 2)
 
 
 ALPHA = 0.95
@@ -62,13 +66,43 @@
     return out
 
 
-def forward_kernel(
-    scale, variables, low, own, high, wq, wk, wv, mixed, hidden, forcing, decode,
-    queries, keys, values, attended, lse, pred, normed, total,
-):
+def forward_kernel(scale, place, low, own, high, hidden, forcing, decode, *refs):
+    pieces, refs = refs[: 2 * len(HOPS)], refs[2 * len(HOPS) :]
+    queries, keys, values, attended, lse, pred, full, normed, total, weights, load, store = refs
     step = pl.program_id(0)
     rows = own.shape[0]
     span = rows + 2 * HALO
+    x, z, core = place[0], place[1], place[2]
+    side = len(HOPS)
+    block = pieces[0].shape[0] // side
+
+    def loads():
+        copies = []
+        for mine in (True, False):
+            which = core if mine else 1 - core
+            for outer, far in enumerate(HOPS):
+                piece = pieces[outer if mine else side + outer]
+                for inner, near in enumerate(HOPS):
+                    along_x = jnp.where(which == 0, near, far)
+                    along_z = jnp.where(which == 0, far, near)
+                    chip = lax.rem(x + along_x, side) * side + lax.rem(z + along_z, side)
+                    copies.append(
+                        pltpu.make_async_copy(
+                            piece.at[pl.ds(inner * block, block)],
+                            weights.at[which, pl.ds(chip * block, block)],
+                            load.at[(0 if mine else side * side) + outer * side + inner],
+                        )
+                    )
+        return copies
+
+    @pl.when(step == 0)
+    def _():
+        copies = loads()
+        for copy in copies:
+            copy.start()
+        for copy in copies:
+            copy.wait()
+        pltpu.make_async_copy(weights, full, store.at[0]).start()
 
     @pl.when(step == 0)
     def _():
@@ -78,9 +112,14 @@
         total[...] = nn(hidden[0], decode[...]) + nn(forcing[...], decode[...])
 
     field = normed[...]
-    queries[...] = nn(field, wq[...]).astype(b16)
-    keys[...] = nn(field, wk[...]).astype(b16)
-    values[...] = nn(field, wv[...]).astype(b16)
+    per_half = pl.num_programs(0) // 2
+    half = step // per_half
+    at = (step - half * per_half) * STEP
+    third = per_half * STEP
+    for index, out in enumerate((queries, keys, values)):
+        cols = pl.ds(pl.multiple_of(index * third + at, STEP), STEP)
+        out[...] = nn(field, weights[half, :, cols]).astype(b16)
+    mixed = weights[0, pl.ds(pl.multiple_of(step * STEP, STEP), STEP), 3 * third :]
     window = window_mask(rows, span)
     masks = head_masks(scale)
     lower = lax.broadcasted_iota(jnp.int32, (rows, LANES), 1) < LANES // 2
@@ -100,10 +139,11 @@
             stats.append(top + jnp.log(norm))
         attended[:, cols] = jnp.where(lower, outs[0], outs[1]).astype(b16)
         lse[:, cols] = jnp.where(lower, stats[0], stats[1])
-    total[...] += nn(attended[...], mixed[...])
+    total[...] += nn(attended[...], mixed)
 
     @pl.when(step == pl.num_programs(0) - 1)
     def _():
+        pltpu.make_async_copy(weights, full, store.at[0]).wait()
         pred[...] = total[...].T[:VROWS].astype(b16)
 
 
@@ -142,7 +182,7 @@
     for index, piece in enumerate(split_bf16(loss, 3)):
         parts = jnp.where(column == variables + index, piece.astype(f32), parts)
     gram[...] = parts.astype(b16)
-    grad_att = nt(grad_t, mixed[...]).astype(b16)
+    grad_att = nt(grad_t, mixed[0]).astype(b16)
     grad_attended[...] = grad_att
     size = width // HEADS
     head = lax.broadcasted_iota(jnp.int32, (HEADS, width), 0)
@@ -220,7 +260,7 @@
     )
     scaled = head_masks(scale)
     plain = head_masks(1.0)
-    grad_att = nt(grad_t[...], mixed[...]).astype(b16)
+    grad_att = nt(grad_t[...], mixed[0]).astype(b16)
     per_step = 2 * (STEP // LANES)
     d_keys, d_values = [], []
     for pair in range(STEP // LANES):
@@ -241,9 +281,9 @@
         d_keys.append(d_key.astype(b16))
         d_values.append(d_value.astype(b16))
     total[...] += (
-        nt(grad_query[...], wq[...])
-        + nt(jnp.concatenate(d_keys, 1), wk[...])
-        + nt(jnp.concatenate(d_values, 1), wv[...])
+        nt(grad_query[...], wq[0])
+        + nt(jnp.concatenate(d_keys, 1), wk[0])
+        + nt(jnp.concatenate(d_values, 1), wv[0])
     )
 
     @pl.when(step == pl.num_programs(0) - 1)
@@ -263,6 +303,57 @@
     count = lax.axis_size(axis)
     pairs = [(source, (source + steps) % count) for source in range(count)]
     return lax.ppermute(value, axis, pairs)
+
+
+def permute(value, moves):
+    pairs = []
+    for x in range(SIDE):
+        for z in range(RING_Z):
+            for y in range(RING_Y):
+                for core in range(2):
+                    dx, dz, dc = moves[core]
+                    at = (x, z, core)
+                    to = ((x + dx) % SIDE, (z + dz) % RING_Z, core ^ dc)
+                    pairs.append(
+                        tuple(
+                            ((px * SIDE + pz % SIDE) * 2 + pc) * 2 * RING_Y + pz // SIDE * RING_Y + y
+                            for px, pz, pc in (at, to)
+                        )
+                    )
+    return lax.ppermute(value, ("ens", "node"), pairs)
+
+
+def ring(value, along):
+    out = [value]
+    for hop in (1, -1, -2):
+        moves = [(hop, 0, 0) if axis == 0 else (0, hop, 0) for axis in along]
+        out.append(permute(value, moves))
+    return out
+
+
+def swapped(value):
+    return permute(value, [(0, 0, 1)] * 2)
+
+
+def gathered(w_query, w_key, w_value, mixed, core):
+    half = w_query.shape[1] // 2
+    both = jnp.stack(
+        [
+            jnp.concatenate(
+                [w[:, at : at + half] for w in (w_query, w_key, w_value)] + [mixed], 1
+            )
+            for at in (0, half)
+        ]
+    )
+    first = core == 0
+    keep = jnp.where(first, both[0], both[1])
+    other = swapped(jnp.where(first, both[1], both[0]))
+    block = jnp.where(
+        first, jnp.concatenate([keep, other], 0), jnp.concatenate([other, keep], 0)
+    )
+    row = jnp.concatenate(ring(block, (0, 1)), 0)
+    mine = ring(row, (1, 0))
+    return mine + [swapped(piece) for piece in mine]
 
 
 def per_device(
@@ -284,8 +375,11 @@
     )
     decode = jnp.pad(w_decode, ((0, 0), (0, LANES - variables)))
     mixed = jnp.dot(w_out, decode, preferred_element_type=f32).astype(b16)
-    packed = jnp.concatenate([w_query, w_key, w_value, mixed], 1)
-    full = lax.all_gather(packed, "ens", axis=0, tiled=True)
+    position = lax.axis_index("ens")
+    core = position % 2
+    place = jnp.stack([position // (2 * SIDE), position // 2 % SIDE, core]).astype(jnp.int32)
+    pieces = gathered(w_query, w_key, w_value, mixed, core)
+    half_width = pieces[0].shape[1]
     xfield = hidden[0].astype(f32) + forcing.astype(f32)
     inverse_rms = lax.rsqrt(jnp.mean(xfield * xfield, -1, keepdims=True) + EPS_NORM)
     normed = (xfield * inverse_rms * norm_gain).astype(b16)
@@ -293,28 +387,31 @@
     high = shifted(normed, "node", -1)
 
     def columns(at):
-        return pl.BlockSpec((width, STEP), lambda i: (0, at * steps + i))
+        per_half = steps // 2
+        return pl.BlockSpec(
+            (1, width, STEP), lambda i: (i // per_half, 0, at * per_half + i % per_half)
+        )
 
     def blocks(height, at=0):
         return pl.BlockSpec((height, STEP), lambda i: (at, i))
 
-    mixed_block = pl.BlockSpec((STEP, LANES), lambda i: (i, 3 * width // LANES))
+    mixed_at = half_width // LANES - 1
+    mixed_block = pl.BlockSpec((1, STEP, LANES), lambda i: (0, i, mixed_at))
+    anywhere = pl.BlockSpec(memory_space=pl.ANY)
     own_block = whole((1, node_rows, width))
-    queries, keys, values, attended, lse, pred = pl.pallas_call(
-        lambda *refs: forward_kernel(scale, variables, *refs),
+    queries, keys, values, attended, lse, pred, full = pl.pallas_call(
+        lambda *refs: forward_kernel(scale, *refs),
         grid=(steps,),
         in_specs=[
+            pl.BlockSpec(memory_space=pltpu.SMEM),
             whole((HALO, width)),
             whole((node_rows, width)),
             whole((HALO, width)),
-            columns(0),
-            columns(1),
-            columns(2),
-            mixed_block,
             own_block,
             whole((node_rows, width)),
             whole((width, LANES)),
-        ],
+        ]
+        + [anywhere] * len(pieces),
         out_specs=[
             blocks(span),
             blocks(span),
@@ -322,6 +419,7 @@
             blocks(node_rows),
             blocks(node_rows),
             whole((VROWS, node_rows)),
+            anywhere,
         ],
         out_shape=[
             shape((span, width), b16),
@@ -330,14 +428,18 @@
             shape((node_rows, width), b16),
             shape((node_rows, width), f32),
             shape((VROWS, node_rows), b16),
+            shape((2, width, half_width), b16),
         ],
         scratch_shapes=[
             pltpu.VMEM((span, width), b16),
             pltpu.VMEM((node_rows, LANES), f32),
+            pltpu.VMEM((2, width, half_width), b16),
+            pltpu.SemaphoreType.DMA((len(pieces) * SIDE,)),
+            pltpu.SemaphoreType.DMA((1,)),
         ],
         compiler_params=params,
         name="forward",
-    )(low, normed, high, full, full, full, full, hidden, forcing, decode)
+    )(place, low, normed, high, hidden, forcing, decode, *pieces)
 
     others = lax.all_to_all(
         jnp.broadcast_to(pred[None], (members,) + pred.shape), "ens", 0, 0, tiled=True
@@ -355,7 +457,7 @@
             whole((VROWS, node_rows)),
             whole((1, node_rows)),
             whole((node_rows, width)),
-            pl.BlockSpec((width, LANES), lambda i: (0, 3 * width // LANES)),
+            pl.BlockSpec((1, width, LANES), lambda i: (0, 0, mixed_at)),
             whole((node_rows, width)),
         ],
         out_specs=[

time: 212 us -> 222 us (1.047)
  starting transfers between devices: 42.9 us -> 89.8 us
  waiting for transfers between devices: 88.2 us -> 60.3 us
  between operations: 16 us -> 2.88 us
  Pallas kernels: 29.5 us -> 33.3 us
  other arithmetic: 4.72 us -> 2.22 us
    all_gather x1 -> x0, waiting for transfers between devices: 57.6 us -> none  [per_device(): full = lax.all_gather(packed, 'ens', axis=0, tiled=True)]
    ppermute x0 -> x11, starting transfers between devices: none -> 51.7 us  [permute(): return lax.ppermute(value, ('ens', 'node'), pairs)]
    ppermute x4, waiting for transfers between devices: 5.5 us -> 23 us  [shifted(): return lax.ppermute(value, axis, pairs)]
    ppermute x0 -> x11, waiting for transfers between devices: none -> 12.3 us  [permute(): return lax.ppermute(value, ('ens', 'node'), pairs)]
    ppermute x4, starting transfers between devices: 27.6 us -> 16.4 us  [shifted(): return lax.ppermute(value, axis, pairs)]
    all_to_all x1, starting transfers between devices: 4.33 us -> 10.6 us  [per_device(): lax.all_to_all(jnp.broadcast_to(pred[None], (members,) + pred.shape), 'en...]
    pallas_call x1, Pallas kernels: 12.3 us -> 16.1 us  [per_device(): pl.pallas_call(lambda *refs: forward_kernel(scale, *refs), grid=(steps,),...]
    unnamed x41 -> x43, local copies, waits for them, and re-layouts: 12.1 us -> 11.9 us
  transfers between devices with their start and end apart: 7 -> 17, of which waited for: 3 -> 7; matrix products, arithmetic and copies ran while one was open for 1% -> 0% of each run, Pallas kernels for 7% -> 7%
where the time goes in v3:
time: 222 us; the launch traced here: 221 us
  starting transfers between devices  89.8 us (40%)
  waiting for transfers between devices  60.3 us (27%)
  Pallas kernels  33.3 us (15%)
  local copies, waits for them, and re-layouts  15.5 us (7%)
  blocking collectives  15 us (7%)
  between operations  2.88 us (1%)
  other arithmetic  2.22 us (1%)
    ppermute x11, starting transfers between devices, permute(): return lax.ppermute(value, ('ens', 'node'), pairs)  51.7 us
    all_to_all x1, waiting for transfers between devices, per_device(): lax.all_to_all(jnp.broadcast_to(pred[None], (members,) + pred.shape), 'en...  25.1 us
    ppermute x4, waiting for transfers between devices, shifted(): return lax.ppermute(value, axis, pairs)  23 us
    ppermute x4, starting transfers between devices, shifted(): return lax.ppermute(value, axis, pairs)  16.4 us
    pallas_call x1, Pallas kernels, per_device(): pl.pallas_call(lambda *refs: forward_kernel(scale, *refs), grid=(steps,),...  16.1 us
    all_to_all x1, blocking collectives, per_device(): lax.all_to_all(gram.reshape(members, rows, LANES), 'ens', 0, 0, tiled=True)  15 us
    ppermute x11, waiting for transfers between devices, permute(): return lax.ppermute(value, ('ens', 'node'), pairs)  12.3 us
    unnamed x43, local copies, waits for them, and re-layouts  11.9 us
  transfers between devices with their start and end apart: 17, of which 7 were waited for; matrix products, arithmetic and copies ran while one was open for 0% of the time, Pallas kernels for 7%

profile of v3, /device:TPU:1, one launch (start us, length us, event | category | flops | bytes accessed | tf_op | source)
XLA Modules:
  0.0 221.0 jit_solution(11119189636198518294)
XLA Ops:
  3.7 8.8 %collective-permute-start.2 = (bf16[32,1664]{1,0:T(8,128)(2,1)S(1)}, bf16[32,1664]{1,0:T(8,128)(2,1)S(1)}, u32[]{:S(2)}, u32[]{:S(2)}) collective-permute-start(bf16[32,1664]{1,0:T(8,128)(2,1)S(1)} %get-tuple-element.30), channel_id=1, source_target_pairs={{0,16},{16,0},{1,17},{17,1},{2,18},{18,2},{3,19},{19,3},{4,20},{20... | collective-permute-start | bytes 319496 | tf_op jit(solution)/shard_map/ppermute | solution.py:323
  15.4 5.3 %collective-permute-start.4 = (bf16[64,1664]{1,0:T(8,128)(2,1)S(1)}, bf16[64,1664]{1,0:T(8,128)(2,1)S(1)}, u32[]{:S(2)}, u32[]{:S(2)}) collective-permute-start(bf16[64,1664]{1,0:T(8,128)(2,1)S(1)} %maximum_select_fusion), channel_id=1, source_target_pairs={{0,384},{16,120},{1,385},{17,121},{2,386},{18,122},{3,387},{19,123... | collective-permute-start | bytes 638984 | tf_op jit(solution)/shard_map/ppermute | solution.py:323
  20.7 3.4 %collective-permute-start.5 = (bf16[64,1664]{1,0:T(8,128)(2,1)S(1)}, bf16[64,1664]{1,0:T(8,128)(2,1)S(1)}, u32[]{:S(2)}, u32[]{:S(2)}) collective-permute-start(bf16[64,1664]{1,0:T(8,128)(2,1)S(1)} %maximum_select_fusion), channel_id=1, source_target_pairs={{0,256},{16,88},{1,257},{17,89},{2,258},{18,90},{3,259},{19,91},{4... | collective-permute-start | bytes 638984 | tf_op jit(solution)/shard_map/ppermute | solution.py:323
  24.1 5.0 %collective-permute-done.5 = bf16[64,1664]{1,0:T(8,128)(2,1)S(1)} collective-permute-done((bf16[64,1664]{1,0:T(8,128)(2,1)S(1)}, bf16[64,1664]{1,0:T(8,128)(2,1)S(1)}, u32[]{:S(2)}, u32[]{:S(2)}) %collective-permute-start.5) | collective-permute-done | bytes 213024 | tf_op jit(solution)/shard_map/ppermute | solution.py:323
  29.2 2.9 %collective-permute-start.6 = (bf16[256,1664]{1,0:T(8,128)(2,1)S(1)}, bf16[256,1664]{1,0:T(8,128)(2,1)}, u32[]{:S(2)}, u32[]{:S(2)}) collective-permute-start(bf16[256,1664]{1,0:T(8,128)(2,1)S(1)} %pad_maximum_fusion.refs_7_), channel_id=1, source_target_pairs={{0,32},{16,144},{1,33},{17,145},{2,34},{18,146},{3,35},{19,147},{4... | collective-permute-start | bytes 2555912 | tf_op jit(solution)/shard_map/ppermute | solution.py:323
  32.1 3.6 %collective-permute-start.7 = (bf16[256,1664]{1,0:T(8,128)(2,1)S(1)}, bf16[256,1664]{1,0:T(8,128)(2,1)}, u32[]{:S(2)}, u32[]{:S(2)}) collective-permute-start(bf16[256,1664]{1,0:T(8,128)(2,1)S(1)} %pad_maximum_fusion.refs_7_), channel_id=1, source_target_pairs={{0,104},{16,400},{1,105},{17,401},{2,106},{18,402},{3,107},{19,403... | collective-permute-start | bytes 2555912 | tf_op jit(solution)/shard_map/ppermute | solution.py:323
  35.7 3.2 %collective-permute-start.8 = (bf16[256,1664]{1,0:T(8,128)(2,1)S(1)}, bf16[256,1664]{1,0:T(8,128)(2,1)}, u32[]{:S(2)}, u32[]{:S(2)}) collective-permute-start(bf16[256,1664]{1,0:T(8,128)(2,1)S(1)} %pad_maximum_fusion.refs_7_), channel_id=1, source_target_pairs={{0,72},{16,272},{1,73},{17,273},{2,74},{18,274},{3,75},{19,275},{4... | collective-permute-start | bytes 2555912 | tf_op jit(solution)/shard_map/ppermute | solution.py:323
  39.1 4.7 %collective-permute-start.9 = (bf16[256,1664]{1,0:T(8,128)(2,1)S(1)}, bf16[256,1664]{1,0:T(8,128)(2,1)}, u32[]{:S(2)}, u32[]{:S(2)}) collective-permute-start(bf16[256,1664]{1,0:T(8,128)(2,1)S(1)} %pad_maximum_fusion.refs_7_), channel_id=1, source_target_pairs={{0,16},{16,0},{1,17},{17,1},{2,18},{18,2},{3,19},{19,3},{4,20},{20... | collective-permute-start | bytes 2555912 | tf_op jit(solution)/shard_map/ppermute | solution.py:323
  44.2 4.3 %collective-permute-start.10 = (bf16[256,1664]{1,0:T(8,128)(2,1)}, bf16[256,1664]{1,0:T(8,128)(2,1)}, u32[]{:S(2)}, u32[]{:S(2)}) collective-permute-start(bf16[256,1664]{1,0:T(8,128)(2,1)} %collective-permute-done.6.refs_8_), channel_id=1, source_target_pairs={{0,16},{16,0},{1,17},{17,1},{2,18},{18,2},{3,19},{19,3},{4,20},{20... | collective-permute-start | bytes 2555912 | tf_op jit(solution)/shard_map/ppermute | solution.py:323
  48.5 5.9 %collective-permute-done.7.refs_9_ = bf16[256,1664]{1,0:T(8,128)(2,1)} collective-permute-done((bf16[256,1664]{1,0:T(8,128)(2,1)S(1)}, bf16[256,1664]{1,0:T(8,128)(2,1)}, u32[]{:S(2)}, u32[]{:S(2)}) %collective-permute-start.7) | collective-permute-done | bytes 852000 | tf_op jit(solution)/shard_map/ppermute | solution.py:323
  56.3 11.8 %collective-permute-start.12 = (bf16[256,1664]{1,0:T(8,128)(2,1)}, bf16[256,1664]{1,0:T(8,128)(2,1)}, u32[]{:S(2)}, u32[]{:S(2)}) collective-permute-start(bf16[256,1664]{1,0:T(8,128)(2,1)} %collective-permute-done.8.refs_10_), channel_id=1, source_target_pairs={{0,16},{16,0},{1,17},{17,1},{2,18},{18,2},{3,19},{19,3},{4,20},{20... | collective-permute-start | bytes 2555912 | tf_op jit(solution)/shard_map/ppermute | solution.py:323
  68.3 3.2 %collective-permute-start = (bf16[128,1024]{1,0:T(8,128)(2,1)S(1)}, bf16[128,1024]{1,0:T(8,128)(2,1)S(1)}, u32[]{:S(2)}, u32[]{:S(2)}) collective-permute-start(bf16[128,1024]{1,0:T(8,128)(2,1)S(1)} %multiply_convert_fusion.refs_2_), channel_id=1, source_target_pairs={{0,1},{1,2},{2,3},{3,4},{4,5},{5,6},{6,7},{7,8},{8,9},{9,10},{10,1... | collective-permute-start | bytes 786440 | tf_op jit(solution)/shard_map/ppermute | solution.py:305
  71.5 16.6 %collective-permute-done.refs_1_ = bf16[128,1024]{1,0:T(8,128)(2,1)S(1)} collective-permute-done((bf16[128,1024]{1,0:T(8,128)(2,1)S(1)}, bf16[128,1024]{1,0:T(8,128)(2,1)S(1)}, u32[]{:S(2)}, u32[]{:S(2)}) %collective-permute-start) | collective-permute-done | bytes 262176 | tf_op jit(solution)/shard_map/ppermute | solution.py:305
  90.2 6.3 %collective-permute-done.1.refs_3_ = bf16[128,1024]{1,0:T(8,128)(2,1)S(1)} collective-permute-done((bf16[128,1024]{1,0:T(8,128)(2,1)S(1)}, bf16[128,1024]{1,0:T(8,128)(2,1)S(1)}, u32[]{:S(2)}, u32[]{:S(2)}) %collective-permute-start.1) | collective-permute-done | bytes 262176 | tf_op jit(solution)/shard_map/ppermute | solution.py:305
  100.1 16.1 %forward.1 = (bf16[384,1024]{1,0:T(8,128)(2,1)S(1)}, bf16[384,1024]{1,0:T(8,128)(2,1)S(1)}, bf16[384,1024]{1,0:T(8,128)(2,1)S(1)}, bf16[128,1024]{1,0:T(8,128)(2...) custom-call(s32[3]{0:T(128)S(1)} %pad_add_fusion.refs_0_, ...), custom_call_target="tpu_custom_call" | custom-call | tf_op jit(solution)/shard_map/forward/pallas_call | solution.py:402
  119.8 10.6 %all-to-all-start = ((bf16[32,112,128]{2,1,0:T(8,128)(2,1)}), bf16[32,112,128]{2,1,0:T(8,128)(2,1)S(1)}, u32[]{:S(2)}, u32[]{:S(2)}) async-start(bf16[32,112,128]{2,1,0:T(8,128)(2,1)} %broadcast_in_dim.8), calls=%async_computation | async-start | bytes 1835008 | tf_op jit(solution)/shard_map/all_to_all | solution.py:444
  130.4 25.1 %all-to-all-done.refs_0_ = bf16[32,112,128]{2,1,0:T(8,128)(2,1)S(1)} async-done(((bf16[32,112,128]{2,1,0:T(8,128)(2,1)}), bf16[32,112,128]{2,1,0:T(8,128)(2,1)S(1)}, u32[]{:S(2)}, u32[]{:S(2)}) %all-to-all-start) | async-done | bytes 917536 | tf_op jit(solution)/shard_map/all_to_all | solution.py:444
  157.5 2.3 %crps.1 = (bf16[1024,128]{1,0:T(8,128)(2,1)S(1)}, bf16[192,128]{1,0:T(8,128)(2,1)S(1)}, bf16[128,1024]{1,0:T(8,128)(2,1)S(1)}) custom-call(bf16[32,112,128]{2,1,0:T(8,128)(2,1)S(1)} %all-to-all-done.refs_0_, bf16[112,128]{1,0:T(8,128)(2,1)S(1)} %get-tuple-element.16.refs_1_, bf16[112,128]{1,0:T(8,128)(2,1)S(1)} %pad.9.refs_2_, f32[1,128]{1,0:T(1,128)S(1)} %bitcast.18, ...), custom_call_target="tpu_custom_call" | custom-call | tf_op jit(solution)/shard_map/crps/pallas_call | solution.py:451
  160.5 15.0 %all_to_all.15 = bf16[32,32,128]{2,1,0:T(8,128)(2,1)S(1)} all-to-all(bf16[32,32,128]{2,1,0:T(8,128)(2,1)S(1)} %bitcast.16), channel_id=1, replica_groups=mesh['ens'=32,'node'=16] {'ens'}, dimensions={0} | all-to-all | bytes 524288 | tf_op jit(solution)/shard_map/all_to_all | solution.py:479
  176.3 11.2 %all-to-all-start.2 = ((f32[16,32,128]{2,1,0:T(8,128)}), f32[16,32,128]{2,1,0:T(8,128)}, u32[]{:S(2)}, u32[]{:S(2)}) async-start(f32[16,32,128]{2,1,0:T(8,128)} %broadcast_in_dim.11), calls=%async_computation.2 | async-start | bytes 524288 | tf_op jit(solution)/shard_map/all_to_all | solution.py:481
  187.5 3.2 %collective-permute-start.13 = (bf16[192,128]{1,0:T(8,128)(2,1)S(1)}, bf16[192,128]{1,0:T(8,128)(2,1)S(1)}, u32[]{:S(2)}, u32[]{:S(2)}) collective-permute-start(bf16[192,128]{1,0:T(8,128)(2,1)S(1)} %get-tuple-element.20.refs_17_), channel_id=1, source_target_pairs={{0,1},{1,2},{2,3},{3,4},{4,5},{5,6},{6,7},{7,8},{8,9},{9,10},{10,1... | collective-permute-start | bytes 147464 | tf_op jit(solution)/shard_map/ppermute | solution.py:305
  190.7 8.1 %collective-permute-start.14 = (bf16[192,128]{1,0:T(8,128)(2,1)S(1)}, bf16[192,128]{1,0:T(8,128)(2,1)S(1)}, u32[]{:S(2)}, u32[]{:S(2)}) collective-permute-start(bf16[192,128]{1,0:T(8,128)(2,1)S(1)} %get-tuple-element.20.refs_17_), channel_id=1, source_target_pairs={{0,15},{1,0},{2,1},{3,2},{4,3},{5,4},{6,5},{7,6},{8,7},{9,8},{10,9... | collective-permute-start | bytes 147464 | tf_op jit(solution)/shard_map/ppermute | solution.py:305
  200.9 5.4 %own_queries.1 = (bf16[128,1024]{1,0:T(8,128)(2,1)S(1)}, f32[128,1024]{1,0:T(8,128)S(1)}, f32[128,1024]{1,0:T(8,128)S(1)}) custom-call(bf16[384,1024]{1,0:T(8,128)(2,1)S(1)} %get-tuple-element.21.refs_0_.refs_2_.refs_3_, bf16[384,1024]{1,0:T(8,128)(2,1)S(1)} %get-tuple-element.22.refs_1_.refs_4_, bf16[384,1024]{1,0:T(8,128)(2,1)S(1)} %copy-done.4, ...), custom_call_target="tpu_custom_call" | custom-call | tf_op jit(solution)/shard_map/own_queries/pallas_call | solution.py:493
  206.4 9.4 %neighbour_queries.1 = bf16[1,128,1024]{2,1,0:T(8,128)(2,1)} custom-call(bf16[192,128]{1,0:T(8,128)(2,1)S(1)} %collective-permute-done.13.refs_0_, bf16[192,128]{1,0:T(8,128)(2,1)S(1)} %collective-permute-done.14.refs_1_, bf16[384,1024]{1,0:T(8,128)(2,1)S(1)} %get-tuple-element.21.refs_0_.refs_2_.refs_3_, ...), custom_call_target="tpu_custom_call" | custom-call | tf_op jit(solution)/shard_map/neighbour_queries/pallas_call | solution.py:513
  (77 shorter events, 26.7 us)
Async XLA Ops:
  1.8 37.1 %copy-start.1 = (bf16[128,1024]{1,0:T(8,128)(2,1)S(1)}, bf16[128,1024]{1,0:T(8,128)(2,1)}, u32[]{:S(2)}) copy-start(bf16[128,1024]{1,0:T(8,128)(2,1)} %refs_14_.1) | copy-start | bytes 786436
  1.8 37.1 %copy-start.2 = (bf16[1,128,1024]{2,1,0:T(8,128)(2,1)S(1)}, bf16[1,128,1024]{2,1,0:T(8,128)(2,1)}, u32[]{:S(2)}) copy-start(bf16[1,128,1024]{2,1,0:T(8,128)(2,1)} %refs_13_.1) | copy-start | bytes 786436
  3.5 64.6 %copy-start.18 = (f32[1024]{0:T(1024)S(1)}, f32[1024]{0:T(1024)}, u32[]{:S(2)}) copy-start(f32[1024]{0:T(1024)} %param.12) | copy-start | bytes 12292
  3.7 9.7 %collective-permute-start.2 = (bf16[32,1664]{1,0:T(8,128)(2,1)S(1)}, bf16[32,1664]{1,0:T(8,128)(2,1)S(1)}, u32[]{:S(2)}, u32[]{:S(2)}) collective-permute-start(bf16[32,1664]{1,0:T(8,128)(2,1)S(1)} %get-tuple-element.30), channel_id=1, source_target_pairs={{0,16},{16,0},{1,17},{17,1},{2,18},{18,2},{3,19},{19,3},{4,20},{20... | collective-permute-start | bytes 319496 | tf_op jit(solution)/shard_map/ppermute | solution.py:323
  13.5 10.6 %collective-permute-start.3 = (bf16[64,1664]{1,0:T(8,128)(2,1)S(1)}, bf16[64,1664]{1,0:T(8,128)(2,1)S(1)}, u32[]{:S(2)}, u32[]{:S(2)}) collective-permute-start(bf16[64,1664]{1,0:T(8,128)(2,1)S(1)} %maximum_select_fusion), channel_id=1, source_target_pairs={{0,128},{16,48},{1,129},{17,49},{2,130},{18,50},{3,131},{19,51},{4... | collective-permute-start | bytes 638984 | tf_op jit(solution)/shard_map/ppermute | solution.py:323
  15.4 8.7 %collective-permute-start.4 = (bf16[64,1664]{1,0:T(8,128)(2,1)S(1)}, bf16[64,1664]{1,0:T(8,128)(2,1)S(1)}, u32[]{:S(2)}, u32[]{:S(2)}) collective-permute-start(bf16[64,1664]{1,0:T(8,128)(2,1)S(1)} %maximum_select_fusion), channel_id=1, source_target_pairs={{0,384},{16,120},{1,385},{17,121},{2,386},{18,122},{3,387},{19,123... | collective-permute-start | bytes 638984 | tf_op jit(solution)/shard_map/ppermute | solution.py:323
  20.7 8.4 %collective-permute-start.5 = (bf16[64,1664]{1,0:T(8,128)(2,1)S(1)}, bf16[64,1664]{1,0:T(8,128)(2,1)S(1)}, u32[]{:S(2)}, u32[]{:S(2)}) collective-permute-start(bf16[64,1664]{1,0:T(8,128)(2,1)S(1)} %maximum_select_fusion), channel_id=1, source_target_pairs={{0,256},{16,88},{1,257},{17,89},{2,258},{18,90},{3,259},{19,91},{4... | collective-permute-start | bytes 638984 | tf_op jit(solution)/shard_map/ppermute | solution.py:323
  29.2 15.0 %collective-permute-start.6 = (bf16[256,1664]{1,0:T(8,128)(2,1)S(1)}, bf16[256,1664]{1,0:T(8,128)(2,1)}, u32[]{:S(2)}, u32[]{:S(2)}) collective-permute-start(bf16[256,1664]{1,0:T(8,128)(2,1)S(1)} %pad_maximum_fusion.refs_7_), channel_id=1, source_target_pairs={{0,32},{16,144},{1,33},{17,145},{2,34},{18,146},{3,35},{19,147},{4... | collective-permute-start | bytes 2555912 | tf_op jit(solution)/shard_map/ppermute | solution.py:323
  32.1 22.4 %collective-permute-start.7 = (bf16[256,1664]{1,0:T(8,128)(2,1)S(1)}, bf16[256,1664]{1,0:T(8,128)(2,1)}, u32[]{:S(2)}, u32[]{:S(2)}) collective-permute-start(bf16[256,1664]{1,0:T(8,128)(2,1)S(1)} %pad_maximum_fusion.refs_7_), channel_id=1, source_target_pairs={{0,104},{16,400},{1,105},{17,401},{2,106},{18,402},{3,107},{19,403... | collective-permute-start | bytes 2555912 | tf_op jit(solution)/shard_map/ppermute | solution.py:323
  35.7 20.7 %collective-permute-start.8 = (bf16[256,1664]{1,0:T(8,128)(2,1)S(1)}, bf16[256,1664]{1,0:T(8,128)(2,1)}, u32[]{:S(2)}, u32[]{:S(2)}) collective-permute-start(bf16[256,1664]{1,0:T(8,128)(2,1)S(1)} %pad_maximum_fusion.refs_7_), channel_id=1, source_target_pairs={{0,72},{16,272},{1,73},{17,273},{2,74},{18,274},{3,75},{19,275},{4... | collective-permute-start | bytes 2555912 | tf_op jit(solution)/shard_map/ppermute | solution.py:323
  39.1 58.2 %collective-permute-start.9 = (bf16[256,1664]{1,0:T(8,128)(2,1)S(1)}, bf16[256,1664]{1,0:T(8,128)(2,1)}, u32[]{:S(2)}, u32[]{:S(2)}) collective-permute-start(bf16[256,1664]{1,0:T(8,128)(2,1)S(1)} %pad_maximum_fusion.refs_7_), channel_id=1, source_target_pairs={{0,16},{16,0},{1,17},{17,1},{2,18},{18,2},{3,19},{19,3},{4,20},{20... | collective-permute-start | bytes 2555912 | tf_op jit(solution)/shard_map/ppermute | solution.py:323
  44.2 53.0 %collective-permute-start.10 = (bf16[256,1664]{1,0:T(8,128)(2,1)}, bf16[256,1664]{1,0:T(8,128)(2,1)}, u32[]{:S(2)}, u32[]{:S(2)}) collective-permute-start(bf16[256,1664]{1,0:T(8,128)(2,1)} %collective-permute-done.6.refs_8_), channel_id=1, source_target_pairs={{0,16},{16,0},{1,17},{17,1},{2,18},{18,2},{3,19},{19,3},{4,20},{20... | collective-permute-start | bytes 2555912 | tf_op jit(solution)/shard_map/ppermute | solution.py:323
  54.4 42.8 %collective-permute-start.11 = (bf16[256,1664]{1,0:T(8,128)(2,1)}, bf16[256,1664]{1,0:T(8,128)(2,1)}, u32[]{:S(2)}, u32[]{:S(2)}) collective-permute-start(bf16[256,1664]{1,0:T(8,128)(2,1)} %collective-permute-done.7.refs_9_), channel_id=1, source_target_pairs={{0,16},{16,0},{1,17},{17,1},{2,18},{18,2},{3,19},{19,3},{4,20},{20... | collective-permute-start | bytes 2555912 | tf_op jit(solution)/shard_map/ppermute | solution.py:323
  56.3 40.9 %collective-permute-start.12 = (bf16[256,1664]{1,0:T(8,128)(2,1)}, bf16[256,1664]{1,0:T(8,128)(2,1)}, u32[]{:S(2)}, u32[]{:S(2)}) collective-permute-start(bf16[256,1664]{1,0:T(8,128)(2,1)} %collective-permute-done.8.refs_10_), channel_id=1, source_target_pairs={{0,16},{16,0},{1,17},{17,1},{2,18},{18,2},{3,19},{19,3},{4,20},{20... | collective-permute-start | bytes 2555912 | tf_op jit(solution)/shard_map/ppermute | solution.py:323
  68.2 29.0 %copy-start.8 = (bf16[128,1024]{1,0:T(8,128)(2,1)}, bf16[128,1024]{1,0:T(8,128)(2,1)S(1)}, u32[]{:S(2)}) copy-start(bf16[128,1024]{1,0:T(8,128)(2,1)S(1)} %multiply_convert_fusion.refs_2_) | copy-start | bytes 786436
  68.3 19.9 %collective-permute-start = (bf16[128,1024]{1,0:T(8,128)(2,1)S(1)}, bf16[128,1024]{1,0:T(8,128)(2,1)S(1)}, u32[]{:S(2)}, u32[]{:S(2)}) collective-permute-start(bf16[128,1024]{1,0:T(8,128)(2,1)S(1)} %multiply_convert_fusion.refs_2_), channel_id=1, source_target_pairs={{0,1},{1,2},{2,3},{3,4},{4,5},{5,6},{6,7},{7,8},{8,9},{9,10},{10,1... | collective-permute-start | bytes 786440 | tf_op jit(solution)/shard_map/ppermute | solution.py:305
  88.1 8.4 %collective-permute-start.1 = (bf16[128,1024]{1,0:T(8,128)(2,1)S(1)}, bf16[128,1024]{1,0:T(8,128)(2,1)S(1)}, u32[]{:S(2)}, u32[]{:S(2)}) collective-permute-start(bf16[128,1024]{1,0:T(8,128)(2,1)S(1)} %multiply_convert_fusion.refs_2_), channel_id=1, source_target_pairs={{0,15},{1,0},{2,1},{3,2},{4,3},{5,4},{6,5},{7,6},{8,7},{9,8},{10,9... | collective-permute-start | bytes 786440 | tf_op jit(solution)/shard_map/ppermute | solution.py:305
  118.8 11.6 %copy-start.20 = (bf16[100,128]{1,0:T(8,128)(2,1)S(1)}, bf16[100,128]{1,0:T(8,128)(2,1)}, u32[]{:S(2)}) copy-start(bf16[100,128]{1,0:T(8,128)(2,1)} %param.18) | copy-start | bytes 76804
  118.8 36.7 %copy-start.19 = (f32[128]{0:T(128)S(1)}, f32[128]{0:T(128)}, u32[]{:S(2)}) copy-start(f32[128]{0:T(128)} %param.19) | copy-start | bytes 1540
  119.8 35.7 %all-to-all-start = ((bf16[32,112,128]{2,1,0:T(8,128)(2,1)}), bf16[32,112,128]{2,1,0:T(8,128)(2,1)S(1)}, u32[]{:S(2)}, u32[]{:S(2)}) async-start(bf16[32,112,128]{2,1,0:T(8,128)(2,1)} %broadcast_in_dim.8), calls=%async_computation | async-start | bytes 1835008 | tf_op jit(solution)/shard_map/all_to_all | solution.py:444
  160.5 38.4 %copy-start.4 = (bf16[384,1024]{1,0:T(8,128)(2,1)S(1)}, bf16[384,1024]{1,0:T(8,128)(2,1)}, u32[]{:S(2)}) copy-start(bf16[384,1024]{1,0:T(8,128)(2,1)} %copy-done.3) | copy-start | bytes 2359300
  176.3 39.5 %all-to-all-start.2 = ((f32[16,32,128]{2,1,0:T(8,128)}), f32[16,32,128]{2,1,0:T(8,128)}, u32[]{:S(2)}, u32[]{:S(2)}) async-start(f32[16,32,128]{2,1,0:T(8,128)} %broadcast_in_dim.11), calls=%async_computation.2 | async-start | bytes 524288 | tf_op jit(solution)/shard_map/all_to_all | solution.py:481
  187.5 18.9 %collective-permute-start.13 = (bf16[192,128]{1,0:T(8,128)(2,1)S(1)}, bf16[192,128]{1,0:T(8,128)(2,1)S(1)}, u32[]{:S(2)}, u32[]{:S(2)}) collective-permute-start(bf16[192,128]{1,0:T(8,128)(2,1)S(1)} %get-tuple-element.20.refs_17_), channel_id=1, source_target_pairs={{0,1},{1,2},{2,3},{3,4},{4,5},{5,6},{6,7},{7,8},{8,9},{9,10},{10,1... | collective-permute-start | bytes 147464 | tf_op jit(solution)/shard_map/ppermute | solution.py:305
  190.7 15.6 %collective-permute-start.14 = (bf16[192,128]{1,0:T(8,128)(2,1)S(1)}, bf16[192,128]{1,0:T(8,128)(2,1)S(1)}, u32[]{:S(2)}, u32[]{:S(2)}) collective-permute-start(bf16[192,128]{1,0:T(8,128)(2,1)S(1)} %get-tuple-element.20.refs_17_), channel_id=1, source_target_pairs={{0,15},{1,0},{2,1},{3,2},{4,3},{5,4},{6,5},{7,6},{8,7},{9,8},{10,9... | collective-permute-start | bytes 147464 | tf_op jit(solution)/shard_map/ppermute | solution.py:305
  (14 other events, 22.7 us)

commit v4 on v3

--- a/solution.py
+++ b/solution.py
@@ -89,7 +89,7 @@
                     copies.append(
                         pltpu.make_async_copy(
                             piece.at[pl.ds(inner * block, block)],
-                            weights.at[which, pl.ds(chip * block, block)],
+                            weights.at[pl.ds((chip * 2 + which) * block, block)],
                             load.at[(0 if mine else side * side) + outer * side + inner],
                         )
                     )
@@ -112,14 +112,12 @@
         total[...] = nn(hidden[0], decode[...]) + nn(forcing[...], decode[...])
 
     field = normed[...]
-    per_half = pl.num_programs(0) // 2
-    half = step // per_half
-    at = (step - half * per_half) * STEP
-    third = per_half * STEP
+    width = own.shape[1]
+    at = step * STEP
     for index, out in enumerate((queries, keys, values)):
-        cols = pl.ds(pl.multiple_of(index * third + at, STEP), STEP)
-        out[...] = nn(field, weights[half, :, cols]).astype(b16)
-    mixed = weights[0, pl.ds(pl.multiple_of(step * STEP, STEP), STEP), 3 * third :]
+        cols = pl.ds(pl.multiple_of(index * width + at, STEP), STEP)
+        out[...] = nn(field, weights[:, cols]).astype(b16)
+    mixed = weights[pl.ds(pl.multiple_of(at, STEP), STEP), 3 * width :]
     window = window_mask(rows, span)
     masks = head_masks(scale)
     lower = lax.broadcasted_iota(jnp.int32, (rows, LANES), 1) < LANES // 2
@@ -148,7 +146,7 @@
 
 
 def loss_kernel(
-    coeff, variables, others, pred, targets, weight, attended, mixed, lse,
+    coeff, variables, others, theirs, pred, targets, weight, attended, mixed, lse,
     gram, halo, grad_attended,
 ):
     own = pred[...].astype(f32)
@@ -157,13 +155,16 @@
 
     def member(index, carry):
         pair_abs, pair_slope = carry
-        delta = own - others[index].astype(f32)
-        square = delta * delta + KAPPA * KAPPA
-        inverse = lax.rsqrt(square)
-        return pair_abs + (square * inverse - KAPPA), pair_slope + delta * inverse
+        for part in (others, theirs):
+            delta = own - part[index].astype(f32)
+            square = delta * delta + KAPPA * KAPPA
+            inverse = lax.rsqrt(square)
+            pair_abs = pair_abs + (square * inverse - KAPPA)
+            pair_slope = pair_slope + delta * inverse
+        return pair_abs, pair_slope
 
     zero = jnp.zeros((VROWS, LANES), f32)
-    pair_abs, pair_slope = lax.fori_loop(0, others.shape[0], member, (zero, zero), unroll=4)
+    pair_abs, pair_slope = lax.fori_loop(0, others.shape[0], member, (zero, zero), unroll=2)
     delta = own - targets[...].astype(f32)
     square = delta * delta + KAPPA * KAPPA
     inverse = lax.rsqrt(square)
@@ -182,7 +183,7 @@
     for index, piece in enumerate(split_bf16(loss, 3)):
         parts = jnp.where(column == variables + index, piece.astype(f32), parts)
     gram[...] = parts.astype(b16)
-    grad_att = nt(grad_t, mixed[0]).astype(b16)
+    grad_att = nt(grad_t, mixed[...]).astype(b16)
     grad_attended[...] = grad_att
     size = width // HEADS
     head = lax.broadcasted_iota(jnp.int32, (HEADS, width), 0)
@@ -260,7 +261,7 @@
     )
     scaled = head_masks(scale)
     plain = head_masks(1.0)
-    grad_att = nt(grad_t[...], mixed[0]).astype(b16)
+    grad_att = nt(grad_t[...], mixed[...]).astype(b16)
     per_step = 2 * (STEP // LANES)
     d_keys, d_values = [], []
     for pair in range(STEP // LANES):
@@ -281,9 +282,9 @@
         d_keys.append(d_key.astype(b16))
         d_values.append(d_value.astype(b16))
     total[...] += (
-        nt(grad_query[...], wq[0])
-        + nt(jnp.concatenate(d_keys, 1), wk[0])
-        + nt(jnp.concatenate(d_values, 1), wv[0])
+        nt(grad_query[...], wq[...])
+        + nt(jnp.concatenate(d_keys, 1), wk[...])
+        + nt(jnp.concatenate(d_values, 1), wv[...])
     )
 
     @pl.when(step == pl.num_programs(0) - 1)
@@ -335,25 +336,25 @@
     return permute(value, [(0, 0, 1)] * 2)
 
 
-def gathered(w_query, w_key, w_value, mixed, core):
-    half = w_query.shape[1] // 2
-    both = jnp.stack(
-        [
-            jnp.concatenate(
-                [w[:, at : at + half] for w in (w_query, w_key, w_value)] + [mixed], 1
-            )
-            for at in (0, half)
-        ]
-    )
-    first = core == 0
-    keep = jnp.where(first, both[0], both[1])
-    other = swapped(jnp.where(first, both[1], both[0]))
-    block = jnp.where(
-        first, jnp.concatenate([keep, other], 0), jnp.concatenate([other, keep], 0)
-    )
-    row = jnp.concatenate(ring(block, (0, 1)), 0)
-    mine = ring(row, (1, 0))
-    return mine + [swapped(piece) for piece in mine]
+def gathered(packed):
+    return ring(jnp.concatenate(ring(packed, (0, 1)), 0), (1, 0))
+
+
+def everyone(value):
+    value = value[None]
+    for phase in range(2):
+        groups = []
+        for core in range(2):
+            for fixed in range(SIDE):
+                chips = [
+                    step * SIDE + fixed if core == phase else fixed * SIDE + step
+                    for step in range(SIDE)
+                ]
+                groups.append([2 * chip + core for chip in chips])
+        spread = jnp.broadcast_to(value[None], (SIDE,) + value.shape)
+        spread = spread.reshape((-1,) + value.shape[1:])
+        value = lax.all_to_all(spread, "ens", 0, 0, tiled=True, axis_index_groups=groups)
+    return value
 
 
 def per_device(
@@ -370,33 +371,39 @@
     variables = w_decode.shape[1]
     steps = width // STEP
     shape = jax.ShapeDtypeStruct
-    params = pltpu.CompilerParams(
-        dimension_semantics=("arbitrary",), vmem_limit_bytes=48 * 1024 * 1024
-    )
+
+    def params(mebibytes):
+        return pltpu.CompilerParams(
+            dimension_semantics=("arbitrary",), vmem_limit_bytes=mebibytes * 1024 * 1024
+        )
+
+    def cost(us):
+        return pl.CostEstimate(
+            flops=us * 10**9, transcendentals=0, bytes_accessed=us * 3 * 10**6
+        )
     decode = jnp.pad(w_decode, ((0, 0), (0, LANES - variables)))
     mixed = jnp.dot(w_out, decode, preferred_element_type=f32).astype(b16)
     position = lax.axis_index("ens")
     core = position % 2
     place = jnp.stack([position // (2 * SIDE), position // 2 % SIDE, core]).astype(jnp.int32)
-    pieces = gathered(w_query, w_key, w_value, mixed, core)
-    half_width = pieces[0].shape[1]
+    mine = gathered(jnp.concatenate([w_query, w_key, w_value, mixed], 1))
     xfield = hidden[0].astype(f32) + forcing.astype(f32)
     inverse_rms = lax.rsqrt(jnp.mean(xfield * xfield, -1, keepdims=True) + EPS_NORM)
     normed = (xfield * inverse_rms * norm_gain).astype(b16)
     low = shifted(normed, "node", 1)
     high = shifted(normed, "node", -1)
+    mine[-1], low, high = lax.optimization_barrier((mine[-1], low, high))
+    pieces = mine + [swapped(piece) for piece in mine]
 
     def columns(at):
-        per_half = steps // 2
-        return pl.BlockSpec(
-            (1, width, STEP), lambda i: (i // per_half, 0, at * per_half + i % per_half)
-        )
+        return pl.BlockSpec((width, STEP), lambda i: (0, at * steps + i))
 
     def blocks(height, at=0):
         return pl.BlockSpec((height, STEP), lambda i: (at, i))
 
-    mixed_at = half_width // LANES - 1
-    mixed_block = pl.BlockSpec((1, STEP, LANES), lambda i: (0, i, mixed_at))
+    mixed_at = 3 * width // LANES
+    packed_width = 3 * width + LANES
+    mixed_block = pl.BlockSpec((STEP, LANES), lambda i: (i, mixed_at))
     anywhere = pl.BlockSpec(memory_space=pl.ANY)
     own_block = whole((1, node_rows, width))
     queries, keys, values, attended, lse, pred, full = pl.pallas_call(
@@ -428,22 +435,22 @@
             shape((node_rows, width), b16),
             shape((node_rows, width), f32),
             shape((VROWS, node_rows), b16),
-            shape((2, width, half_width), b16),
+            shape((width, packed_width), b16),
         ],
         scratch_shapes=[
             pltpu.VMEM((span, width), b16),
             pltpu.VMEM((node_rows, LANES), f32),
-            pltpu.VMEM((2, width, half_width), b16),
+            pltpu.VMEM((width, packed_width), b16),
             pltpu.SemaphoreType.DMA((len(pieces) * SIDE,)),
             pltpu.SemaphoreType.DMA((1,)),
         ],
-        compiler_params=params,
+        compiler_params=params(24),
+        cost_estimate=cost(12),
         name="forward",
     )(place, low, normed, high, hidden, forcing, decode, *pieces)
 
-    others = lax.all_to_all(
-        jnp.broadcast_to(pred[None], (members,) + pred.shape), "ens", 0, 0, tiled=True
-    )
+    others = everyone(pred)
+    theirs = swapped(others)
     eps = (1.0 - ALPHA) / members
     coeff = (1.0 - eps) / (2.0 * (members - 1))
     truth = jnp.pad(targets, ((0, VROWS - variables), (0, 0)))
@@ -452,12 +459,13 @@
         lambda *refs: loss_kernel(coeff, variables, *refs),
         grid=(1,),
         in_specs=[
-            whole((members, VROWS, node_rows)),
+            whole(others.shape),
+            whole(others.shape),
             whole((VROWS, node_rows)),
             whole((VROWS, node_rows)),
             whole((1, node_rows)),
             whole((node_rows, width)),
-            pl.BlockSpec((1, width, LANES), lambda i: (0, 0, mixed_at)),
+            pl.BlockSpec((width, LANES), lambda i: (0, mixed_at)),
             whole((node_rows, width)),
         ],
         out_specs=[
@@ -470,9 +478,10 @@
             shape((payload, node_rows), b16),
             shape((node_rows, width), b16),
         ],
-        compiler_params=params,
+        compiler_params=params(12),
+        cost_estimate=cost(3),
         name="crps",
-    )(others, pred, truth, area_weight[None], attended, full, lse)
+    )(others, theirs, pred, truth, area_weight[None], attended, full, lse)
 
     halo_low = shifted(halo, "node", 1)
     halo_high = shifted(halo, "node", -1)
@@ -506,7 +515,8 @@
             shape((node_rows, width), f32),
             shape((node_rows, width), f32),
         ],
-        compiler_params=params,
+        compiler_params=params(12),
+        cost_estimate=cost(6),
         name="own_queries",
     )(queries, keys, values, grad_attended, lse)
 
@@ -541,7 +551,8 @@
             pltpu.VMEM((2, HEADS, 2 * HALO), f32),
             pltpu.VMEM((node_rows, width), f32),
         ],
-        compiler_params=params,
+        compiler_params=params(16),
+        cost_estimate=cost(9),
         name="neighbour_queries",
     )(
         halo_low, halo_high, queries, queries, keys, values, grad_query, key_part, value_part,

time: 222 us -> 188 us (0.85)
  waiting for transfers between devices: 60.3 us -> 13.2 us
  local copies, waits for them, and re-layouts: 15.5 us -> 24.6 us
  starting transfers between devices: 89.8 us -> 92.5 us
    all_to_all x1, waiting for transfers between devices: 25.1 us -> 1 us  [per_device(): lax.all_to_all(gram.reshape(members, rows, LANES), 'ens', 0, 0, tiled=True)]
    ppermute x4, waiting for transfers between devices: 23 us -> 4.72 us  [shifted(): return lax.ppermute(value, axis, pairs)]
    unnamed x43 -> x57, local copies, waits for them, and re-layouts: 11.9 us -> 22.6 us
    ppermute x11, starting transfers between devices: 51.7 us -> 58.6 us  [permute(): return lax.ppermute(value, ('ens', 'node'), pairs)]
    ppermute x4, starting transfers between devices: 16.4 us -> 22.6 us  [shifted(): return lax.ppermute(value, axis, pairs)]
    all_to_all x1, starting transfers between devices: 10.6 us -> 4.47 us  [per_device(): lax.all_to_all(gram.reshape(members, rows, LANES), 'ens', 0, 0, tiled=True)]
    ppermute x11, waiting for transfers between devices: 12.3 us -> 7.47 us  [permute(): return lax.ppermute(value, ('ens', 'node'), pairs)]
    all_to_all x1, starting transfers between devices: 11.2 us -> 6.84 us  [per_device(): lax.all_to_all(jnp.broadcast_to(part[None], (shards,) + part.shape), 'nod...]
  transfers between devices with their start and end apart: 17 -> 17, of which waited for: 7 -> 5; matrix products, arithmetic and copies ran while one was open for 0% -> 1% of each run, Pallas kernels for 7% -> 8%
where the time goes in v4:
time: 188 us; the launch traced here: 187 us
  starting transfers between devices  92.5 us (49%)
  Pallas kernels  32.9 us (18%)
  local copies, waits for them, and re-layouts  24.6 us (13%)
  blocking collectives  16.9 us (9%)
  waiting for transfers between devices  13.2 us (7%)
  other arithmetic  3.01 us (2%)
  between operations  2.93 us (2%)
    ppermute x11, starting transfers between devices, permute(): return lax.ppermute(value, ('ens', 'node'), pairs)  58.6 us
    unnamed x57, local copies, waits for them, and re-layouts  22.6 us
    ppermute x4, starting transfers between devices, shifted(): return lax.ppermute(value, axis, pairs)  22.6 us
    all_to_all x2, blocking collectives, everyone(): lax.all_to_all(spread, 'ens', 0, 0, tiled=True, axis_index_groups=groups)  16.9 us
    pallas_call x1, Pallas kernels, per_device(): pl.pallas_call(lambda *refs: forward_kernel(scale, *refs), grid=(steps,),...  16.8 us
    pallas_call x1, Pallas kernels, per_device(): pl.pallas_call(lambda *refs: halo_kernel(scale, *refs), grid=(steps,), in...  8.67 us
    ppermute x11, waiting for transfers between devices, permute(): return lax.ppermute(value, ('ens', 'node'), pairs)  7.47 us
    all_to_all x1, starting transfers between devices, per_device(): lax.all_to_all(jnp.broadcast_to(part[None], (shards,) + part.shape), 'nod...  6.84 us
  transfers between devices with their start and end apart: 17, of which 5 were waited for; matrix products, arithmetic and copies ran while one was open for 1% of the time, Pallas kernels for 8%

profile of v4, /device:TPU:1, one launch (start us, length us, event | category | flops | bytes accessed | tf_op | source)
XLA Modules:
  0.0 186.9 jit_solution(214630584191536042)
XLA Ops:
  3.0 4.8 %collective-permute-start = (bf16[32,3200]{1,0:T(8,128)(2,1)S(1)}, bf16[32,3200]{1,0:T(8,128)(2,1)S(1)}, u32[]{:S(2)}, u32[]{:S(2)}) collective-permute-start(bf16[32,3200]{1,0:T(8,128)(2,1)S(1)} %pad_maximum_fusion.1), channel_id=1, source_target_pairs={{0,128},{16,48},{1,129},{17,49},{2,130},{18,50},{3,131},{19,51},{4... | collective-permute-start | bytes 614408 | tf_op jit(solution)/shard_map/ppermute | solution.py:324
  7.8 8.6 %collective-permute-start.1 = (bf16[32,3200]{1,0:T(8,128)(2,1)S(1)}, bf16[32,3200]{1,0:T(8,128)(2,1)S(1)}, u32[]{:S(2)}, u32[]{:S(2)}) collective-permute-start(bf16[32,3200]{1,0:T(8,128)(2,1)S(1)} %pad_maximum_fusion.1), channel_id=1, source_target_pairs={{0,384},{16,120},{1,385},{17,121},{2,386},{18,122},{3,387},{19,123... | collective-permute-start | bytes 614408 | tf_op jit(solution)/shard_map/ppermute | solution.py:324
  16.4 3.4 %collective-permute-start.2 = (bf16[32,3200]{1,0:T(8,128)(2,1)S(1)}, bf16[32,3200]{1,0:T(8,128)(2,1)S(1)}, u32[]{:S(2)}, u32[]{:S(2)}) collective-permute-start(bf16[32,3200]{1,0:T(8,128)(2,1)S(1)} %pad_maximum_fusion.1), channel_id=1, source_target_pairs={{0,256},{16,88},{1,257},{17,89},{2,258},{18,90},{3,259},{19,91},{4... | collective-permute-start | bytes 614408 | tf_op jit(solution)/shard_map/ppermute | solution.py:324
  19.8 4.7 %collective-permute-done.2 = bf16[32,3200]{1,0:T(8,128)(2,1)S(1)} collective-permute-done((bf16[32,3200]{1,0:T(8,128)(2,1)S(1)}, bf16[32,3200]{1,0:T(8,128)(2,1)S(1)}, u32[]{:S(2)}, u32[]{:S(2)}) %collective-permute-start.2) | collective-permute-done | bytes 204832 | tf_op jit(solution)/shard_map/ppermute | solution.py:324
  25.5 4.4 %collective-permute-start.3 = (bf16[128,3200]{1,0:T(8,128)(2,1)S(1)}, bf16[128,3200]{1,0:T(8,128)(2,1)S(1)}, u32[]{:S(2)}, u32[]{:S(2)}) collective-permute-start(bf16[128,3200]{1,0:T(8,128)(2,1)S(1)} %pad_maximum_fusion.refs_7_), channel_id=1, source_target_pairs={{0,72},{16,272},{1,73},{17,273},{2,74},{18,274},{3,75},{19,275},{4... | collective-permute-start | bytes 2457608 | tf_op jit(solution)/shard_map/ppermute | solution.py:324
  29.9 2.8 %collective-permute-start.7 = (bf16[128,3200]{1,0:T(8,128)(2,1)S(1)}, bf16[128,3200]{1,0:T(8,128)(2,1)}, u32[]{:S(2)}, u32[]{:S(2)}) collective-permute-start(bf16[128,3200]{1,0:T(8,128)(2,1)S(1)} %pad_maximum_fusion.refs_7_), channel_id=1, source_target_pairs={{0,104},{16,400},{1,105},{17,401},{2,106},{18,402},{3,107},{19,403... | collective-permute-start | bytes 2457608 | tf_op jit(solution)/shard_map/ppermute | solution.py:324
  35.5 3.2 %collective-permute-start.4 = (bf16[128,1024]{1,0:T(8,128)(2,1)S(1)}, bf16[128,1024]{1,0:T(8,128)(2,1)S(1)}, u32[]{:S(2)}, u32[]{:S(2)}) collective-permute-start(bf16[128,1024]{1,0:T(8,128)(2,1)S(1)} %multiply_convert_fusion.refs_2_), channel_id=1, source_target_pairs={{0,1},{1,2},{2,3},{3,4},{4,5},{5,6},{6,7},{7,8},{8,9},{9,10},{10,1... | collective-permute-start | bytes 786440 | tf_op jit(solution)/shard_map/ppermute | solution.py:306
  38.7 8.1 %collective-permute-start.5 = (bf16[128,1024]{1,0:T(8,128)(2,1)S(1)}, bf16[128,1024]{1,0:T(8,128)(2,1)S(1)}, u32[]{:S(2)}, u32[]{:S(2)}) collective-permute-start(bf16[128,1024]{1,0:T(8,128)(2,1)S(1)} %multiply_convert_fusion.refs_2_), channel_id=1, source_target_pairs={{0,15},{1,0},{2,1},{3,2},{4,3},{5,4},{6,5},{7,6},{8,7},{9,8},{10,9... | collective-permute-start | bytes 786440 | tf_op jit(solution)/shard_map/ppermute | solution.py:306
  46.8 4.7 %collective-permute-done.4.refs_1_ = bf16[128,1024]{1,0:T(8,128)(2,1)S(1)} collective-permute-done((bf16[128,1024]{1,0:T(8,128)(2,1)S(1)}, bf16[128,1024]{1,0:T(8,128)(2,1)S(1)}, u32[]{:S(2)}, u32[]{:S(2)}) %collective-permute-start.4) | collective-permute-done | bytes 262176 | tf_op jit(solution)/shard_map/ppermute | solution.py:306
  51.5 8.6 %collective-permute-start.8 = (bf16[128,3200]{1,0:T(8,128)(2,1)S(1)}, bf16[128,3200]{1,0:T(8,128)(2,1)}, u32[]{:S(2)}, u32[]{:S(2)}) collective-permute-start(bf16[128,3200]{1,0:T(8,128)(2,1)S(1)} %pad_maximum_fusion.refs_7_), channel_id=1, source_target_pairs={{0,16},{16,0},{1,17},{17,1},{2,18},{18,2},{3,19},{19,3},{4,20},{20... | collective-permute-start | bytes 2457608 | tf_op jit(solution)/shard_map/ppermute | solution.py:324
  60.2 6.4 %collective-permute-start.11 = (bf16[128,3200]{1,0:T(8,128)(2,1)S(1)}, bf16[128,3200]{1,0:T(8,128)(2,1)}, u32[]{:S(2)}, u32[]{:S(2)}) collective-permute-start(bf16[128,3200]{1,0:T(8,128)(2,1)S(1)} %collective-permute-done.3.refs_10_), channel_id=1, source_target_pairs={{0,16},{16,0},{1,17},{17,1},{2,18},{18,2},{3,19},{19,3},{4,20},{20... | collective-permute-start | bytes 2457608 | tf_op jit(solution)/shard_map/ppermute | solution.py:324
  66.5 8.8 %collective-permute-start.10 = (bf16[128,3200]{1,0:T(8,128)(2,1)}, bf16[128,3200]{1,0:T(8,128)(2,1)}, u32[]{:S(2)}, u32[]{:S(2)}) collective-permute-start(bf16[128,3200]{1,0:T(8,128)(2,1)} %collective-permute-done.7.refs_9_), channel_id=1, source_target_pairs={{0,16},{16,0},{1,17},{17,1},{2,18},{18,2},{3,19},{19,3},{4,20},{20... | collective-permute-start | bytes 2457608 | tf_op jit(solution)/shard_map/ppermute | solution.py:324
  79.9 16.8 %forward.1 = (bf16[384,1024]{1,0:T(8,128)(2,1)S(1)}, bf16[384,1024]{1,0:T(8,128)(2,1)S(1)}, bf16[384,1024]{1,0:T(8,128)(2,1)S(1)}, bf16[128,1024]{1,0:T(8,128)(2...) custom-call(s32[3]{0:T(128)S(1)} %pad_add_fusion.refs_0_, ...), custom_call_target="tpu_custom_call" | custom-call | flops 12000000000 | bytes 36000000 | tf_op jit(solution)/shard_map/forward/pallas_call | solution.py:409
  96.7 2.7 %copy-done.5 = bf16[1024,3200]{1,0:T(8,128)(2,1)} copy-done((bf16[1024,3200]{1,0:T(8,128)(2,1)}, bf16[1024,3200]{1,0:T(8,128)(2,1)S(1)}, u32[]{:S(2)}) %copy-start.5) | copy-done | bytes 6553624
  101.2 7.2 %all_to_all.20 = bf16[4,112,128]{2,1,0:T(8,128)(2,1)S(1)} all-to-all(bf16[4,112,128]{2,1,0:T(8,128)(2,1)S(1)} %reshape.44), channel_id=1, replica_groups={{0,128,256,384},{32,160,288,416},{64,192,320,448},{96,224,352,480},{16,..., dimensions={0} | all-to-all | bytes 229376 | tf_op jit(solution)/shard_map/all_to_all | solution.py:356
  108.5 9.7 %all_to_all.21.refs_0_ = bf16[16,112,128]{2,1,0:T(8,128)(2,1)S(1)} all-to-all(bf16[16,112,128]{2,1,0:T(8,128)(2,1)S(1)} %bitcast.19), channel_id=1, replica_groups={{0,32,64,96},{128,160,192,224},{256,288,320,352},{384,416,448,480},{16,..., dimensions={0} | all-to-all | bytes 917504 | tf_op jit(solution)/shard_map/all_to_all | solution.py:356
  118.1 6.5 %collective-permute-start.12 = (bf16[16,112,128]{2,1,0:T(8,128)(2,1)S(1)}, bf16[16,112,128]{2,1,0:T(8,128)(2,1)S(1)}, u32[]{:S(2)}, u32[]{:S(2)}) collective-permute-start(bf16[16,112,128]{2,1,0:T(8,128)(2,1)S(1)} %all_to_all.21.refs_0_), channel_id=1, source_target_pairs={{0,16},{16,0},{1,17},{17,1},{2,18},{18,2},{3,19},{19,3},{4,20},{20... | collective-permute-start | bytes 1376264 | tf_op jit(solution)/shard_map/ppermute | solution.py:324
  126.1 2.9 %copy-done.6 = bf16[1024,3200]{1,0:T(8,128)(2,1)S(1)} copy-done((bf16[1024,3200]{1,0:T(8,128)(2,1)S(1)}, bf16[1024,3200]{1,0:T(8,128)(2,1)}, u32[]{:S(2)}) %copy-start.6) | copy-done | bytes 6553624
  134.8 9.4 %collective-permute-start.14 = (bf16[192,128]{1,0:T(8,128)(2,1)S(1)}, bf16[192,128]{1,0:T(8,128)(2,1)S(1)}, u32[]{:S(2)}, u32[]{:S(2)}) collective-permute-start(bf16[192,128]{1,0:T(8,128)(2,1)S(1)} %get-tuple-element.26.refs_17_), channel_id=1, source_target_pairs={{0,15},{1,0},{2,1},{3,2},{4,3},{5,4},{6,5},{7,6},{8,7},{9,8},{10,9... | collective-permute-start | bytes 147464 | tf_op jit(solution)/shard_map/ppermute | solution.py:306
  144.2 4.5 %all-to-all-start.2 = ((bf16[32,32,128]{2,1,0:T(8,128)(2,1)}), bf16[32,32,128]{2,1,0:T(8,128)(2,1)S(1)}, u32[]{:S(2)}, u32[]{:S(2)}) async-start(bf16[32,32,128]{2,1,0:T(8,128)(2,1)} %bitcast.9), calls=%async_computation.2 | async-start | bytes 524288 | tf_op jit(solution)/shard_map/all_to_all | solution.py:488
  152.0 5.4 %own_queries.1 = (bf16[128,1024]{1,0:T(8,128)(2,1)S(1)}, f32[128,1024]{1,0:T(8,128)S(1)}, f32[128,1024]{1,0:T(8,128)S(1)}) custom-call(bf16[384,1024]{1,0:T(8,128)(2,1)S(1)} %copy-done.9, bf16[384,1024]{1,0:T(8,128)(2,1)S(1)} %copy-done.11, bf16[384,1024]{1,0:T(8,128)(2,1)S(1)} %copy-done.14, bf16[128,1024]{1,0:T(8,128)(2,1)S(1)} %get-tuple-element.30.refs_3_, ...), custom_call_target="tpu_custom_call" | custom-call | flops 6000000000 | bytes 18000000 | tf_op jit(solution)/shard_map/own_queries/pallas_call | solution.py:502
  160.8 6.8 %all-to-all-start.3 = ((f32[16,32,128]{2,1,0:T(8,128)}), f32[16,32,128]{2,1,0:T(8,128)S(1)}, u32[]{:S(2)}, u32[]{:S(2)}) async-start(f32[16,32,128]{2,1,0:T(8,128)} %broadcast_in_dim.11), calls=%async_computation.3 | async-start | bytes 524288 | tf_op jit(solution)/shard_map/all_to_all | solution.py:490
  167.7 2.9 %copy-done.7 = bf16[1024,3200]{1,0:T(8,128)(2,1)S(1)} copy-done((bf16[1024,3200]{1,0:T(8,128)(2,1)S(1)}, bf16[1024,3200]{1,0:T(8,128)(2,1)}, u32[]{:S(2)}) %copy-start.7) | copy-done | bytes 6553624
  174.9 8.7 %neighbour_queries.1 = bf16[1,128,1024]{2,1,0:T(8,128)(2,1)} custom-call(bf16[192,128]{1,0:T(8,128)(2,1)S(1)} %collective-permute-done.13.refs_0_, bf16[192,128]{1,0:T(8,128)(2,1)S(1)} %collective-permute-done.14.refs_1_, bf16[384,1024]{1,0:T(8,128)(2,1)S(1)} %copy-done.9, bf16[384,1024]{1,0:T(8,128)(2,1)S(1)} %copy-done.9, ...), custom_call_target="tpu_custom_call" | custom-call | flops 8999999488 | bytes 27000000 | tf_op jit(solution)/shard_map/neighbour_queries/pallas_call | solution.py:523
  (90 shorter events, 32.2 us)
Async XLA Ops:
  0.6 34.6 %copy-start.2 = (bf16[1,128,1024]{2,1,0:T(8,128)(2,1)S(1)}, bf16[1,128,1024]{2,1,0:T(8,128)(2,1)}, u32[]{:S(2)}) copy-start(bf16[1,128,1024]{2,1,0:T(8,128)(2,1)} %refs_13_.1) | copy-start | bytes 786436
  0.7 34.6 %copy-start.1 = (bf16[128,1024]{1,0:T(8,128)(2,1)S(1)}, bf16[128,1024]{1,0:T(8,128)(2,1)}, u32[]{:S(2)}) copy-start(bf16[128,1024]{1,0:T(8,128)(2,1)} %refs_14_.1) | copy-start | bytes 786436
  0.7 34.7 %copy-start.3 = (f32[1024]{0:T(1024)S(1)}, f32[1024]{0:T(1024)}, u32[]{:S(2)}) copy-start(f32[1024]{0:T(1024)} %param.12) | copy-start | bytes 12292
  3.0 16.8 %collective-permute-start = (bf16[32,3200]{1,0:T(8,128)(2,1)S(1)}, bf16[32,3200]{1,0:T(8,128)(2,1)S(1)}, u32[]{:S(2)}, u32[]{:S(2)}) collective-permute-start(bf16[32,3200]{1,0:T(8,128)(2,1)S(1)} %pad_maximum_fusion.1), channel_id=1, source_target_pairs={{0,128},{16,48},{1,129},{17,49},{2,130},{18,50},{3,131},{19,51},{4... | collective-permute-start | bytes 614408 | tf_op jit(solution)/shard_map/ppermute | solution.py:324
  7.8 12.0 %collective-permute-start.1 = (bf16[32,3200]{1,0:T(8,128)(2,1)S(1)}, bf16[32,3200]{1,0:T(8,128)(2,1)S(1)}, u32[]{:S(2)}, u32[]{:S(2)}) collective-permute-start(bf16[32,3200]{1,0:T(8,128)(2,1)S(1)} %pad_maximum_fusion.1), channel_id=1, source_target_pairs={{0,384},{16,120},{1,385},{17,121},{2,386},{18,122},{3,387},{19,123... | collective-permute-start | bytes 614408 | tf_op jit(solution)/shard_map/ppermute | solution.py:324
  16.4 8.1 %collective-permute-start.2 = (bf16[32,3200]{1,0:T(8,128)(2,1)S(1)}, bf16[32,3200]{1,0:T(8,128)(2,1)S(1)}, u32[]{:S(2)}, u32[]{:S(2)}) collective-permute-start(bf16[32,3200]{1,0:T(8,128)(2,1)S(1)} %pad_maximum_fusion.1), channel_id=1, source_target_pairs={{0,256},{16,88},{1,257},{17,89},{2,258},{18,90},{3,259},{19,91},{4... | collective-permute-start | bytes 614408 | tf_op jit(solution)/shard_map/ppermute | solution.py:324
  25.5 34.7 %collective-permute-start.3 = (bf16[128,3200]{1,0:T(8,128)(2,1)S(1)}, bf16[128,3200]{1,0:T(8,128)(2,1)S(1)}, u32[]{:S(2)}, u32[]{:S(2)}) collective-permute-start(bf16[128,3200]{1,0:T(8,128)(2,1)S(1)} %pad_maximum_fusion.refs_7_), channel_id=1, source_target_pairs={{0,72},{16,272},{1,73},{17,273},{2,74},{18,274},{3,75},{19,275},{4... | collective-permute-start | bytes 2457608 | tf_op jit(solution)/shard_map/ppermute | solution.py:324
  29.9 36.6 %collective-permute-start.7 = (bf16[128,3200]{1,0:T(8,128)(2,1)S(1)}, bf16[128,3200]{1,0:T(8,128)(2,1)}, u32[]{:S(2)}, u32[]{:S(2)}) collective-permute-start(bf16[128,3200]{1,0:T(8,128)(2,1)S(1)} %pad_maximum_fusion.refs_7_), channel_id=1, source_target_pairs={{0,104},{16,400},{1,105},{17,401},{2,106},{18,402},{3,107},{19,403... | collective-permute-start | bytes 2457608 | tf_op jit(solution)/shard_map/ppermute | solution.py:324
  32.7 42.6 %collective-permute-start.6 = (bf16[128,3200]{1,0:T(8,128)(2,1)S(1)}, bf16[128,3200]{1,0:T(8,128)(2,1)}, u32[]{:S(2)}, u32[]{:S(2)}) collective-permute-start(bf16[128,3200]{1,0:T(8,128)(2,1)S(1)} %pad_maximum_fusion.refs_7_), channel_id=1, source_target_pairs={{0,32},{16,144},{1,33},{17,145},{2,34},{18,146},{3,35},{19,147},{4... | collective-permute-start | bytes 2457608 | tf_op jit(solution)/shard_map/ppermute | solution.py:324
  35.5 16.0 %collective-permute-start.4 = (bf16[128,1024]{1,0:T(8,128)(2,1)S(1)}, bf16[128,1024]{1,0:T(8,128)(2,1)S(1)}, u32[]{:S(2)}, u32[]{:S(2)}) collective-permute-start(bf16[128,1024]{1,0:T(8,128)(2,1)S(1)} %multiply_convert_fusion.refs_2_), channel_id=1, source_target_pairs={{0,1},{1,2},{2,3},{3,4},{4,5},{5,6},{6,7},{7,8},{8,9},{9,10},{10,1... | collective-permute-start | bytes 786440 | tf_op jit(solution)/shard_map/ppermute | solution.py:306
  38.7 21.4 %collective-permute-start.5 = (bf16[128,1024]{1,0:T(8,128)(2,1)S(1)}, bf16[128,1024]{1,0:T(8,128)(2,1)S(1)}, u32[]{:S(2)}, u32[]{:S(2)}) collective-permute-start(bf16[128,1024]{1,0:T(8,128)(2,1)S(1)} %multiply_convert_fusion.refs_2_), channel_id=1, source_target_pairs={{0,15},{1,0},{2,1},{3,2},{4,3},{5,4},{6,5},{7,6},{8,7},{9,8},{10,9... | collective-permute-start | bytes 786440 | tf_op jit(solution)/shard_map/ppermute | solution.py:306
  51.5 26.9 %collective-permute-start.8 = (bf16[128,3200]{1,0:T(8,128)(2,1)S(1)}, bf16[128,3200]{1,0:T(8,128)(2,1)}, u32[]{:S(2)}, u32[]{:S(2)}) collective-permute-start(bf16[128,3200]{1,0:T(8,128)(2,1)S(1)} %pad_maximum_fusion.refs_7_), channel_id=1, source_target_pairs={{0,16},{16,0},{1,17},{17,1},{2,18},{18,2},{3,19},{19,3},{4,20},{20... | collective-permute-start | bytes 2457608 | tf_op jit(solution)/shard_map/ppermute | solution.py:324
  60.2 18.2 %collective-permute-start.11 = (bf16[128,3200]{1,0:T(8,128)(2,1)S(1)}, bf16[128,3200]{1,0:T(8,128)(2,1)}, u32[]{:S(2)}, u32[]{:S(2)}) collective-permute-start(bf16[128,3200]{1,0:T(8,128)(2,1)S(1)} %collective-permute-done.3.refs_10_), channel_id=1, source_target_pairs={{0,16},{16,0},{1,17},{17,1},{2,18},{18,2},{3,19},{19,3},{4,20},{20... | collective-permute-start | bytes 2457608 | tf_op jit(solution)/shard_map/ppermute | solution.py:324
  66.5 11.9 %collective-permute-start.10 = (bf16[128,3200]{1,0:T(8,128)(2,1)}, bf16[128,3200]{1,0:T(8,128)(2,1)}, u32[]{:S(2)}, u32[]{:S(2)}) collective-permute-start(bf16[128,3200]{1,0:T(8,128)(2,1)} %collective-permute-done.7.refs_9_), channel_id=1, source_target_pairs={{0,16},{16,0},{1,17},{17,1},{2,18},{18,2},{3,19},{19,3},{4,20},{20... | collective-permute-start | bytes 2457608 | tf_op jit(solution)/shard_map/ppermute | solution.py:324
  75.3 4.6 %collective-permute-start.9 = (bf16[128,3200]{1,0:T(8,128)(2,1)}, bf16[128,3200]{1,0:T(8,128)(2,1)}, u32[]{:S(2)}, u32[]{:S(2)}) collective-permute-start(bf16[128,3200]{1,0:T(8,128)(2,1)} %collective-permute-done.6.refs_8_), channel_id=1, source_target_pairs={{0,16},{16,0},{1,17},{17,1},{2,18},{18,2},{3,19},{19,3},{4,20},{20... | collective-permute-start | bytes 2457608 | tf_op jit(solution)/shard_map/ppermute | solution.py:324
  101.1 23.5 %copy-start.8 = (bf16[384,1024]{1,0:T(8,128)(2,1)}, bf16[384,1024]{1,0:T(8,128)(2,1)S(1)}, u32[]{:S(2)}) copy-start(bf16[384,1024]{1,0:T(8,128)(2,1)S(1)} %get-tuple-element.27.refs_0_.refs_2_.refs_3_) | copy-start | bytes 2359300
  101.1 23.5 %copy-start.10 = (bf16[384,1024]{1,0:T(8,128)(2,1)}, bf16[384,1024]{1,0:T(8,128)(2,1)S(1)}, u32[]{:S(2)}) copy-start(bf16[384,1024]{1,0:T(8,128)(2,1)S(1)} %get-tuple-element.28.refs_1_.refs_4_) | copy-start | bytes 2359300
  101.1 23.5 %copy-start.23 = (bf16[128,1024]{1,0:T(8,128)(2,1)}, bf16[128,1024]{1,0:T(8,128)(2,1)S(1)}, u32[]{:S(2)}) copy-start(bf16[128,1024]{1,0:T(8,128)(2,1)S(1)} %get-tuple-element.23.refs_5_) | copy-start | bytes 786436
  101.1 24.9 %copy-start.4 = (f32[128]{0:T(128)S(1)}, f32[128]{0:T(128)}, u32[]{:S(2)}) copy-start(f32[128]{0:T(128)} %param.19) | copy-start | bytes 1540
  118.1 7.9 %collective-permute-start.12 = (bf16[16,112,128]{2,1,0:T(8,128)(2,1)S(1)}, bf16[16,112,128]{2,1,0:T(8,128)(2,1)S(1)}, u32[]{:S(2)}, u32[]{:S(2)}) collective-permute-start(bf16[16,112,128]{2,1,0:T(8,128)(2,1)S(1)} %all_to_all.21.refs_0_), channel_id=1, source_target_pairs={{0,16},{16,0},{1,17},{17,1},{2,18},{18,2},{3,19},{19,3},{4,20},{20... | collective-permute-start | bytes 1376264 | tf_op jit(solution)/shard_map/ppermute | solution.py:324
  132.9 34.8 %collective-permute-start.13 = (bf16[192,128]{1,0:T(8,128)(2,1)S(1)}, bf16[192,128]{1,0:T(8,128)(2,1)S(1)}, u32[]{:S(2)}, u32[]{:S(2)}) collective-permute-start(bf16[192,128]{1,0:T(8,128)(2,1)S(1)} %get-tuple-element.26.refs_17_), channel_id=1, source_target_pairs={{0,1},{1,2},{2,3},{3,4},{4,5},{5,6},{6,7},{7,8},{8,9},{9,10},{10,1... | collective-permute-start | bytes 147464 | tf_op jit(solution)/shard_map/ppermute | solution.py:306
  134.8 32.9 %collective-permute-start.14 = (bf16[192,128]{1,0:T(8,128)(2,1)S(1)}, bf16[192,128]{1,0:T(8,128)(2,1)S(1)}, u32[]{:S(2)}, u32[]{:S(2)}) collective-permute-start(bf16[192,128]{1,0:T(8,128)(2,1)S(1)} %get-tuple-element.26.refs_17_), channel_id=1, source_target_pairs={{0,15},{1,0},{2,1},{3,2},{4,3},{5,4},{6,5},{7,6},{8,7},{9,8},{10,9... | collective-permute-start | bytes 147464 | tf_op jit(solution)/shard_map/ppermute | solution.py:306
  144.2 15.9 %all-to-all-start.2 = ((bf16[32,32,128]{2,1,0:T(8,128)(2,1)}), bf16[32,32,128]{2,1,0:T(8,128)(2,1)S(1)}, u32[]{:S(2)}, u32[]{:S(2)}) async-start(bf16[32,32,128]{2,1,0:T(8,128)(2,1)} %bitcast.9), calls=%async_computation.2 | async-start | bytes 524288 | tf_op jit(solution)/shard_map/all_to_all | solution.py:488
  160.8 22.8 %all-to-all-start.3 = ((f32[16,32,128]{2,1,0:T(8,128)}), f32[16,32,128]{2,1,0:T(8,128)S(1)}, u32[]{:S(2)}, u32[]{:S(2)}) async-start(f32[16,32,128]{2,1,0:T(8,128)} %broadcast_in_dim.11), calls=%async_computation.3 | async-start | bytes 524288 | tf_op jit(solution)/shard_map/all_to_all | solution.py:490
  (21 other events, 90.5 us)

commit v5 on v4

--- a/solution.py
+++ b/solution.py
@@ -313,6 +313,8 @@
             for y in range(RING_Y):
                 for core in range(2):
                     dx, dz, dc = moves[core]
+                    dz = -dz if dz == -2 and z % 2 == 0 else dz
+                    dx = -dx if dx == -2 and x % 2 == 0 else dx
                     at = (x, z, core)
                     to = ((x + dx) % SIDE, (z + dz) % RING_Z, core ^ dc)
                     pairs.append(
@@ -336,8 +338,8 @@
     return permute(value, [(0, 0, 1)] * 2)
 
 
-def gathered(packed):
-    return ring(jnp.concatenate(ring(packed, (0, 1)), 0), (1, 0))
+def gathered(row):
+    return ring(row, (1, 0))
 
 
 def everyone(value):
@@ -386,13 +388,15 @@
     position = lax.axis_index("ens")
     core = position % 2
     place = jnp.stack([position // (2 * SIDE), position // 2 % SIDE, core]).astype(jnp.int32)
-    mine = gathered(jnp.concatenate([w_query, w_key, w_value, mixed], 1))
+    row = ring(jnp.concatenate([w_query, w_key, w_value, mixed], 1), (0, 1))
     xfield = hidden[0].astype(f32) + forcing.astype(f32)
     inverse_rms = lax.rsqrt(jnp.mean(xfield * xfield, -1, keepdims=True) + EPS_NORM)
     normed = (xfield * inverse_rms * norm_gain).astype(b16)
     low = shifted(normed, "node", 1)
     high = shifted(normed, "node", -1)
-    mine[-1], low, high = lax.optimization_barrier((mine[-1], low, high))
+    row = jnp.concatenate(row, 0)
+    row, low, high = lax.optimization_barrier((row, low, high))
+    mine = gathered(row)
     pieces = mine + [swapped(piece) for piece in mine]
 
     def columns(at):
@@ -429,13 +433,13 @@
             anywhere,
         ],
         out_shape=[
-            shape((span, width), b16),
-            shape((span, width), b16),
-            shape((span, width), b16),
-            shape((node_rows, width), b16),
-            shape((node_rows, width), f32),
-            shape((VROWS, node_rows), b16),
-            shape((width, packed_width), b16),
+            pltpu.HBM((span, width), b16),
+            pltpu.HBM((span, width), b16),
+            pltpu.HBM((span, width), b16),
+            pltpu.HBM((node_rows, width), b16),
+            pltpu.HBM((node_rows, width), f32),
+            pltpu.HBM((VROWS, node_rows), b16),
+            pltpu.HBM((width, packed_width), b16),
         ],
         scratch_shapes=[
             pltpu.VMEM((span, width), b16),
@@ -511,9 +515,9 @@
         ],
         out_specs=[blocks(node_rows)] * 3,
         out_shape=[
-            shape((node_rows, width), b16),
-            shape((node_rows, width), f32),
-            shape((node_rows, width), f32),
+            pltpu.HBM((node_rows, width), b16),
+            pltpu.HBM((node_rows, width), f32),
+            pltpu.HBM((node_rows, width), f32),
         ],
         compiler_params=params(12),
         cost_estimate=cost(6),

time: 188 us -> 181 us (0.963)
  starting transfers between devices: 92.5 us -> 80.3 us
  waiting for transfers between devices: 13.2 us -> 21.8 us
  local copies, waits for them, and re-layouts: 24.6 us -> 18.4 us
    ppermute x11, starting transfers between devices: 58.6 us -> 47.3 us  [permute(): return lax.ppermute(value, ('ens', 'node'), pairs)]
    unnamed x57 -> x49, local copies, waits for them, and re-layouts: 22.6 us -> 16.6 us
    ppermute x11, waiting for transfers between devices: 7.47 us -> 12.4 us  [permute(): return lax.ppermute(value, ('ens', 'node'), pairs)]
    ppermute x4, waiting for transfers between devices: 4.72 us -> 7.32 us  [shifted(): return lax.ppermute(value, axis, pairs)]
    all_to_all x1, starting transfers between devices: 6.84 us -> 4.49 us  [per_device(): lax.all_to_all(jnp.broadcast_to(part[None], (shards,) + part.shape), 'nod...]
  transfers between devices with their start and end apart: 17 -> 17, of which waited for: 5 -> 6; matrix products, arithmetic and copies ran while one was open for 1% -> 1% of each run, Pallas kernels for 8% -> 8%
where the time goes in v5:
time: 181 us; the launch traced here: 179 us
  starting transfers between devices  80.3 us (44%)
  Pallas kernels  33.9 us (19%)
  waiting for transfers between devices  21.8 us (12%)
  local copies, waits for them, and re-layouts  18.4 us (10%)
  blocking collectives  17.9 us (10%)
  other arithmetic  3.15 us (2%)
  between operations  2.92 us (2%)
    ppermute x11, starting transfers between devices, permute(): return lax.ppermute(value, ('ens', 'node'), pairs)  47.3 us
    ppermute x4, starting transfers between devices, shifted(): return lax.ppermute(value, axis, pairs)  24.3 us
    all_to_all x2, blocking collectives, everyone(): lax.all_to_all(spread, 'ens', 0, 0, tiled=True, axis_index_groups=groups)  17.9 us
    pallas_call x1, Pallas kernels, per_device(): pl.pallas_call(lambda *refs: forward_kernel(scale, *refs), grid=(steps,),...  17.2 us
    unnamed x49, local copies, waits for them, and re-layouts  16.6 us
    ppermute x11, waiting for transfers between devices, permute(): return lax.ppermute(value, ('ens', 'node'), pairs)  12.4 us
    pallas_call x1, Pallas kernels, per_device(): pl.pallas_call(lambda *refs: halo_kernel(scale, *refs), grid=(steps,), in...  8.66 us
    ppermute x4, waiting for transfers between devices, shifted(): return lax.ppermute(value, axis, pairs)  7.32 us
  transfers between devices with their start and end apart: 17, of which 6 were waited for; matrix products, arithmetic and copies ran while one was open for 1% of the time, Pallas kernels for 8%

profile of v5, /device:TPU:1, one launch (start us, length us, event | category | flops | bytes accessed | tf_op | source)
XLA Modules:
  0.0 179.3 jit_solution(16798766243870755436)
XLA Ops:
  3.0 4.8 %collective-permute-start = (bf16[32,3200]{1,0:T(8,128)(2,1)S(1)}, bf16[32,3200]{1,0:T(8,128)(2,1)S(1)}, u32[]{:S(2)}, u32[]{:S(2)}) collective-permute-start(bf16[32,3200]{1,0:T(8,128)(2,1)S(1)} %pad_maximum_fusion.1), channel_id=1, source_target_pairs={{0,128},{16,48},{1,129},{17,49},{2,130},{18,50},{3,131},{19,51},{4... | collective-permute-start | bytes 614408 | tf_op jit(solution)/shard_map/ppermute | solution.py:326
  7.9 8.6 %collective-permute-start.1 = (bf16[32,3200]{1,0:T(8,128)(2,1)S(1)}, bf16[32,3200]{1,0:T(8,128)(2,1)S(1)}, u32[]{:S(2)}, u32[]{:S(2)}) collective-permute-start(bf16[32,3200]{1,0:T(8,128)(2,1)S(1)} %pad_maximum_fusion.1), channel_id=1, source_target_pairs={{0,384},{16,120},{1,385},{17,121},{2,386},{18,122},{3,387},{19,123... | collective-permute-start | bytes 614408 | tf_op jit(solution)/shard_map/ppermute | solution.py:326
  19.7 3.2 %collective-permute-start.3 = (bf16[128,1024]{1,0:T(8,128)(2,1)S(1)}, bf16[128,1024]{1,0:T(8,128)(2,1)S(1)}, u32[]{:S(2)}, u32[]{:S(2)}) collective-permute-start(bf16[128,1024]{1,0:T(8,128)(2,1)S(1)} %multiply_convert_fusion.refs_2_), channel_id=1, source_target_pairs={{0,1},{1,2},{2,3},{3,4},{4,5},{5,6},{6,7},{7,8},{8,9},{9,10},{10,1... | collective-permute-start | bytes 786440 | tf_op jit(solution)/shard_map/ppermute | solution.py:306
  23.0 8.1 %collective-permute-start.4 = (bf16[128,1024]{1,0:T(8,128)(2,1)S(1)}, bf16[128,1024]{1,0:T(8,128)(2,1)S(1)}, u32[]{:S(2)}, u32[]{:S(2)}) collective-permute-start(bf16[128,1024]{1,0:T(8,128)(2,1)S(1)} %multiply_convert_fusion.refs_2_), channel_id=1, source_target_pairs={{0,15},{1,0},{2,1},{3,2},{4,3},{5,4},{6,5},{7,6},{8,7},{9,8},{10,9... | collective-permute-start | bytes 786440 | tf_op jit(solution)/shard_map/ppermute | solution.py:306
  31.2 7.3 %collective-permute-done.3.refs_1_ = bf16[128,1024]{1,0:T(8,128)(2,1)S(1)} collective-permute-done((bf16[128,1024]{1,0:T(8,128)(2,1)S(1)}, bf16[128,1024]{1,0:T(8,128)(2,1)S(1)}, u32[]{:S(2)}, u32[]{:S(2)}) %collective-permute-start.3) | collective-permute-done | bytes 262176 | tf_op jit(solution)/shard_map/ppermute | solution.py:306
  38.5 6.8 %collective-permute-start.6 = (bf16[128,3200]{1,0:T(8,128)(2,1)S(1)}, bf16[128,3200]{1,0:T(8,128)(2,1)S(1)}, u32[]{:S(2)}, u32[]{:S(2)}) collective-permute-start(bf16[128,3200]{1,0:T(8,128)(2,1)S(1)} %pad_maximum_fusion.refs_7_), channel_id=1, source_target_pairs={{0,104},{16,400},{1,105},{17,401},{2,106},{18,402},{3,107},{19,403... | collective-permute-start | bytes 2457608 | tf_op jit(solution)/shard_map/ppermute | solution.py:326
  45.3 2.1 %collective-permute-start.7 = (bf16[128,3200]{1,0:T(8,128)(2,1)S(1)}, bf16[128,3200]{1,0:T(8,128)(2,1)}, u32[]{:S(2)}, u32[]{:S(2)}) collective-permute-start(bf16[128,3200]{1,0:T(8,128)(2,1)S(1)} %pad_maximum_fusion.refs_7_), channel_id=1, source_target_pairs={{0,64},{16,272},{1,65},{17,273},{2,66},{18,274},{3,67},{19,275},{4... | collective-permute-start | bytes 2457608 | tf_op jit(solution)/shard_map/ppermute | solution.py:326
  47.4 2.3 %collective-permute-start.5 = (bf16[128,3200]{1,0:T(8,128)(2,1)S(1)}, bf16[128,3200]{1,0:T(8,128)(2,1)}, u32[]{:S(2)}, u32[]{:S(2)}) collective-permute-start(bf16[128,3200]{1,0:T(8,128)(2,1)S(1)} %pad_maximum_fusion.refs_7_), channel_id=1, source_target_pairs={{0,32},{16,144},{1,33},{17,145},{2,34},{18,146},{3,35},{19,147},{4... | collective-permute-start | bytes 2457608 | tf_op jit(solution)/shard_map/ppermute | solution.py:326
  49.7 5.4 %collective-permute-start.8 = (bf16[128,3200]{1,0:T(8,128)(2,1)S(1)}, bf16[128,3200]{1,0:T(8,128)(2,1)}, u32[]{:S(2)}, u32[]{:S(2)}) collective-permute-start(bf16[128,3200]{1,0:T(8,128)(2,1)S(1)} %pad_maximum_fusion.refs_7_), channel_id=1, source_target_pairs={{0,16},{16,0},{1,17},{17,1},{2,18},{18,2},{3,19},{19,3},{4,20},{20... | collective-permute-start | bytes 2457608 | tf_op jit(solution)/shard_map/ppermute | solution.py:326
  55.2 8.2 %collective-permute-done.6.refs_9_ = bf16[128,3200]{1,0:T(8,128)(2,1)S(1)} collective-permute-done((bf16[128,3200]{1,0:T(8,128)(2,1)S(1)}, bf16[128,3200]{1,0:T(8,128)(2,1)S(1)}, u32[]{:S(2)}, u32[]{:S(2)}) %collective-permute-start.6) | collective-permute-done | bytes 819232 | tf_op jit(solution)/shard_map/ppermute | solution.py:326
  63.4 2.9 %collective-permute-start.10 = (bf16[128,3200]{1,0:T(8,128)(2,1)S(1)}, bf16[128,3200]{1,0:T(8,128)(2,1)}, u32[]{:S(2)}, u32[]{:S(2)}) collective-permute-start(bf16[128,3200]{1,0:T(8,128)(2,1)S(1)} %collective-permute-done.6.refs_9_), channel_id=1, source_target_pairs={{0,16},{16,0},{1,17},{17,1},{2,18},{18,2},{3,19},{19,3},{4,20},{20... | collective-permute-start | bytes 2457608 | tf_op jit(solution)/shard_map/ppermute | solution.py:326
  69.1 3.8 %collective-permute-start.9 = (bf16[128,3200]{1,0:T(8,128)(2,1)}, bf16[128,3200]{1,0:T(8,128)(2,1)}, u32[]{:S(2)}, u32[]{:S(2)}) collective-permute-start(bf16[128,3200]{1,0:T(8,128)(2,1)} %collective-permute-done.5.refs_8_), channel_id=1, source_target_pairs={{0,16},{16,0},{1,17},{17,1},{2,18},{18,2},{3,19},{19,3},{4,20},{20... | collective-permute-start | bytes 2457608 | tf_op jit(solution)/shard_map/ppermute | solution.py:326
  73.1 2.1 %collective-permute-done.9.refs_12_ = bf16[128,3200]{1,0:T(8,128)(2,1)} collective-permute-done((bf16[128,3200]{1,0:T(8,128)(2,1)}, bf16[128,3200]{1,0:T(8,128)(2,1)}, u32[]{:S(2)}, u32[]{:S(2)}) %collective-permute-start.9) | collective-permute-done | bytes 819232 | tf_op jit(solution)/shard_map/ppermute | solution.py:326
  75.1 17.2 %forward.1 = (bf16[384,1024]{1,0:T(8,128)(2,1)}, bf16[384,1024]{1,0:T(8,128)(2,1)}, bf16[384,1024]{1,0:T(8,128)(2,1)}, bf16[128,1024]{1,0:T(8,128)(2,1)}, f32[12...) custom-call(s32[3]{0:T(128)S(1)} %pad_add_fusion.refs_0_, ...), custom_call_target="tpu_custom_call" | custom-call | flops 12000000000 | bytes 36000000 | tf_op jit(solution)/shard_map/forward/pallas_call | solution.py:413
  93.2 7.1 %all_to_all.20 = bf16[4,112,128]{2,1,0:T(8,128)(2,1)S(1)} all-to-all(bf16[4,112,128]{2,1,0:T(8,128)(2,1)S(1)} %reshape.44), channel_id=1, replica_groups={{0,128,256,384},{32,160,288,416},{64,192,320,448},{96,224,352,480},{16,..., dimensions={0} | all-to-all | bytes 229376 | tf_op jit(solution)/shard_map/all_to_all | solution.py:358
  100.4 10.8 %all_to_all.21.refs_0_ = bf16[16,112,128]{2,1,0:T(8,128)(2,1)S(1)} all-to-all(bf16[16,112,128]{2,1,0:T(8,128)(2,1)S(1)} %bitcast.19), channel_id=1, replica_groups={{0,32,64,96},{128,160,192,224},{256,288,320,352},{384,416,448,480},{16,..., dimensions={0} | all-to-all | bytes 917504 | tf_op jit(solution)/shard_map/all_to_all | solution.py:358
  111.1 6.7 %collective-permute-start.12 = (bf16[16,112,128]{2,1,0:T(8,128)(2,1)S(1)}, bf16[16,112,128]{2,1,0:T(8,128)(2,1)S(1)}, u32[]{:S(2)}, u32[]{:S(2)}) collective-permute-start(bf16[16,112,128]{2,1,0:T(8,128)(2,1)S(1)} %all_to_all.21.refs_0_), channel_id=1, source_target_pairs={{0,16},{16,0},{1,17},{17,1},{2,18},{18,2},{3,19},{19,3},{4,20},{20... | collective-permute-start | bytes 1376264 | tf_op jit(solution)/shard_map/ppermute | solution.py:326
  119.3 2.9 %copy-done.6 = bf16[1024,3200]{1,0:T(8,128)(2,1)S(1)} copy-done((bf16[1024,3200]{1,0:T(8,128)(2,1)S(1)}, bf16[1024,3200]{1,0:T(8,128)(2,1)}, u32[]{:S(2)}) %copy-start.6) | copy-done | bytes 6553624
  127.1 11.1 %collective-permute-start.14 = (bf16[192,128]{1,0:T(8,128)(2,1)S(1)}, bf16[192,128]{1,0:T(8,128)(2,1)S(1)}, u32[]{:S(2)}, u32[]{:S(2)}) collective-permute-start(bf16[192,128]{1,0:T(8,128)(2,1)S(1)} %get-tuple-element.26.refs_17_), channel_id=1, source_target_pairs={{0,15},{1,0},{2,1},{3,2},{4,3},{5,4},{6,5},{7,6},{8,7},{9,8},{10,9... | collective-permute-start | bytes 147464 | tf_op jit(solution)/shard_map/ppermute | solution.py:306
  138.2 4.2 %all-to-all-start.2 = ((bf16[32,32,128]{2,1,0:T(8,128)(2,1)}), bf16[32,32,128]{2,1,0:T(8,128)(2,1)S(1)}, u32[]{:S(2)}, u32[]{:S(2)}) async-start(bf16[32,32,128]{2,1,0:T(8,128)(2,1)} %bitcast.9), calls=%async_computation.2 | async-start | bytes 524288 | tf_op jit(solution)/shard_map/all_to_all | solution.py:492
  145.7 6.1 %own_queries.1 = (bf16[128,1024]{1,0:T(8,128)(2,1)}, f32[128,1024]{1,0:T(8,128)}, f32[128,1024]{1,0:T(8,128)}) custom-call(bf16[384,1024]{1,0:T(8,128)(2,1)S(1)} %copy-done.8, bf16[384,1024]{1,0:T(8,128)(2,1)S(1)} %copy-done.9, bf16[384,1024]{1,0:T(8,128)(2,1)S(1)} %copy-done.11, bf16[128,1024]{1,0:T(8,128)(2,1)S(1)} %get-tuple-element.30.refs_3_, ...), custom_call_target="tpu_custom_call" | custom-call | flops 6000000000 | bytes 18000000 | tf_op jit(solution)/shard_map/own_queries/pallas_call | solution.py:506
  154.6 4.5 %all-to-all-start.3 = ((f32[16,32,128]{2,1,0:T(8,128)}), f32[16,32,128]{2,1,0:T(8,128)S(1)}, u32[]{:S(2)}, u32[]{:S(2)}) async-start(f32[16,32,128]{2,1,0:T(8,128)} %broadcast_in_dim.11), calls=%async_computation.3 | async-start | bytes 524288 | tf_op jit(solution)/shard_map/all_to_all | solution.py:494
  159.1 2.9 %copy-done.7 = bf16[1024,3200]{1,0:T(8,128)(2,1)S(1)} copy-done((bf16[1024,3200]{1,0:T(8,128)(2,1)S(1)}, bf16[1024,3200]{1,0:T(8,128)(2,1)}, u32[]{:S(2)}) %copy-start.7) | copy-done | bytes 6553624
  167.3 8.7 %neighbour_queries.1 = bf16[1,128,1024]{2,1,0:T(8,128)(2,1)} custom-call(bf16[192,128]{1,0:T(8,128)(2,1)S(1)} %collective-permute-done.13.refs_0_, bf16[192,128]{1,0:T(8,128)(2,1)S(1)} %collective-permute-done.14.refs_1_, bf16[384,1024]{1,0:T(8,128)(2,1)S(1)} %copy-done.8, bf16[384,1024]{1,0:T(8,128)(2,1)S(1)} %copy-done.8, ...), custom_call_target="tpu_custom_call" | custom-call | flops 8999999488 | bytes 27000000 | tf_op jit(solution)/shard_map/neighbour_queries/pallas_call | solution.py:527
  (82 shorter events, 28.8 us)
Async XLA Ops:
  0.6 30.5 %copy-start.22 = (bf16[32,1024]{1,0:T(8,128)(2,1)S(1)}, bf16[32,1024]{1,0:T(8,128)(2,1)}, u32[]{:S(2)}) copy-start(bf16[32,1024]{1,0:T(8,128)(2,1)} %param.13) | copy-start | bytes 196612
  0.7 30.4 %copy-start.21 = (bf16[32,1024]{1,0:T(8,128)(2,1)S(1)}, bf16[32,1024]{1,0:T(8,128)(2,1)}, u32[]{:S(2)}) copy-start(bf16[32,1024]{1,0:T(8,128)(2,1)} %param.14) | copy-start | bytes 196612
  0.7 30.4 %copy-start.20 = (bf16[32,1024]{1,0:T(8,128)(2,1)S(1)}, bf16[32,1024]{1,0:T(8,128)(2,1)}, u32[]{:S(2)}) copy-start(bf16[32,1024]{1,0:T(8,128)(2,1)} %param.15) | copy-start | bytes 196612
  3.0 28.0 %collective-permute-start = (bf16[32,3200]{1,0:T(8,128)(2,1)S(1)}, bf16[32,3200]{1,0:T(8,128)(2,1)S(1)}, u32[]{:S(2)}, u32[]{:S(2)}) collective-permute-start(bf16[32,3200]{1,0:T(8,128)(2,1)S(1)} %pad_maximum_fusion.1), channel_id=1, source_target_pairs={{0,128},{16,48},{1,129},{17,49},{2,130},{18,50},{3,131},{19,51},{4... | collective-permute-start | bytes 614408 | tf_op jit(solution)/shard_map/ppermute | solution.py:326
  7.9 23.2 %collective-permute-start.1 = (bf16[32,3200]{1,0:T(8,128)(2,1)S(1)}, bf16[32,3200]{1,0:T(8,128)(2,1)S(1)}, u32[]{:S(2)}, u32[]{:S(2)}) collective-permute-start(bf16[32,3200]{1,0:T(8,128)(2,1)S(1)} %pad_maximum_fusion.1), channel_id=1, source_target_pairs={{0,384},{16,120},{1,385},{17,121},{2,386},{18,122},{3,387},{19,123... | collective-permute-start | bytes 614408 | tf_op jit(solution)/shard_map/ppermute | solution.py:326
  16.5 14.6 %collective-permute-start.2 = (bf16[32,3200]{1,0:T(8,128)(2,1)S(1)}, bf16[32,3200]{1,0:T(8,128)(2,1)S(1)}, u32[]{:S(2)}, u32[]{:S(2)}) collective-permute-start(bf16[32,3200]{1,0:T(8,128)(2,1)S(1)} %pad_maximum_fusion.1), channel_id=1, source_target_pairs={{0,256},{16,80},{1,257},{17,81},{2,258},{18,82},{3,259},{19,83},{4... | collective-permute-start | bytes 614408 | tf_op jit(solution)/shard_map/ppermute | solution.py:326
  19.7 18.8 %collective-permute-start.3 = (bf16[128,1024]{1,0:T(8,128)(2,1)S(1)}, bf16[128,1024]{1,0:T(8,128)(2,1)S(1)}, u32[]{:S(2)}, u32[]{:S(2)}) collective-permute-start(bf16[128,1024]{1,0:T(8,128)(2,1)S(1)} %multiply_convert_fusion.refs_2_), channel_id=1, source_target_pairs={{0,1},{1,2},{2,3},{3,4},{4,5},{5,6},{6,7},{7,8},{8,9},{9,10},{10,1... | collective-permute-start | bytes 786440 | tf_op jit(solution)/shard_map/ppermute | solution.py:306
  23.0 15.6 %collective-permute-start.4 = (bf16[128,1024]{1,0:T(8,128)(2,1)S(1)}, bf16[128,1024]{1,0:T(8,128)(2,1)S(1)}, u32[]{:S(2)}, u32[]{:S(2)}) collective-permute-start(bf16[128,1024]{1,0:T(8,128)(2,1)S(1)} %multiply_convert_fusion.refs_2_), channel_id=1, source_target_pairs={{0,15},{1,0},{2,1},{3,2},{4,3},{5,4},{6,5},{7,6},{8,7},{9,8},{10,9... | collective-permute-start | bytes 786440 | tf_op jit(solution)/shard_map/ppermute | solution.py:306
  38.5 24.8 %collective-permute-start.6 = (bf16[128,3200]{1,0:T(8,128)(2,1)S(1)}, bf16[128,3200]{1,0:T(8,128)(2,1)S(1)}, u32[]{:S(2)}, u32[]{:S(2)}) collective-permute-start(bf16[128,3200]{1,0:T(8,128)(2,1)S(1)} %pad_maximum_fusion.refs_7_), channel_id=1, source_target_pairs={{0,104},{16,400},{1,105},{17,401},{2,106},{18,402},{3,107},{19,403... | collective-permute-start | bytes 2457608 | tf_op jit(solution)/shard_map/ppermute | solution.py:326
  45.3 21.0 %collective-permute-start.7 = (bf16[128,3200]{1,0:T(8,128)(2,1)S(1)}, bf16[128,3200]{1,0:T(8,128)(2,1)}, u32[]{:S(2)}, u32[]{:S(2)}) collective-permute-start(bf16[128,3200]{1,0:T(8,128)(2,1)S(1)} %pad_maximum_fusion.refs_7_), channel_id=1, source_target_pairs={{0,64},{16,272},{1,65},{17,273},{2,66},{18,274},{3,67},{19,275},{4... | collective-permute-start | bytes 2457608 | tf_op jit(solution)/shard_map/ppermute | solution.py:326
  47.4 21.7 %collective-permute-start.5 = (bf16[128,3200]{1,0:T(8,128)(2,1)S(1)}, bf16[128,3200]{1,0:T(8,128)(2,1)}, u32[]{:S(2)}, u32[]{:S(2)}) collective-permute-start(bf16[128,3200]{1,0:T(8,128)(2,1)S(1)} %pad_maximum_fusion.refs_7_), channel_id=1, source_target_pairs={{0,32},{16,144},{1,33},{17,145},{2,34},{18,146},{3,35},{19,147},{4... | collective-permute-start | bytes 2457608 | tf_op jit(solution)/shard_map/ppermute | solution.py:326
  49.7 23.3 %collective-permute-start.8 = (bf16[128,3200]{1,0:T(8,128)(2,1)S(1)}, bf16[128,3200]{1,0:T(8,128)(2,1)}, u32[]{:S(2)}, u32[]{:S(2)}) collective-permute-start(bf16[128,3200]{1,0:T(8,128)(2,1)S(1)} %pad_maximum_fusion.refs_7_), channel_id=1, source_target_pairs={{0,16},{16,0},{1,17},{17,1},{2,18},{18,2},{3,19},{19,3},{4,20},{20... | collective-permute-start | bytes 2457608 | tf_op jit(solution)/shard_map/ppermute | solution.py:326
  63.4 9.7 %collective-permute-start.10 = (bf16[128,3200]{1,0:T(8,128)(2,1)S(1)}, bf16[128,3200]{1,0:T(8,128)(2,1)}, u32[]{:S(2)}, u32[]{:S(2)}) collective-permute-start(bf16[128,3200]{1,0:T(8,128)(2,1)S(1)} %collective-permute-done.6.refs_9_), channel_id=1, source_target_pairs={{0,16},{16,0},{1,17},{17,1},{2,18},{18,2},{3,19},{19,3},{4,20},{20... | collective-permute-start | bytes 2457608 | tf_op jit(solution)/shard_map/ppermute | solution.py:326
  66.3 6.8 %collective-permute-start.11 = (bf16[128,3200]{1,0:T(8,128)(2,1)}, bf16[128,3200]{1,0:T(8,128)(2,1)}, u32[]{:S(2)}, u32[]{:S(2)}) collective-permute-start(bf16[128,3200]{1,0:T(8,128)(2,1)} %collective-permute-done.7.refs_10_), channel_id=1, source_target_pairs={{0,16},{16,0},{1,17},{17,1},{2,18},{18,2},{3,19},{19,3},{4,20},{20... | collective-permute-start | bytes 2457608 | tf_op jit(solution)/shard_map/ppermute | solution.py:326
  69.1 6.0 %collective-permute-start.9 = (bf16[128,3200]{1,0:T(8,128)(2,1)}, bf16[128,3200]{1,0:T(8,128)(2,1)}, u32[]{:S(2)}, u32[]{:S(2)}) collective-permute-start(bf16[128,3200]{1,0:T(8,128)(2,1)} %collective-permute-done.5.refs_8_), channel_id=1, source_target_pairs={{0,16},{16,0},{1,17},{17,1},{2,18},{18,2},{3,19},{19,3},{4,20},{20... | collective-permute-start | bytes 2457608 | tf_op jit(solution)/shard_map/ppermute | solution.py:326
  92.4 25.5 %copy-start.23 = (bf16[100,128]{1,0:T(8,128)(2,1)S(1)}, bf16[100,128]{1,0:T(8,128)(2,1)}, u32[]{:S(2)}) copy-start(bf16[100,128]{1,0:T(8,128)(2,1)} %param.18) | copy-start | bytes 76804
  92.4 26.9 %copy-start.3 = (bf16[112,128]{1,0:T(8,128)(2,1)S(1)}, bf16[112,128]{1,0:T(8,128)(2,1)}, u32[]{:S(2)}) copy-start(bf16[112,128]{1,0:T(8,128)(2,1)} %get-tuple-element.22.refs_2_) | copy-start | bytes 86020
  92.4 26.9 %copy-start.5 = (f32[128]{0:T(128)S(1)}, f32[128]{0:T(128)}, u32[]{:S(2)}) copy-start(f32[128]{0:T(128)} %param.19) | copy-start | bytes 1540
  92.4 26.9 %copy-start.18 = (bf16[128,1024]{1,0:T(8,128)(2,1)S(1)}, bf16[128,1024]{1,0:T(8,128)(2,1)}, u32[]{:S(2)}) copy-start(bf16[128,1024]{1,0:T(8,128)(2,1)} %get-tuple-element.23.refs_5_) | copy-start | bytes 786436
  111.1 8.1 %collective-permute-start.12 = (bf16[16,112,128]{2,1,0:T(8,128)(2,1)S(1)}, bf16[16,112,128]{2,1,0:T(8,128)(2,1)S(1)}, u32[]{:S(2)}, u32[]{:S(2)}) collective-permute-start(bf16[16,112,128]{2,1,0:T(8,128)(2,1)S(1)} %all_to_all.21.refs_0_), channel_id=1, source_target_pairs={{0,16},{16,0},{1,17},{17,1},{2,18},{18,2},{3,19},{19,3},{4,20},{20... | collective-permute-start | bytes 1376264 | tf_op jit(solution)/shard_map/ppermute | solution.py:326
  125.2 33.9 %collective-permute-start.13 = (bf16[192,128]{1,0:T(8,128)(2,1)S(1)}, bf16[192,128]{1,0:T(8,128)(2,1)S(1)}, u32[]{:S(2)}, u32[]{:S(2)}) collective-permute-start(bf16[192,128]{1,0:T(8,128)(2,1)S(1)} %get-tuple-element.26.refs_17_), channel_id=1, source_target_pairs={{0,1},{1,2},{2,3},{3,4},{4,5},{5,6},{6,7},{7,8},{8,9},{9,10},{10,1... | collective-permute-start | bytes 147464 | tf_op jit(solution)/shard_map/ppermute | solution.py:306
  127.1 32.0 %collective-permute-start.14 = (bf16[192,128]{1,0:T(8,128)(2,1)S(1)}, bf16[192,128]{1,0:T(8,128)(2,1)S(1)}, u32[]{:S(2)}, u32[]{:S(2)}) collective-permute-start(bf16[192,128]{1,0:T(8,128)(2,1)S(1)} %get-tuple-element.26.refs_17_), channel_id=1, source_target_pairs={{0,15},{1,0},{2,1},{3,2},{4,3},{5,4},{6,5},{7,6},{8,7},{9,8},{10,9... | collective-permute-start | bytes 147464 | tf_op jit(solution)/shard_map/ppermute | solution.py:306
  138.2 15.6 %all-to-all-start.2 = ((bf16[32,32,128]{2,1,0:T(8,128)(2,1)}), bf16[32,32,128]{2,1,0:T(8,128)(2,1)S(1)}, u32[]{:S(2)}, u32[]{:S(2)}) async-start(bf16[32,32,128]{2,1,0:T(8,128)(2,1)} %bitcast.9), calls=%async_computation.2 | async-start | bytes 524288 | tf_op jit(solution)/shard_map/all_to_all | solution.py:492
  154.6 21.4 %all-to-all-start.3 = ((f32[16,32,128]{2,1,0:T(8,128)}), f32[16,32,128]{2,1,0:T(8,128)S(1)}, u32[]{:S(2)}, u32[]{:S(2)}) async-start(f32[16,32,128]{2,1,0:T(8,128)} %broadcast_in_dim.11), calls=%async_computation.3 | async-start | bytes 524288 | tf_op jit(solution)/shard_map/all_to_all | solution.py:494
  (17 other events, 101.3 us)

commit v6 on v5

v6 whole, which is shorter than its diff:
```python
import math

import jax
import jax.numpy as jnp
from jax import lax
from jax.experimental import pallas as pl
from jax.experimental.pallas import tpu as pltpu
from jax.sharding import PartitionSpec as P

HEADS = 16
HALO = 128
LANES = 128
STEP = 256
VROWS = 112
SIDE = 4
RING_Z = 8
RING_Y = 8
HOPS = (0, SIDE - 1, 1, 2)


ALPHA = 0.95
KAPPA = 0.25
EPS_NORM = 1e-05
FAR = -1e30

f32 = jnp.float32
b16 = jnp.bfloat16


def nn(a, b):
    return lax.dot_general(a, b, (((1,), (0,)), ((), ())), preferred_element_type=f32)


def nt(a, b):
    return lax.dot_general(a, b, (((1,), (1,)), ((), ())), preferred_element_type=f32)


def tn(a, b):
    return lax.dot_general(a, b, (((0,), (0,)), ((), ())), preferred_element_type=f32)


def whole(shape):
    return pl.BlockSpec(shape, lambda i: (0,) * len(shape))


def head_masks(value):
    lane = lax.broadcasted_iota(jnp.int32, (1, LANES), 1)
    first = jnp.where(lane < LANES // 2, value, 0.0).astype(b16)
    second = jnp.where(lane < LANES // 2, 0.0, value).astype(b16)
    return first, second


def window_mask(rows, span):
    offset = lax.broadcasted_iota(jnp.int32, (rows, span), 1) - lax.broadcasted_iota(
        jnp.int32, (rows, span), 0
    )
    return (offset >= 0) & (offset <= 2 * HALO)


def split_bf16(value, pieces):
    out = []
    for _ in range(pieces):
        piece = value.astype(b16)
        out.append(piece)
        value = value - piece.astype(f32)
    return out


def forward_kernel(scale, place, low, own, high, hidden, forcing, decode, *refs):
    pieces, refs = refs[: 2 * len(HOPS)], refs[2 * len(HOPS) :]
    (
        queries_out, keys_out, values_out, attended, lse_out, pred, mixed, full,
        queries, keys, values, lse, normed, weights, store,
    ) = refs
    rows, width = own.shape
    span = rows + 2 * HALO
    x, z, core = place[0], place[1], place[2]
    side = len(HOPS)
    block = pieces[0].shape[0] // side
    for mine in (True, False):
        which = core if mine else 1 - core
        for outer, far in enumerate(HOPS):
            piece = pieces[outer if mine else side + outer]
            for inner, near in enumerate(HOPS):
                along_x = jnp.where(which == 0, near, far)
                along_z = jnp.where(which == 0, far, near)
                chip = lax.rem(x + along_x, side) * side + lax.rem(z + along_z, side)
                at = pl.multiple_of((chip * 2 + which) * block, block)
                weights[pl.ds(at, block), :] = piece[inner * block : (inner + 1) * block, :]
    stores = [pltpu.make_async_copy(weights, full, store.at[0])]
    stores[0].start()
    mixed[...] = weights[:, 3 * width :]
    normed[:HALO] = low[...]
    normed[HALO : HALO + rows] = own[...]
    normed[HALO + rows :] = high[...]
    total = nn(hidden[0], decode[...]) + nn(forcing[...], decode[...])
    window = window_mask(rows, span)
    masks = head_masks(scale)
    lower = lax.broadcasted_iota(jnp.int32, (rows, LANES), 1) < LANES // 2
    pairs = STEP // LANES
    for at in range(0, width, STEP):
        cols = slice(at, at + STEP)
        field = normed[...]
        projected = [
            nn(field, weights[:, index * width + at : index * width + at + STEP]).astype(b16)
            for index in range(3)
        ]
        query, key, value = projected
        for part, scratch, out in zip(
            projected, (queries, keys, values), (queries_out, keys_out, values_out), strict=True
        ):
            scratch[:, cols] = part
            stores.append(
                pltpu.make_async_copy(scratch.at[:, cols], out.at[:, cols], store.at[len(stores)])
            )
            stores[-1].start()
        scores = []
        for pair in range(pairs):
            lanes = slice(pair * LANES, (pair + 1) * LANES)
            for mask in masks:
                scores.append(nt(query[HALO : HALO + rows, lanes] * mask, key[:, lanes]))
        scores = [jnp.where(window, score, FAR) for score in scores]
        tops = [jnp.max(score, -1, keepdims=True) for score in scores]
        expos = [jnp.exp(score - top) for score, top in zip(scores, tops, strict=True)]
        norms = [jnp.sum(expo, -1, keepdims=True) for expo in expos]
        probs = [(expo * (1.0 / norm)).astype(b16) for expo, norm in zip(expos, norms, strict=True)]
        outs = [
            nn(prob, value[:, index // 2 * LANES : (index // 2 + 1) * LANES])
            for index, prob in enumerate(probs)
        ]
        stats = [top + jnp.log(norm) for top, norm in zip(tops, norms, strict=True)]
        result = jnp.concatenate(
            [jnp.where(lower, outs[2 * n], outs[2 * n + 1]).astype(b16) for n in range(pairs)], 1
        )
        attended[:, cols] = result
        lse[:, cols] = jnp.concatenate(
            [jnp.where(lower, stats[2 * n], stats[2 * n + 1]) for n in range(pairs)], 1
        )
        stores.append(
            pltpu.make_async_copy(lse.at[:, cols], lse_out.at[:, cols], store.at[len(stores)])
        )
        stores[-1].start()
        total = total + nn(result, mixed[cols, :])
    pred[...] = total.T[:VROWS].astype(b16)
    for copy in stores:
        copy.wait()


def loss_kernel(
    coeff, variables, others, theirs, pred, targets, weight, attended, mixed, lse,
    gram, halo,
):
    own = pred[...].astype(f32)
    rows = attended.shape[0]
    width = attended.shape[1]

    def member(index, carry):
        pair_abs, pair_slope = carry
        for part in (others, theirs):
            delta = own - part[index].astype(f32)
            square = delta * delta + KAPPA * KAPPA
            inverse = lax.rsqrt(square)
            pair_abs = pair_abs + (square * inverse - KAPPA)
            pair_slope = pair_slope + delta * inverse
        return pair_abs, pair_slope

    zero = jnp.zeros((VROWS, LANES), f32)
    pair_abs, pair_slope = lax.fori_loop(0, others.shape[0], member, (zero, zero), unroll=2)
    delta = own - targets[...].astype(f32)
    square = delta * delta + KAPPA * KAPPA
    inverse = lax.rsqrt(square)
    real = lax.broadcasted_iota(jnp.int32, (VROWS, LANES), 0) < variables
    scale = weight[...]
    entries = jnp.where(real, scale * (square * inverse - KAPPA - coeff * pair_abs), 0.0)
    loss = jnp.sum(jnp.sum(entries, 0, keepdims=True), 1, keepdims=True)
    grad = jnp.where(real, scale * (delta * inverse - 2.0 * coeff * pair_slope), 0.0)
    grad_b = grad.astype(b16)
    halo[:VROWS] = grad_b
    grad_full = jnp.concatenate([grad, jnp.zeros((LANES - VROWS, LANES), f32)], 0)
    grad_t = grad_full.T.astype(b16)
    parts = nn(grad_full.astype(b16), attended[...])
    parts = parts.T
    column = lax.broadcasted_iota(jnp.int32, (width, LANES), 1)
    for index, piece in enumerate(split_bf16(loss, 3)):
        parts = jnp.where(column == variables + index, piece.astype(f32), parts)
    gram[...] = parts.astype(b16)
    grad_att = nt(grad_t, mixed[...]).astype(b16)
    size = width // HEADS
    head = lax.broadcasted_iota(jnp.int32, (HEADS, width), 0)
    feature = lax.broadcasted_iota(jnp.int32, (HEADS, width), 1)
    inside = jnp.where((feature >= head * size) & (feature < (head + 1) * size), 1.0, 0.0)
    chosen = jnp.where(feature == head * size, 1.0, 0.0).astype(b16)
    inside = inside.astype(b16)
    product = grad_att.astype(f32) * attended[...].astype(f32)
    row_delta = sum(nt(inside, piece) for piece in split_bf16(product, 2))
    row_lse = sum(nt(chosen, piece) for piece in split_bf16(lse[...], 3))
    at = VROWS
    for piece in split_bf16(row_delta, 2) + split_bf16(row_lse, 3):
        halo[at : at + HEADS] = piece
        at += HEADS


def backward_kernel(
    scale, low, own, high, hidden, forcing, inverse_rms, gain, decode, mixed,
    queries_in, keys_in, values_in, lse_in, full,
    grad_hidden, queries, keys, values, lse, weights, grad_t, stats, load,
):
    rows, width = lse.shape
    span = keys.shape[0]
    loads = []

    def fetch(source, target):
        loads.append(pltpu.make_async_copy(source, target, load.at[len(loads)]))
        loads[-1].start()

    fetch(queries_in, queries)
    fetch(keys_in, keys)
    fetch(values_in, values)
    fetch(lse_in, lse)
    for at in range(0, width, STEP):
        for index in range(3):
            cols = slice(index * width + at, index * width + at + STEP)
            fetch(full.at[:, cols], weights.at[:, cols])

    zero = jnp.zeros((LANES - VROWS, LANES), b16)
    for side, part in enumerate((own, low, high)):
        grad = jnp.concatenate([part[:VROWS], zero], 0)
        grad_t[side * rows : (side + 1) * rows] = grad.astype(f32).T.astype(b16)
    for side, part in enumerate((low, high)):
        at = slice(side * HALO, (side + 1) * HALO)
        pieces = [part[VROWS + HEADS * n : VROWS + HEADS * (n + 1)].astype(f32) for n in range(5)]
        stats[0, :, at] = pieces[0] + pieces[1]
        stats[1, :, at] = pieces[2] + pieces[3] + pieces[4]
    grad_resid = nt(grad_t[:rows], decode[...])

    window = window_mask(rows, span)
    key_at = lax.broadcasted_iota(jnp.int32, (rows, 2 * HALO), 0)
    query_at = lax.broadcasted_iota(jnp.int32, (rows, 2 * HALO), 1)
    reach = ((query_at < HALO) & (query_at >= key_at)) | (
        (query_at >= HALO) & (query_at - HALO <= key_at)
    )
    scaled = head_masks(scale)
    plain = head_masks(1.0)
    center = slice(HALO, HALO + rows)
    halves = [(pair, half) for pair in range(STEP // LANES) for half in range(2)]
    total = jnp.zeros((rows, width), f32)
    for copy in loads[:4]:
        copy.wait()
    for at in range(0, width, STEP):
        step = at // STEP
        grad_att = nt(grad_t[...], mixed[at : at + STEP, :]).astype(b16)
        lanes = [slice(at + pair * LANES, at + (pair + 1) * LANES) for pair in range(STEP // LANES)]
        query = [queries[center, cols] for cols in lanes]
        key = [keys[:, cols] for cols in lanes]
        value = [values[:, cols] for cols in lanes]
        far_query = [
            jnp.concatenate([queries[:HALO, cols], queries[HALO + rows :, cols]], 0)
            for cols in lanes
        ]
        grad = [grad_att[:rows, n * LANES : (n + 1) * LANES] for n in range(len(lanes))]
        far_grad = [grad_att[rows:, n * LANES : (n + 1) * LANES] for n in range(len(lanes))]
        scores = [nt(query[p] * scaled[h], key[p]) for p, h in halves]
        d_probs = [nt(grad[p] * plain[h], value[p]) for p, h in halves]
        probs = []
        for (p, h), score in zip(halves, scores, strict=True):
            start = lanes[p].start + h * (LANES // 2)
            probs.append(jnp.where(window, jnp.exp(score - lse[:, start : start + 1]), 0.0))
        deltas = [
            jnp.sum(prob * d_prob, -1, keepdims=True)
            for prob, d_prob in zip(probs, d_probs, strict=True)
        ]
        d_scores = [
            (prob * (d_prob - delta)).astype(b16)
            for prob, d_prob, delta in zip(probs, d_probs, deltas, strict=True)
        ]
        probs = [prob.astype(b16) for prob in probs]
        far_scores = [nt(key[p][center] * scaled[h], far_query[p]) for p, h in halves]
        far_d_probs = [nt(value[p][center] * plain[h], far_grad[p]) for p, h in halves]
        far_probs, far_d_scores = [], []
        for (p, h), score, d_prob in zip(halves, far_scores, far_d_probs, strict=True):
            row = 2 * (step * len(lanes) + p) + h
            prob = jnp.where(reach, jnp.exp(score - stats[1, row : row + 1, :]), 0.0)
            far_d_scores.append((prob * (d_prob - stats[0, row : row + 1, :])).astype(b16))
            far_probs.append(prob.astype(b16))
        d_query, d_key, d_value = [], [], []
        for p in range(len(lanes)):
            first, second = 2 * p, 2 * p + 1
            d_query.append(
                nn(d_scores[first], key[p] * scaled[0]) + nn(d_scores[second], key[p] * scaled[1])
            )
            d_key.append(
                tn(d_scores[first][:, center], query[p] * scaled[0])
                + tn(d_scores[second][:, center], query[p] * scaled[1])
                + nn(far_d_scores[first], far_query[p] * scaled[0])
                + nn(far_d_scores[second], far_query[p] * scaled[1])
            )
            d_value.append(
                tn(probs[first][:, center], grad[p] * plain[0])
                + tn(probs[second][:, center], grad[p] * plain[1])
                + nn(far_probs[first], far_grad[p] * plain[0])
                + nn(far_probs[second], far_grad[p] * plain[1])
            )
        for index, part in enumerate((d_query, d_key, d_value)):
            loads[4 + 3 * step + index].wait()
            part = jnp.concatenate(part, 1).astype(b16)
            cols = slice(index * width + at, index * width + at + STEP)
            total = total + nt(part, weights[:, cols])
    xfield = hidden[0].astype(f32) + forcing[...].astype(f32)
    inverse = inverse_rms[...]
    grad = gain[...] * total
    mean = jnp.mean(xfield * grad, -1, keepdims=True)
    result = grad_resid + inverse * grad - xfield * (inverse * inverse * inverse * mean)
    grad_hidden[0] = result.astype(b16)


def shifted(value, axis, steps):
    count = lax.axis_size(axis)
    pairs = [(source, (source + steps) % count) for source in range(count)]
    return lax.ppermute(value, axis, pairs)


def permute(value, moves):
    pairs = []
    for x in range(SIDE):
        for z in range(RING_Z):
            for y in range(RING_Y):
                for core in range(2):
                    dx, dz, dc = moves[core]
                    dz = -dz if dz == -2 and z % 2 == 0 else dz
                    dx = -dx if dx == -2 and x % 2 == 0 else dx
                    at = (x, z, core)
                    to = ((x + dx) % SIDE, (z + dz) % RING_Z, core ^ dc)
                    pairs.append(
                        tuple(
                            ((px * SIDE + pz % SIDE) * 2 + pc) * 2 * RING_Y + pz // SIDE * RING_Y + y
                            for px, pz, pc in (at, to)
                        )
                    )
    return lax.ppermute(value, ("ens", "node"), pairs)


def ring(value, along, before=()):
    out = [value]
    for hop in (1, -1, -2):
        if hop == -2 and before:
            value, *before = lax.optimization_barrier((value, *before))
        moves = [(hop, 0, 0) if axis == 0 else (0, hop, 0) for axis in along]
        out.append(permute(value, moves))
    return out + list(before)


def swapped(value):
    return permute(value, [(0, 0, 1)] * 2)


def everyone(value):
    value = value[None]
    for phase in range(2):
        groups = []
        for core in range(2):
            for fixed in range(SIDE):
                chips = [
                    step * SIDE + fixed if core == phase else fixed * SIDE + step
                    for step in range(SIDE)
                ]
                groups.append([2 * chip + core for chip in chips])
        spread = jnp.broadcast_to(value[None], (SIDE,) + value.shape)
        spread = spread.reshape((-1,) + value.shape[1:])
        value = lax.all_to_all(spread, "ens", 0, 0, tiled=True, axis_index_groups=groups)
    return value


def per_device(
    hidden, forcing, norm_gain, w_query, w_key, w_value, w_out, w_decode, targets, area_weight
):
    node_rows = hidden.shape[1]
    width = hidden.shape[2]
    head_size = width // HEADS
    span = node_rows + 2 * HALO
    scale = 1.0 / math.sqrt(head_size)
    members = lax.axis_size("ens")
    shards = lax.axis_size("node")
    rows = w_query.shape[0]
    variables = w_decode.shape[1]
    steps = width // STEP
    shape = jax.ShapeDtypeStruct

    def params(mebibytes):
        return pltpu.CompilerParams(vmem_limit_bytes=mebibytes * 1024 * 1024)

    def cost(us):
        return pl.CostEstimate(
            flops=us * 10**9, transcendentals=0, bytes_accessed=us * 3 * 10**6
        )
    decode = jnp.pad(w_decode, ((0, 0), (0, LANES - variables)))
    mixed = jnp.dot(w_out, decode, preferred_element_type=f32).astype(b16)
    position = lax.axis_index("ens")
    core = position % 2
    place = jnp.stack([position // (2 * SIDE), position // 2 % SIDE, core]).astype(jnp.int32)
    row = ring(jnp.concatenate([w_query, w_key, w_value, mixed], 1), (0, 1))
    xfield = hidden[0].astype(f32) + forcing.astype(f32)
    inverse_rms = lax.rsqrt(jnp.mean(xfield * xfield, -1, keepdims=True) + EPS_NORM)
    normed = (xfield * inverse_rms * norm_gain).astype(b16)
    low = shifted(normed, "node", 1)
    high = shifted(normed, "node", -1)
    *mine, low, high = ring(jnp.concatenate(row, 0), (1, 0), (low, high))
    pieces = mine + [swapped(piece) for piece in mine]

    packed_width = 3 * width + LANES
    in_vmem = pl.BlockSpec(memory_space=pltpu.VMEM)
    in_hbm = pl.BlockSpec(memory_space=pltpu.HBM)

    def held(value):
        return pltpu.with_memory_space_constraint(value, pltpu.HBM)

    queries, keys, values, attended, lse, pred, mixed, full = pl.pallas_call(
        lambda *refs: forward_kernel(scale, *refs),
        in_specs=[pl.BlockSpec(memory_space=pltpu.SMEM)] + [in_vmem] * (6 + len(pieces)),
        out_specs=[in_hbm, in_hbm, in_hbm, in_vmem, in_hbm, in_vmem, in_vmem, in_hbm],
        out_shape=[
            pltpu.HBM((span, width), b16),
            pltpu.HBM((span, width), b16),
            pltpu.HBM((span, width), b16),
            shape((node_rows, width), b16),
            pltpu.HBM((node_rows, width), f32),
            shape((VROWS, node_rows), b16),
            shape((width, LANES), b16),
            pltpu.HBM((width, packed_width), b16),
        ],
        scratch_shapes=[
            pltpu.VMEM((span, width), b16),
            pltpu.VMEM((span, width), b16),
            pltpu.VMEM((span, width), b16),
            pltpu.VMEM((node_rows, width), f32),
            pltpu.VMEM((span, width), b16),
            pltpu.VMEM((width, packed_width), b16),
            pltpu.SemaphoreType.DMA((1 + 4 * steps,)),
        ],
        compiler_params=params(24),
        cost_estimate=cost(9),
        name="forward",
    )(place, low, normed, high, hidden, forcing, decode, *pieces)

    others = everyone(pred)
    theirs = swapped(others)
    eps = (1.0 - ALPHA) / members
    coeff = (1.0 - eps) / (2.0 * (members - 1))
    truth = jnp.pad(targets, ((0, VROWS - variables), (0, 0)))
    payload = VROWS + 5 * HEADS
    gram, halo = pl.pallas_call(
        lambda *refs: loss_kernel(coeff, variables, *refs),
        grid=(1,),
        in_specs=[
            whole(others.shape),
            whole(others.shape),
            whole((VROWS, node_rows)),
            whole((VROWS, node_rows)),
            whole((1, node_rows)),
            whole((node_rows, width)),
            whole((width, LANES)),
            whole((node_rows, width)),
        ],
        out_specs=[
            whole((width, LANES)),
            whole((payload, node_rows)),
        ],
        out_shape=[
            shape((width, LANES), b16),
            shape((payload, node_rows), b16),
        ],
        compiler_params=params(12),
        cost_estimate=cost(3),
        name="crps",
    )(others, theirs, pred, truth, area_weight[None], attended, mixed, lse)

    halo_low = shifted(halo, "node", 1)
    halo_high = shifted(halo, "node", -1)
    parts = lax.all_to_all(gram.reshape(members, rows, LANES), "ens", 0, 0, tiled=True)
    part = jnp.sum(parts.astype(f32), 0)
    parts = lax.all_to_all(
        jnp.broadcast_to(part[None], (shards,) + part.shape), "node", 0, 0, tiled=True
    )
    total = jnp.sum(parts, 0)
    grad_out_proj = lax.dot_general(
        total[:, :variables],
        w_decode.astype(f32),
        (((1,), (1,)), ((), ())),
        preferred_element_type=f32,
    )
    loss = jnp.sum(total[0, variables : variables + 3]) / (members * node_rows * shards * variables)

    grad_hidden = pl.pallas_call(
        lambda *refs: backward_kernel(scale, *refs),
        in_specs=[in_vmem] * 9 + [in_hbm] * 5,
        out_specs=in_vmem,
        out_shape=shape((1, node_rows, width), b16),
        scratch_shapes=[
            pltpu.VMEM((span, width), b16),
            pltpu.VMEM((span, width), b16),
            pltpu.VMEM((span, width), b16),
            pltpu.VMEM((node_rows, width), f32),
            pltpu.VMEM((width, 3 * width), b16),
            pltpu.VMEM((span, LANES), b16),
            pltpu.VMEM((2, HEADS, 2 * HALO), f32),
            pltpu.SemaphoreType.DMA((4 + 3 * steps,)),
        ],
        compiler_params=params(24),
        cost_estimate=cost(12),
        name="backward",
    )(
        halo_low, halo, halo_high, hidden, forcing, inverse_rms, norm_gain[None], decode, mixed,
        *[held(part) for part in (queries, keys, values, lse, full)],
    )
    return (grad_hidden, grad_out_proj, loss)


def solution(mesh):
    placed = (
        P("ens", "node", None),
        P("node", None),
        P(),
        P("ens", None),
        P("ens", None),
        P("ens", None),
        P("ens", None),
        P(),
        P(None, "node"),
        P("node"),
    )
    return jax.shard_map(
        per_device,
        mesh=mesh,
        in_specs=placed,
        out_specs=(P("ens", "node", None), P("ens", None), P()),
        check_vma=False,
    )
```

time: 181 us -> 147 us (0.81)
  local copies, waits for them, and re-layouts: 18.4 us -> 2.26 us
  waiting for transfers between devices: 21.8 us -> 7.76 us
  Pallas kernels: 33.9 us -> 21 us
  starting transfers between devices: 80.3 us -> 91.3 us
    unnamed x49 -> x23, local copies, waits for them, and re-layouts: 16.6 us -> 1.27 us
    pallas_call x3 -> x2, Pallas kernels: 31.9 us -> 19 us  [the longest x1 10.2 us: per_device(): pl.pallas_call(lambda *refs: backward_kernel(scale, *refs), in_specs=[in_...]
    ppermute x11, starting transfers between devices: 47.3 us -> 57.4 us  [permute(): return lax.ppermute(value, ('ens', 'node'), pairs)]
    ppermute x11, waiting for transfers between devices: 12.4 us -> 3.85 us  [permute(): return lax.ppermute(value, ('ens', 'node'), pairs)]
    ppermute x4, waiting for transfers between devices: 7.32 us -> 1 us  [shifted(): return lax.ppermute(value, axis, pairs)]
    all_to_all x1, starting transfers between devices: 4.49 us -> 7.47 us  [per_device(): lax.all_to_all(jnp.broadcast_to(part[None], (shards,) + part.shape), 'nod...]
    all_to_all x1, waiting for transfers between devices: 0.01 us -> 2.65 us  [per_device(): lax.all_to_all(jnp.broadcast_to(part[None], (shards,) + part.shape), 'nod...]
  transfers between devices with their start and end apart: 17 -> 17, of which waited for: 6 -> 6; matrix products, arithmetic and copies ran while one was open for 1% -> 2% of each run, Pallas kernels for 8% -> 7%
where the time goes in v6:
time: 147 us; the launch traced here: 146 us
  starting transfers between devices  91.3 us (62%)
  Pallas kernels  21 us (14%)
  blocking collectives  16.3 us (11%)
  waiting for transfers between devices  7.76 us (5%)
  other arithmetic  3.15 us (2%)
  between operations  2.9 us (2%)
  local copies, waits for them, and re-layouts  2.26 us (2%)
    ppermute x11, starting transfers between devices, permute(): return lax.ppermute(value, ('ens', 'node'), pairs)  57.4 us
    ppermute x4, starting transfers between devices, shifted(): return lax.ppermute(value, axis, pairs)  22.6 us
    all_to_all x2, blocking collectives, everyone(): lax.all_to_all(spread, 'ens', 0, 0, tiled=True, axis_index_groups=groups)  16.3 us
    pallas_call x1, Pallas kernels, per_device(): pl.pallas_call(lambda *refs: backward_kernel(scale, *refs), in_specs=[in_...  10.2 us
    pallas_call x1, Pallas kernels, per_device(): pl.pallas_call(lambda *refs: forward_kernel(scale, *refs), in_specs=[pl.B...  8.84 us
    all_to_all x1, starting transfers between devices, per_device(): lax.all_to_all(jnp.broadcast_to(part[None], (shards,) + part.shape), 'nod...  7.47 us
    all_to_all x1, starting transfers between devices, per_device(): lax.all_to_all(gram.reshape(members, rows, LANES), 'ens', 0, 0, tiled=True)  3.9 us
    ppermute x11, waiting for transfers between devices, permute(): return lax.ppermute(value, ('ens', 'node'), pairs)  3.85 us
  transfers between devices with their start and end apart: 17, of which 6 were waited for; matrix products, arithmetic and copies ran while one was open for 2% of the time, Pallas kernels for 7%

profile of v6, /device:TPU:1, one launch (start us, length us, event | category | flops | bytes accessed | tf_op | source)
XLA Modules:
  0.0 145.7 jit_solution(14573459645793866498)
XLA Ops:
  3.0 4.8 %collective-permute-start = (bf16[32,3200]{1,0:T(8,128)(2,1)S(1)}, bf16[32,3200]{1,0:T(8,128)(2,1)S(1)}, u32[]{:S(2)}, u32[]{:S(2)}) collective-permute-start(bf16[32,3200]{1,0:T(8,128)(2,1)S(1)} %pad_maximum_fusion.1), channel_id=1, source_target_pairs={{0,128},{16,48},{1,129},{17,49},{2,130},{18,50},{3,131},{19,51},{4... | collective-permute-start | bytes 614408 | tf_op jit(solution)/shard_map/ppermute | solution.py:339
  7.9 8.6 %collective-permute-start.1 = (bf16[32,3200]{1,0:T(8,128)(2,1)S(1)}, bf16[32,3200]{1,0:T(8,128)(2,1)S(1)}, u32[]{:S(2)}, u32[]{:S(2)}) collective-permute-start(bf16[32,3200]{1,0:T(8,128)(2,1)S(1)} %pad_maximum_fusion.1), channel_id=1, source_target_pairs={{0,384},{16,120},{1,385},{17,121},{2,386},{18,122},{3,387},{19,123... | collective-permute-start | bytes 614408 | tf_op jit(solution)/shard_map/ppermute | solution.py:339
  16.5 1.9 %collective-permute-start.2 = (bf16[32,3200]{1,0:T(8,128)(2,1)S(1)}, bf16[32,3200]{1,0:T(8,128)(2,1)S(1)}, u32[]{:S(2)}, u32[]{:S(2)}) collective-permute-start(bf16[32,3200]{1,0:T(8,128)(2,1)S(1)} %pad_maximum_fusion.1), channel_id=1, source_target_pairs={{0,256},{16,80},{1,257},{17,81},{2,258},{18,82},{3,259},{19,83},{4... | collective-permute-start | bytes 614408 | tf_op jit(solution)/shard_map/ppermute | solution.py:339
  19.7 3.2 %collective-permute-start.3 = (bf16[128,1024]{1,0:T(8,128)(2,1)S(1)}, bf16[128,1024]{1,0:T(8,128)(2,1)S(1)}, u32[]{:S(2)}, u32[]{:S(2)}) collective-permute-start(bf16[128,1024]{1,0:T(8,128)(2,1)S(1)} %multiply_convert_fusion.refs_2_), channel_id=1, source_target_pairs={{0,1},{1,2},{2,3},{3,4},{4,5},{5,6},{6,7},{7,8},{8,9},{9,10},{10,1... | collective-permute-start | bytes 786440 | tf_op jit(solution)/shard_map/ppermute | solution.py:319
  23.0 8.1 %collective-permute-start.4 = (bf16[128,1024]{1,0:T(8,128)(2,1)S(1)}, bf16[128,1024]{1,0:T(8,128)(2,1)S(1)}, u32[]{:S(2)}, u32[]{:S(2)}) collective-permute-start(bf16[128,1024]{1,0:T(8,128)(2,1)S(1)} %multiply_convert_fusion.refs_2_), channel_id=1, source_target_pairs={{0,15},{1,0},{2,1},{3,2},{4,3},{5,4},{6,5},{7,6},{8,7},{9,8},{10,9... | collective-permute-start | bytes 786440 | tf_op jit(solution)/shard_map/ppermute | solution.py:319
  31.2 4.4 %collective-permute-start.6 = (bf16[128,3200]{1,0:T(8,128)(2,1)S(1)}, bf16[128,3200]{1,0:T(8,128)(2,1)S(1)}, u32[]{:S(2)}, u32[]{:S(2)}) collective-permute-start(bf16[128,3200]{1,0:T(8,128)(2,1)S(1)} %pad_maximum_fusion.refs_7_), channel_id=1, source_target_pairs={{0,104},{16,400},{1,105},{17,401},{2,106},{18,402},{3,107},{19,403... | collective-permute-start | bytes 2457608 | tf_op jit(solution)/shard_map/ppermute | solution.py:339
  35.6 1.9 %collective-permute-start.5 = (bf16[128,3200]{1,0:T(8,128)(2,1)S(1)}, bf16[128,3200]{1,0:T(8,128)(2,1)}, u32[]{:S(2)}, u32[]{:S(2)}) collective-permute-start(bf16[128,3200]{1,0:T(8,128)(2,1)S(1)} %pad_maximum_fusion.refs_7_), channel_id=1, source_target_pairs={{0,32},{16,144},{1,33},{17,145},{2,34},{18,146},{3,35},{19,147},{4... | collective-permute-start | bytes 2457608 | tf_op jit(solution)/shard_map/ppermute | solution.py:339
  38.5 4.4 %collective-permute-start.7 = (bf16[128,3200]{1,0:T(8,128)(2,1)S(1)}, bf16[128,3200]{1,0:T(8,128)(2,1)}, u32[]{:S(2)}, u32[]{:S(2)}) collective-permute-start(bf16[128,3200]{1,0:T(8,128)(2,1)S(1)} %pad_maximum_fusion.refs_7_), channel_id=1, source_target_pairs={{0,64},{16,272},{1,65},{17,273},{2,66},{18,274},{3,67},{19,275},{4... | collective-permute-start | bytes 2457608 | tf_op jit(solution)/shard_map/ppermute | solution.py:339
  42.9 5.9 %collective-permute-start.8 = (bf16[128,3200]{1,0:T(8,128)(2,1)S(1)}, bf16[128,3200]{1,0:T(8,128)(2,1)}, u32[]{:S(2)}, u32[]{:S(2)}) collective-permute-start(bf16[128,3200]{1,0:T(8,128)(2,1)S(1)} %pad_maximum_fusion.refs_7_), channel_id=1, source_target_pairs={{0,16},{16,0},{1,17},{17,1},{2,18},{18,2},{3,19},{19,3},{4,20},{20... | collective-permute-start | bytes 2457608 | tf_op jit(solution)/shard_map/ppermute | solution.py:339
  48.8 11.4 %collective-permute-start.10 = (bf16[128,3200]{1,0:T(8,128)(2,1)S(1)}, bf16[128,3200]{1,0:T(8,128)(2,1)}, u32[]{:S(2)}, u32[]{:S(2)}) collective-permute-start(bf16[128,3200]{1,0:T(8,128)(2,1)S(1)} %collective-permute-done.6.refs_9_), channel_id=1, source_target_pairs={{0,16},{16,0},{1,17},{17,1},{2,18},{18,2},{3,19},{19,3},{4,20},{20... | collective-permute-start | bytes 2457608 | tf_op jit(solution)/shard_map/ppermute | solution.py:339
  60.2 5.7 %collective-permute-start.9 = (bf16[128,3200]{1,0:T(8,128)(2,1)}, bf16[128,3200]{1,0:T(8,128)(2,1)}, u32[]{:S(2)}, u32[]{:S(2)}) collective-permute-start(bf16[128,3200]{1,0:T(8,128)(2,1)} %collective-permute-done.5.refs_8_), channel_id=1, source_target_pairs={{0,16},{16,0},{1,17},{17,1},{2,18},{18,2},{3,19},{19,3},{4,20},{20... | collective-permute-start | bytes 2457608 | tf_op jit(solution)/shard_map/ppermute | solution.py:339
  65.9 1.9 %collective-permute-start.11 = (bf16[128,3200]{1,0:T(8,128)(2,1)}, bf16[128,3200]{1,0:T(8,128)(2,1)}, u32[]{:S(2)}, u32[]{:S(2)}) collective-permute-start(bf16[128,3200]{1,0:T(8,128)(2,1)} %collective-permute-done.7.refs_10_), channel_id=1, source_target_pairs={{0,16},{16,0},{1,17},{17,1},{2,18},{18,2},{3,19},{19,3},{4,20},{20... | collective-permute-start | bytes 2457608 | tf_op jit(solution)/shard_map/ppermute | solution.py:339
  68.2 2.3 %collective-permute-done.11.refs_14_ = bf16[128,3200]{1,0:T(8,128)(2,1)} collective-permute-done((bf16[128,3200]{1,0:T(8,128)(2,1)}, bf16[128,3200]{1,0:T(8,128)(2,1)}, u32[]{:S(2)}, u32[]{:S(2)}) %collective-permute-start.11) | collective-permute-done | bytes 819232 | tf_op jit(solution)/shard_map/ppermute | solution.py:339
  70.5 8.8 %forward.1 = (bf16[384,1024]{1,0:T(8,128)(2,1)}, bf16[384,1024]{1,0:T(8,128)(2,1)}, bf16[384,1024]{1,0:T(8,128)(2,1)}, bf16[128,1024]{1,0:T(8,128)(2,1)S(1)}, f3...) custom-call(s32[3]{0:T(128)S(1)} %pad_add_fusion.refs_0_, ...), custom_call_target="tpu_custom_call" | custom-call | flops 8999999488 | bytes 27000000 | tf_op jit(solution)/shard_map/forward/pallas_call | solution.py:416
  79.4 7.2 %all_to_all.20 = bf16[4,112,128]{2,1,0:T(8,128)(2,1)S(1)} all-to-all(bf16[4,112,128]{2,1,0:T(8,128)(2,1)S(1)} %reshape.44), channel_id=1, replica_groups={{0,128,256,384},{32,160,288,416},{64,192,320,448},{96,224,352,480},{16,..., dimensions={0} | all-to-all | bytes 229376 | tf_op jit(solution)/shard_map/all_to_all | solution.py:369
  86.7 9.1 %all_to_all.21.refs_0_ = bf16[16,112,128]{2,1,0:T(8,128)(2,1)S(1)} all-to-all(bf16[16,112,128]{2,1,0:T(8,128)(2,1)S(1)} %bitcast.19), channel_id=1, replica_groups={{0,32,64,96},{128,160,192,224},{256,288,320,352},{384,416,448,480},{16,..., dimensions={0} | all-to-all | bytes 917504 | tf_op jit(solution)/shard_map/all_to_all | solution.py:369
  95.8 6.5 %collective-permute-start.12 = (bf16[16,112,128]{2,1,0:T(8,128)(2,1)S(1)}, bf16[16,112,128]{2,1,0:T(8,128)(2,1)S(1)}, u32[]{:S(2)}, u32[]{:S(2)}) collective-permute-start(bf16[16,112,128]{2,1,0:T(8,128)(2,1)S(1)} %all_to_all.21.refs_0_), channel_id=1, source_target_pairs={{0,16},{16,0},{1,17},{17,1},{2,18},{18,2},{3,19},{19,3},{4,20},{20... | collective-permute-start | bytes 1376264 | tf_op jit(solution)/shard_map/ppermute | solution.py:339
  103.7 1.9 %crps.1 = (bf16[1024,128]{1,0:T(8,128)(2,1)}, bf16[192,128]{1,0:T(8,128)(2,1)S(1)}) custom-call(bf16[16,112,128]{2,1,0:T(8,128)(2,1)S(1)} %all_to_all.21.refs_0_, bf16[16,112,128]{2,1,0:T(8,128)(2,1)S(1)} %collective-permute-done.12.refs_1_, bf16[112,128]{1,0:T(8,128)(2,1)S(1)} %get-tuple-element.19.refs_2_, bf16[112,128]{1,0:T(8,128)(2,1)S(1)} %pad.9.refs_3_, ...), custom_call_target="tpu_custom_call" | custom-call | flops 3000000000 | bytes 9000000 | tf_op jit(solution)/shard_map/crps/pallas_call | solution.py:450
  105.6 3.9 %all-to-all-start.2 = ((bf16[32,32,128]{2,1,0:T(8,128)(2,1)}), bf16[32,32,128]{2,1,0:T(8,128)(2,1)S(1)}, u32[]{:S(2)}, u32[]{:S(2)}) async-start(bf16[32,32,128]{2,1,0:T(8,128)(2,1)} %bitcast.9), calls=%async_computation.2 | async-start | bytes 524288 | tf_op jit(solution)/shard_map/all_to_all | solution.py:478
  109.7 1.9 %collective-permute-start.13 = (bf16[192,128]{1,0:T(8,128)(2,1)S(1)}, bf16[192,128]{1,0:T(8,128)(2,1)S(1)}, u32[]{:S(2)}, u32[]{:S(2)}) collective-permute-start(bf16[192,128]{1,0:T(8,128)(2,1)S(1)} %get-tuple-element.23.refs_1_), channel_id=1, source_target_pairs={{0,1},{1,2},{2,3},{3,4},{4,5},{5,6},{6,7},{7,8},{8,9},{9,10},{10,1... | collective-permute-start | bytes 147464 | tf_op jit(solution)/shard_map/ppermute | solution.py:319
  111.6 9.4 %collective-permute-start.14 = (bf16[192,128]{1,0:T(8,128)(2,1)S(1)}, bf16[192,128]{1,0:T(8,128)(2,1)S(1)}, u32[]{:S(2)}, u32[]{:S(2)}) collective-permute-start(bf16[192,128]{1,0:T(8,128)(2,1)S(1)} %get-tuple-element.23.refs_1_), channel_id=1, source_target_pairs={{0,15},{1,0},{2,1},{3,2},{4,3},{5,4},{6,5},{7,6},{8,7},{9,8},{10,9... | collective-permute-start | bytes 147464 | tf_op jit(solution)/shard_map/ppermute | solution.py:319
  122.0 7.5 %all-to-all-start.3 = ((f32[16,32,128]{2,1,0:T(8,128)}), f32[16,32,128]{2,1,0:T(8,128)S(1)}, u32[]{:S(2)}, u32[]{:S(2)}) async-start(f32[16,32,128]{2,1,0:T(8,128)} %broadcast_in_dim.11), calls=%async_computation.3 | async-start | bytes 524288 | tf_op jit(solution)/shard_map/all_to_all | solution.py:480
  129.5 10.2 %backward.1 = bf16[1,128,1024]{2,1,0:T(8,128)(2,1)} custom-call(bf16[192,128]{1,0:T(8,128)(2,1)S(1)} %collective-permute-done.13.refs_0_, bf16[192,128]{1,0:T(8,128)(2,1)S(1)} %get-tuple-element.23.refs_1_, bf16[192,128]{1,0:T(8,128)(2,1)S(1)} %collective-permute-done.14.refs_2_, bf16[1,128,1024]{2,1,0:T(8,128)(2,1)S(1)} %copy-done.2, ...), custom_call_target="tpu_custom_call" | custom-call | flops 12000000000 | bytes 36000000 | tf_op jit(solution)/shard_map/backward/pallas_call | solution.py:492
  139.7 2.7 %all-to-all-done.3 = f32[16,32,128]{2,1,0:T(8,128)S(1)} async-done(((f32[16,32,128]{2,1,0:T(8,128)}), f32[16,32,128]{2,1,0:T(8,128)S(1)}, u32[]{:S(2)}, u32[]{:S(2)}) %all-to-all-start.3) | async-done | bytes 262176 | tf_op jit(solution)/shard_map/all_to_all | solution.py:480
  (55 shorter events, 9.2 us)
Async XLA Ops:
  0.6 30.5 %copy-start.9 = (bf16[32,1024]{1,0:T(8,128)(2,1)S(1)}, bf16[32,1024]{1,0:T(8,128)(2,1)}, u32[]{:S(2)}) copy-start(bf16[32,1024]{1,0:T(8,128)(2,1)} %param.13) | copy-start | bytes 196612
  0.7 30.4 %copy-start.8 = (bf16[32,1024]{1,0:T(8,128)(2,1)S(1)}, bf16[32,1024]{1,0:T(8,128)(2,1)}, u32[]{:S(2)}) copy-start(bf16[32,1024]{1,0:T(8,128)(2,1)} %param.14) | copy-start | bytes 196612
  0.7 30.4 %copy-start.7 = (bf16[32,1024]{1,0:T(8,128)(2,1)S(1)}, bf16[32,1024]{1,0:T(8,128)(2,1)}, u32[]{:S(2)}) copy-start(bf16[32,1024]{1,0:T(8,128)(2,1)} %param.15) | copy-start | bytes 196612
  0.7 18.9 %copy-start.2 = (bf16[1,128,1024]{2,1,0:T(8,128)(2,1)S(1)}, bf16[1,128,1024]{2,1,0:T(8,128)(2,1)}, u32[]{:S(2)}) copy-start(bf16[1,128,1024]{2,1,0:T(8,128)(2,1)} %refs_3_.1) | copy-start | bytes 786436
  3.0 28.0 %collective-permute-start = (bf16[32,3200]{1,0:T(8,128)(2,1)S(1)}, bf16[32,3200]{1,0:T(8,128)(2,1)S(1)}, u32[]{:S(2)}, u32[]{:S(2)}) collective-permute-start(bf16[32,3200]{1,0:T(8,128)(2,1)S(1)} %pad_maximum_fusion.1), channel_id=1, source_target_pairs={{0,128},{16,48},{1,129},{17,49},{2,130},{18,50},{3,131},{19,51},{4... | collective-permute-start | bytes 614408 | tf_op jit(solution)/shard_map/ppermute | solution.py:339
  7.9 23.2 %collective-permute-start.1 = (bf16[32,3200]{1,0:T(8,128)(2,1)S(1)}, bf16[32,3200]{1,0:T(8,128)(2,1)S(1)}, u32[]{:S(2)}, u32[]{:S(2)}) collective-permute-start(bf16[32,3200]{1,0:T(8,128)(2,1)S(1)} %pad_maximum_fusion.1), channel_id=1, source_target_pairs={{0,384},{16,120},{1,385},{17,121},{2,386},{18,122},{3,387},{19,123... | collective-permute-start | bytes 614408 | tf_op jit(solution)/shard_map/ppermute | solution.py:339
  16.5 14.6 %collective-permute-start.2 = (bf16[32,3200]{1,0:T(8,128)(2,1)S(1)}, bf16[32,3200]{1,0:T(8,128)(2,1)S(1)}, u32[]{:S(2)}, u32[]{:S(2)}) collective-permute-start(bf16[32,3200]{1,0:T(8,128)(2,1)S(1)} %pad_maximum_fusion.1), channel_id=1, source_target_pairs={{0,256},{16,80},{1,257},{17,81},{2,258},{18,82},{3,259},{19,83},{4... | collective-permute-start | bytes 614408 | tf_op jit(solution)/shard_map/ppermute | solution.py:339
  19.7 18.8 %collective-permute-start.3 = (bf16[128,1024]{1,0:T(8,128)(2,1)S(1)}, bf16[128,1024]{1,0:T(8,128)(2,1)S(1)}, u32[]{:S(2)}, u32[]{:S(2)}) collective-permute-start(bf16[128,1024]{1,0:T(8,128)(2,1)S(1)} %multiply_convert_fusion.refs_2_), channel_id=1, source_target_pairs={{0,1},{1,2},{2,3},{3,4},{4,5},{5,6},{6,7},{7,8},{8,9},{9,10},{10,1... | collective-permute-start | bytes 786440 | tf_op jit(solution)/shard_map/ppermute | solution.py:319
  23.0 15.6 %collective-permute-start.4 = (bf16[128,1024]{1,0:T(8,128)(2,1)S(1)}, bf16[128,1024]{1,0:T(8,128)(2,1)S(1)}, u32[]{:S(2)}, u32[]{:S(2)}) collective-permute-start(bf16[128,1024]{1,0:T(8,128)(2,1)S(1)} %multiply_convert_fusion.refs_2_), channel_id=1, source_target_pairs={{0,15},{1,0},{2,1},{3,2},{4,3},{5,4},{6,5},{7,6},{8,7},{9,8},{10,9... | collective-permute-start | bytes 786440 | tf_op jit(solution)/shard_map/ppermute | solution.py:319
  31.2 17.6 %collective-permute-start.6 = (bf16[128,3200]{1,0:T(8,128)(2,1)S(1)}, bf16[128,3200]{1,0:T(8,128)(2,1)S(1)}, u32[]{:S(2)}, u32[]{:S(2)}) collective-permute-start(bf16[128,3200]{1,0:T(8,128)(2,1)S(1)} %pad_maximum_fusion.refs_7_), channel_id=1, source_target_pairs={{0,104},{16,400},{1,105},{17,401},{2,106},{18,402},{3,107},{19,403... | collective-permute-start | bytes 2457608 | tf_op jit(solution)/shard_map/ppermute | solution.py:339
  35.6 24.6 %collective-permute-start.5 = (bf16[128,3200]{1,0:T(8,128)(2,1)S(1)}, bf16[128,3200]{1,0:T(8,128)(2,1)}, u32[]{:S(2)}, u32[]{:S(2)}) collective-permute-start(bf16[128,3200]{1,0:T(8,128)(2,1)S(1)} %pad_maximum_fusion.refs_7_), channel_id=1, source_target_pairs={{0,32},{16,144},{1,33},{17,145},{2,34},{18,146},{3,35},{19,147},{4... | collective-permute-start | bytes 2457608 | tf_op jit(solution)/shard_map/ppermute | solution.py:339
  38.5 27.4 %collective-permute-start.7 = (bf16[128,3200]{1,0:T(8,128)(2,1)S(1)}, bf16[128,3200]{1,0:T(8,128)(2,1)}, u32[]{:S(2)}, u32[]{:S(2)}) collective-permute-start(bf16[128,3200]{1,0:T(8,128)(2,1)S(1)} %pad_maximum_fusion.refs_7_), channel_id=1, source_target_pairs={{0,64},{16,272},{1,65},{17,273},{2,66},{18,274},{3,67},{19,275},{4... | collective-permute-start | bytes 2457608 | tf_op jit(solution)/shard_map/ppermute | solution.py:339
  42.9 25.1 %collective-permute-start.8 = (bf16[128,3200]{1,0:T(8,128)(2,1)S(1)}, bf16[128,3200]{1,0:T(8,128)(2,1)}, u32[]{:S(2)}, u32[]{:S(2)}) collective-permute-start(bf16[128,3200]{1,0:T(8,128)(2,1)S(1)} %pad_maximum_fusion.refs_7_), channel_id=1, source_target_pairs={{0,16},{16,0},{1,17},{17,1},{2,18},{18,2},{3,19},{19,3},{4,20},{20... | collective-permute-start | bytes 2457608 | tf_op jit(solution)/shard_map/ppermute | solution.py:339
  48.8 19.2 %collective-permute-start.10 = (bf16[128,3200]{1,0:T(8,128)(2,1)S(1)}, bf16[128,3200]{1,0:T(8,128)(2,1)}, u32[]{:S(2)}, u32[]{:S(2)}) collective-permute-start(bf16[128,3200]{1,0:T(8,128)(2,1)S(1)} %collective-permute-done.6.refs_9_), channel_id=1, source_target_pairs={{0,16},{16,0},{1,17},{17,1},{2,18},{18,2},{3,19},{19,3},{4,20},{20... | collective-permute-start | bytes 2457608 | tf_op jit(solution)/shard_map/ppermute | solution.py:339
  60.2 8.0 %collective-permute-start.9 = (bf16[128,3200]{1,0:T(8,128)(2,1)}, bf16[128,3200]{1,0:T(8,128)(2,1)}, u32[]{:S(2)}, u32[]{:S(2)}) collective-permute-start(bf16[128,3200]{1,0:T(8,128)(2,1)} %collective-permute-done.5.refs_8_), channel_id=1, source_target_pairs={{0,16},{16,0},{1,17},{17,1},{2,18},{18,2},{3,19},{19,3},{4,20},{20... | collective-permute-start | bytes 2457608 | tf_op jit(solution)/shard_map/ppermute | solution.py:339
  65.9 4.6 %collective-permute-start.11 = (bf16[128,3200]{1,0:T(8,128)(2,1)}, bf16[128,3200]{1,0:T(8,128)(2,1)}, u32[]{:S(2)}, u32[]{:S(2)}) collective-permute-start(bf16[128,3200]{1,0:T(8,128)(2,1)} %collective-permute-done.7.refs_10_), channel_id=1, source_target_pairs={{0,16},{16,0},{1,17},{17,1},{2,18},{18,2},{3,19},{19,3},{4,20},{20... | collective-permute-start | bytes 2457608 | tf_op jit(solution)/shard_map/ppermute | solution.py:339
  79.3 22.9 %copy-start.10 = (bf16[100,128]{1,0:T(8,128)(2,1)S(1)}, bf16[100,128]{1,0:T(8,128)(2,1)}, u32[]{:S(2)}) copy-start(bf16[100,128]{1,0:T(8,128)(2,1)} %param.18) | copy-start | bytes 76804
  79.3 24.3 %copy-start.4 = (f32[128]{0:T(128)S(1)}, f32[128]{0:T(128)}, u32[]{:S(2)}) copy-start(f32[128]{0:T(128)} %param.19) | copy-start | bytes 1540
  79.3 24.3 %copy-start.5 = (f32[128,1024]{1,0:T(8,128)S(1)}, f32[128,1024]{1,0:T(8,128)}, u32[]{:S(2)}) copy-start(f32[128,1024]{1,0:T(8,128)} %get-tuple-element.22.refs_7_.refs_12_) | copy-start | bytes 1572868
  95.8 7.9 %collective-permute-start.12 = (bf16[16,112,128]{2,1,0:T(8,128)(2,1)S(1)}, bf16[16,112,128]{2,1,0:T(8,128)(2,1)S(1)}, u32[]{:S(2)}, u32[]{:S(2)}) collective-permute-start(bf16[16,112,128]{2,1,0:T(8,128)(2,1)S(1)} %all_to_all.21.refs_0_), channel_id=1, source_target_pairs={{0,16},{16,0},{1,17},{17,1},{2,18},{18,2},{3,19},{19,3},{4,20},{20... | collective-permute-start | bytes 1376264 | tf_op jit(solution)/shard_map/ppermute | solution.py:339
  105.6 15.6 %all-to-all-start.2 = ((bf16[32,32,128]{2,1,0:T(8,128)(2,1)}), bf16[32,32,128]{2,1,0:T(8,128)(2,1)S(1)}, u32[]{:S(2)}, u32[]{:S(2)}) async-start(bf16[32,32,128]{2,1,0:T(8,128)(2,1)} %bitcast.9), calls=%async_computation.2 | async-start | bytes 524288 | tf_op jit(solution)/shard_map/all_to_all | solution.py:478
  109.7 19.8 %collective-permute-start.13 = (bf16[192,128]{1,0:T(8,128)(2,1)S(1)}, bf16[192,128]{1,0:T(8,128)(2,1)S(1)}, u32[]{:S(2)}, u32[]{:S(2)}) collective-permute-start(bf16[192,128]{1,0:T(8,128)(2,1)S(1)} %get-tuple-element.23.refs_1_), channel_id=1, source_target_pairs={{0,1},{1,2},{2,3},{3,4},{4,5},{5,6},{6,7},{7,8},{8,9},{9,10},{10,1... | collective-permute-start | bytes 147464 | tf_op jit(solution)/shard_map/ppermute | solution.py:319
  111.6 17.9 %collective-permute-start.14 = (bf16[192,128]{1,0:T(8,128)(2,1)S(1)}, bf16[192,128]{1,0:T(8,128)(2,1)S(1)}, u32[]{:S(2)}, u32[]{:S(2)}) collective-permute-start(bf16[192,128]{1,0:T(8,128)(2,1)S(1)} %get-tuple-element.23.refs_1_), channel_id=1, source_target_pairs={{0,15},{1,0},{2,1},{3,2},{4,3},{5,4},{6,5},{7,6},{8,7},{9,8},{10,9... | collective-permute-start | bytes 147464 | tf_op jit(solution)/shard_map/ppermute | solution.py:319
  122.0 20.3 %all-to-all-start.3 = ((f32[16,32,128]{2,1,0:T(8,128)}), f32[16,32,128]{2,1,0:T(8,128)S(1)}, u32[]{:S(2)}, u32[]{:S(2)}) async-start(f32[16,32,128]{2,1,0:T(8,128)} %broadcast_in_dim.11), calls=%async_computation.3 | async-start | bytes 524288 | tf_op jit(solution)/shard_map/all_to_all | solution.py:480
  (4 other events, 52.0 us)

commit v7 on v6

v7 whole, which is shorter than its diff:
```python
import math

import jax
import jax.numpy as jnp
from jax import lax
from jax.experimental import pallas as pl
from jax.experimental.pallas import tpu as pltpu
from jax.sharding import PartitionSpec as P

HEADS = 16
HALO = 128
LANES = 128
STEP = 256
VROWS = 112
SIDE = 4
RING_Z = 8
RING_Y = 8
HOPS = (0, SIDE - 1, 1, 2)


ALPHA = 0.95
KAPPA = 0.25
EPS_NORM = 1e-05
FAR = -1e30

f32 = jnp.float32
b16 = jnp.bfloat16


def nn(a, b):
    return lax.dot_general(a, b, (((1,), (0,)), ((), ())), preferred_element_type=f32)


def nt(a, b):
    return lax.dot_general(a, b, (((1,), (1,)), ((), ())), preferred_element_type=f32)


def tn(a, b):
    return lax.dot_general(a, b, (((0,), (0,)), ((), ())), preferred_element_type=f32)


def whole(shape):
    return pl.BlockSpec(shape, lambda i: (0,) * len(shape))


def head_masks(value):
    lane = lax.broadcasted_iota(jnp.int32, (1, LANES), 1)
    first = jnp.where(lane < LANES // 2, value, 0.0).astype(b16)
    second = jnp.where(lane < LANES // 2, 0.0, value).astype(b16)
    return first, second


def window_mask(rows, span):
    offset = lax.broadcasted_iota(jnp.int32, (rows, span), 1) - lax.broadcasted_iota(
        jnp.int32, (rows, span), 0
    )
    return (offset >= 0) & (offset <= 2 * HALO)


def split_bf16(value, pieces):
    out = []
    for _ in range(pieces):
        piece = value.astype(b16)
        out.append(piece)
        value = value - piece.astype(f32)
    return out


def forward_kernel(scale, place, own, other, hidden, forcing, decode, *refs):
    pieces, refs = refs[: len(HOPS)], refs[len(HOPS) :]
    (
        queries_out, keys_out, values_out, attended, lse, pred, mixed, full,
        queries, keys, values, weights, store,
    ) = refs
    span = own.shape[0]
    rows = span - 2 * HALO
    width = attended.shape[2]
    x, z, core = place[0], place[1], place[2]
    side = len(HOPS)
    block = pieces[0].shape[0] // side
    for outer, far in enumerate(HOPS):
        for inner, near in enumerate(HOPS):
            along_x = jnp.where(core == 0, near, far)
            along_z = jnp.where(core == 0, far, near)
            chip = lax.rem(x + along_x, side) * side + lax.rem(z + along_z, side)
            at = pl.multiple_of(chip * block, block)
            weights[pl.ds(at, block), :] = pieces[outer][inner * block : (inner + 1) * block, :]
    stores = [pltpu.make_async_copy(weights, full, store.at[0])]
    stores[0].start()
    mixed[...] = weights[pl.ds(pl.multiple_of(core * width, width), width), 3 * width :]
    window = window_mask(rows, span)
    masks = head_masks(scale)
    lower = lax.broadcasted_iota(jnp.int32, (rows, LANES), 1) < LANES // 2
    pairs = STEP // LANES
    for member, field_ref in enumerate((own, other)):
        if member == 0:
            total = nn(hidden[0], decode[...]) + nn(forcing[...], decode[...])
        else:
            total = jnp.zeros((rows, LANES), f32)
        for at in range(0, width, STEP):
            cols = slice(at, at + STEP)
            field = field_ref[...]
            projected = [
                nn(field, weights[:, index * width + at : index * width + at + STEP]).astype(b16)
                for index in range(3)
            ]
            query, key, value = projected
            for part, scratch, out in zip(
                projected, (queries, keys, values), (queries_out, keys_out, values_out), strict=True
            ):
                scratch[member, :, cols] = part
                stores.append(
                    pltpu.make_async_copy(
                        scratch.at[member, :, cols],
                        out.at[member, :, cols],
                        store.at[len(stores)],
                    )
                )
                stores[-1].start()
            scores = []
            for pair in range(pairs):
                lanes = slice(pair * LANES, (pair + 1) * LANES)
                for mask in masks:
                    scores.append(nt(query[HALO : HALO + rows, lanes] * mask, key[:, lanes]))
            scores = [jnp.where(window, score, FAR) for score in scores]
            tops = [jnp.max(score, -1, keepdims=True) for score in scores]
            expos = [jnp.exp(score - top) for score, top in zip(scores, tops, strict=True)]
            norms = [jnp.sum(expo, -1, keepdims=True) for expo in expos]
            probs = [
                (expo * (1.0 / norm)).astype(b16) for expo, norm in zip(expos, norms, strict=True)
            ]
            outs = [
                nn(prob, value[:, index // 2 * LANES : (index // 2 + 1) * LANES])
                for index, prob in enumerate(probs)
            ]
            stats = [top + jnp.log(norm) for top, norm in zip(tops, norms, strict=True)]
            result = jnp.concatenate(
                [jnp.where(lower, outs[2 * n], outs[2 * n + 1]).astype(b16) for n in range(pairs)],
                1,
            )
            attended[member, :, cols] = result
            lse[member, :, cols] = jnp.concatenate(
                [jnp.where(lower, stats[2 * n], stats[2 * n + 1]) for n in range(pairs)], 1
            )
            total = total + nn(result, mixed[cols, :])
        pred[member] = total.T[:VROWS]
    for copy in stores:
        copy.wait()


def loss_kernel(
    coeff, variables, place, others, theirs, preds, targets, weight, attended, mixed, lse,
    gram, halo,
):
    rows, width = attended.shape[1:]
    heads = HEADS // 2
    truth = targets[...].astype(f32)
    scale = weight[...]
    real = lax.broadcasted_iota(jnp.int32, (VROWS, LANES), 0) < variables
    size = width // heads
    head = lax.broadcasted_iota(jnp.int32, (heads, width), 0)
    feature = lax.broadcasted_iota(jnp.int32, (heads, width), 1)
    inside = jnp.where((feature >= head * size) & (feature < (head + 1) * size), 1.0, 0.0)
    chosen = jnp.where(feature == head * size, 1.0, 0.0).astype(b16)
    inside = inside.astype(b16)
    own, other = preds[0].astype(f32), preds[1].astype(f32)

    def member(index, carry):
        pair_abs, slope_own, slope_other = carry
        for part in (others, theirs):
            value = part[index].astype(f32)
            delta = own - value
            square = delta * delta + KAPPA * KAPPA
            inverse = lax.rsqrt(square)
            pair_abs = pair_abs + (square * inverse - KAPPA)
            slope_own = slope_own + delta * inverse
            delta = other - value
            slope_other = slope_other + delta * lax.rsqrt(delta * delta + KAPPA * KAPPA)
        return pair_abs, slope_own, slope_other

    zero = jnp.zeros((VROWS, LANES), f32)
    pair_abs, *slopes = lax.fori_loop(0, others.shape[0], member, (zero, zero, zero), unroll=2)
    parts = jnp.zeros((LANES, width), f32)
    row_delta, row_lse = [], []
    for index, value in enumerate((own, other)):
        delta = value - truth
        square = delta * delta + KAPPA * KAPPA
        inverse = lax.rsqrt(square)
        if index == 0:
            entries = scale * (square * inverse - KAPPA - coeff * pair_abs)
            entries = jnp.where(real, entries, 0.0)
            loss = jnp.sum(jnp.sum(entries, 0, keepdims=True), 1, keepdims=True)
        grad = jnp.where(real, scale * (delta * inverse - 2.0 * coeff * slopes[index]), 0.0)
        halo[index * VROWS : (index + 1) * VROWS] = grad.astype(b16)
        grad_full = jnp.concatenate([grad, jnp.zeros((LANES - VROWS, LANES), f32)], 0)
        grad_t = grad_full.T.astype(b16)
        parts = parts + nn(grad_full.astype(b16), attended[index])
        grad_att = nt(grad_t, mixed[...]).astype(b16)
        product = grad_att.astype(f32) * attended[index].astype(f32)
        row_delta.append(sum(nt(inside, piece) for piece in split_bf16(product, 2)))
        row_lse.append(sum(nt(chosen, piece) for piece in split_bf16(lse[index], 3)))
    at = 2 * VROWS
    for pieces in (
        split_bf16(jnp.concatenate(row_delta, 0), 2),
        split_bf16(jnp.concatenate(row_lse, 0), 3),
    ):
        for piece in pieces:
            halo[at : at + HEADS] = piece
            at += HEADS
    column = lax.broadcasted_iota(jnp.int32, (width, LANES), 1)
    parts = parts.T
    blank = jnp.zeros((width, LANES), f32)
    for index, piece in enumerate(split_bf16(loss, 3)):
        parts = jnp.where(column == variables + index, piece.astype(f32), parts)
        blank = jnp.where(column == variables + index, piece.astype(f32), blank)
    core = place[2]
    gram[pl.ds(pl.multiple_of(core * width, width), width), :] = parts.astype(b16)
    gram[pl.ds(pl.multiple_of((1 - core) * width, width), width), :] = blank.astype(b16)


def middle_kernel(variables, parts, spread):
    total = parts[0].astype(f32)
    for index in range(1, parts.shape[0]):
        total = total + parts[index].astype(f32)
    column = lax.broadcasted_iota(jnp.int32, total.shape, 1)
    spare = (column >= variables) & (column < variables + 3)
    loss = jnp.sum(jnp.where(spare, total, 0.0), 1, keepdims=True)
    for index, piece in enumerate(split_bf16(loss, 3)):
        total = jnp.where(column == variables + index, piece.astype(f32), total)
    total = total.astype(b16)
    for index in range(spread.shape[0]):
        spread[index] = total


def backward_kernel(
    scale, low, own, high, mixed, queries_in, keys_in, values_in, lse_in, full,
    total_own, total_other, queries, keys, values, lse, weights, grad_t, stats, load,
):
    rows, width = lse.shape[1:]
    span = keys.shape[1]
    loads = []

    def fetch(source, target):
        loads.append(pltpu.make_async_copy(source, target, load.at[len(loads)]))
        loads[-1].start()

    fetch(queries_in, queries)
    fetch(keys_in, keys)
    fetch(values_in, values)
    fetch(lse_in, lse)
    for at in range(0, width, STEP):
        for index in range(3):
            cols = slice(index * width + at, index * width + at + STEP)
            fetch(full.at[:, cols], weights.at[:, cols])

    zero = jnp.zeros((LANES - VROWS, LANES), b16)
    for member in range(2):
        for side, part in enumerate((own, low, high)):
            grad = jnp.concatenate([part[member * VROWS : (member + 1) * VROWS], zero], 0)
            grad_t[member, side * rows : (side + 1) * rows] = grad.astype(f32).T.astype(b16)
    first_stat = 2 * VROWS
    for side, part in enumerate((low, high)):
        at = slice(side * HALO, (side + 1) * HALO)
        pieces = [
            part[first_stat + HEADS * n : first_stat + HEADS * (n + 1)].astype(f32)
            for n in range(5)
        ]
        stats[0, :, at] = pieces[0] + pieces[1]
        stats[1, :, at] = pieces[2] + pieces[3] + pieces[4]

    window = window_mask(rows, span)
    key_at = lax.broadcasted_iota(jnp.int32, (rows, 2 * HALO), 0)
    query_at = lax.broadcasted_iota(jnp.int32, (rows, 2 * HALO), 1)
    reach = ((query_at < HALO) & (query_at >= key_at)) | (
        (query_at >= HALO) & (query_at - HALO <= key_at)
    )
    scaled = head_masks(scale)
    plain = head_masks(1.0)
    center = slice(HALO, HALO + rows)
    halves = [(pair, half) for pair in range(STEP // LANES) for half in range(2)]
    for copy in loads[:4]:
        copy.wait()
    for member in (1, 0):
        total = jnp.zeros((rows, weights.shape[0]), f32)
        for at in range(0, width, STEP):
            step = at // STEP
            grad_att = nt(grad_t[member], mixed[at : at + STEP, :]).astype(b16)
            lanes = [
                slice(at + pair * LANES, at + (pair + 1) * LANES) for pair in range(STEP // LANES)
            ]
            query = [queries[member, center, cols] for cols in lanes]
            key = [keys[member, :, cols] for cols in lanes]
            value = [values[member, :, cols] for cols in lanes]
            far_query = [
                jnp.concatenate(
                    [queries[member, :HALO, cols], queries[member, HALO + rows :, cols]], 0
                )
                for cols in lanes
            ]
            grad = [grad_att[:rows, n * LANES : (n + 1) * LANES] for n in range(len(lanes))]
            far_grad = [grad_att[rows:, n * LANES : (n + 1) * LANES] for n in range(len(lanes))]
            scores = [nt(query[p] * scaled[h], key[p]) for p, h in halves]
            d_probs = [nt(grad[p] * plain[h], value[p]) for p, h in halves]
            probs = []
            for (p, h), score in zip(halves, scores, strict=True):
                start = lanes[p].start + h * (LANES // 2)
                probs.append(
                    jnp.where(window, jnp.exp(score - lse[member, :, start : start + 1]), 0.0)
                )
            deltas = [
                jnp.sum(prob * d_prob, -1, keepdims=True)
                for prob, d_prob in zip(probs, d_probs, strict=True)
            ]
            d_scores = [
                (prob * (d_prob - delta)).astype(b16)
                for prob, d_prob, delta in zip(probs, d_probs, deltas, strict=True)
            ]
            probs = [prob.astype(b16) for prob in probs]
            far_scores = [nt(key[p][center] * scaled[h], far_query[p]) for p, h in halves]
            far_d_probs = [nt(value[p][center] * plain[h], far_grad[p]) for p, h in halves]
            far_probs, far_d_scores = [], []
            for (p, h), score, d_prob in zip(halves, far_scores, far_d_probs, strict=True):
                row = member * (HEADS // 2) + 2 * (step * len(lanes) + p) + h
                prob = jnp.where(reach, jnp.exp(score - stats[1, row : row + 1, :]), 0.0)
                far_d_scores.append((prob * (d_prob - stats[0, row : row + 1, :])).astype(b16))
                far_probs.append(prob.astype(b16))
            d_query, d_key, d_value = [], [], []
            for p in range(len(lanes)):
                first, second = 2 * p, 2 * p + 1
                d_query.append(
                    nn(d_scores[first], key[p] * scaled[0])
                    + nn(d_scores[second], key[p] * scaled[1])
                )
                d_key.append(
                    tn(d_scores[first][:, center], query[p] * scaled[0])
                    + tn(d_scores[second][:, center], query[p] * scaled[1])
                    + nn(far_d_scores[first], far_query[p] * scaled[0])
                    + nn(far_d_scores[second], far_query[p] * scaled[1])
                )
                d_value.append(
                    tn(probs[first][:, center], grad[p] * plain[0])
                    + tn(probs[second][:, center], grad[p] * plain[1])
                    + nn(far_probs[first], far_grad[p] * plain[0])
                    + nn(far_probs[second], far_grad[p] * plain[1])
                )
            for index, part in enumerate((d_query, d_key, d_value)):
                if member == 1:
                    loads[4 + 3 * step + index].wait()
                part = jnp.concatenate(part, 1).astype(b16)
                cols = slice(index * width + at, index * width + at + STEP)
                total = total + nt(part, weights[:, cols])
        if member == 1:
            total_other[...] = total.astype(b16)
        else:
            total_own[...] = total


def final_kernel(
    own, hidden, forcing, inverse_rms, gain, decode, total_own, from_partner, grad_hidden
):
    zero = jnp.zeros((LANES - VROWS, LANES), b16)
    grad_t = jnp.concatenate([own[:VROWS], zero], 0).astype(f32).T.astype(b16)
    grad_resid = nt(grad_t, decode[...])
    xfield = hidden[0].astype(f32) + forcing[...].astype(f32)
    inverse = inverse_rms[...]
    grad = gain[...] * (total_own[...] + from_partner[...].astype(f32))
    mean = jnp.mean(xfield * grad, -1, keepdims=True)
    result = grad_resid + inverse * grad - xfield * (inverse * inverse * inverse * mean)
    grad_hidden[0] = result.astype(b16)


def shifted(value, axis, steps):
    count = lax.axis_size(axis)
    pairs = [(source, (source + steps) % count) for source in range(count)]
    return lax.ppermute(value, axis, pairs)


def permute(value, moves):
    pairs = []
    for x in range(SIDE):
        for z in range(RING_Z):
            for y in range(RING_Y):
                for core in range(2):
                    dx, dz, dc = moves[core]
                    dz = -dz if dz == -2 and z % 2 == 0 else dz
                    dx = -dx if dx == -2 and x % 2 == 0 else dx
                    at = (x, z, core)
                    to = ((x + dx) % SIDE, (z + dz) % RING_Z, core ^ dc)
                    pairs.append(
                        tuple(
                            ((px * SIDE + pz % SIDE) * 2 + pc) * 2 * RING_Y + pz // SIDE * RING_Y + y
                            for px, pz, pc in (at, to)
                        )
                    )
    return lax.ppermute(value, ("ens", "node"), pairs)


def ring(value, along, before=()):
    out = [value]
    for hop in (1, -1, -2):
        if hop == -2 and before:
            value, *before = lax.optimization_barrier((value, *before))
        moves = [(hop, 0, 0) if axis == 0 else (0, hop, 0) for axis in along]
        out.append(permute(value, moves))
    return out + list(before)


def swapped(value):
    return permute(value, [(0, 0, 1)] * 2)


def everyone(value):
    value = value[None]
    for phase in range(2):
        groups = []
        for core in range(2):
            for fixed in range(SIDE):
                chips = [
                    step * SIDE + fixed if core == phase else fixed * SIDE + step
                    for step in range(SIDE)
                ]
                groups.append([2 * chip + core for chip in chips])
        spread = jnp.broadcast_to(value[None], (SIDE,) + value.shape)
        spread = spread.reshape((-1,) + value.shape[1:])
        value = lax.all_to_all(spread, "ens", 0, 0, tiled=True, axis_index_groups=groups)
    return value


def per_device(
    hidden, forcing, norm_gain, w_query, w_key, w_value, w_out, w_decode, targets, area_weight
):
    node_rows = hidden.shape[1]
    width = hidden.shape[2]
    head_size = width // HEADS
    span = node_rows + 2 * HALO
    scale = 1.0 / math.sqrt(head_size)
    members = lax.axis_size("ens")
    shards = lax.axis_size("node")
    rows = w_query.shape[0]
    variables = w_decode.shape[1]
    steps = width // STEP
    shape = jax.ShapeDtypeStruct

    def params(mebibytes):
        return pltpu.CompilerParams(vmem_limit_bytes=mebibytes * 1024 * 1024)

    def cost(us):
        return pl.CostEstimate(
            flops=us * 10**9, transcendentals=0, bytes_accessed=us * 3 * 10**6
        )
    decode = jnp.pad(w_decode, ((0, 0), (0, LANES - variables)))
    mixed = jnp.dot(w_out, decode, preferred_element_type=f32).astype(b16)
    position = lax.axis_index("ens")
    core = position % 2
    place = jnp.stack([position // (2 * SIDE), position // 2 % SIDE, core]).astype(jnp.int32)
    half = width // 2
    both = [
        jnp.concatenate([w[:, at : at + half] for w in (w_query, w_key, w_value)] + [mixed], 1)
        for at in (0, half)
    ]
    keep = jnp.where(core == 0, both[0], both[1])
    partner = swapped(jnp.where(core == 0, both[1], both[0]))
    block = jnp.where(
        core == 0,
        jnp.concatenate([keep, partner], 0),
        jnp.concatenate([partner, keep], 0),
    )
    row = ring(block, (0, 1))
    xfield = hidden[0].astype(f32) + forcing.astype(f32)
    inverse_rms = lax.rsqrt(jnp.mean(xfield * xfield, -1, keepdims=True) + EPS_NORM)
    normed = (xfield * inverse_rms * norm_gain).astype(b16)
    low = shifted(normed, "node", 1)
    high = shifted(normed, "node", -1)
    *pieces, low, high = ring(jnp.concatenate(row, 0), (1, 0), (low, high))
    field = jnp.concatenate([low, normed, high], 0)
    other_field = swapped(field)
    packed_width = 3 * half + LANES

    in_vmem = pl.BlockSpec(memory_space=pltpu.VMEM)
    in_hbm = pl.BlockSpec(memory_space=pltpu.HBM)

    def held(value):
        return pltpu.with_memory_space_constraint(value, pltpu.HBM)

    in_smem = pl.BlockSpec(memory_space=pltpu.SMEM)
    queries, keys, values, attended, lse, partial, mixed, full = pl.pallas_call(
        lambda *refs: forward_kernel(scale, *refs),
        in_specs=[in_smem] + [in_vmem] * (5 + len(pieces)),
        out_specs=[in_hbm, in_hbm, in_hbm, in_vmem, in_vmem, in_vmem, in_vmem, in_hbm],
        out_shape=[
            pltpu.HBM((2, span, half), b16),
            pltpu.HBM((2, span, half), b16),
            pltpu.HBM((2, span, half), b16),
            shape((2, node_rows, half), b16),
            shape((2, node_rows, half), f32),
            shape((2, VROWS, node_rows), f32),
            shape((half, LANES), b16),
            pltpu.HBM((width, packed_width), b16),
        ],
        scratch_shapes=[
            pltpu.VMEM((2, span, half), b16),
            pltpu.VMEM((2, span, half), b16),
            pltpu.VMEM((2, span, half), b16),
            pltpu.VMEM((width, packed_width), b16),
            pltpu.SemaphoreType.DMA((1 + 3 * steps,)),
        ],
        compiler_params=params(24),
        cost_estimate=cost(8),
        name="forward",
    )(place, field, other_field, hidden, forcing, decode, *pieces)
    preds = (partial + swapped(partial)[::-1]).astype(b16)

    others = everyone(preds[0])
    theirs = swapped(others)
    eps = (1.0 - ALPHA) / members
    coeff = (1.0 - eps) / (2.0 * (members - 1))
    truth = jnp.pad(targets, ((0, VROWS - variables), (0, 0)))
    payload = 2 * VROWS + 5 * HEADS
    gram, halo = pl.pallas_call(
        lambda *refs: loss_kernel(coeff, variables, *refs),
        in_specs=[in_smem] + [in_vmem] * 8,
        out_specs=[in_vmem] * 2,
        out_shape=[shape((width, LANES), b16), shape((payload, node_rows), b16)],
        compiler_params=params(12),
        cost_estimate=cost(3),
        name="crps",
    )(place, others, theirs, preds, truth, area_weight[None], attended, mixed, lse)

    halo_low = shifted(halo, "node", 1)
    halo_high = shifted(halo, "node", -1)
    parts = lax.all_to_all(gram.reshape(members, rows, LANES), "ens", 0, 0, tiled=True)
    spread = pl.pallas_call(
        lambda *refs: middle_kernel(variables, *refs),
        in_specs=[in_vmem],
        out_specs=in_vmem,
        out_shape=shape((shards, rows, LANES), b16),
        compiler_params=params(8),
        cost_estimate=cost(1),
        name="middle",
    )(parts)
    parts = lax.all_to_all(spread, "node", 0, 0, tiled=True)
    total = jnp.sum(parts.astype(f32), 0)
    grad_out_proj = lax.dot_general(
        total[:, :variables],
        w_decode.astype(f32),
        (((1,), (1,)), ((), ())),
        preferred_element_type=f32,
    )
    loss = jnp.sum(total[0, variables : variables + 3]) / (members * node_rows * shards * variables)

    total_own, total_other = pl.pallas_call(
        lambda *refs: backward_kernel(scale, *refs),
        in_specs=[in_vmem] * 4 + [in_hbm] * 5,
        out_specs=[in_vmem] * 2,
        out_shape=[shape((node_rows, width), f32), shape((node_rows, width), b16)],
        scratch_shapes=[
            pltpu.VMEM((2, span, half), b16),
            pltpu.VMEM((2, span, half), b16),
            pltpu.VMEM((2, span, half), b16),
            pltpu.VMEM((2, node_rows, half), f32),
            pltpu.VMEM((width, 3 * half), b16),
            pltpu.VMEM((2, span, LANES), b16),
            pltpu.VMEM((2, HEADS, 2 * HALO), f32),
            pltpu.SemaphoreType.DMA((4 + 3 * steps // 2,)),
        ],
        compiler_params=params(24),
        cost_estimate=cost(10),
        name="backward",
    )(halo_low, halo, halo_high, mixed, *[held(part) for part in (queries, keys, values, lse, full)])
    grad_hidden = pl.pallas_call(
        final_kernel,
        in_specs=[in_vmem] * 8,
        out_specs=in_vmem,
        out_shape=shape((1, node_rows, width), b16),
        compiler_params=params(12),
        cost_estimate=cost(2),
        name="final",
    )(
        halo, hidden, forcing, inverse_rms, norm_gain[None], decode, total_own,
        swapped(total_other),
    )
    return (grad_hidden, grad_out_proj, loss)


def solution(mesh):
    placed = (
        P("ens", "node", None),
        P("node", None),
        P(),
        P("ens", None),
        P("ens", None),
        P("ens", None),
        P("ens", None),
        P(),
        P(None, "node"),
        P("node"),
    )
    return jax.shard_map(
        per_device,
        mesh=mesh,
        in_specs=placed,
        out_specs=(P("ens", "node", None), P("ens", None), P()),
        check_vma=False,
    )
```

time: 147 us -> 157 us (1.068)
  waiting for transfers between devices: 7.76 us -> 21.5 us
  starting transfers between devices: 91.3 us -> 85.4 us
  blocking collectives: 16.3 us -> 18.6 us
  other arithmetic: 3.15 us -> 1.29 us
  local copies, waits for them, and re-layouts: 2.26 us -> 4.1 us
    all_to_all x1, waiting for transfers between devices: 2.65 us -> 10.2 us  [per_device(): parts = lax.all_to_all(spread, 'node', 0, 0, tiled=True)]
    ppermute x11, starting transfers between devices: 57.4 us -> 50.2 us  [permute(): return lax.ppermute(value, ('ens', 'node'), pairs)]
    ppermute x11, waiting for transfers between devices: 3.85 us -> 9.32 us  [permute(): return lax.ppermute(value, ('ens', 'node'), pairs)]
    all_to_all x2, blocking collectives: 16.3 us -> 18.6 us  [everyone(): lax.all_to_all(spread, 'ens', 0, 0, tiled=True, axis_index_groups=groups)]
    pallas_call x2 -> x4, Pallas kernels: 10.8 us -> 12.9 us  [the longest x1 7.91 us: per_device(): pl.pallas_call(lambda *refs: forward_kernel(scale, *refs), in_specs=[in_s...]
    slice x0 -> x2, local copies, waits for them, and re-layouts: none -> 1.67 us  [per_device(): w[:, at:at + half]]
    pallas_call x1, Pallas kernels: 10.2 us -> 8.51 us  [per_device(): pl.pallas_call(lambda *refs: backward_kernel(scale, *refs), in_specs=[in_...]
  transfers between devices with their start and end apart: 17 -> 17, of which waited for: 6 -> 8; matrix products, arithmetic and copies ran while one was open for 2% -> 1% of each run, Pallas kernels for 7% -> 7%
where the time goes in v7:
time: 157 us; the launch traced here: 156 us
  starting transfers between devices  85.4 us (54%)
  waiting for transfers between devices  21.5 us (14%)
  Pallas kernels  21.4 us (14%)
  blocking collectives  18.6 us (12%)
  local copies, waits for them, and re-layouts  4.1 us (3%)
  between operations  2.88 us (2%)
    ppermute x11, starting transfers between devices, permute(): return lax.ppermute(value, ('ens', 'node'), pairs)  50.2 us
    ppermute x4, starting transfers between devices, shifted(): return lax.ppermute(value, axis, pairs)  22.6 us
    all_to_all x2, blocking collectives, everyone(): lax.all_to_all(spread, 'ens', 0, 0, tiled=True, axis_index_groups=groups)  18.6 us
    all_to_all x1, waiting for transfers between devices, per_device(): parts = lax.all_to_all(spread, 'node', 0, 0, tiled=True)  10.2 us
    ppermute x11, waiting for transfers between devices, permute(): return lax.ppermute(value, ('ens', 'node'), pairs)  9.32 us
    pallas_call x1, Pallas kernels, per_device(): pl.pallas_call(lambda *refs: backward_kernel(scale, *refs), in_specs=[in_...  8.51 us
    all_to_all x1, starting transfers between devices, per_device(): parts = lax.all_to_all(spread, 'node', 0, 0, tiled=True)  8.19 us
    pallas_call x1, Pallas kernels, per_device(): pl.pallas_call(lambda *refs: forward_kernel(scale, *refs), in_specs=[in_s...  7.91 us
  transfers between devices with their start and end apart: 17, of which 8 were waited for; matrix products, arithmetic and copies ran while one was open for 1% of the time, Pallas kernels for 7%

profile of v7, /device:TPU:1, one launch (start us, length us, event | category | flops | bytes accessed | tf_op | source)
XLA Modules:
  0.0 156.1 jit_solution(16423941006537512373)
XLA Ops:
  3.8 8.8 %collective-permute-start = (bf16[32,1664]{1,0:T(8,128)(2,1)S(1)}, bf16[32,1664]{1,0:T(8,128)(2,1)S(1)}, u32[]{:S(2)}, u32[]{:S(2)}) collective-permute-start(bf16[32,1664]{1,0:T(8,128)(2,1)S(1)} %get-tuple-element.34), channel_id=1, source_target_pairs={{0,16},{16,0},{1,17},{17,1},{2,18},{18,2},{3,19},{19,3},{4,20},{20... | collective-permute-start | bytes 319496 | tf_op jit(solution)/shard_map/ppermute | solution.py:395
  13.5 1.9 %collective-permute-start.1 = (bf16[64,1664]{1,0:T(8,128)(2,1)S(1)}, bf16[64,1664]{1,0:T(8,128)(2,1)S(1)}, u32[]{:S(2)}, u32[]{:S(2)}) collective-permute-start(bf16[64,1664]{1,0:T(8,128)(2,1)S(1)} %maximum_select_fusion), channel_id=1, source_target_pairs={{0,128},{16,48},{1,129},{17,49},{2,130},{18,50},{3,131},{19,51},{4... | collective-permute-start | bytes 638984 | tf_op jit(solution)/shard_map/ppermute | solution.py:395
  15.5 5.3 %collective-permute-start.2 = (bf16[64,1664]{1,0:T(8,128)(2,1)S(1)}, bf16[64,1664]{1,0:T(8,128)(2,1)S(1)}, u32[]{:S(2)}, u32[]{:S(2)}) collective-permute-start(bf16[64,1664]{1,0:T(8,128)(2,1)S(1)} %maximum_select_fusion), channel_id=1, source_target_pairs={{0,384},{16,120},{1,385},{17,121},{2,386},{18,122},{3,387},{19,123... | collective-permute-start | bytes 638984 | tf_op jit(solution)/shard_map/ppermute | solution.py:395
  20.8 1.9 %collective-permute-start.3 = (bf16[64,1664]{1,0:T(8,128)(2,1)S(1)}, bf16[64,1664]{1,0:T(8,128)(2,1)S(1)}, u32[]{:S(2)}, u32[]{:S(2)}) collective-permute-start(bf16[64,1664]{1,0:T(8,128)(2,1)S(1)} %maximum_select_fusion), channel_id=1, source_target_pairs={{0,256},{16,80},{1,257},{17,81},{2,258},{18,82},{3,259},{19,83},{4... | collective-permute-start | bytes 638984 | tf_op jit(solution)/shard_map/ppermute | solution.py:395
  22.8 3.2 %collective-permute-start.4 = (bf16[128,1024]{1,0:T(8,128)(2,1)S(1)}, bf16[128,1024]{1,0:T(8,128)(2,1)S(1)}, u32[]{:S(2)}, u32[]{:S(2)}) collective-permute-start(bf16[128,1024]{1,0:T(8,128)(2,1)S(1)} %multiply_convert_fusion), channel_id=1, source_target_pairs={{0,1},{1,2},{2,3},{3,4},{4,5},{5,6},{6,7},{7,8},{8,9},{9,10},{10,1... | collective-permute-start | bytes 786440 | tf_op jit(solution)/shard_map/ppermute | solution.py:375
  26.0 8.1 %collective-permute-start.5 = (bf16[128,1024]{1,0:T(8,128)(2,1)S(1)}, bf16[128,1024]{1,0:T(8,128)(2,1)S(1)}, u32[]{:S(2)}, u32[]{:S(2)}) collective-permute-start(bf16[128,1024]{1,0:T(8,128)(2,1)S(1)} %multiply_convert_fusion), channel_id=1, source_target_pairs={{0,15},{1,0},{2,1},{3,2},{4,3},{5,4},{6,5},{7,6},{8,7},{9,8},{10,9... | collective-permute-start | bytes 786440 | tf_op jit(solution)/shard_map/ppermute | solution.py:375
  34.3 3.1 %collective-permute-start.7 = (bf16[256,1664]{1,0:T(8,128)(2,1)S(1)}, bf16[256,1664]{1,0:T(8,128)(2,1)S(1)}, u32[]{:S(2)}, u32[]{:S(2)}) collective-permute-start(bf16[256,1664]{1,0:T(8,128)(2,1)S(1)} %pad_maximum_fusion.refs_6_), channel_id=1, source_target_pairs={{0,32},{16,144},{1,33},{17,145},{2,34},{18,146},{3,35},{19,147},{4... | collective-permute-start | bytes 2555912 | tf_op jit(solution)/shard_map/ppermute | solution.py:395
  37.4 3.4 %collective-permute-start.8 = (bf16[256,1664]{1,0:T(8,128)(2,1)S(1)}, bf16[256,1664]{1,0:T(8,128)(2,1)}, u32[]{:S(2)}, u32[]{:S(2)}) collective-permute-start(bf16[256,1664]{1,0:T(8,128)(2,1)S(1)} %pad_maximum_fusion.refs_6_), channel_id=1, source_target_pairs={{0,104},{16,400},{1,105},{17,401},{2,106},{18,402},{3,107},{19,403... | collective-permute-start | bytes 2555912 | tf_op jit(solution)/shard_map/ppermute | solution.py:395
  42.3 4.5 %collective-permute-start.9 = (bf16[256,1664]{1,0:T(8,128)(2,1)S(1)}, bf16[256,1664]{1,0:T(8,128)(2,1)}, u32[]{:S(2)}, u32[]{:S(2)}) collective-permute-start(bf16[256,1664]{1,0:T(8,128)(2,1)S(1)} %pad_maximum_fusion.refs_6_), channel_id=1, source_target_pairs={{0,64},{16,272},{1,65},{17,273},{2,66},{18,274},{3,67},{19,275},{4... | collective-permute-start | bytes 2555912 | tf_op jit(solution)/shard_map/ppermute | solution.py:395
  46.8 5.2 %collective-permute-start.6 = (bf16[384,1024]{1,0:T(8,128)(2,1)S(1)}, bf16[384,1024]{1,0:T(8,128)(2,1)}, u32[]{:S(2)}, u32[]{:S(2)}) collective-permute-start(bf16[384,1024]{1,0:T(8,128)(2,1)S(1)} %pad_maximum_fusion.1.refs_1_), channel_id=1, source_target_pairs={{0,16},{16,0},{1,17},{17,1},{2,18},{18,2},{3,19},{19,3},{4,20},{20... | collective-permute-start | bytes 2359304 | tf_op jit(solution)/shard_map/ppermute | solution.py:395
  54.1 5.3 %collective-permute-done.9.refs_9_ = bf16[256,1664]{1,0:T(8,128)(2,1)} collective-permute-done((bf16[256,1664]{1,0:T(8,128)(2,1)S(1)}, bf16[256,1664]{1,0:T(8,128)(2,1)}, u32[]{:S(2)}, u32[]{:S(2)}) %collective-permute-start.9) | collective-permute-done | bytes 852000 | tf_op jit(solution)/shard_map/ppermute | solution.py:395
  59.4 7.9 %forward.1 = (bf16[2,384,512]{2,1,0:T(8,128)(2,1)}, bf16[2,384,512]{2,1,0:T(8,128)(2,1)}, bf16[2,384,512]{2,1,0:T(8,128)(2,1)}, bf16[2,128,512]{2,1,0:T(8,128)(2...) custom-call(s32[3]{0:T(128)S(1)} %pad_add_fusion.refs_0_, ...), custom_call_target="tpu_custom_call" | custom-call | flops 8000000000 | bytes 24000000 | tf_op jit(solution)/shard_map/forward/pallas_call | solution.py:486
  67.4 6.6 %collective-permute-start.10 = (f32[2,112,128]{2,1,0:T(8,128)S(1)}, f32[2,112,128]{2,1,0:T(8,128)S(1)}, u32[]{:S(2)}, u32[]{:S(2)}) collective-permute-start(f32[2,112,128]{2,1,0:T(8,128)S(1)} %get-tuple-element.21), channel_id=1, source_target_pairs={{0,16},{16,0},{1,17},{17,1},{2,18},{18,2},{3,19},{19,3},{4,20},{20... | collective-permute-start | bytes 344072 | tf_op jit(solution)/shard_map/ppermute | solution.py:395
  75.0 9.5 %all_to_all.20 = bf16[4,112,128]{2,1,0:T(8,128)(2,1)S(1)} all-to-all(bf16[4,112,128]{2,1,0:T(8,128)(2,1)S(1)} %reshape.43), channel_id=1, replica_groups={{0,128,256,384},{32,160,288,416},{64,192,320,448},{96,224,352,480},{16,..., dimensions={0} | all-to-all | bytes 229376 | tf_op jit(solution)/shard_map/all_to_all | solution.py:425
  84.5 9.1 %all_to_all.21.refs_1_ = bf16[16,112,128]{2,1,0:T(8,128)(2,1)S(1)} all-to-all(bf16[16,112,128]{2,1,0:T(8,128)(2,1)S(1)} %bitcast.21), channel_id=1, replica_groups={{0,32,64,96},{128,160,192,224},{256,288,320,352},{384,416,448,480},{16,..., dimensions={0} | all-to-all | bytes 917504 | tf_op jit(solution)/shard_map/all_to_all | solution.py:425
  93.6 7.0 %collective-permute-start.11 = (bf16[16,112,128]{2,1,0:T(8,128)(2,1)S(1)}, bf16[16,112,128]{2,1,0:T(8,128)(2,1)S(1)}, u32[]{:S(2)}, u32[]{:S(2)}) collective-permute-start(bf16[16,112,128]{2,1,0:T(8,128)(2,1)S(1)} %all_to_all.21.refs_1_), channel_id=1, source_target_pairs={{0,16},{16,0},{1,17},{17,1},{2,18},{18,2},{3,19},{19,3},{4,20},{20... | collective-permute-start | bytes 1376264 | tf_op jit(solution)/shard_map/ppermute | solution.py:395
  102.0 3.1 %crps.1 = (bf16[1024,128]{1,0:T(8,128)(2,1)}, bf16[304,128]{1,0:T(8,128)(2,1)S(1)}) custom-call(s32[3]{0:T(128)S(1)} %pad_add_fusion.refs_0_, bf16[16,112,128]{2,1,0:T(8,128)(2,1)S(1)} %all_to_all.21.refs_1_, bf16[16,112,128]{2,1,0:T(8,128)(2,1)S(1)} %collective-permute-done.11.refs_2_, bf16[2,112,128]{2,1,0:T(8,128)(2,1)S(1)} %add_convert_fusion.refs_3_, ...), custom_call_target="tpu_custom_call" | custom-call | flops 3000000000 | bytes 9000000 | tf_op jit(solution)/shard_map/crps/pallas_call | solution.py:519
  105.2 1.9 %collective-permute-start.12 = (bf16[304,128]{1,0:T(8,128)(2,1)S(1)}, bf16[304,128]{1,0:T(8,128)(2,1)S(1)}, u32[]{:S(2)}, u32[]{:S(2)}) collective-permute-start(bf16[304,128]{1,0:T(8,128)(2,1)S(1)} %get-tuple-element.25.refs_1_.own), channel_id=1, source_target_pairs={{0,1},{1,2},{2,3},{3,4},{4,5},{5,6},{6,7},{7,8},{8,9},{9,10},{10,1... | collective-permute-start | bytes 233480 | tf_op jit(solution)/shard_map/ppermute | solution.py:375
  107.1 9.4 %collective-permute-start.13 = (bf16[304,128]{1,0:T(8,128)(2,1)S(1)}, bf16[304,128]{1,0:T(8,128)(2,1)S(1)}, u32[]{:S(2)}, u32[]{:S(2)}) collective-permute-start(bf16[304,128]{1,0:T(8,128)(2,1)S(1)} %get-tuple-element.25.refs_1_.own), channel_id=1, source_target_pairs={{0,15},{1,0},{2,1},{3,2},{4,3},{5,4},{6,5},{7,6},{8,7},{9,8},{10,9... | collective-permute-start | bytes 233480 | tf_op jit(solution)/shard_map/ppermute | solution.py:375
  116.5 4.5 %all-to-all-start.2 = ((bf16[32,32,128]{2,1,0:T(8,128)(2,1)}), bf16[32,32,128]{2,1,0:T(8,128)(2,1)S(1)}, u32[]{:S(2)}, u32[]{:S(2)}) async-start(bf16[32,32,128]{2,1,0:T(8,128)(2,1)} %bitcast.10), calls=%async_computation.2 | async-start | bytes 524288 | tf_op jit(solution)/shard_map/all_to_all | solution.py:531
  121.0 8.5 %backward.1 = (f32[128,1024]{1,0:T(8,128)S(1)}, bf16[128,1024]{1,0:T(8,128)(2,1)S(1)}) custom-call(bf16[304,128]{1,0:T(8,128)(2,1)S(1)} %collective-permute-done.12.refs_0_, bf16[304,128]{1,0:T(8,128)(2,1)S(1)} %get-tuple-element.25.refs_1_.own, bf16[304,128]{1,0:T(8,128)(2,1)S(1)} %collective-permute-done.13.refs_2_, ...), custom_call_target="tpu_custom_call" | custom-call | flops 10000000000 | bytes 30000000 | tf_op jit(solution)/shard_map/backward/pallas_call | solution.py:551
  129.5 2.4 %collective-permute-start.14 = (bf16[128,1024]{1,0:T(8,128)(2,1)S(1)}, bf16[128,1024]{1,0:T(8,128)(2,1)S(1)}, u32[]{:S(2)}, u32[]{:S(2)}) collective-permute-start(bf16[128,1024]{1,0:T(8,128)(2,1)S(1)} %get-tuple-element.31), channel_id=1, source_target_pairs={{0,16},{16,0},{1,17},{17,1},{2,18},{18,2},{3,19},{19,3},{4,20},{20... | collective-permute-start | bytes 786440 | tf_op jit(solution)/shard_map/ppermute | solution.py:395
  133.1 8.2 %all-to-all-start.3 = ((bf16[16,32,128]{2,1,0:T(8,128)(2,1)}), bf16[16,32,128]{2,1,0:T(8,128)(2,1)S(1)}, u32[]{:S(2)}, u32[]{:S(2)}) async-start(bf16[16,32,128]{2,1,0:T(8,128)(2,1)} %middle.1), calls=%async_computation.3 | async-start | bytes 262144 | tf_op jit(solution)/shard_map/all_to_all | solution.py:541
  142.5 10.2 %all-to-all-done.3 = bf16[16,32,128]{2,1,0:T(8,128)(2,1)S(1)} async-done(((bf16[16,32,128]{2,1,0:T(8,128)(2,1)}), bf16[16,32,128]{2,1,0:T(8,128)(2,1)S(1)}, u32[]{:S(2)}, u32[]{:S(2)}) %all-to-all-start.3) | async-done | bytes 131104 | tf_op jit(solution)/shard_map/all_to_all | solution.py:541
  (57 shorter events, 14.1 us)
Async XLA Ops:
  0.6 11.9 %copy-start.2 = (bf16[1,128,1024]{2,1,0:T(8,128)(2,1)S(1)}, bf16[1,128,1024]{2,1,0:T(8,128)(2,1)}, u32[]{:S(2)}) copy-start(bf16[1,128,1024]{2,1,0:T(8,128)(2,1)} %hidden.1) | copy-start | bytes 786436
  0.7 11.9 %copy-start.1 = (bf16[128,1024]{1,0:T(8,128)(2,1)S(1)}, bf16[128,1024]{1,0:T(8,128)(2,1)}, u32[]{:S(2)}) copy-start(bf16[128,1024]{1,0:T(8,128)(2,1)} %forcing.1) | copy-start | bytes 786436
  0.7 22.0 %copy-start.3 = (f32[1024]{0:T(1024)S(1)}, f32[1024]{0:T(1024)}, u32[]{:S(2)}) copy-start(f32[1024]{0:T(1024)} %param.12) | copy-start | bytes 12292
  1.9 32.4 %copy-start.6 = (bf16[1024,100]{1,0:T(8,128)(2,1)}, bf16[1024,100]{1,0:T(8,128)(2,1)S(1)}, u32[]{:S(2)}) copy-start(bf16[1024,100]{1,0:T(8,128)(2,1)S(1)} %copy.15) | copy-start | bytes 614404
  3.8 9.7 %collective-permute-start = (bf16[32,1664]{1,0:T(8,128)(2,1)S(1)}, bf16[32,1664]{1,0:T(8,128)(2,1)S(1)}, u32[]{:S(2)}, u32[]{:S(2)}) collective-permute-start(bf16[32,1664]{1,0:T(8,128)(2,1)S(1)} %get-tuple-element.34), channel_id=1, source_target_pairs={{0,16},{16,0},{1,17},{17,1},{2,18},{18,2},{3,19},{19,3},{4,20},{20... | collective-permute-start | bytes 319496 | tf_op jit(solution)/shard_map/ppermute | solution.py:395
  13.5 20.6 %collective-permute-start.1 = (bf16[64,1664]{1,0:T(8,128)(2,1)S(1)}, bf16[64,1664]{1,0:T(8,128)(2,1)S(1)}, u32[]{:S(2)}, u32[]{:S(2)}) collective-permute-start(bf16[64,1664]{1,0:T(8,128)(2,1)S(1)} %maximum_select_fusion), channel_id=1, source_target_pairs={{0,128},{16,48},{1,129},{17,49},{2,130},{18,50},{3,131},{19,51},{4... | collective-permute-start | bytes 638984 | tf_op jit(solution)/shard_map/ppermute | solution.py:395
  15.5 18.7 %collective-permute-start.2 = (bf16[64,1664]{1,0:T(8,128)(2,1)S(1)}, bf16[64,1664]{1,0:T(8,128)(2,1)S(1)}, u32[]{:S(2)}, u32[]{:S(2)}) collective-permute-start(bf16[64,1664]{1,0:T(8,128)(2,1)S(1)} %maximum_select_fusion), channel_id=1, source_target_pairs={{0,384},{16,120},{1,385},{17,121},{2,386},{18,122},{3,387},{19,123... | collective-permute-start | bytes 638984 | tf_op jit(solution)/shard_map/ppermute | solution.py:395
  20.8 13.4 %collective-permute-start.3 = (bf16[64,1664]{1,0:T(8,128)(2,1)S(1)}, bf16[64,1664]{1,0:T(8,128)(2,1)S(1)}, u32[]{:S(2)}, u32[]{:S(2)}) collective-permute-start(bf16[64,1664]{1,0:T(8,128)(2,1)S(1)} %maximum_select_fusion), channel_id=1, source_target_pairs={{0,256},{16,80},{1,257},{17,81},{2,258},{18,82},{3,259},{19,83},{4... | collective-permute-start | bytes 638984 | tf_op jit(solution)/shard_map/ppermute | solution.py:395
  22.8 19.4 %collective-permute-start.4 = (bf16[128,1024]{1,0:T(8,128)(2,1)S(1)}, bf16[128,1024]{1,0:T(8,128)(2,1)S(1)}, u32[]{:S(2)}, u32[]{:S(2)}) collective-permute-start(bf16[128,1024]{1,0:T(8,128)(2,1)S(1)} %multiply_convert_fusion), channel_id=1, source_target_pairs={{0,1},{1,2},{2,3},{3,4},{4,5},{5,6},{6,7},{7,8},{8,9},{9,10},{10,1... | collective-permute-start | bytes 786440 | tf_op jit(solution)/shard_map/ppermute | solution.py:375
  26.0 16.2 %collective-permute-start.5 = (bf16[128,1024]{1,0:T(8,128)(2,1)S(1)}, bf16[128,1024]{1,0:T(8,128)(2,1)S(1)}, u32[]{:S(2)}, u32[]{:S(2)}) collective-permute-start(bf16[128,1024]{1,0:T(8,128)(2,1)S(1)} %multiply_convert_fusion), channel_id=1, source_target_pairs={{0,15},{1,0},{2,1},{3,2},{4,3},{5,4},{6,5},{7,6},{8,7},{9,8},{10,9... | collective-permute-start | bytes 786440 | tf_op jit(solution)/shard_map/ppermute | solution.py:375
  34.3 25.2 %collective-permute-start.7 = (bf16[256,1664]{1,0:T(8,128)(2,1)S(1)}, bf16[256,1664]{1,0:T(8,128)(2,1)S(1)}, u32[]{:S(2)}, u32[]{:S(2)}) collective-permute-start(bf16[256,1664]{1,0:T(8,128)(2,1)S(1)} %pad_maximum_fusion.refs_6_), channel_id=1, source_target_pairs={{0,32},{16,144},{1,33},{17,145},{2,34},{18,146},{3,35},{19,147},{4... | collective-permute-start | bytes 2555912 | tf_op jit(solution)/shard_map/ppermute | solution.py:395
  37.4 22.0 %collective-permute-start.8 = (bf16[256,1664]{1,0:T(8,128)(2,1)S(1)}, bf16[256,1664]{1,0:T(8,128)(2,1)}, u32[]{:S(2)}, u32[]{:S(2)}) collective-permute-start(bf16[256,1664]{1,0:T(8,128)(2,1)S(1)} %pad_maximum_fusion.refs_6_), channel_id=1, source_target_pairs={{0,104},{16,400},{1,105},{17,401},{2,106},{18,402},{3,107},{19,403... | collective-permute-start | bytes 2555912 | tf_op jit(solution)/shard_map/ppermute | solution.py:395
  42.3 17.2 %collective-permute-start.9 = (bf16[256,1664]{1,0:T(8,128)(2,1)S(1)}, bf16[256,1664]{1,0:T(8,128)(2,1)}, u32[]{:S(2)}, u32[]{:S(2)}) collective-permute-start(bf16[256,1664]{1,0:T(8,128)(2,1)S(1)} %pad_maximum_fusion.refs_6_), channel_id=1, source_target_pairs={{0,64},{16,272},{1,65},{17,273},{2,66},{18,274},{3,67},{19,275},{4... | collective-permute-start | bytes 2555912 | tf_op jit(solution)/shard_map/ppermute | solution.py:395
  46.8 7.3 %collective-permute-start.6 = (bf16[384,1024]{1,0:T(8,128)(2,1)S(1)}, bf16[384,1024]{1,0:T(8,128)(2,1)}, u32[]{:S(2)}, u32[]{:S(2)}) collective-permute-start(bf16[384,1024]{1,0:T(8,128)(2,1)S(1)} %pad_maximum_fusion.1.refs_1_), channel_id=1, source_target_pairs={{0,16},{16,0},{1,17},{17,1},{2,18},{18,2},{3,19},{19,3},{4,20},{20... | collective-permute-start | bytes 2359304 | tf_op jit(solution)/shard_map/ppermute | solution.py:395
  67.3 37.8 %copy-start.5 = (f32[2,128,512]{2,1,0:T(8,128)}, f32[2,128,512]{2,1,0:T(8,128)S(1)}, u32[]{:S(2)}) copy-start(f32[2,128,512]{2,1,0:T(8,128)S(1)} %get-tuple-element.24.refs_8_.refs_7_) | copy-start | bytes 1572868
  67.4 33.3 %copy-start.8 = (bf16[100,128]{1,0:T(8,128)(2,1)S(1)}, bf16[100,128]{1,0:T(8,128)(2,1)}, u32[]{:S(2)}) copy-start(bf16[100,128]{1,0:T(8,128)(2,1)} %param.18) | copy-start | bytes 76804
  67.4 34.7 %copy-start.4 = (f32[128]{0:T(128)S(1)}, f32[128]{0:T(128)}, u32[]{:S(2)}) copy-start(f32[128]{0:T(128)} %param.19) | copy-start | bytes 1540
  67.4 7.6 %collective-permute-start.10 = (f32[2,112,128]{2,1,0:T(8,128)S(1)}, f32[2,112,128]{2,1,0:T(8,128)S(1)}, u32[]{:S(2)}, u32[]{:S(2)}) collective-permute-start(f32[2,112,128]{2,1,0:T(8,128)S(1)} %get-tuple-element.21), channel_id=1, source_target_pairs={{0,16},{16,0},{1,17},{17,1},{2,18},{18,2},{3,19},{19,3},{4,20},{20... | collective-permute-start | bytes 344072 | tf_op jit(solution)/shard_map/ppermute | solution.py:395
  93.6 8.4 %collective-permute-start.11 = (bf16[16,112,128]{2,1,0:T(8,128)(2,1)S(1)}, bf16[16,112,128]{2,1,0:T(8,128)(2,1)S(1)}, u32[]{:S(2)}, u32[]{:S(2)}) collective-permute-start(bf16[16,112,128]{2,1,0:T(8,128)(2,1)S(1)} %all_to_all.21.refs_1_), channel_id=1, source_target_pairs={{0,16},{16,0},{1,17},{17,1},{2,18},{18,2},{3,19},{19,3},{4,20},{20... | collective-permute-start | bytes 1376264 | tf_op jit(solution)/shard_map/ppermute | solution.py:395
  105.2 15.8 %collective-permute-start.12 = (bf16[304,128]{1,0:T(8,128)(2,1)S(1)}, bf16[304,128]{1,0:T(8,128)(2,1)S(1)}, u32[]{:S(2)}, u32[]{:S(2)}) collective-permute-start(bf16[304,128]{1,0:T(8,128)(2,1)S(1)} %get-tuple-element.25.refs_1_.own), channel_id=1, source_target_pairs={{0,1},{1,2},{2,3},{3,4},{4,5},{5,6},{6,7},{7,8},{8,9},{9,10},{10,1... | collective-permute-start | bytes 233480 | tf_op jit(solution)/shard_map/ppermute | solution.py:375
  107.1 13.9 %collective-permute-start.13 = (bf16[304,128]{1,0:T(8,128)(2,1)S(1)}, bf16[304,128]{1,0:T(8,128)(2,1)S(1)}, u32[]{:S(2)}, u32[]{:S(2)}) collective-permute-start(bf16[304,128]{1,0:T(8,128)(2,1)S(1)} %get-tuple-element.25.refs_1_.own), channel_id=1, source_target_pairs={{0,15},{1,0},{2,1},{3,2},{4,3},{5,4},{6,5},{7,6},{8,7},{9,8},{10,9... | collective-permute-start | bytes 233480 | tf_op jit(solution)/shard_map/ppermute | solution.py:375
  116.5 15.9 %all-to-all-start.2 = ((bf16[32,32,128]{2,1,0:T(8,128)(2,1)}), bf16[32,32,128]{2,1,0:T(8,128)(2,1)S(1)}, u32[]{:S(2)}, u32[]{:S(2)}) async-start(bf16[32,32,128]{2,1,0:T(8,128)(2,1)} %bitcast.10), calls=%async_computation.2 | async-start | bytes 524288 | tf_op jit(solution)/shard_map/all_to_all | solution.py:531
  129.5 12.0 %collective-permute-start.14 = (bf16[128,1024]{1,0:T(8,128)(2,1)S(1)}, bf16[128,1024]{1,0:T(8,128)(2,1)S(1)}, u32[]{:S(2)}, u32[]{:S(2)}) collective-permute-start(bf16[128,1024]{1,0:T(8,128)(2,1)S(1)} %get-tuple-element.31), channel_id=1, source_target_pairs={{0,16},{16,0},{1,17},{17,1},{2,18},{18,2},{3,19},{19,3},{4,20},{20... | collective-permute-start | bytes 786440 | tf_op jit(solution)/shard_map/ppermute | solution.py:395
  133.1 19.6 %all-to-all-start.3 = ((bf16[16,32,128]{2,1,0:T(8,128)(2,1)}), bf16[16,32,128]{2,1,0:T(8,128)(2,1)S(1)}, u32[]{:S(2)}, u32[]{:S(2)}) async-start(bf16[16,32,128]{2,1,0:T(8,128)(2,1)} %middle.1), calls=%async_computation.3 | async-start | bytes 262144 | tf_op jit(solution)/shard_map/all_to_all | solution.py:541
  (2 other events, 14.3 us)

commit v8 on v7

--- a/solution.py
+++ b/solution.py
@@ -396,13 +396,13 @@
 
 
 def ring(value, along, before=()):
-    out = [value]
-    for hop in (1, -1, -2):
-        if hop == -2 and before:
+    blocks = {0: value}
+    for hop in (-2, 1, -1):
+        if hop == -1 and before:
             value, *before = lax.optimization_barrier((value, *before))
         moves = [(hop, 0, 0) if axis == 0 else (0, hop, 0) for axis in along]
-        out.append(permute(value, moves))
-    return out + list(before)
+        blocks[hop] = permute(value, moves)
+    return [blocks[0], blocks[1], blocks[-1], blocks[-2], *before]
 
 
 def swapped(value):
@@ -538,6 +538,7 @@
         cost_estimate=cost(1),
         name="middle",
     )(parts)
+    halo, spread = lax.optimization_barrier((halo, spread))
     parts = lax.all_to_all(spread, "node", 0, 0, tiled=True)
     total = jnp.sum(parts.astype(f32), 0)
     grad_out_proj = lax.dot_general(

time: 157 us -> 147 us (0.936)
  waiting for transfers between devices: 21.5 us -> 13.8 us
  starting transfers between devices: 85.4 us -> 83.8 us
    all_to_all x1, waiting for transfers between devices: 10.2 us -> 0.56 us  [per_device(): parts = lax.all_to_all(spread, 'node', 0, 0, tiled=True)]
    ppermute x11, waiting for transfers between devices: 9.32 us -> 12.4 us  [permute(): return lax.ppermute(value, ('ens', 'node'), pairs)]
  transfers between devices with their start and end apart: 17 -> 17, of which waited for: 8 -> 8; matrix products, arithmetic and copies ran while one was open for 1% -> 2% of each run, Pallas kernels for 7% -> 6%
where the time goes in v8:
time: 147 us; the launch traced here: 146 us
  starting transfers between devices  83.8 us (57%)
  Pallas kernels  21.4 us (15%)
  blocking collectives  17.7 us (12%)
  waiting for transfers between devices  13.8 us (9%)
  local copies, waits for them, and re-layouts  4.1 us (3%)
  between operations  2.88 us (2%)
    ppermute x11, starting transfers between devices, permute(): return lax.ppermute(value, ('ens', 'node'), pairs)  49.6 us
    ppermute x4, starting transfers between devices, shifted(): return lax.ppermute(value, axis, pairs)  22.6 us
    all_to_all x2, blocking collectives, everyone(): lax.all_to_all(spread, 'ens', 0, 0, tiled=True, axis_index_groups=groups)  17.7 us
    ppermute x11, waiting for transfers between devices, permute(): return lax.ppermute(value, ('ens', 'node'), pairs)  12.4 us
    pallas_call x1, Pallas kernels, per_device(): pl.pallas_call(lambda *refs: backward_kernel(scale, *refs), in_specs=[in_...  8.57 us
    pallas_call x1, Pallas kernels, per_device(): pl.pallas_call(lambda *refs: forward_kernel(scale, *refs), in_specs=[in_s...  7.9 us
    all_to_all x1, starting transfers between devices, per_device(): parts = lax.all_to_all(spread, 'node', 0, 0, tiled=True)  7.74 us
    all_to_all x1, starting transfers between devices, per_device(): lax.all_to_all(gram.reshape(members, rows, LANES), 'ens', 0, 0, tiled=True)  3.9 us
  transfers between devices with their start and end apart: 17, of which 8 were waited for; matrix products, arithmetic and copies ran while one was open for 2% of the time, Pallas kernels for 6%

profile of v8, /device:TPU:1, one launch (start us, length us, event | category | flops | bytes accessed | tf_op | source)
XLA Modules:
  0.0 146.0 jit_solution(104701911053438438)
XLA Ops:
  3.8 8.8 %collective-permute-start = (bf16[32,1664]{1,0:T(8,128)(2,1)S(1)}, bf16[32,1664]{1,0:T(8,128)(2,1)S(1)}, u32[]{:S(2)}, u32[]{:S(2)}) collective-permute-start(bf16[32,1664]{1,0:T(8,128)(2,1)S(1)} %get-tuple-element.38), channel_id=1, source_target_pairs={{0,16},{16,0},{1,17},{17,1},{2,18},{18,2},{3,19},{19,3},{4,20},{20... | collective-permute-start | bytes 319496 | tf_op jit(solution)/shard_map/ppermute | solution.py:395
  13.5 1.9 %collective-permute-start.1 = (bf16[64,1664]{1,0:T(8,128)(2,1)S(1)}, bf16[64,1664]{1,0:T(8,128)(2,1)S(1)}, u32[]{:S(2)}, u32[]{:S(2)}) collective-permute-start(bf16[64,1664]{1,0:T(8,128)(2,1)S(1)} %maximum_select_fusion), channel_id=1, source_target_pairs={{0,128},{16,48},{1,129},{17,49},{2,130},{18,50},{3,131},{19,51},{4... | collective-permute-start | bytes 638984 | tf_op jit(solution)/shard_map/ppermute | solution.py:395
  15.5 5.3 %collective-permute-start.2 = (bf16[64,1664]{1,0:T(8,128)(2,1)S(1)}, bf16[64,1664]{1,0:T(8,128)(2,1)S(1)}, u32[]{:S(2)}, u32[]{:S(2)}) collective-permute-start(bf16[64,1664]{1,0:T(8,128)(2,1)S(1)} %maximum_select_fusion), channel_id=1, source_target_pairs={{0,384},{16,120},{1,385},{17,121},{2,386},{18,122},{3,387},{19,123... | collective-permute-start | bytes 638984 | tf_op jit(solution)/shard_map/ppermute | solution.py:395
  20.8 1.9 %collective-permute-start.3 = (bf16[64,1664]{1,0:T(8,128)(2,1)S(1)}, bf16[64,1664]{1,0:T(8,128)(2,1)S(1)}, u32[]{:S(2)}, u32[]{:S(2)}) collective-permute-start(bf16[64,1664]{1,0:T(8,128)(2,1)S(1)} %maximum_select_fusion), channel_id=1, source_target_pairs={{0,256},{16,80},{1,257},{17,81},{2,258},{18,82},{3,259},{19,83},{4... | collective-permute-start | bytes 638984 | tf_op jit(solution)/shard_map/ppermute | solution.py:395
  22.8 3.2 %collective-permute-start.4 = (bf16[128,1024]{1,0:T(8,128)(2,1)S(1)}, bf16[128,1024]{1,0:T(8,128)(2,1)S(1)}, u32[]{:S(2)}, u32[]{:S(2)}) collective-permute-start(bf16[128,1024]{1,0:T(8,128)(2,1)S(1)} %multiply_convert_fusion), channel_id=1, source_target_pairs={{0,1},{1,2},{2,3},{3,4},{4,5},{5,6},{6,7},{7,8},{8,9},{9,10},{10,1... | collective-permute-start | bytes 786440 | tf_op jit(solution)/shard_map/ppermute | solution.py:375
  26.0 8.1 %collective-permute-start.5 = (bf16[128,1024]{1,0:T(8,128)(2,1)S(1)}, bf16[128,1024]{1,0:T(8,128)(2,1)S(1)}, u32[]{:S(2)}, u32[]{:S(2)}) collective-permute-start(bf16[128,1024]{1,0:T(8,128)(2,1)S(1)} %multiply_convert_fusion), channel_id=1, source_target_pairs={{0,15},{1,0},{2,1},{3,2},{4,3},{5,4},{6,5},{7,6},{8,7},{9,8},{10,9... | collective-permute-start | bytes 786440 | tf_op jit(solution)/shard_map/ppermute | solution.py:375
  34.3 3.1 %collective-permute-start.7 = (bf16[256,1664]{1,0:T(8,128)(2,1)S(1)}, bf16[256,1664]{1,0:T(8,128)(2,1)S(1)}, u32[]{:S(2)}, u32[]{:S(2)}) collective-permute-start(bf16[256,1664]{1,0:T(8,128)(2,1)S(1)} %pad_maximum_fusion.refs_6_), channel_id=1, source_target_pairs={{0,32},{16,144},{1,33},{17,145},{2,34},{18,146},{3,35},{19,147},{4... | collective-permute-start | bytes 2555912 | tf_op jit(solution)/shard_map/ppermute | solution.py:395
  37.4 4.4 %collective-permute-start.9 = (bf16[256,1664]{1,0:T(8,128)(2,1)S(1)}, bf16[256,1664]{1,0:T(8,128)(2,1)}, u32[]{:S(2)}, u32[]{:S(2)}) collective-permute-start(bf16[256,1664]{1,0:T(8,128)(2,1)S(1)} %pad_maximum_fusion.refs_6_), channel_id=1, source_target_pairs={{0,64},{16,272},{1,65},{17,273},{2,66},{18,274},{3,67},{19,275},{4... | collective-permute-start | bytes 2555912 | tf_op jit(solution)/shard_map/ppermute | solution.py:395
  42.3 5.9 %collective-permute-start.8 = (bf16[256,1664]{1,0:T(8,128)(2,1)S(1)}, bf16[256,1664]{1,0:T(8,128)(2,1)}, u32[]{:S(2)}, u32[]{:S(2)}) collective-permute-start(bf16[256,1664]{1,0:T(8,128)(2,1)S(1)} %pad_maximum_fusion.refs_6_), channel_id=1, source_target_pairs={{0,104},{16,400},{1,105},{17,401},{2,106},{18,402},{3,107},{19,403... | collective-permute-start | bytes 2555912 | tf_op jit(solution)/shard_map/ppermute | solution.py:395
  48.3 2.2 %collective-permute-start.6 = (bf16[384,1024]{1,0:T(8,128)(2,1)S(1)}, bf16[384,1024]{1,0:T(8,128)(2,1)}, u32[]{:S(2)}, u32[]{:S(2)}) collective-permute-start(bf16[384,1024]{1,0:T(8,128)(2,1)S(1)} %pad_maximum_fusion.1.refs_1_), channel_id=1, source_target_pairs={{0,16},{16,0},{1,17},{17,1},{2,18},{18,2},{3,19},{19,3},{4,20},{20... | collective-permute-start | bytes 2359304 | tf_op jit(solution)/shard_map/ppermute | solution.py:395
  52.6 8.4 %collective-permute-done.8.refs_8_ = bf16[256,1664]{1,0:T(8,128)(2,1)} collective-permute-done((bf16[256,1664]{1,0:T(8,128)(2,1)S(1)}, bf16[256,1664]{1,0:T(8,128)(2,1)}, u32[]{:S(2)}, u32[]{:S(2)}) %collective-permute-start.8) | collective-permute-done | bytes 852000 | tf_op jit(solution)/shard_map/ppermute | solution.py:395
  61.0 7.9 %forward.1 = (bf16[2,384,512]{2,1,0:T(8,128)(2,1)}, bf16[2,384,512]{2,1,0:T(8,128)(2,1)}, bf16[2,384,512]{2,1,0:T(8,128)(2,1)}, bf16[2,128,512]{2,1,0:T(8,128)(2...) custom-call(s32[3]{0:T(128)S(1)} %pad_add_fusion.refs_0_, ...), custom_call_target="tpu_custom_call" | custom-call | flops 8000000000 | bytes 24000000 | tf_op jit(solution)/shard_map/forward/pallas_call | solution.py:486
  68.9 6.8 %collective-permute-start.10 = (f32[2,112,128]{2,1,0:T(8,128)S(1)}, f32[2,112,128]{2,1,0:T(8,128)S(1)}, u32[]{:S(2)}, u32[]{:S(2)}) collective-permute-start(f32[2,112,128]{2,1,0:T(8,128)S(1)} %get-tuple-element.23), channel_id=1, source_target_pairs={{0,16},{16,0},{1,17},{17,1},{2,18},{18,2},{3,19},{19,3},{4,20},{20... | collective-permute-start | bytes 344072 | tf_op jit(solution)/shard_map/ppermute | solution.py:395
  76.7 8.7 %all_to_all.20 = bf16[4,112,128]{2,1,0:T(8,128)(2,1)S(1)} all-to-all(bf16[4,112,128]{2,1,0:T(8,128)(2,1)S(1)} %reshape.43), channel_id=1, replica_groups={{0,128,256,384},{32,160,288,416},{64,192,320,448},{96,224,352,480},{16,..., dimensions={0} | all-to-all | bytes 229376 | tf_op jit(solution)/shard_map/all_to_all | solution.py:425
  85.5 9.1 %all_to_all.21.refs_1_ = bf16[16,112,128]{2,1,0:T(8,128)(2,1)S(1)} all-to-all(bf16[16,112,128]{2,1,0:T(8,128)(2,1)S(1)} %bitcast.21), channel_id=1, replica_groups={{0,32,64,96},{128,160,192,224},{256,288,320,352},{384,416,448,480},{16,..., dimensions={0} | all-to-all | bytes 917504 | tf_op jit(solution)/shard_map/all_to_all | solution.py:425
  94.5 7.0 %collective-permute-start.11 = (bf16[16,112,128]{2,1,0:T(8,128)(2,1)S(1)}, bf16[16,112,128]{2,1,0:T(8,128)(2,1)S(1)}, u32[]{:S(2)}, u32[]{:S(2)}) collective-permute-start(bf16[16,112,128]{2,1,0:T(8,128)(2,1)S(1)} %all_to_all.21.refs_1_), channel_id=1, source_target_pairs={{0,16},{16,0},{1,17},{17,1},{2,18},{18,2},{3,19},{19,3},{4,20},{20... | collective-permute-start | bytes 1376264 | tf_op jit(solution)/shard_map/ppermute | solution.py:395
  101.5 1.4 collective-permute-done.11.refs_2_
  102.9 3.1 %crps.1 = (bf16[1024,128]{1,0:T(8,128)(2,1)}, bf16[304,128]{1,0:T(8,128)(2,1)S(1)}) custom-call(s32[3]{0:T(128)S(1)} %pad_add_fusion.refs_0_, bf16[16,112,128]{2,1,0:T(8,128)(2,1)S(1)} %all_to_all.21.refs_1_, bf16[16,112,128]{2,1,0:T(8,128)(2,1)S(1)} %collective-permute-done.11.refs_2_, bf16[2,112,128]{2,1,0:T(8,128)(2,1)S(1)} %add_convert_fusion.refs_3_, ...), custom_call_target="tpu_custom_call" | custom-call | flops 3000000000 | bytes 9000000 | tf_op jit(solution)/shard_map/crps/pallas_call | solution.py:519
  106.1 3.9 %all-to-all-start.2 = ((bf16[32,32,128]{2,1,0:T(8,128)(2,1)}), bf16[32,32,128]{2,1,0:T(8,128)(2,1)S(1)}, u32[]{:S(2)}, u32[]{:S(2)}) async-start(bf16[32,32,128]{2,1,0:T(8,128)(2,1)} %bitcast.8), calls=%async_computation.2 | async-start | bytes 524288 | tf_op jit(solution)/shard_map/all_to_all | solution.py:531
  110.1 1.9 %collective-permute-start.12 = (bf16[304,128]{1,0:T(8,128)(2,1)S(1)}, bf16[304,128]{1,0:T(8,128)(2,1)S(1)}, u32[]{:S(2)}, u32[]{:S(2)}) collective-permute-start(bf16[304,128]{1,0:T(8,128)(2,1)S(1)} %get-tuple-element.29.refs_1_.own), channel_id=1, source_target_pairs={{0,1},{1,2},{2,3},{3,4},{4,5},{5,6},{6,7},{7,8},{8,9},{9,10},{10,1... | collective-permute-start | bytes 233480 | tf_op jit(solution)/shard_map/ppermute | solution.py:375
  112.0 9.4 %collective-permute-start.13 = (bf16[304,128]{1,0:T(8,128)(2,1)S(1)}, bf16[304,128]{1,0:T(8,128)(2,1)S(1)}, u32[]{:S(2)}, u32[]{:S(2)}) collective-permute-start(bf16[304,128]{1,0:T(8,128)(2,1)S(1)} %get-tuple-element.29.refs_1_.own), channel_id=1, source_target_pairs={{0,15},{1,0},{2,1},{3,2},{4,3},{5,4},{6,5},{7,6},{8,7},{9,8},{10,9... | collective-permute-start | bytes 233480 | tf_op jit(solution)/shard_map/ppermute | solution.py:375
  122.4 7.7 %all-to-all-start.3 = ((bf16[16,32,128]{2,1,0:T(8,128)(2,1)}), bf16[16,32,128]{2,1,0:T(8,128)(2,1)S(1)}, u32[]{:S(2)}, u32[]{:S(2)}) async-start(bf16[16,32,128]{2,1,0:T(8,128)(2,1)} %middle.1), calls=%async_computation.3 | async-start | bytes 262144 | tf_op jit(solution)/shard_map/all_to_all | solution.py:542
  130.2 8.6 %backward.1 = (f32[128,1024]{1,0:T(8,128)S(1)}, bf16[128,1024]{1,0:T(8,128)(2,1)S(1)}) custom-call(bf16[304,128]{1,0:T(8,128)(2,1)S(1)} %collective-permute-done.12.refs_0_, bf16[304,128]{1,0:T(8,128)(2,1)S(1)} %get-tuple-element.29.refs_1_.own, bf16[304,128]{1,0:T(8,128)(2,1)S(1)} %collective-permute-done.13.refs_2_, ...), custom_call_target="tpu_custom_call" | custom-call | flops 10000000000 | bytes 30000000 | tf_op jit(solution)/shard_map/backward/pallas_call | solution.py:552
  138.8 2.2 %collective-permute-start.14 = (bf16[128,1024]{1,0:T(8,128)(2,1)S(1)}, bf16[128,1024]{1,0:T(8,128)(2,1)S(1)}, u32[]{:S(2)}, u32[]{:S(2)}) collective-permute-start(bf16[128,1024]{1,0:T(8,128)(2,1)S(1)} %get-tuple-element.35), channel_id=1, source_target_pairs={{0,16},{16,0},{1,17},{17,1},{2,18},{18,2},{3,19},{19,3},{4,20},{20... | collective-permute-start | bytes 786440 | tf_op jit(solution)/shard_map/ppermute | solution.py:395
  (57 shorter events, 12.2 us)
Async XLA Ops:
  0.6 11.9 %copy-start.2 = (bf16[1,128,1024]{2,1,0:T(8,128)(2,1)S(1)}, bf16[1,128,1024]{2,1,0:T(8,128)(2,1)}, u32[]{:S(2)}) copy-start(bf16[1,128,1024]{2,1,0:T(8,128)(2,1)} %hidden.1) | copy-start | bytes 786436
  0.7 22.0 %copy-start.3 = (f32[1024]{0:T(1024)S(1)}, f32[1024]{0:T(1024)}, u32[]{:S(2)}) copy-start(f32[1024]{0:T(1024)} %param.12) | copy-start | bytes 12292
  1.9 32.4 %copy-start.6 = (bf16[1024,100]{1,0:T(8,128)(2,1)}, bf16[1024,100]{1,0:T(8,128)(2,1)S(1)}, u32[]{:S(2)}) copy-start(bf16[1024,100]{1,0:T(8,128)(2,1)S(1)} %copy.15) | copy-start | bytes 614404
  3.8 9.7 %collective-permute-start = (bf16[32,1664]{1,0:T(8,128)(2,1)S(1)}, bf16[32,1664]{1,0:T(8,128)(2,1)S(1)}, u32[]{:S(2)}, u32[]{:S(2)}) collective-permute-start(bf16[32,1664]{1,0:T(8,128)(2,1)S(1)} %get-tuple-element.38), channel_id=1, source_target_pairs={{0,16},{16,0},{1,17},{17,1},{2,18},{18,2},{3,19},{19,3},{4,20},{20... | collective-permute-start | bytes 319496 | tf_op jit(solution)/shard_map/ppermute | solution.py:395
  13.5 20.6 %collective-permute-start.1 = (bf16[64,1664]{1,0:T(8,128)(2,1)S(1)}, bf16[64,1664]{1,0:T(8,128)(2,1)S(1)}, u32[]{:S(2)}, u32[]{:S(2)}) collective-permute-start(bf16[64,1664]{1,0:T(8,128)(2,1)S(1)} %maximum_select_fusion), channel_id=1, source_target_pairs={{0,128},{16,48},{1,129},{17,49},{2,130},{18,50},{3,131},{19,51},{4... | collective-permute-start | bytes 638984 | tf_op jit(solution)/shard_map/ppermute | solution.py:395
  15.5 18.7 %collective-permute-start.2 = (bf16[64,1664]{1,0:T(8,128)(2,1)S(1)}, bf16[64,1664]{1,0:T(8,128)(2,1)S(1)}, u32[]{:S(2)}, u32[]{:S(2)}) collective-permute-start(bf16[64,1664]{1,0:T(8,128)(2,1)S(1)} %maximum_select_fusion), channel_id=1, source_target_pairs={{0,384},{16,120},{1,385},{17,121},{2,386},{18,122},{3,387},{19,123... | collective-permute-start | bytes 638984 | tf_op jit(solution)/shard_map/ppermute | solution.py:395
  20.8 13.4 %collective-permute-start.3 = (bf16[64,1664]{1,0:T(8,128)(2,1)S(1)}, bf16[64,1664]{1,0:T(8,128)(2,1)S(1)}, u32[]{:S(2)}, u32[]{:S(2)}) collective-permute-start(bf16[64,1664]{1,0:T(8,128)(2,1)S(1)} %maximum_select_fusion), channel_id=1, source_target_pairs={{0,256},{16,80},{1,257},{17,81},{2,258},{18,82},{3,259},{19,83},{4... | collective-permute-start | bytes 638984 | tf_op jit(solution)/shard_map/ppermute | solution.py:395
  22.8 19.4 %collective-permute-start.4 = (bf16[128,1024]{1,0:T(8,128)(2,1)S(1)}, bf16[128,1024]{1,0:T(8,128)(2,1)S(1)}, u32[]{:S(2)}, u32[]{:S(2)}) collective-permute-start(bf16[128,1024]{1,0:T(8,128)(2,1)S(1)} %multiply_convert_fusion), channel_id=1, source_target_pairs={{0,1},{1,2},{2,3},{3,4},{4,5},{5,6},{6,7},{7,8},{8,9},{9,10},{10,1... | collective-permute-start | bytes 786440 | tf_op jit(solution)/shard_map/ppermute | solution.py:375
  26.0 16.2 %collective-permute-start.5 = (bf16[128,1024]{1,0:T(8,128)(2,1)S(1)}, bf16[128,1024]{1,0:T(8,128)(2,1)S(1)}, u32[]{:S(2)}, u32[]{:S(2)}) collective-permute-start(bf16[128,1024]{1,0:T(8,128)(2,1)S(1)} %multiply_convert_fusion), channel_id=1, source_target_pairs={{0,15},{1,0},{2,1},{3,2},{4,3},{5,4},{6,5},{7,6},{8,7},{9,8},{10,9... | collective-permute-start | bytes 786440 | tf_op jit(solution)/shard_map/ppermute | solution.py:375
  34.3 26.7 %collective-permute-start.7 = (bf16[256,1664]{1,0:T(8,128)(2,1)S(1)}, bf16[256,1664]{1,0:T(8,128)(2,1)S(1)}, u32[]{:S(2)}, u32[]{:S(2)}) collective-permute-start(bf16[256,1664]{1,0:T(8,128)(2,1)S(1)} %pad_maximum_fusion.refs_6_), channel_id=1, source_target_pairs={{0,32},{16,144},{1,33},{17,145},{2,34},{18,146},{3,35},{19,147},{4... | collective-permute-start | bytes 2555912 | tf_op jit(solution)/shard_map/ppermute | solution.py:395
  37.4 23.6 %collective-permute-start.9 = (bf16[256,1664]{1,0:T(8,128)(2,1)S(1)}, bf16[256,1664]{1,0:T(8,128)(2,1)}, u32[]{:S(2)}, u32[]{:S(2)}) collective-permute-start(bf16[256,1664]{1,0:T(8,128)(2,1)S(1)} %pad_maximum_fusion.refs_6_), channel_id=1, source_target_pairs={{0,64},{16,272},{1,65},{17,273},{2,66},{18,274},{3,67},{19,275},{4... | collective-permute-start | bytes 2555912 | tf_op jit(solution)/shard_map/ppermute | solution.py:395
  42.3 18.7 %collective-permute-start.8 = (bf16[256,1664]{1,0:T(8,128)(2,1)S(1)}, bf16[256,1664]{1,0:T(8,128)(2,1)}, u32[]{:S(2)}, u32[]{:S(2)}) collective-permute-start(bf16[256,1664]{1,0:T(8,128)(2,1)S(1)} %pad_maximum_fusion.refs_6_), channel_id=1, source_target_pairs={{0,104},{16,400},{1,105},{17,401},{2,106},{18,402},{3,107},{19,403... | collective-permute-start | bytes 2555912 | tf_op jit(solution)/shard_map/ppermute | solution.py:395
  48.3 4.3 %collective-permute-start.6 = (bf16[384,1024]{1,0:T(8,128)(2,1)S(1)}, bf16[384,1024]{1,0:T(8,128)(2,1)}, u32[]{:S(2)}, u32[]{:S(2)}) collective-permute-start(bf16[384,1024]{1,0:T(8,128)(2,1)S(1)} %pad_maximum_fusion.1.refs_1_), channel_id=1, source_target_pairs={{0,16},{16,0},{1,17},{17,1},{2,18},{18,2},{3,19},{19,3},{4,20},{20... | collective-permute-start | bytes 2359304 | tf_op jit(solution)/shard_map/ppermute | solution.py:395
  68.9 37.2 %copy-start.5 = (f32[2,128,512]{2,1,0:T(8,128)}, f32[2,128,512]{2,1,0:T(8,128)S(1)}, u32[]{:S(2)}) copy-start(f32[2,128,512]{2,1,0:T(8,128)S(1)} %get-tuple-element.26.refs_8_.refs_7_) | copy-start | bytes 1572868
  68.9 32.6 %copy-start.8 = (bf16[100,128]{1,0:T(8,128)(2,1)S(1)}, bf16[100,128]{1,0:T(8,128)(2,1)}, u32[]{:S(2)}) copy-start(bf16[100,128]{1,0:T(8,128)(2,1)} %param.18) | copy-start | bytes 76804
  68.9 34.0 %copy-start.4 = (f32[128]{0:T(128)S(1)}, f32[128]{0:T(128)}, u32[]{:S(2)}) copy-start(f32[128]{0:T(128)} %param.19) | copy-start | bytes 1540
  68.9 7.7 %collective-permute-start.10 = (f32[2,112,128]{2,1,0:T(8,128)S(1)}, f32[2,112,128]{2,1,0:T(8,128)S(1)}, u32[]{:S(2)}, u32[]{:S(2)}) collective-permute-start(f32[2,112,128]{2,1,0:T(8,128)S(1)} %get-tuple-element.23), channel_id=1, source_target_pairs={{0,16},{16,0},{1,17},{17,1},{2,18},{18,2},{3,19},{19,3},{4,20},{20... | collective-permute-start | bytes 344072 | tf_op jit(solution)/shard_map/ppermute | solution.py:395
  94.5 8.4 %collective-permute-start.11 = (bf16[16,112,128]{2,1,0:T(8,128)(2,1)S(1)}, bf16[16,112,128]{2,1,0:T(8,128)(2,1)S(1)}, u32[]{:S(2)}, u32[]{:S(2)}) collective-permute-start(bf16[16,112,128]{2,1,0:T(8,128)(2,1)S(1)} %all_to_all.21.refs_1_), channel_id=1, source_target_pairs={{0,16},{16,0},{1,17},{17,1},{2,18},{18,2},{3,19},{19,3},{4,20},{20... | collective-permute-start | bytes 1376264 | tf_op jit(solution)/shard_map/ppermute | solution.py:395
  106.1 15.6 %all-to-all-start.2 = ((bf16[32,32,128]{2,1,0:T(8,128)(2,1)}), bf16[32,32,128]{2,1,0:T(8,128)(2,1)S(1)}, u32[]{:S(2)}, u32[]{:S(2)}) async-start(bf16[32,32,128]{2,1,0:T(8,128)(2,1)} %bitcast.8), calls=%async_computation.2 | async-start | bytes 524288 | tf_op jit(solution)/shard_map/all_to_all | solution.py:531
  110.1 20.1 %collective-permute-start.12 = (bf16[304,128]{1,0:T(8,128)(2,1)S(1)}, bf16[304,128]{1,0:T(8,128)(2,1)S(1)}, u32[]{:S(2)}, u32[]{:S(2)}) collective-permute-start(bf16[304,128]{1,0:T(8,128)(2,1)S(1)} %get-tuple-element.29.refs_1_.own), channel_id=1, source_target_pairs={{0,1},{1,2},{2,3},{3,4},{4,5},{5,6},{6,7},{7,8},{8,9},{9,10},{10,1... | collective-permute-start | bytes 233480 | tf_op jit(solution)/shard_map/ppermute | solution.py:375
  112.0 18.2 %collective-permute-start.13 = (bf16[304,128]{1,0:T(8,128)(2,1)S(1)}, bf16[304,128]{1,0:T(8,128)(2,1)S(1)}, u32[]{:S(2)}, u32[]{:S(2)}) collective-permute-start(bf16[304,128]{1,0:T(8,128)(2,1)S(1)} %get-tuple-element.29.refs_1_.own), channel_id=1, source_target_pairs={{0,15},{1,0},{2,1},{3,2},{4,3},{5,4},{6,5},{7,6},{8,7},{9,8},{10,9... | collective-permute-start | bytes 233480 | tf_op jit(solution)/shard_map/ppermute | solution.py:375
  122.4 19.2 %all-to-all-start.3 = ((bf16[16,32,128]{2,1,0:T(8,128)(2,1)}), bf16[16,32,128]{2,1,0:T(8,128)(2,1)S(1)}, u32[]{:S(2)}, u32[]{:S(2)}) async-start(bf16[16,32,128]{2,1,0:T(8,128)(2,1)} %middle.1), calls=%async_computation.3 | async-start | bytes 262144 | tf_op jit(solution)/shard_map/all_to_all | solution.py:542
  130.2 12.8 %copy-start.7 = (bf16[1024,100]{0,1:T(8,128)(2,1)S(1)}, bf16[1024,100]{0,1:T(8,128)(2,1)}, u32[]{:S(2)}) copy-start(bf16[1024,100]{0,1:T(8,128)(2,1)} %param.17) | copy-start | bytes 614404
  138.8 5.0 %collective-permute-start.14 = (bf16[128,1024]{1,0:T(8,128)(2,1)S(1)}, bf16[128,1024]{1,0:T(8,128)(2,1)S(1)}, u32[]{:S(2)}, u32[]{:S(2)}) collective-permute-start(bf16[128,1024]{1,0:T(8,128)(2,1)S(1)} %get-tuple-element.35), channel_id=1, source_target_pairs={{0,16},{16,0},{1,17},{17,1},{2,18},{18,2},{3,19},{19,3},{4,20},{20... | collective-permute-start | bytes 786440 | tf_op jit(solution)/shard_map/ppermute | solution.py:395
  (2 other events, 14.9 us)

commit v9 on v6

--- a/solution.py
+++ b/solution.py
@@ -66,7 +66,7 @@
     return out
 
 
-def forward_kernel(scale, place, low, own, high, hidden, forcing, decode, *refs):
+def forward_kernel(scale, place, low, own, high, wrapped, hidden, forcing, decode_t, *refs):
     pieces, refs = refs[: 2 * len(HOPS)], refs[2 * len(HOPS) :]
     (
         queries_out, keys_out, values_out, attended, lse_out, pred, mixed, full,
@@ -90,10 +90,11 @@
     stores = [pltpu.make_async_copy(weights, full, store.at[0])]
     stores[0].start()
     mixed[...] = weights[:, 3 * width :]
-    normed[:HALO] = low[...]
+    at_y = place[3]
+    normed[:HALO] = jnp.where(at_y == 0, wrapped[...], low[...])
     normed[HALO : HALO + rows] = own[...]
-    normed[HALO + rows :] = high[...]
-    total = nn(hidden[0], decode[...]) + nn(forcing[...], decode[...])
+    normed[HALO + rows :] = jnp.where(at_y == RING_Y - 1, wrapped[...], high[...])
+    total = nt(hidden[0], decode_t[...]) + nt(forcing[...], decode_t[...])
     window = window_mask(rows, span)
     masks = head_masks(scale)
     lower = lax.broadcasted_iota(jnp.int32, (rows, LANES), 1) < LANES // 2
@@ -200,8 +201,34 @@
         at += HEADS
 
 
+def middle_kernel(variables, parts, spread):
+    total = parts[0].astype(f32)
+    for index in range(1, parts.shape[0]):
+        total = total + parts[index].astype(f32)
+    column = lax.broadcasted_iota(jnp.int32, total.shape, 1)
+    spare = (column >= variables) & (column < variables + 3)
+    loss = jnp.sum(jnp.where(spare, total, 0.0), 1, keepdims=True)
+    for index, piece in enumerate(split_bf16(loss, 3)):
+        total = jnp.where(column == variables + index, piece.astype(f32), total)
+    total = total.astype(b16)
+    for index in range(spread.shape[0]):
+        spread[index] = total
+
+
+def last_kernel(variables, factor, parts, decode_t, grad_out, loss):
+    total = parts[0].astype(f32)
+    for index in range(1, parts.shape[0]):
+        total = total + parts[index].astype(f32)
+    column = lax.broadcasted_iota(jnp.int32, total.shape, 1)
+    spare = (column >= variables) & (column < variables + 3)
+    first = jnp.sum(jnp.where(spare, total, 0.0), 1, keepdims=True)[:1]
+    loss[...] = jnp.broadcast_to(first * factor, loss.shape)
+    real = jnp.where(column < variables, total, 0.0)
+    grad_out[...] = sum(nn(piece, decode_t[...]) for piece in split_bf16(real, 2))
+
+
 def backward_kernel(
-    scale, low, own, high, hidden, forcing, inverse_rms, gain, decode, mixed,
+    scale, place, low_part, own, high_part, wrapped, hidden, forcing, inverse_rms, gain, decode_t, mixed,
     queries_in, keys_in, values_in, lse_in, full,
     grad_hidden, queries, keys, values, lse, weights, grad_t, stats, load,
 ):
@@ -222,8 +249,11 @@
             cols = slice(index * width + at, index * width + at + STEP)
             fetch(full.at[:, cols], weights.at[:, cols])
 
+    at_y = place[3]
+    low = jnp.where(at_y == 0, wrapped[...], low_part[...])
+    high = jnp.where(at_y == RING_Y - 1, wrapped[...], high_part[...])
     zero = jnp.zeros((LANES - VROWS, LANES), b16)
-    for side, part in enumerate((own, low, high)):
+    for side, part in enumerate((own[...], low, high)):
         grad = jnp.concatenate([part[:VROWS], zero], 0)
         grad_t[side * rows : (side + 1) * rows] = grad.astype(f32).T.astype(b16)
     for side, part in enumerate((low, high)):
@@ -231,7 +261,7 @@
         pieces = [part[VROWS + HEADS * n : VROWS + HEADS * (n + 1)].astype(f32) for n in range(5)]
         stats[0, :, at] = pieces[0] + pieces[1]
         stats[1, :, at] = pieces[2] + pieces[3] + pieces[4]
-    grad_resid = nt(grad_t[:rows], decode[...])
+    grad_resid = nn(grad_t[:rows], decode_t[...])
 
     window = window_mask(rows, span)
     key_at = lax.broadcasted_iota(jnp.int32, (rows, 2 * HALO), 0)
@@ -313,10 +343,13 @@
     grad_hidden[0] = result.astype(b16)
 
 
-def shifted(value, axis, steps):
-    count = lax.axis_size(axis)
-    pairs = [(source, (source + steps) % count) for source in range(count)]
-    return lax.ppermute(value, axis, pairs)
+def halos(value):
+    up = [(n, n + 1) for n in range(2 * RING_Y) if n % RING_Y < RING_Y - 1]
+    turn = [(RING_Y - 1, RING_Y), (2 * RING_Y - 1, 0)]
+    low = lax.ppermute(value, "node", up)
+    high = lax.ppermute(value, "node", [(b, a) for a, b in up])
+    wrapped = lax.ppermute(value, "node", turn + [(b, a) for a, b in turn])
+    return low, high, wrapped
 
 
 def permute(value, moves):
@@ -355,15 +388,9 @@
 
 def everyone(value):
     value = value[None]
-    for phase in range(2):
-        groups = []
-        for core in range(2):
-            for fixed in range(SIDE):
-                chips = [
-                    step * SIDE + fixed if core == phase else fixed * SIDE + step
-                    for step in range(SIDE)
-                ]
-                groups.append([2 * chip + core for chip in chips])
+    chips = [[x * SIDE + z for z in range(SIDE)] for x in range(SIDE)]
+    for lines in (chips, list(zip(*chips, strict=True))):
+        groups = [[2 * chip + core for chip in line] for core in range(2) for line in lines]
         spread = jnp.broadcast_to(value[None], (SIDE,) + value.shape)
         spread = spread.reshape((-1,) + value.shape[1:])
         value = lax.all_to_all(spread, "ens", 0, 0, tiled=True, axis_index_groups=groups)
@@ -392,21 +419,24 @@
         return pl.CostEstimate(
             flops=us * 10**9, transcendentals=0, bytes_accessed=us * 3 * 10**6
         )
-    decode = jnp.pad(w_decode, ((0, 0), (0, LANES - variables)))
-    mixed = jnp.dot(w_out, decode, preferred_element_type=f32).astype(b16)
+    decode_t = jnp.pad(w_decode.T, ((0, LANES - variables), (0, 0)))
+    mixed = nt(w_out, decode_t).astype(b16)
     position = lax.axis_index("ens")
     core = position % 2
-    place = jnp.stack([position // (2 * SIDE), position // 2 % SIDE, core]).astype(jnp.int32)
-    row = ring(jnp.concatenate([w_query, w_key, w_value, mixed], 1), (0, 1))
+    at_y = lax.axis_index("node") % RING_Y
+    place = jnp.stack([position // (2 * SIDE), position // 2 % SIDE, core, at_y])
+    place = place.astype(jnp.int32)
+    packed = jnp.concatenate([w_query, w_key, w_value, mixed], 1)
     xfield = hidden[0].astype(f32) + forcing.astype(f32)
     inverse_rms = lax.rsqrt(jnp.mean(xfield * xfield, -1, keepdims=True) + EPS_NORM)
     normed = (xfield * inverse_rms * norm_gain).astype(b16)
-    low = shifted(normed, "node", 1)
-    high = shifted(normed, "node", -1)
-    *mine, low, high = ring(jnp.concatenate(row, 0), (1, 0), (low, high))
+    low, high, wrapped = halos(normed)
+    row = ring(packed, (0, 1))
+    *mine, low, high, wrapped = ring(jnp.concatenate(row, 0), (1, 0), (low, high, wrapped))
     pieces = mine + [swapped(piece) for piece in mine]
 
     packed_width = 3 * width + LANES
+    in_smem = pl.BlockSpec(memory_space=pltpu.SMEM)
     in_vmem = pl.BlockSpec(memory_space=pltpu.VMEM)
     in_hbm = pl.BlockSpec(memory_space=pltpu.HBM)
 
@@ -415,7 +445,7 @@
 
     queries, keys, values, attended, lse, pred, mixed, full = pl.pallas_call(
         lambda *refs: forward_kernel(scale, *refs),
-        in_specs=[pl.BlockSpec(memory_space=pltpu.SMEM)] + [in_vmem] * (6 + len(pieces)),
+        in_specs=[in_smem] + [in_vmem] * (7 + len(pieces)),
         out_specs=[in_hbm, in_hbm, in_hbm, in_vmem, in_hbm, in_vmem, in_vmem, in_hbm],
         out_shape=[
             pltpu.HBM((span, width), b16),
@@ -439,7 +469,7 @@
         compiler_params=params(24),
         cost_estimate=cost(9),
         name="forward",
-    )(place, low, normed, high, hidden, forcing, decode, *pieces)
+    )(place, low, normed, high, wrapped, hidden, forcing, decode_t, *pieces)
 
     others = everyone(pred)
     theirs = swapped(others)
@@ -473,25 +503,33 @@
         name="crps",
     )(others, theirs, pred, truth, area_weight[None], attended, mixed, lse)
 
-    halo_low = shifted(halo, "node", 1)
-    halo_high = shifted(halo, "node", -1)
+    halo_low, halo_high, halo_wrapped = halos(halo)
     parts = lax.all_to_all(gram.reshape(members, rows, LANES), "ens", 0, 0, tiled=True)
-    part = jnp.sum(parts.astype(f32), 0)
-    parts = lax.all_to_all(
-        jnp.broadcast_to(part[None], (shards,) + part.shape), "node", 0, 0, tiled=True
-    )
-    total = jnp.sum(parts, 0)
-    grad_out_proj = lax.dot_general(
-        total[:, :variables],
-        w_decode.astype(f32),
-        (((1,), (1,)), ((), ())),
-        preferred_element_type=f32,
-    )
-    loss = jnp.sum(total[0, variables : variables + 3]) / (members * node_rows * shards * variables)
+    spread = pl.pallas_call(
+        lambda *refs: middle_kernel(variables, *refs),
+        in_specs=[in_vmem],
+        out_specs=in_vmem,
+        out_shape=shape((shards, rows, LANES), b16),
+        compiler_params=params(8),
+        cost_estimate=cost(1),
+        name="middle",
+    )(parts)
+    halo, spread = lax.optimization_barrier((halo, spread))
+    parts = lax.all_to_all(spread, "node", 0, 0, tiled=True)
+    factor = 1.0 / (members * node_rows * shards * variables)
+    grad_out_proj, loss = pl.pallas_call(
+        lambda *refs: last_kernel(variables, factor, *refs),
+        in_specs=[in_vmem] * 2,
+        out_specs=[in_vmem] * 2,
+        out_shape=[shape((rows, width), f32), shape((1, LANES), f32)],
+        compiler_params=params(8),
+        cost_estimate=cost(1),
+        name="last",
+    )(parts, decode_t)
 
     grad_hidden = pl.pallas_call(
         lambda *refs: backward_kernel(scale, *refs),
-        in_specs=[in_vmem] * 9 + [in_hbm] * 5,
+        in_specs=[in_smem] + [in_vmem] * 10 + [in_hbm] * 5,
         out_specs=in_vmem,
         out_shape=shape((1, node_rows, width), b16),
         scratch_shapes=[
@@ -508,10 +546,11 @@
         cost_estimate=cost(12),
         name="backward",
     )(
-        halo_low, halo, halo_high, hidden, forcing, inverse_rms, norm_gain[None], decode, mixed,
+        place, halo_low, halo, halo_high, halo_wrapped, hidden, forcing, inverse_rms,
+        norm_gain[None], decode_t, mixed,
         *[held(part) for part in (queries, keys, values, lse, full)],
     )
-    return (grad_hidden, grad_out_proj, loss)
+    return (grad_hidden, grad_out_proj, loss[0, 0])
 
 
 def solution(mesh):

time: 147 us -> 146 us (level)
  waiting for transfers between devices: 7.76 us -> 3.27 us
  blocking collectives: 16.3 us -> 18.5 us
  Pallas kernels: 21 us -> 23.1 us
  between operations: 2.9 us -> 1.17 us
    all_to_all x1, starting transfers between devices: 7.47 us -> 5.18 us  [per_device(): parts = lax.all_to_all(spread, 'node', 0, 0, tiled=True)]
    ppermute x4 -> x6, starting transfers between devices: 22.6 us -> 24.9 us  [the longest x2 17.7 us: halos(): wrapped = lax.ppermute(value, 'node', turn + [(b, a) for a, b in turn])]
    all_to_all x2, blocking collectives: 16.3 us -> 18.5 us  [everyone(): lax.all_to_all(spread, 'ens', 0, 0, tiled=True, axis_index_groups=groups)]
    all_to_all x1, waiting for transfers between devices: 2.65 us -> 0.68 us  [per_device(): parts = lax.all_to_all(spread, 'node', 0, 0, tiled=True)]
    pallas_call x1 -> x3, Pallas kernels: 8.84 us -> 10.5 us  [the longest x1 8.79 us: per_device(): pl.pallas_call(lambda *refs: forward_kernel(scale, *refs), in_specs=[in_s...]
  transfers between devices with their start and end apart: 17 -> 19, of which waited for: 6 -> 3; matrix products, arithmetic and copies ran while one was open for 2% -> 2% of each run, Pallas kernels for 7% -> 8%
where the time goes in v9:
time: 146 us; the launch traced here: 145 us
  starting transfers between devices  92.3 us (63%)
  Pallas kernels  23.1 us (16%)
  blocking collectives  18.5 us (13%)
  other arithmetic  3.5 us (2%)
  waiting for transfers between devices  3.27 us (2%)
  local copies, waits for them, and re-layouts  2.01 us (1%)
    ppermute x11, starting transfers between devices, permute(): return lax.ppermute(value, ('ens', 'node'), pairs)  57.7 us
    all_to_all x2, blocking collectives, everyone(): lax.all_to_all(spread, 'ens', 0, 0, tiled=True, axis_index_groups=groups)  18.5 us
    ppermute x2, starting transfers between devices, halos(): wrapped = lax.ppermute(value, 'node', turn + [(b, a) for a, b in turn])  17.7 us
    pallas_call x1, Pallas kernels, per_device(): pl.pallas_call(lambda *refs: backward_kernel(scale, *refs), in_specs=[in_...  10.7 us
    pallas_call x1, Pallas kernels, per_device(): pl.pallas_call(lambda *refs: forward_kernel(scale, *refs), in_specs=[in_s...  8.79 us
    all_to_all x1, starting transfers between devices, per_device(): parts = lax.all_to_all(spread, 'node', 0, 0, tiled=True)  5.18 us
    ppermute x2, starting transfers between devices, halos(): low = lax.ppermute(value, 'node', up)  4.64 us
    all_to_all x1, starting transfers between devices, per_device(): lax.all_to_all(gram.reshape(members, rows, LANES), 'ens', 0, 0, tiled=True)  4.59 us
  transfers between devices with their start and end apart: 19, of which 3 were waited for; matrix products, arithmetic and copies ran while one was open for 2% of the time, Pallas kernels for 8%

profile of v9, /device:TPU:1, one launch (start us, length us, event | category | flops | bytes accessed | tf_op | source)
XLA Modules:
  0.0 145.0 jit_solution(16333150346386254395)
XLA Ops:
  3.5 4.8 %collective-permute-start = (bf16[32,3200]{1,0:T(8,128)(2,1)S(1)}, bf16[32,3200]{1,0:T(8,128)(2,1)S(1)}, u32[]{:S(2)}, u32[]{:S(2)}) collective-permute-start(bf16[32,3200]{1,0:T(8,128)(2,1)S(1)} %pad_maximum_fusion.1), channel_id=1, source_target_pairs={{0,128},{16,48},{1,129},{17,49},{2,130},{18,50},{3,131},{19,51},{4... | collective-permute-start | bytes 614408 | tf_op jit(solution)/shard_map/ppermute | solution.py:372
  8.4 8.6 %collective-permute-start.1 = (bf16[32,3200]{1,0:T(8,128)(2,1)S(1)}, bf16[32,3200]{1,0:T(8,128)(2,1)S(1)}, u32[]{:S(2)}, u32[]{:S(2)}) collective-permute-start(bf16[32,3200]{1,0:T(8,128)(2,1)S(1)} %pad_maximum_fusion.1), channel_id=1, source_target_pairs={{0,384},{16,120},{1,385},{17,121},{2,386},{18,122},{3,387},{19,123... | collective-permute-start | bytes 614408 | tf_op jit(solution)/shard_map/ppermute | solution.py:372
  17.0 1.9 %collective-permute-start.2 = (bf16[32,3200]{1,0:T(8,128)(2,1)S(1)}, bf16[32,3200]{1,0:T(8,128)(2,1)S(1)}, u32[]{:S(2)}, u32[]{:S(2)}) collective-permute-start(bf16[32,3200]{1,0:T(8,128)(2,1)S(1)} %pad_maximum_fusion.1), channel_id=1, source_target_pairs={{0,256},{16,80},{1,257},{17,81},{2,258},{18,82},{3,259},{19,83},{4... | collective-permute-start | bytes 614408 | tf_op jit(solution)/shard_map/ppermute | solution.py:372
  21.3 3.2 %collective-permute-start.3 = (bf16[128,1024]{1,0:T(8,128)(2,1)S(1)}, bf16[128,1024]{1,0:T(8,128)(2,1)S(1)}, u32[]{:S(2)}, u32[]{:S(2)}) collective-permute-start(bf16[128,1024]{1,0:T(8,128)(2,1)S(1)} %multiply_convert_fusion.refs_2_), channel_id=1, source_target_pairs={{0,1},{1,2},{2,3},{3,4},{4,5},{5,6},{6,7},{8,9},{9,10},{10,11},{11... | collective-permute-start | bytes 786440 | tf_op jit(solution)/shard_map/ppermute | solution.py:349
  24.5 1.3 collective-permute-start.4
  25.9 9.1 %collective-permute-start.5 = (bf16[128,1024]{1,0:T(8,128)(2,1)S(1)}, bf16[128,1024]{1,0:T(8,128)(2,1)S(1)}, u32[]{:S(2)}, u32[]{:S(2)}) collective-permute-start(bf16[128,1024]{1,0:T(8,128)(2,1)S(1)} %multiply_convert_fusion.refs_2_), channel_id=1, source_target_pairs={{7,8},{15,0},{8,7},{0,15},{23,24},{31,16},{24,23},{16,31},{39,40},... | collective-permute-start | bytes 786440 | tf_op jit(solution)/shard_map/ppermute | solution.py:351
  35.1 3.1 %collective-permute-start.6 = (bf16[128,3200]{1,0:T(8,128)(2,1)S(1)}, bf16[128,3200]{1,0:T(8,128)(2,1)S(1)}, u32[]{:S(2)}, u32[]{:S(2)}) collective-permute-start(bf16[128,3200]{1,0:T(8,128)(2,1)S(1)} %pad_maximum_fusion.refs_8_), channel_id=1, source_target_pairs={{0,32},{16,144},{1,33},{17,145},{2,34},{18,146},{3,35},{19,147},{4... | collective-permute-start | bytes 2457608 | tf_op jit(solution)/shard_map/ppermute | solution.py:372
  38.2 3.4 %collective-permute-start.7 = (bf16[128,3200]{1,0:T(8,128)(2,1)S(1)}, bf16[128,3200]{1,0:T(8,128)(2,1)}, u32[]{:S(2)}, u32[]{:S(2)}) collective-permute-start(bf16[128,3200]{1,0:T(8,128)(2,1)S(1)} %pad_maximum_fusion.refs_8_), channel_id=1, source_target_pairs={{0,104},{16,400},{1,105},{17,401},{2,106},{18,402},{3,107},{19,403... | collective-permute-start | bytes 2457608 | tf_op jit(solution)/shard_map/ppermute | solution.py:372
  41.6 7.6 %collective-permute-start.8 = (bf16[128,3200]{1,0:T(8,128)(2,1)S(1)}, bf16[128,3200]{1,0:T(8,128)(2,1)}, u32[]{:S(2)}, u32[]{:S(2)}) collective-permute-start(bf16[128,3200]{1,0:T(8,128)(2,1)S(1)} %pad_maximum_fusion.refs_8_), channel_id=1, source_target_pairs={{0,64},{16,272},{1,65},{17,273},{2,66},{18,274},{3,67},{19,275},{4... | collective-permute-start | bytes 2457608 | tf_op jit(solution)/shard_map/ppermute | solution.py:372
  49.2 5.6 %collective-permute-start.9 = (bf16[128,3200]{1,0:T(8,128)(2,1)S(1)}, bf16[128,3200]{1,0:T(8,128)(2,1)}, u32[]{:S(2)}, u32[]{:S(2)}) collective-permute-start(bf16[128,3200]{1,0:T(8,128)(2,1)S(1)} %pad_maximum_fusion.refs_8_), channel_id=1, source_target_pairs={{0,16},{16,0},{1,17},{17,1},{2,18},{18,2},{3,19},{19,3},{4,20},{20... | collective-permute-start | bytes 2457608 | tf_op jit(solution)/shard_map/ppermute | solution.py:372
  54.9 13.0 %collective-permute-start.10 = (bf16[128,3200]{1,0:T(8,128)(2,1)S(1)}, bf16[128,3200]{1,0:T(8,128)(2,1)}, u32[]{:S(2)}, u32[]{:S(2)}) collective-permute-start(bf16[128,3200]{1,0:T(8,128)(2,1)S(1)} %collective-permute-done.6.refs_9_), channel_id=1, source_target_pairs={{0,16},{16,0},{1,17},{17,1},{2,18},{18,2},{3,19},{19,3},{4,20},{20... | collective-permute-start | bytes 2457608 | tf_op jit(solution)/shard_map/ppermute | solution.py:372
  67.9 1.9 %collective-permute-start.11 = (bf16[128,3200]{1,0:T(8,128)(2,1)}, bf16[128,3200]{1,0:T(8,128)(2,1)}, u32[]{:S(2)}, u32[]{:S(2)}) collective-permute-start(bf16[128,3200]{1,0:T(8,128)(2,1)} %collective-permute-done.7.refs_10_), channel_id=1, source_target_pairs={{0,16},{16,0},{1,17},{17,1},{2,18},{18,2},{3,19},{19,3},{4,20},{20... | collective-permute-start | bytes 2457608 | tf_op jit(solution)/shard_map/ppermute | solution.py:372
  69.9 2.4 %collective-permute-start.12 = (bf16[128,3200]{1,0:T(8,128)(2,1)}, bf16[128,3200]{1,0:T(8,128)(2,1)}, u32[]{:S(2)}, u32[]{:S(2)}) collective-permute-start(bf16[128,3200]{1,0:T(8,128)(2,1)} %collective-permute-done.8.refs_11_), channel_id=1, source_target_pairs={{0,16},{16,0},{1,17},{17,1},{2,18},{18,2},{3,19},{19,3},{4,20},{20... | collective-permute-start | bytes 2457608 | tf_op jit(solution)/shard_map/ppermute | solution.py:372
  74.6 8.8 %forward.1 = (bf16[384,1024]{1,0:T(8,128)(2,1)}, bf16[384,1024]{1,0:T(8,128)(2,1)}, bf16[384,1024]{1,0:T(8,128)(2,1)}, bf16[128,1024]{1,0:T(8,128)(2,1)S(1)}, f3...) custom-call(s32[4]{0:T(128)S(1)} %pad_add_fusion.refs_0_, ...), custom_call_target="tpu_custom_call" | custom-call | flops 8999999488 | bytes 27000000 | tf_op jit(solution)/shard_map/forward/pallas_call | solution.py:446
  83.4 7.3 %all_to_all.20 = bf16[4,112,128]{2,1,0:T(8,128)(2,1)S(1)} all-to-all(bf16[4,112,128]{2,1,0:T(8,128)(2,1)S(1)} %reshape.43), channel_id=1, replica_groups={{0,32,64,96},{128,160,192,224},{256,288,320,352},{384,416,448,480},{16,..., dimensions={0} | all-to-all | bytes 229376 | tf_op jit(solution)/shard_map/all_to_all | solution.py:396
  90.9 11.2 %all_to_all.21.refs_0_ = bf16[16,112,128]{2,1,0:T(8,128)(2,1)S(1)} all-to-all(bf16[16,112,128]{2,1,0:T(8,128)(2,1)S(1)} %bitcast.22), channel_id=1, replica_groups={{0,128,256,384},{32,160,288,416},{64,192,320,448},{96,224,352,480},{16,..., dimensions={0} | all-to-all | bytes 917504 | tf_op jit(solution)/shard_map/all_to_all | solution.py:396
  102.0 5.2 %collective-permute-start.13 = (bf16[16,112,128]{2,1,0:T(8,128)(2,1)S(1)}, bf16[16,112,128]{2,1,0:T(8,128)(2,1)S(1)}, u32[]{:S(2)}, u32[]{:S(2)}) collective-permute-start(bf16[16,112,128]{2,1,0:T(8,128)(2,1)S(1)} %all_to_all.21.refs_0_), channel_id=1, source_target_pairs={{0,16},{16,0},{1,17},{17,1},{2,18},{18,2},{3,19},{19,3},{4,20},{20... | collective-permute-start | bytes 1376264 | tf_op jit(solution)/shard_map/ppermute | solution.py:372
  107.3 1.4 collective-permute-done.13.refs_1_
  108.7 1.9 %crps.1 = (bf16[1024,128]{1,0:T(8,128)(2,1)}, bf16[192,128]{1,0:T(8,128)(2,1)S(1)}) custom-call(bf16[16,112,128]{2,1,0:T(8,128)(2,1)S(1)} %all_to_all.21.refs_0_, bf16[16,112,128]{2,1,0:T(8,128)(2,1)S(1)} %collective-permute-done.13.refs_1_, bf16[112,128]{1,0:T(8,128)(2,1)S(1)} %get-tuple-element.25.refs_2_, bf16[112,128]{1,0:T(8,128)(2,1)S(1)} %pad.9.refs_3_, ...), custom_call_target="tpu_custom_call" | custom-call | flops 3000000000 | bytes 9000000 | tf_op jit(solution)/shard_map/crps/pallas_call | solution.py:480
  110.7 4.6 %all-to-all-start.2 = ((bf16[32,32,128]{2,1,0:T(8,128)(2,1)}), bf16[32,32,128]{2,1,0:T(8,128)(2,1)S(1)}, u32[]{:S(2)}, u32[]{:S(2)}) async-start(bf16[32,32,128]{2,1,0:T(8,128)(2,1)} %bitcast.9), calls=%async_computation.2 | async-start | bytes 524288 | tf_op jit(solution)/shard_map/all_to_all | solution.py:507
  115.4 1.4 collective-permute-start.14
  118.1 8.5 %collective-permute-start.16 = (bf16[192,128]{1,0:T(8,128)(2,1)S(1)}, bf16[192,128]{1,0:T(8,128)(2,1)S(1)}, u32[]{:S(2)}, u32[]{:S(2)}) collective-permute-start(bf16[192,128]{1,0:T(8,128)(2,1)S(1)} %get-tuple-element.31.refs_2_), channel_id=1, source_target_pairs={{7,8},{15,0},{8,7},{0,15},{23,24},{31,16},{24,23},{16,31},{39,40},... | collective-permute-start | bytes 147464 | tf_op jit(solution)/shard_map/ppermute | solution.py:351
  127.5 5.2 %all-to-all-start.3 = ((bf16[16,32,128]{2,1,0:T(8,128)(2,1)}), bf16[16,32,128]{2,1,0:T(8,128)(2,1)S(1)}, u32[]{:S(2)}, u32[]{:S(2)}) async-start(bf16[16,32,128]{2,1,0:T(8,128)(2,1)} %middle.1), calls=%async_computation.3 | async-start | bytes 262144 | tf_op jit(solution)/shard_map/all_to_all | solution.py:518
  132.7 10.7 %backward.1 = bf16[1,128,1024]{2,1,0:T(8,128)(2,1)} custom-call(s32[4]{0:T(128)S(1)} %pad_add_fusion.refs_0_, bf16[192,128]{1,0:T(8,128)(2,1)S(1)} %collective-permute-done.14.refs_1_, bf16[192,128]{1,0:T(8,128)(2,1)S(1)} %get-tuple-element.31.refs_2_, bf16[192,128]{1,0:T(8,128)(2,1)S(1)} %collective-permute-done.15.refs_3_, ...), custom_call_target="tpu_custom_call" | custom-call | flops 12000000000 | bytes 36000000 | tf_op jit(solution)/shard_map/backward/pallas_call | solution.py:530
  (57 shorter events, 11.4 us)
Async XLA Ops:
  0.6 34.3 %copy-start.10 = (bf16[32,1024]{1,0:T(8,128)(2,1)S(1)}, bf16[32,1024]{1,0:T(8,128)(2,1)}, u32[]{:S(2)}) copy-start(bf16[32,1024]{1,0:T(8,128)(2,1)} %param.13) | copy-start | bytes 196612
  0.7 34.3 %copy-start.9 = (bf16[32,1024]{1,0:T(8,128)(2,1)S(1)}, bf16[32,1024]{1,0:T(8,128)(2,1)}, u32[]{:S(2)}) copy-start(bf16[32,1024]{1,0:T(8,128)(2,1)} %param.14) | copy-start | bytes 196612
  0.7 34.3 %copy-start.8 = (bf16[32,1024]{1,0:T(8,128)(2,1)S(1)}, bf16[32,1024]{1,0:T(8,128)(2,1)}, u32[]{:S(2)}) copy-start(bf16[32,1024]{1,0:T(8,128)(2,1)} %param.15) | copy-start | bytes 196612
  3.5 22.3 %collective-permute-start = (bf16[32,3200]{1,0:T(8,128)(2,1)S(1)}, bf16[32,3200]{1,0:T(8,128)(2,1)S(1)}, u32[]{:S(2)}, u32[]{:S(2)}) collective-permute-start(bf16[32,3200]{1,0:T(8,128)(2,1)S(1)} %pad_maximum_fusion.1), channel_id=1, source_target_pairs={{0,128},{16,48},{1,129},{17,49},{2,130},{18,50},{3,131},{19,51},{4... | collective-permute-start | bytes 614408 | tf_op jit(solution)/shard_map/ppermute | solution.py:372
  8.4 26.6 %collective-permute-start.1 = (bf16[32,3200]{1,0:T(8,128)(2,1)S(1)}, bf16[32,3200]{1,0:T(8,128)(2,1)S(1)}, u32[]{:S(2)}, u32[]{:S(2)}) collective-permute-start(bf16[32,3200]{1,0:T(8,128)(2,1)S(1)} %pad_maximum_fusion.1), channel_id=1, source_target_pairs={{0,384},{16,120},{1,385},{17,121},{2,386},{18,122},{3,387},{19,123... | collective-permute-start | bytes 614408 | tf_op jit(solution)/shard_map/ppermute | solution.py:372
  17.0 18.0 %collective-permute-start.2 = (bf16[32,3200]{1,0:T(8,128)(2,1)S(1)}, bf16[32,3200]{1,0:T(8,128)(2,1)S(1)}, u32[]{:S(2)}, u32[]{:S(2)}) collective-permute-start(bf16[32,3200]{1,0:T(8,128)(2,1)S(1)} %pad_maximum_fusion.1), channel_id=1, source_target_pairs={{0,256},{16,80},{1,257},{17,81},{2,258},{18,82},{3,259},{19,83},{4... | collective-permute-start | bytes 614408 | tf_op jit(solution)/shard_map/ppermute | solution.py:372
  20.1 54.5 %copy-start.1 = (bf16[128,1024]{1,0:T(8,128)(2,1)S(1)}, bf16[128,1024]{1,0:T(8,128)(2,1)}, u32[]{:S(2)}) copy-start(bf16[128,1024]{1,0:T(8,128)(2,1)} %refs_6_.3) | copy-start | bytes 786436
  20.1 54.5 %copy-start.2 = (bf16[1,128,1024]{2,1,0:T(8,128)(2,1)S(1)}, bf16[1,128,1024]{2,1,0:T(8,128)(2,1)}, u32[]{:S(2)}) copy-start(bf16[1,128,1024]{2,1,0:T(8,128)(2,1)} %refs_5_.3) | copy-start | bytes 786436
  21.3 20.3 %collective-permute-start.3 = (bf16[128,1024]{1,0:T(8,128)(2,1)S(1)}, bf16[128,1024]{1,0:T(8,128)(2,1)S(1)}, u32[]{:S(2)}, u32[]{:S(2)}) collective-permute-start(bf16[128,1024]{1,0:T(8,128)(2,1)S(1)} %multiply_convert_fusion.refs_2_), channel_id=1, source_target_pairs={{0,1},{1,2},{2,3},{3,4},{4,5},{5,6},{6,7},{8,9},{9,10},{10,11},{11... | collective-permute-start | bytes 786440 | tf_op jit(solution)/shard_map/ppermute | solution.py:349
  24.5 17.1 %collective-permute-start.4 = (bf16[128,1024]{1,0:T(8,128)(2,1)S(1)}, bf16[128,1024]{1,0:T(8,128)(2,1)S(1)}, u32[]{:S(2)}, u32[]{:S(2)}) collective-permute-start(bf16[128,1024]{1,0:T(8,128)(2,1)S(1)} %multiply_convert_fusion.refs_2_), channel_id=1, source_target_pairs={{1,0},{2,1},{3,2},{4,3},{5,4},{6,5},{7,6},{9,8},{10,9},{11,10},{12... | collective-permute-start | bytes 786440 | tf_op jit(solution)/shard_map/ppermute | solution.py:350
  25.9 15.8 %collective-permute-start.5 = (bf16[128,1024]{1,0:T(8,128)(2,1)S(1)}, bf16[128,1024]{1,0:T(8,128)(2,1)S(1)}, u32[]{:S(2)}, u32[]{:S(2)}) collective-permute-start(bf16[128,1024]{1,0:T(8,128)(2,1)S(1)} %multiply_convert_fusion.refs_2_), channel_id=1, source_target_pairs={{7,8},{15,0},{8,7},{0,15},{23,24},{31,16},{24,23},{16,31},{39,40},... | collective-permute-start | bytes 786440 | tf_op jit(solution)/shard_map/ppermute | solution.py:351
  35.1 19.8 %collective-permute-start.6 = (bf16[128,3200]{1,0:T(8,128)(2,1)S(1)}, bf16[128,3200]{1,0:T(8,128)(2,1)S(1)}, u32[]{:S(2)}, u32[]{:S(2)}) collective-permute-start(bf16[128,3200]{1,0:T(8,128)(2,1)S(1)} %pad_maximum_fusion.refs_8_), channel_id=1, source_target_pairs={{0,32},{16,144},{1,33},{17,145},{2,34},{18,146},{3,35},{19,147},{4... | collective-permute-start | bytes 2457608 | tf_op jit(solution)/shard_map/ppermute | solution.py:372
  38.2 29.7 %collective-permute-start.7 = (bf16[128,3200]{1,0:T(8,128)(2,1)S(1)}, bf16[128,3200]{1,0:T(8,128)(2,1)}, u32[]{:S(2)}, u32[]{:S(2)}) collective-permute-start(bf16[128,3200]{1,0:T(8,128)(2,1)S(1)} %pad_maximum_fusion.refs_8_), channel_id=1, source_target_pairs={{0,104},{16,400},{1,105},{17,401},{2,106},{18,402},{3,107},{19,403... | collective-permute-start | bytes 2457608 | tf_op jit(solution)/shard_map/ppermute | solution.py:372
  41.6 28.2 %collective-permute-start.8 = (bf16[128,3200]{1,0:T(8,128)(2,1)S(1)}, bf16[128,3200]{1,0:T(8,128)(2,1)}, u32[]{:S(2)}, u32[]{:S(2)}) collective-permute-start(bf16[128,3200]{1,0:T(8,128)(2,1)S(1)} %pad_maximum_fusion.refs_8_), channel_id=1, source_target_pairs={{0,64},{16,272},{1,65},{17,273},{2,66},{18,274},{3,67},{19,275},{4... | collective-permute-start | bytes 2457608 | tf_op jit(solution)/shard_map/ppermute | solution.py:372
  49.2 24.2 %collective-permute-start.9 = (bf16[128,3200]{1,0:T(8,128)(2,1)S(1)}, bf16[128,3200]{1,0:T(8,128)(2,1)}, u32[]{:S(2)}, u32[]{:S(2)}) collective-permute-start(bf16[128,3200]{1,0:T(8,128)(2,1)S(1)} %pad_maximum_fusion.refs_8_), channel_id=1, source_target_pairs={{0,16},{16,0},{1,17},{17,1},{2,18},{18,2},{3,19},{19,3},{4,20},{20... | collective-permute-start | bytes 2457608 | tf_op jit(solution)/shard_map/ppermute | solution.py:372
  54.9 18.5 %collective-permute-start.10 = (bf16[128,3200]{1,0:T(8,128)(2,1)S(1)}, bf16[128,3200]{1,0:T(8,128)(2,1)}, u32[]{:S(2)}, u32[]{:S(2)}) collective-permute-start(bf16[128,3200]{1,0:T(8,128)(2,1)S(1)} %collective-permute-done.6.refs_9_), channel_id=1, source_target_pairs={{0,16},{16,0},{1,17},{17,1},{2,18},{18,2},{3,19},{19,3},{4,20},{20... | collective-permute-start | bytes 2457608 | tf_op jit(solution)/shard_map/ppermute | solution.py:372
  67.9 5.5 %collective-permute-start.11 = (bf16[128,3200]{1,0:T(8,128)(2,1)}, bf16[128,3200]{1,0:T(8,128)(2,1)}, u32[]{:S(2)}, u32[]{:S(2)}) collective-permute-start(bf16[128,3200]{1,0:T(8,128)(2,1)} %collective-permute-done.7.refs_10_), channel_id=1, source_target_pairs={{0,16},{16,0},{1,17},{17,1},{2,18},{18,2},{3,19},{19,3},{4,20},{20... | collective-permute-start | bytes 2457608 | tf_op jit(solution)/shard_map/ppermute | solution.py:372
  69.9 4.7 %collective-permute-start.12 = (bf16[128,3200]{1,0:T(8,128)(2,1)}, bf16[128,3200]{1,0:T(8,128)(2,1)}, u32[]{:S(2)}, u32[]{:S(2)}) collective-permute-start(bf16[128,3200]{1,0:T(8,128)(2,1)} %collective-permute-done.8.refs_11_), channel_id=1, source_target_pairs={{0,16},{16,0},{1,17},{17,1},{2,18},{18,2},{3,19},{19,3},{4,20},{20... | collective-permute-start | bytes 2457608 | tf_op jit(solution)/shard_map/ppermute | solution.py:372
  102.0 6.7 %collective-permute-start.13 = (bf16[16,112,128]{2,1,0:T(8,128)(2,1)S(1)}, bf16[16,112,128]{2,1,0:T(8,128)(2,1)S(1)}, u32[]{:S(2)}, u32[]{:S(2)}) collective-permute-start(bf16[16,112,128]{2,1,0:T(8,128)(2,1)S(1)} %all_to_all.21.refs_0_), channel_id=1, source_target_pairs={{0,16},{16,0},{1,17},{17,1},{2,18},{18,2},{3,19},{19,3},{4,20},{20... | collective-permute-start | bytes 1376264 | tf_op jit(solution)/shard_map/ppermute | solution.py:372
  110.7 16.0 %all-to-all-start.2 = ((bf16[32,32,128]{2,1,0:T(8,128)(2,1)}), bf16[32,32,128]{2,1,0:T(8,128)(2,1)S(1)}, u32[]{:S(2)}, u32[]{:S(2)}) async-start(bf16[32,32,128]{2,1,0:T(8,128)(2,1)} %bitcast.9), calls=%async_computation.2 | async-start | bytes 524288 | tf_op jit(solution)/shard_map/all_to_all | solution.py:507
  115.4 17.3 %collective-permute-start.14 = (bf16[192,128]{1,0:T(8,128)(2,1)S(1)}, bf16[192,128]{1,0:T(8,128)(2,1)S(1)}, u32[]{:S(2)}, u32[]{:S(2)}) collective-permute-start(bf16[192,128]{1,0:T(8,128)(2,1)S(1)} %get-tuple-element.31.refs_2_), channel_id=1, source_target_pairs={{0,1},{1,2},{2,3},{3,4},{4,5},{5,6},{6,7},{8,9},{9,10},{10,11},{11... | collective-permute-start | bytes 147464 | tf_op jit(solution)/shard_map/ppermute | solution.py:349
  116.8 15.9 %collective-permute-start.15 = (bf16[192,128]{1,0:T(8,128)(2,1)S(1)}, bf16[192,128]{1,0:T(8,128)(2,1)S(1)}, u32[]{:S(2)}, u32[]{:S(2)}) collective-permute-start(bf16[192,128]{1,0:T(8,128)(2,1)S(1)} %get-tuple-element.31.refs_2_), channel_id=1, source_target_pairs={{1,0},{2,1},{3,2},{4,3},{5,4},{6,5},{7,6},{9,8},{10,9},{11,10},{12... | collective-permute-start | bytes 147464 | tf_op jit(solution)/shard_map/ppermute | solution.py:350
  118.1 14.6 %collective-permute-start.16 = (bf16[192,128]{1,0:T(8,128)(2,1)S(1)}, bf16[192,128]{1,0:T(8,128)(2,1)S(1)}, u32[]{:S(2)}, u32[]{:S(2)}) collective-permute-start(bf16[192,128]{1,0:T(8,128)(2,1)S(1)} %get-tuple-element.31.refs_2_), channel_id=1, source_target_pairs={{7,8},{15,0},{8,7},{0,15},{23,24},{31,16},{24,23},{16,31},{39,40},... | collective-permute-start | bytes 147464 | tf_op jit(solution)/shard_map/ppermute | solution.py:351
  127.5 16.6 %all-to-all-start.3 = ((bf16[16,32,128]{2,1,0:T(8,128)(2,1)}), bf16[16,32,128]{2,1,0:T(8,128)(2,1)S(1)}, u32[]{:S(2)}, u32[]{:S(2)}) async-start(bf16[16,32,128]{2,1,0:T(8,128)(2,1)} %middle.1), calls=%async_computation.3 | async-start | bytes 262144 | tf_op jit(solution)/shard_map/all_to_all | solution.py:518
  (7 other events, 137.3 us)

commit v10 on v9

--- a/solution.py
+++ b/solution.py
@@ -66,7 +66,7 @@
     return out
 
 
-def forward_kernel(scale, place, low, own, high, wrapped, hidden, forcing, decode_t, *refs):
+def forward_kernel(scale, place, near, own, far, hidden, forcing, decode_t, *refs):
     pieces, refs = refs[: 2 * len(HOPS)], refs[2 * len(HOPS) :]
     (
         queries_out, keys_out, values_out, attended, lse_out, pred, mixed, full,
@@ -79,21 +79,21 @@
     block = pieces[0].shape[0] // side
     for mine in (True, False):
         which = core if mine else 1 - core
-        for outer, far in enumerate(HOPS):
+        for outer, second in enumerate(HOPS):
             piece = pieces[outer if mine else side + outer]
-            for inner, near in enumerate(HOPS):
-                along_x = jnp.where(which == 0, near, far)
-                along_z = jnp.where(which == 0, far, near)
+            for inner, first in enumerate(HOPS):
+                along_x = jnp.where(which == 0, first, second)
+                along_z = jnp.where(which == 0, second, first)
                 chip = lax.rem(x + along_x, side) * side + lax.rem(z + along_z, side)
                 at = pl.multiple_of((chip * 2 + which) * block, block)
                 weights[pl.ds(at, block), :] = piece[inner * block : (inner + 1) * block, :]
     stores = [pltpu.make_async_copy(weights, full, store.at[0])]
     stores[0].start()
     mixed[...] = weights[:, 3 * width :]
-    at_y = place[3]
-    normed[:HALO] = jnp.where(at_y == 0, wrapped[...], low[...])
+    even = place[3] == 0
+    normed[:HALO] = jnp.where(even, near[...], far[...])
     normed[HALO : HALO + rows] = own[...]
-    normed[HALO + rows :] = jnp.where(at_y == RING_Y - 1, wrapped[...], high[...])
+    normed[HALO + rows :] = jnp.where(even, far[...], near[...])
     total = nt(hidden[0], decode_t[...]) + nt(forcing[...], decode_t[...])
     window = window_mask(rows, span)
     masks = head_masks(scale)
@@ -228,7 +228,7 @@
 
 
 def backward_kernel(
-    scale, place, low_part, own, high_part, wrapped, hidden, forcing, inverse_rms, gain, decode_t, mixed,
+    scale, place, near, own, far, hidden, forcing, inverse_rms, gain, decode_t, mixed,
     queries_in, keys_in, values_in, lse_in, full,
     grad_hidden, queries, keys, values, lse, weights, grad_t, stats, load,
 ):
@@ -249,9 +249,9 @@
             cols = slice(index * width + at, index * width + at + STEP)
             fetch(full.at[:, cols], weights.at[:, cols])
 
-    at_y = place[3]
-    low = jnp.where(at_y == 0, wrapped[...], low_part[...])
-    high = jnp.where(at_y == RING_Y - 1, wrapped[...], high_part[...])
+    even = place[3] == 0
+    low = jnp.where(even, near[...], far[...])
+    high = jnp.where(even, far[...], near[...])
     zero = jnp.zeros((LANES - VROWS, LANES), b16)
     for side, part in enumerate((own[...], low, high)):
         grad = jnp.concatenate([part[:VROWS], zero], 0)
@@ -344,12 +344,11 @@
 
 
 def halos(value):
-    up = [(n, n + 1) for n in range(2 * RING_Y) if n % RING_Y < RING_Y - 1]
-    turn = [(RING_Y - 1, RING_Y), (2 * RING_Y - 1, 0)]
-    low = lax.ppermute(value, "node", up)
-    high = lax.ppermute(value, "node", [(b, a) for a, b in up])
-    wrapped = lax.ppermute(value, "node", turn + [(b, a) for a, b in turn])
-    return low, high, wrapped
+    count = 2 * RING_Y
+    return tuple(
+        lax.ppermute(value, "node", [(n, (n + (1 if n % 2 == odd else -1)) % count) for n in range(count)])
+        for odd in (1, 0)
+    )
 
 
 def permute(value, moves):
@@ -423,16 +422,16 @@
     mixed = nt(w_out, decode_t).astype(b16)
     position = lax.axis_index("ens")
     core = position % 2
-    at_y = lax.axis_index("node") % RING_Y
-    place = jnp.stack([position // (2 * SIDE), position // 2 % SIDE, core, at_y])
+    parity = lax.axis_index("node") % 2
+    place = jnp.stack([position // (2 * SIDE), position // 2 % SIDE, core, parity])
     place = place.astype(jnp.int32)
     packed = jnp.concatenate([w_query, w_key, w_value, mixed], 1)
     xfield = hidden[0].astype(f32) + forcing.astype(f32)
     inverse_rms = lax.rsqrt(jnp.mean(xfield * xfield, -1, keepdims=True) + EPS_NORM)
     normed = (xfield * inverse_rms * norm_gain).astype(b16)
-    low, high, wrapped = halos(normed)
+    near, far = halos(normed)
     row = ring(packed, (0, 1))
-    *mine, low, high, wrapped = ring(jnp.concatenate(row, 0), (1, 0), (low, high, wrapped))
+    *mine, near, far = ring(jnp.concatenate(row, 0), (1, 0), (near, far))
     pieces = mine + [swapped(piece) for piece in mine]
 
     packed_width = 3 * width + LANES
@@ -445,7 +444,7 @@
 
     queries, keys, values, attended, lse, pred, mixed, full = pl.pallas_call(
         lambda *refs: forward_kernel(scale, *refs),
-        in_specs=[in_smem] + [in_vmem] * (7 + len(pieces)),
+        in_specs=[in_smem] + [in_vmem] * (6 + len(pieces)),
         out_specs=[in_hbm, in_hbm, in_hbm, in_vmem, in_hbm, in_vmem, in_vmem, in_hbm],
         out_shape=[
             pltpu.HBM((span, width), b16),
@@ -469,7 +468,7 @@
         compiler_params=params(24),
         cost_estimate=cost(9),
         name="forward",
-    )(place, low, normed, high, wrapped, hidden, forcing, decode_t, *pieces)
+    )(place, near, normed, far, hidden, forcing, decode_t, *pieces)
 
     others = everyone(pred)
     theirs = swapped(others)
@@ -503,7 +502,7 @@
         name="crps",
     )(others, theirs, pred, truth, area_weight[None], attended, mixed, lse)
 
-    halo_low, halo_high, halo_wrapped = halos(halo)
+    halo_near, halo_far = halos(halo)
     parts = lax.all_to_all(gram.reshape(members, rows, LANES), "ens", 0, 0, tiled=True)
     spread = pl.pallas_call(
         lambda *refs: middle_kernel(variables, *refs),
@@ -529,7 +528,7 @@
 
     grad_hidden = pl.pallas_call(
         lambda *refs: backward_kernel(scale, *refs),
-        in_specs=[in_smem] + [in_vmem] * 10 + [in_hbm] * 5,
+        in_specs=[in_smem] + [in_vmem] * 9 + [in_hbm] * 5,
         out_specs=in_vmem,
         out_shape=shape((1, node_rows, width), b16),
         scratch_shapes=[
@@ -546,7 +545,7 @@
         cost_estimate=cost(12),
         name="backward",
     )(
-        place, halo_low, halo, halo_high, halo_wrapped, hidden, forcing, inverse_rms,
+        place, halo_near, halo, halo_far, hidden, forcing, inverse_rms,
         norm_gain[None], decode_t, mixed,
         *[held(part) for part in (queries, keys, values, lse, full)],
     )

time: 146 us -> 143 us (0.979)
  starting transfers between devices: 92.3 us -> 77.4 us
  waiting for transfers between devices: 3.27 us -> 14.2 us
  blocking collectives: 18.5 us -> 20.2 us
    ppermute x11, starting transfers between devices: 57.7 us -> 43.8 us  [permute(): return lax.ppermute(value, ('ens', 'node'), pairs)]
    ppermute x11, waiting for transfers between devices: 2.57 us -> 10.4 us  [permute(): return lax.ppermute(value, ('ens', 'node'), pairs)]
    ppermute x6 -> x4, starting transfers between devices: 24.9 us -> 20.7 us  [halos(): lax.ppermute(value, 'node', [(n, (n + (1 if n % 2 == odd else -1)) % coun...]
    all_to_all x1, starting transfers between devices: 5.18 us -> 8.37 us  [per_device(): parts = lax.all_to_all(spread, 'node', 0, 0, tiled=True)]
    ppermute x6 -> x4, waiting for transfers between devices: 0.02 us -> 2.06 us  [halos(): lax.ppermute(value, 'node', [(n, (n + (1 if n % 2 == odd else -1)) % coun...]
    all_to_all x2, blocking collectives: 18.5 us -> 20.2 us  [everyone(): lax.all_to_all(spread, 'ens', 0, 0, tiled=True, axis_index_groups=groups)]
  transfers between devices with their start and end apart: 19 -> 17, of which waited for: 3 -> 6; matrix products, arithmetic and copies ran while one was open for 2% -> 2% of each run, Pallas kernels for 8% -> 8%
where the time goes in v10:
time: 143 us; the launch traced here: 142 us
  starting transfers between devices  77.4 us (54%)
  Pallas kernels  23.1 us (16%)
  blocking collectives  20.2 us (14%)
  waiting for transfers between devices  14.2 us (10%)
  other arithmetic  3.52 us (2%)
    ppermute x11, starting transfers between devices, permute(): return lax.ppermute(value, ('ens', 'node'), pairs)  43.8 us
    ppermute x4, starting transfers between devices, halos(): lax.ppermute(value, 'node', [(n, (n + (1 if n % 2 == odd else -1)) % coun...  20.7 us
    all_to_all x2, blocking collectives, everyone(): lax.all_to_all(spread, 'ens', 0, 0, tiled=True, axis_index_groups=groups)  20.2 us
    pallas_call x1, Pallas kernels, per_device(): pl.pallas_call(lambda *refs: backward_kernel(scale, *refs), in_specs=[in_...  10.7 us
    ppermute x11, waiting for transfers between devices, permute(): return lax.ppermute(value, ('ens', 'node'), pairs)  10.4 us
    pallas_call x1, Pallas kernels, per_device(): pl.pallas_call(lambda *refs: forward_kernel(scale, *refs), in_specs=[in_s...  8.83 us
    all_to_all x1, starting transfers between devices, per_device(): parts = lax.all_to_all(spread, 'node', 0, 0, tiled=True)  8.37 us
    all_to_all x1, starting transfers between devices, per_device(): lax.all_to_all(gram.reshape(members, rows, LANES), 'ens', 0, 0, tiled=True)  4.59 us
  transfers between devices with their start and end apart: 17, of which 6 were waited for; matrix products, arithmetic and copies ran while one was open for 2% of the time, Pallas kernels for 8%

profile of v10, /device:TPU:1, one launch (start us, length us, event | category | flops | bytes accessed | tf_op | source)
XLA Modules:
  0.0 141.6 jit_solution(12058965709669319933)
XLA Ops:
  3.6 4.8 %collective-permute-start = (bf16[32,3200]{1,0:T(8,128)(2,1)S(1)}, bf16[32,3200]{1,0:T(8,128)(2,1)S(1)}, u32[]{:S(2)}, u32[]{:S(2)}) collective-permute-start(bf16[32,3200]{1,0:T(8,128)(2,1)S(1)} %pad_maximum_fusion.1), channel_id=1, source_target_pairs={{0,128},{16,48},{1,129},{17,49},{2,130},{18,50},{3,131},{19,51},{4... | collective-permute-start | bytes 614408 | tf_op jit(solution)/shard_map/ppermute | solution.py:371
  8.4 8.6 %collective-permute-start.1 = (bf16[32,3200]{1,0:T(8,128)(2,1)S(1)}, bf16[32,3200]{1,0:T(8,128)(2,1)S(1)}, u32[]{:S(2)}, u32[]{:S(2)}) collective-permute-start(bf16[32,3200]{1,0:T(8,128)(2,1)S(1)} %pad_maximum_fusion.1), channel_id=1, source_target_pairs={{0,384},{16,120},{1,385},{17,121},{2,386},{18,122},{3,387},{19,123... | collective-permute-start | bytes 614408 | tf_op jit(solution)/shard_map/ppermute | solution.py:371
  17.0 1.9 %collective-permute-start.2 = (bf16[32,3200]{1,0:T(8,128)(2,1)S(1)}, bf16[32,3200]{1,0:T(8,128)(2,1)S(1)}, u32[]{:S(2)}, u32[]{:S(2)}) collective-permute-start(bf16[32,3200]{1,0:T(8,128)(2,1)S(1)} %pad_maximum_fusion.1), channel_id=1, source_target_pairs={{0,256},{16,80},{1,257},{17,81},{2,258},{18,82},{3,259},{19,83},{4... | collective-permute-start | bytes 614408 | tf_op jit(solution)/shard_map/ppermute | solution.py:371
  21.4 8.3 %collective-permute-start.3 = (bf16[128,1024]{1,0:T(8,128)(2,1)S(1)}, bf16[128,1024]{1,0:T(8,128)(2,1)S(1)}, u32[]{:S(2)}, u32[]{:S(2)}) collective-permute-start(bf16[128,1024]{1,0:T(8,128)(2,1)S(1)} %multiply_convert_fusion.refs_2_), channel_id=1, source_target_pairs={{0,15},{1,2},{2,1},{3,4},{4,3},{5,6},{6,5},{7,8},{8,7},{9,10},{10,... | collective-permute-start | bytes 786440 | tf_op jit(solution)/shard_map/ppermute | solution.py:349
  29.7 1.9 %collective-permute-start.4 = (bf16[128,1024]{1,0:T(8,128)(2,1)S(1)}, bf16[128,1024]{1,0:T(8,128)(2,1)S(1)}, u32[]{:S(2)}, u32[]{:S(2)}) collective-permute-start(bf16[128,1024]{1,0:T(8,128)(2,1)S(1)} %multiply_convert_fusion.refs_2_), channel_id=1, source_target_pairs={{0,1},{1,0},{2,3},{3,2},{4,5},{5,4},{6,7},{7,6},{8,9},{9,8},{10,11... | collective-permute-start | bytes 786440 | tf_op jit(solution)/shard_map/ppermute | solution.py:349
  31.8 4.4 %collective-permute-start.6 = (bf16[128,3200]{1,0:T(8,128)(2,1)S(1)}, bf16[128,3200]{1,0:T(8,128)(2,1)S(1)}, u32[]{:S(2)}, u32[]{:S(2)}) collective-permute-start(bf16[128,3200]{1,0:T(8,128)(2,1)S(1)} %pad_maximum_fusion.refs_7_), channel_id=1, source_target_pairs={{0,104},{16,400},{1,105},{17,401},{2,106},{18,402},{3,107},{19,403... | collective-permute-start | bytes 2457608 | tf_op jit(solution)/shard_map/ppermute | solution.py:371
  36.1 1.9 %collective-permute-start.5 = (bf16[128,3200]{1,0:T(8,128)(2,1)S(1)}, bf16[128,3200]{1,0:T(8,128)(2,1)}, u32[]{:S(2)}, u32[]{:S(2)}) collective-permute-start(bf16[128,3200]{1,0:T(8,128)(2,1)S(1)} %pad_maximum_fusion.refs_7_), channel_id=1, source_target_pairs={{0,32},{16,144},{1,33},{17,145},{2,34},{18,146},{3,35},{19,147},{4... | collective-permute-start | bytes 2457608 | tf_op jit(solution)/shard_map/ppermute | solution.py:371
  38.1 2.1 %collective-permute-done.3.refs_1_ = bf16[128,1024]{1,0:T(8,128)(2,1)S(1)} collective-permute-done((bf16[128,1024]{1,0:T(8,128)(2,1)S(1)}, bf16[128,1024]{1,0:T(8,128)(2,1)S(1)}, u32[]{:S(2)}, u32[]{:S(2)}) %collective-permute-start.3) | collective-permute-done | bytes 262176 | tf_op jit(solution)/shard_map/ppermute | solution.py:349
  40.1 4.4 %collective-permute-start.7 = (bf16[128,3200]{1,0:T(8,128)(2,1)S(1)}, bf16[128,3200]{1,0:T(8,128)(2,1)}, u32[]{:S(2)}, u32[]{:S(2)}) collective-permute-start(bf16[128,3200]{1,0:T(8,128)(2,1)S(1)} %pad_maximum_fusion.refs_7_), channel_id=1, source_target_pairs={{0,64},{16,272},{1,65},{17,273},{2,66},{18,274},{3,67},{19,275},{4... | collective-permute-start | bytes 2457608 | tf_op jit(solution)/shard_map/ppermute | solution.py:371
  44.5 6.0 %collective-permute-start.8 = (bf16[128,3200]{1,0:T(8,128)(2,1)S(1)}, bf16[128,3200]{1,0:T(8,128)(2,1)}, u32[]{:S(2)}, u32[]{:S(2)}) collective-permute-start(bf16[128,3200]{1,0:T(8,128)(2,1)S(1)} %pad_maximum_fusion.refs_7_), channel_id=1, source_target_pairs={{0,16},{16,0},{1,17},{17,1},{2,18},{18,2},{3,19},{19,3},{4,20},{20... | collective-permute-start | bytes 2457608 | tf_op jit(solution)/shard_map/ppermute | solution.py:371
  50.5 2.2 %collective-permute-start.10 = (bf16[128,3200]{1,0:T(8,128)(2,1)S(1)}, bf16[128,3200]{1,0:T(8,128)(2,1)}, u32[]{:S(2)}, u32[]{:S(2)}) collective-permute-start(bf16[128,3200]{1,0:T(8,128)(2,1)S(1)} %collective-permute-done.6.refs_9_), channel_id=1, source_target_pairs={{0,16},{16,0},{1,17},{17,1},{2,18},{18,2},{3,19},{19,3},{4,20},{20... | collective-permute-start | bytes 2457608 | tf_op jit(solution)/shard_map/ppermute | solution.py:371
  52.7 6.9 %collective-permute-done.5.refs_8_ = bf16[128,3200]{1,0:T(8,128)(2,1)} collective-permute-done((bf16[128,3200]{1,0:T(8,128)(2,1)S(1)}, bf16[128,3200]{1,0:T(8,128)(2,1)}, u32[]{:S(2)}, u32[]{:S(2)}) %collective-permute-start.5) | collective-permute-done | bytes 819232 | tf_op jit(solution)/shard_map/ppermute | solution.py:371
  61.6 2.4 %collective-permute-start.11 = (bf16[128,3200]{1,0:T(8,128)(2,1)}, bf16[128,3200]{1,0:T(8,128)(2,1)}, u32[]{:S(2)}, u32[]{:S(2)}) collective-permute-start(bf16[128,3200]{1,0:T(8,128)(2,1)} %collective-permute-done.7.refs_10_), channel_id=1, source_target_pairs={{0,16},{16,0},{1,17},{17,1},{2,18},{18,2},{3,19},{19,3},{4,20},{20... | collective-permute-start | bytes 2457608 | tf_op jit(solution)/shard_map/ppermute | solution.py:371
  64.2 2.1 %collective-permute-done.11.refs_14_ = bf16[128,3200]{1,0:T(8,128)(2,1)} collective-permute-done((bf16[128,3200]{1,0:T(8,128)(2,1)}, bf16[128,3200]{1,0:T(8,128)(2,1)}, u32[]{:S(2)}, u32[]{:S(2)}) %collective-permute-start.11) | collective-permute-done | bytes 819232 | tf_op jit(solution)/shard_map/ppermute | solution.py:371
  66.3 8.8 %forward.1 = (bf16[384,1024]{1,0:T(8,128)(2,1)}, bf16[384,1024]{1,0:T(8,128)(2,1)}, bf16[384,1024]{1,0:T(8,128)(2,1)}, bf16[128,1024]{1,0:T(8,128)(2,1)S(1)}, f3...) custom-call(s32[4]{0:T(128)S(1)} %pad_add_fusion.refs_0_, ...), custom_call_target="tpu_custom_call" | custom-call | flops 8999999488 | bytes 27000000 | tf_op jit(solution)/shard_map/forward/pallas_call | solution.py:445
  75.1 10.3 %all_to_all.20 = bf16[4,112,128]{2,1,0:T(8,128)(2,1)S(1)} all-to-all(bf16[4,112,128]{2,1,0:T(8,128)(2,1)S(1)} %reshape.43), channel_id=1, replica_groups={{0,32,64,96},{128,160,192,224},{256,288,320,352},{384,416,448,480},{16,..., dimensions={0} | all-to-all | bytes 229376 | tf_op jit(solution)/shard_map/all_to_all | solution.py:395
  85.5 9.9 %all_to_all.21.refs_0_ = bf16[16,112,128]{2,1,0:T(8,128)(2,1)S(1)} all-to-all(bf16[16,112,128]{2,1,0:T(8,128)(2,1)S(1)} %bitcast.22), channel_id=1, replica_groups={{0,128,256,384},{32,160,288,416},{64,192,320,448},{96,224,352,480},{16,..., dimensions={0} | all-to-all | bytes 917504 | tf_op jit(solution)/shard_map/all_to_all | solution.py:395
  95.4 5.2 %collective-permute-start.12 = (bf16[16,112,128]{2,1,0:T(8,128)(2,1)S(1)}, bf16[16,112,128]{2,1,0:T(8,128)(2,1)S(1)}, u32[]{:S(2)}, u32[]{:S(2)}) collective-permute-start(bf16[16,112,128]{2,1,0:T(8,128)(2,1)S(1)} %all_to_all.21.refs_0_), channel_id=1, source_target_pairs={{0,16},{16,0},{1,17},{17,1},{2,18},{18,2},{3,19},{19,3},{4,20},{20... | collective-permute-start | bytes 1376264 | tf_op jit(solution)/shard_map/ppermute | solution.py:371
  102.1 1.9 %crps.1 = (bf16[1024,128]{1,0:T(8,128)(2,1)}, bf16[192,128]{1,0:T(8,128)(2,1)S(1)}) custom-call(bf16[16,112,128]{2,1,0:T(8,128)(2,1)S(1)} %all_to_all.21.refs_0_, bf16[16,112,128]{2,1,0:T(8,128)(2,1)S(1)} %collective-permute-done.12.refs_1_, bf16[112,128]{1,0:T(8,128)(2,1)S(1)} %get-tuple-element.23.refs_2_, bf16[112,128]{1,0:T(8,128)(2,1)S(1)} %pad.9.refs_3_, ...), custom_call_target="tpu_custom_call" | custom-call | flops 3000000000 | bytes 9000000 | tf_op jit(solution)/shard_map/crps/pallas_call | solution.py:479
  104.0 4.6 %all-to-all-start.2 = ((bf16[32,32,128]{2,1,0:T(8,128)(2,1)}), bf16[32,32,128]{2,1,0:T(8,128)(2,1)S(1)}, u32[]{:S(2)}, u32[]{:S(2)}) async-start(bf16[32,32,128]{2,1,0:T(8,128)(2,1)} %bitcast.9), calls=%async_computation.2 | async-start | bytes 524288 | tf_op jit(solution)/shard_map/all_to_all | solution.py:506
  108.7 8.5 %collective-permute-start.13 = (bf16[192,128]{1,0:T(8,128)(2,1)S(1)}, bf16[192,128]{1,0:T(8,128)(2,1)S(1)}, u32[]{:S(2)}, u32[]{:S(2)}) collective-permute-start(bf16[192,128]{1,0:T(8,128)(2,1)S(1)} %get-tuple-element.29.refs_2_), channel_id=1, source_target_pairs={{0,15},{1,2},{2,1},{3,4},{4,3},{5,6},{6,5},{7,8},{8,7},{9,10},{10,... | collective-permute-start | bytes 147464 | tf_op jit(solution)/shard_map/ppermute | solution.py:349
  117.2 1.9 %collective-permute-start.14 = (bf16[192,128]{1,0:T(8,128)(2,1)S(1)}, bf16[192,128]{1,0:T(8,128)(2,1)S(1)}, u32[]{:S(2)}, u32[]{:S(2)}) collective-permute-start(bf16[192,128]{1,0:T(8,128)(2,1)S(1)} %get-tuple-element.29.refs_2_), channel_id=1, source_target_pairs={{0,1},{1,0},{2,3},{3,2},{4,5},{5,4},{6,7},{7,6},{8,9},{9,8},{10,11... | collective-permute-start | bytes 147464 | tf_op jit(solution)/shard_map/ppermute | solution.py:349
  121.0 8.4 %all-to-all-start.3 = ((bf16[16,32,128]{2,1,0:T(8,128)(2,1)}), bf16[16,32,128]{2,1,0:T(8,128)(2,1)S(1)}, u32[]{:S(2)}, u32[]{:S(2)}) async-start(bf16[16,32,128]{2,1,0:T(8,128)(2,1)} %middle.1), calls=%async_computation.3 | async-start | bytes 262144 | tf_op jit(solution)/shard_map/all_to_all | solution.py:517
  129.4 10.7 %backward.1 = bf16[1,128,1024]{2,1,0:T(8,128)(2,1)} custom-call(s32[4]{0:T(128)S(1)} %pad_add_fusion.refs_0_, bf16[192,128]{1,0:T(8,128)(2,1)S(1)} %collective-permute-done.13.refs_1_, bf16[192,128]{1,0:T(8,128)(2,1)S(1)} %get-tuple-element.29.refs_2_, bf16[192,128]{1,0:T(8,128)(2,1)S(1)} %collective-permute-done.14.refs_3_, ...), custom_call_target="tpu_custom_call" | custom-call | flops 12000000000 | bytes 36000000 | tf_op jit(solution)/shard_map/backward/pallas_call | solution.py:529
  (51 shorter events, 12.4 us)
Async XLA Ops:
  0.6 31.0 %copy-start.9 = (bf16[32,1024]{1,0:T(8,128)(2,1)S(1)}, bf16[32,1024]{1,0:T(8,128)(2,1)}, u32[]{:S(2)}) copy-start(bf16[32,1024]{1,0:T(8,128)(2,1)} %param.13) | copy-start | bytes 196612
  0.7 31.0 %copy-start.8 = (bf16[32,1024]{1,0:T(8,128)(2,1)S(1)}, bf16[32,1024]{1,0:T(8,128)(2,1)}, u32[]{:S(2)}) copy-start(bf16[32,1024]{1,0:T(8,128)(2,1)} %param.14) | copy-start | bytes 196612
  0.7 31.0 %copy-start.7 = (bf16[32,1024]{1,0:T(8,128)(2,1)S(1)}, bf16[32,1024]{1,0:T(8,128)(2,1)}, u32[]{:S(2)}) copy-start(bf16[32,1024]{1,0:T(8,128)(2,1)} %param.15) | copy-start | bytes 196612
  2.6 61.4 %copy-start.6 = (bf16[1024,100]{0,1:T(8,128)(2,1)S(1)}, bf16[1024,100]{0,1:T(8,128)(2,1)}, u32[]{:S(2)}) copy-start(bf16[1024,100]{0,1:T(8,128)(2,1)} %param.17) | copy-start | bytes 614404
  3.6 28.1 %collective-permute-start = (bf16[32,3200]{1,0:T(8,128)(2,1)S(1)}, bf16[32,3200]{1,0:T(8,128)(2,1)S(1)}, u32[]{:S(2)}, u32[]{:S(2)}) collective-permute-start(bf16[32,3200]{1,0:T(8,128)(2,1)S(1)} %pad_maximum_fusion.1), channel_id=1, source_target_pairs={{0,128},{16,48},{1,129},{17,49},{2,130},{18,50},{3,131},{19,51},{4... | collective-permute-start | bytes 614408 | tf_op jit(solution)/shard_map/ppermute | solution.py:371
  8.4 23.2 %collective-permute-start.1 = (bf16[32,3200]{1,0:T(8,128)(2,1)S(1)}, bf16[32,3200]{1,0:T(8,128)(2,1)S(1)}, u32[]{:S(2)}, u32[]{:S(2)}) collective-permute-start(bf16[32,3200]{1,0:T(8,128)(2,1)S(1)} %pad_maximum_fusion.1), channel_id=1, source_target_pairs={{0,384},{16,120},{1,385},{17,121},{2,386},{18,122},{3,387},{19,123... | collective-permute-start | bytes 614408 | tf_op jit(solution)/shard_map/ppermute | solution.py:371
  17.0 14.6 %collective-permute-start.2 = (bf16[32,3200]{1,0:T(8,128)(2,1)S(1)}, bf16[32,3200]{1,0:T(8,128)(2,1)S(1)}, u32[]{:S(2)}, u32[]{:S(2)}) collective-permute-start(bf16[32,3200]{1,0:T(8,128)(2,1)S(1)} %pad_maximum_fusion.1), channel_id=1, source_target_pairs={{0,256},{16,80},{1,257},{17,81},{2,258},{18,82},{3,259},{19,83},{4... | collective-permute-start | bytes 614408 | tf_op jit(solution)/shard_map/ppermute | solution.py:371
  20.1 46.1 %copy-start.1 = (bf16[128,1024]{1,0:T(8,128)(2,1)S(1)}, bf16[128,1024]{1,0:T(8,128)(2,1)}, u32[]{:S(2)}) copy-start(bf16[128,1024]{1,0:T(8,128)(2,1)} %refs_5_.3) | copy-start | bytes 786436
  20.1 46.1 %copy-start.2 = (bf16[1,128,1024]{2,1,0:T(8,128)(2,1)S(1)}, bf16[1,128,1024]{2,1,0:T(8,128)(2,1)}, u32[]{:S(2)}) copy-start(bf16[1,128,1024]{2,1,0:T(8,128)(2,1)} %refs_4_.3) | copy-start | bytes 786436
  21.4 18.8 %collective-permute-start.3 = (bf16[128,1024]{1,0:T(8,128)(2,1)S(1)}, bf16[128,1024]{1,0:T(8,128)(2,1)S(1)}, u32[]{:S(2)}, u32[]{:S(2)}) collective-permute-start(bf16[128,1024]{1,0:T(8,128)(2,1)S(1)} %multiply_convert_fusion.refs_2_), channel_id=1, source_target_pairs={{0,15},{1,2},{2,1},{3,4},{4,3},{5,6},{6,5},{7,8},{8,7},{9,10},{10,... | collective-permute-start | bytes 786440 | tf_op jit(solution)/shard_map/ppermute | solution.py:349
  29.7 10.4 %collective-permute-start.4 = (bf16[128,1024]{1,0:T(8,128)(2,1)S(1)}, bf16[128,1024]{1,0:T(8,128)(2,1)S(1)}, u32[]{:S(2)}, u32[]{:S(2)}) collective-permute-start(bf16[128,1024]{1,0:T(8,128)(2,1)S(1)} %multiply_convert_fusion.refs_2_), channel_id=1, source_target_pairs={{0,1},{1,0},{2,3},{3,2},{4,5},{5,4},{6,7},{7,6},{8,9},{9,8},{10,11... | collective-permute-start | bytes 786440 | tf_op jit(solution)/shard_map/ppermute | solution.py:349
  31.8 18.8 %collective-permute-start.6 = (bf16[128,3200]{1,0:T(8,128)(2,1)S(1)}, bf16[128,3200]{1,0:T(8,128)(2,1)S(1)}, u32[]{:S(2)}, u32[]{:S(2)}) collective-permute-start(bf16[128,3200]{1,0:T(8,128)(2,1)S(1)} %pad_maximum_fusion.refs_7_), channel_id=1, source_target_pairs={{0,104},{16,400},{1,105},{17,401},{2,106},{18,402},{3,107},{19,403... | collective-permute-start | bytes 2457608 | tf_op jit(solution)/shard_map/ppermute | solution.py:371
  36.1 23.5 %collective-permute-start.5 = (bf16[128,3200]{1,0:T(8,128)(2,1)S(1)}, bf16[128,3200]{1,0:T(8,128)(2,1)}, u32[]{:S(2)}, u32[]{:S(2)}) collective-permute-start(bf16[128,3200]{1,0:T(8,128)(2,1)S(1)} %pad_maximum_fusion.refs_7_), channel_id=1, source_target_pairs={{0,32},{16,144},{1,33},{17,145},{2,34},{18,146},{3,35},{19,147},{4... | collective-permute-start | bytes 2457608 | tf_op jit(solution)/shard_map/ppermute | solution.py:371
  40.1 21.4 %collective-permute-start.7 = (bf16[128,3200]{1,0:T(8,128)(2,1)S(1)}, bf16[128,3200]{1,0:T(8,128)(2,1)}, u32[]{:S(2)}, u32[]{:S(2)}) collective-permute-start(bf16[128,3200]{1,0:T(8,128)(2,1)S(1)} %pad_maximum_fusion.refs_7_), channel_id=1, source_target_pairs={{0,64},{16,272},{1,65},{17,273},{2,66},{18,274},{3,67},{19,275},{4... | collective-permute-start | bytes 2457608 | tf_op jit(solution)/shard_map/ppermute | solution.py:371
  44.5 19.6 %collective-permute-start.8 = (bf16[128,3200]{1,0:T(8,128)(2,1)S(1)}, bf16[128,3200]{1,0:T(8,128)(2,1)}, u32[]{:S(2)}, u32[]{:S(2)}) collective-permute-start(bf16[128,3200]{1,0:T(8,128)(2,1)S(1)} %pad_maximum_fusion.refs_7_), channel_id=1, source_target_pairs={{0,16},{16,0},{1,17},{17,1},{2,18},{18,2},{3,19},{19,3},{4,20},{20... | collective-permute-start | bytes 2457608 | tf_op jit(solution)/shard_map/ppermute | solution.py:371
  50.5 13.6 %collective-permute-start.10 = (bf16[128,3200]{1,0:T(8,128)(2,1)S(1)}, bf16[128,3200]{1,0:T(8,128)(2,1)}, u32[]{:S(2)}, u32[]{:S(2)}) collective-permute-start(bf16[128,3200]{1,0:T(8,128)(2,1)S(1)} %collective-permute-done.6.refs_9_), channel_id=1, source_target_pairs={{0,16},{16,0},{1,17},{17,1},{2,18},{18,2},{3,19},{19,3},{4,20},{20... | collective-permute-start | bytes 2457608 | tf_op jit(solution)/shard_map/ppermute | solution.py:371
  59.6 4.6 %collective-permute-start.9 = (bf16[128,3200]{1,0:T(8,128)(2,1)}, bf16[128,3200]{1,0:T(8,128)(2,1)}, u32[]{:S(2)}, u32[]{:S(2)}) collective-permute-start(bf16[128,3200]{1,0:T(8,128)(2,1)} %collective-permute-done.5.refs_8_), channel_id=1, source_target_pairs={{0,16},{16,0},{1,17},{17,1},{2,18},{18,2},{3,19},{19,3},{4,20},{20... | collective-permute-start | bytes 2457608 | tf_op jit(solution)/shard_map/ppermute | solution.py:371
  61.6 4.7 %collective-permute-start.11 = (bf16[128,3200]{1,0:T(8,128)(2,1)}, bf16[128,3200]{1,0:T(8,128)(2,1)}, u32[]{:S(2)}, u32[]{:S(2)}) collective-permute-start(bf16[128,3200]{1,0:T(8,128)(2,1)} %collective-permute-done.7.refs_10_), channel_id=1, source_target_pairs={{0,16},{16,0},{1,17},{17,1},{2,18},{18,2},{3,19},{19,3},{4,20},{20... | collective-permute-start | bytes 2457608 | tf_op jit(solution)/shard_map/ppermute | solution.py:371
  75.1 26.9 %copy-start.4 = (f32[128]{0:T(128)S(1)}, f32[128]{0:T(128)}, u32[]{:S(2)}) copy-start(f32[128]{0:T(128)} %param.19) | copy-start | bytes 1540
  95.4 6.7 %collective-permute-start.12 = (bf16[16,112,128]{2,1,0:T(8,128)(2,1)S(1)}, bf16[16,112,128]{2,1,0:T(8,128)(2,1)S(1)}, u32[]{:S(2)}, u32[]{:S(2)}) collective-permute-start(bf16[16,112,128]{2,1,0:T(8,128)(2,1)S(1)} %all_to_all.21.refs_0_), channel_id=1, source_target_pairs={{0,16},{16,0},{1,17},{17,1},{2,18},{18,2},{3,19},{19,3},{4,20},{20... | collective-permute-start | bytes 1376264 | tf_op jit(solution)/shard_map/ppermute | solution.py:371
  104.0 16.2 %all-to-all-start.2 = ((bf16[32,32,128]{2,1,0:T(8,128)(2,1)}), bf16[32,32,128]{2,1,0:T(8,128)(2,1)S(1)}, u32[]{:S(2)}, u32[]{:S(2)}) async-start(bf16[32,32,128]{2,1,0:T(8,128)(2,1)} %bitcast.9), calls=%async_computation.2 | async-start | bytes 524288 | tf_op jit(solution)/shard_map/all_to_all | solution.py:506
  108.7 20.6 %collective-permute-start.13 = (bf16[192,128]{1,0:T(8,128)(2,1)S(1)}, bf16[192,128]{1,0:T(8,128)(2,1)S(1)}, u32[]{:S(2)}, u32[]{:S(2)}) collective-permute-start(bf16[192,128]{1,0:T(8,128)(2,1)S(1)} %get-tuple-element.29.refs_2_), channel_id=1, source_target_pairs={{0,15},{1,2},{2,1},{3,4},{4,3},{5,6},{6,5},{7,8},{8,7},{9,10},{10,... | collective-permute-start | bytes 147464 | tf_op jit(solution)/shard_map/ppermute | solution.py:349
  117.2 12.1 %collective-permute-start.14 = (bf16[192,128]{1,0:T(8,128)(2,1)S(1)}, bf16[192,128]{1,0:T(8,128)(2,1)S(1)}, u32[]{:S(2)}, u32[]{:S(2)}) collective-permute-start(bf16[192,128]{1,0:T(8,128)(2,1)S(1)} %get-tuple-element.29.refs_2_), channel_id=1, source_target_pairs={{0,1},{1,0},{2,3},{3,2},{4,5},{5,4},{6,7},{7,6},{8,9},{9,8},{10,11... | collective-permute-start | bytes 147464 | tf_op jit(solution)/shard_map/ppermute | solution.py:349
  121.0 19.8 %all-to-all-start.3 = ((bf16[16,32,128]{2,1,0:T(8,128)(2,1)}), bf16[16,32,128]{2,1,0:T(8,128)(2,1)S(1)}, u32[]{:S(2)}, u32[]{:S(2)}) async-start(bf16[16,32,128]{2,1,0:T(8,128)(2,1)} %middle.1), calls=%async_computation.3 | async-start | bytes 262144 | tf_op jit(solution)/shard_map/all_to_all | solution.py:517
  (4 other events, 74.0 us)

commit v11 on v10

--- a/solution.py
+++ b/solution.py
@@ -431,7 +431,8 @@
     normed = (xfield * inverse_rms * norm_gain).astype(b16)
     near, far = halos(normed)
     row = ring(packed, (0, 1))
-    *mine, near, far = ring(jnp.concatenate(row, 0), (1, 0), (near, far))
+    *mine, far = ring(jnp.concatenate(row, 0), (1, 0), (far,))
+    mine[3], near = lax.optimization_barrier((mine[3], near))
     pieces = mine + [swapped(piece) for piece in mine]
 
     packed_width = 3 * width + LANES

time: 143 us -> 145 us (1.014)
  starting transfers between devices: 77.4 us -> 87.2 us
  waiting for transfers between devices: 14.2 us -> 9.9 us
  blocking collectives: 20.2 us -> 16.6 us
    ppermute x11, starting transfers between devices: 43.8 us -> 58.4 us  [permute(): return lax.ppermute(value, ('ens', 'node'), pairs)]
    ppermute x11, waiting for transfers between devices: 10.4 us -> 5.68 us  [permute(): return lax.ppermute(value, ('ens', 'node'), pairs)]
    all_to_all x2, blocking collectives: 20.2 us -> 16.6 us  [everyone(): lax.all_to_all(spread, 'ens', 0, 0, tiled=True, axis_index_groups=groups)]
    all_to_all x1, starting transfers between devices: 8.37 us -> 5.49 us  [per_device(): parts = lax.all_to_all(spread, 'node', 0, 0, tiled=True)]
    all_to_all x1, waiting for transfers between devices: 1.01 us -> 3.5 us  [per_device(): lax.all_to_all(gram.reshape(members, rows, LANES), 'ens', 0, 0, tiled=True)]
    ppermute x4, waiting for transfers between devices: 2.06 us -> 0.01 us  [halos(): lax.ppermute(value, 'node', [(n, (n + (1 if n % 2 == odd else -1)) % coun...]
    ppermute x4, starting transfers between devices: 20.7 us -> 18.7 us  [halos(): lax.ppermute(value, 'node', [(n, (n + (1 if n % 2 == odd else -1)) % coun...]
  transfers between devices with their start and end apart: 17 -> 17, of which waited for: 6 -> 7; matrix products, arithmetic and copies ran while one was open for 2% -> 2% of each run, Pallas kernels for 8% -> 8%
where the time goes in v11:
time: 145 us; the launch traced here: 144 us
  starting transfers between devices  87.2 us (60%)
  Pallas kernels  23.1 us (16%)
  blocking collectives  16.6 us (11%)
  waiting for transfers between devices  9.9 us (7%)
  other arithmetic  3.52 us (2%)
    ppermute x11, starting transfers between devices, permute(): return lax.ppermute(value, ('ens', 'node'), pairs)  58.4 us
    ppermute x4, starting transfers between devices, halos(): lax.ppermute(value, 'node', [(n, (n + (1 if n % 2 == odd else -1)) % coun...  18.7 us
    all_to_all x2, blocking collectives, everyone(): lax.all_to_all(spread, 'ens', 0, 0, tiled=True, axis_index_groups=groups)  16.6 us
    pallas_call x1, Pallas kernels, per_device(): pl.pallas_call(lambda *refs: backward_kernel(scale, *refs), in_specs=[in_...  10.7 us
    pallas_call x1, Pallas kernels, per_device(): pl.pallas_call(lambda *refs: forward_kernel(scale, *refs), in_specs=[in_s...  8.83 us
    ppermute x11, waiting for transfers between devices, permute(): return lax.ppermute(value, ('ens', 'node'), pairs)  5.68 us
    all_to_all x1, starting transfers between devices, per_device(): parts = lax.all_to_all(spread, 'node', 0, 0, tiled=True)  5.49 us
    all_to_all x1, starting transfers between devices, per_device(): lax.all_to_all(gram.reshape(members, rows, LANES), 'ens', 0, 0, tiled=True)  4.69 us
  transfers between devices with their start and end apart: 17, of which 7 were waited for; matrix products, arithmetic and copies ran while one was open for 2% of the time, Pallas kernels for 8%

profile of v11, /device:TPU:1, one launch (start us, length us, event | category | flops | bytes accessed | tf_op | source)
XLA Modules:
  0.0 143.6 jit_solution(6477396283102050266)
XLA Ops:
  3.6 4.8 %collective-permute-start = (bf16[32,3200]{1,0:T(8,128)(2,1)S(1)}, bf16[32,3200]{1,0:T(8,128)(2,1)S(1)}, u32[]{:S(2)}, u32[]{:S(2)}) collective-permute-start(bf16[32,3200]{1,0:T(8,128)(2,1)S(1)} %pad_maximum_fusion.1), channel_id=1, source_target_pairs={{0,128},{16,48},{1,129},{17,49},{2,130},{18,50},{3,131},{19,51},{4... | collective-permute-start | bytes 614408 | tf_op jit(solution)/shard_map/ppermute | solution.py:371
  8.4 8.6 %collective-permute-start.1 = (bf16[32,3200]{1,0:T(8,128)(2,1)S(1)}, bf16[32,3200]{1,0:T(8,128)(2,1)S(1)}, u32[]{:S(2)}, u32[]{:S(2)}) collective-permute-start(bf16[32,3200]{1,0:T(8,128)(2,1)S(1)} %pad_maximum_fusion.1), channel_id=1, source_target_pairs={{0,384},{16,120},{1,385},{17,121},{2,386},{18,122},{3,387},{19,123... | collective-permute-start | bytes 614408 | tf_op jit(solution)/shard_map/ppermute | solution.py:371
  17.0 1.9 %collective-permute-start.2 = (bf16[32,3200]{1,0:T(8,128)(2,1)S(1)}, bf16[32,3200]{1,0:T(8,128)(2,1)S(1)}, u32[]{:S(2)}, u32[]{:S(2)}) collective-permute-start(bf16[32,3200]{1,0:T(8,128)(2,1)S(1)} %pad_maximum_fusion.1), channel_id=1, source_target_pairs={{0,256},{16,80},{1,257},{17,81},{2,258},{18,82},{3,259},{19,83},{4... | collective-permute-start | bytes 614408 | tf_op jit(solution)/shard_map/ppermute | solution.py:371
  21.4 3.2 %collective-permute-start.3 = (bf16[128,1024]{1,0:T(8,128)(2,1)S(1)}, bf16[128,1024]{1,0:T(8,128)(2,1)S(1)}, u32[]{:S(2)}, u32[]{:S(2)}) collective-permute-start(bf16[128,1024]{1,0:T(8,128)(2,1)S(1)} %multiply_convert_fusion.refs_2_), channel_id=1, source_target_pairs={{0,1},{1,0},{2,3},{3,2},{4,5},{5,4},{6,7},{7,6},{8,9},{9,8},{10,11... | collective-permute-start | bytes 786440 | tf_op jit(solution)/shard_map/ppermute | solution.py:349
  26.0 4.1 %collective-permute-start.7 = (bf16[128,3200]{1,0:T(8,128)(2,1)S(1)}, bf16[128,3200]{1,0:T(8,128)(2,1)S(1)}, u32[]{:S(2)}, u32[]{:S(2)}) collective-permute-start(bf16[128,3200]{1,0:T(8,128)(2,1)S(1)} %pad_maximum_fusion.refs_7_), channel_id=1, source_target_pairs={{0,104},{16,400},{1,105},{17,401},{2,106},{18,402},{3,107},{19,403... | collective-permute-start | bytes 2457608 | tf_op jit(solution)/shard_map/ppermute | solution.py:371
  30.1 1.9 %collective-permute-start.6 = (bf16[128,3200]{1,0:T(8,128)(2,1)S(1)}, bf16[128,3200]{1,0:T(8,128)(2,1)}, u32[]{:S(2)}, u32[]{:S(2)}) collective-permute-start(bf16[128,3200]{1,0:T(8,128)(2,1)S(1)} %pad_maximum_fusion.refs_7_), channel_id=1, source_target_pairs={{0,32},{16,144},{1,33},{17,145},{2,34},{18,146},{3,35},{19,147},{4... | collective-permute-start | bytes 2457608 | tf_op jit(solution)/shard_map/ppermute | solution.py:371
  32.0 3.6 %collective-permute-start.4 = (bf16[128,3200]{1,0:T(8,128)(2,1)S(1)}, bf16[128,3200]{1,0:T(8,128)(2,1)}, u32[]{:S(2)}, u32[]{:S(2)}) collective-permute-start(bf16[128,3200]{1,0:T(8,128)(2,1)S(1)} %pad_maximum_fusion.refs_7_), channel_id=1, source_target_pairs={{0,64},{16,272},{1,65},{17,273},{2,66},{18,274},{3,67},{19,275},{4... | collective-permute-start | bytes 2457608 | tf_op jit(solution)/shard_map/ppermute | solution.py:371
  35.7 7.5 %collective-permute-start.5 = (bf16[128,1024]{1,0:T(8,128)(2,1)S(1)}, bf16[128,1024]{1,0:T(8,128)(2,1)S(1)}, u32[]{:S(2)}, u32[]{:S(2)}) collective-permute-start(bf16[128,1024]{1,0:T(8,128)(2,1)S(1)} %multiply_convert_fusion.refs_2_), channel_id=1, source_target_pairs={{0,15},{1,2},{2,1},{3,4},{4,3},{5,6},{6,5},{7,8},{8,7},{9,10},{10,... | collective-permute-start | bytes 786440 | tf_op jit(solution)/shard_map/ppermute | solution.py:349
  43.2 4.4 %collective-permute-start.8 = (bf16[128,3200]{1,0:T(8,128)(2,1)S(1)}, bf16[128,3200]{1,0:T(8,128)(2,1)}, u32[]{:S(2)}, u32[]{:S(2)}) collective-permute-start(bf16[128,3200]{1,0:T(8,128)(2,1)S(1)} %pad_maximum_fusion.refs_7_), channel_id=1, source_target_pairs={{0,16},{16,0},{1,17},{17,1},{2,18},{18,2},{3,19},{19,3},{4,20},{20... | collective-permute-start | bytes 2457608 | tf_op jit(solution)/shard_map/ppermute | solution.py:371
  48.1 16.5 %collective-permute-start.10 = (bf16[128,3200]{1,0:T(8,128)(2,1)S(1)}, bf16[128,3200]{1,0:T(8,128)(2,1)}, u32[]{:S(2)}, u32[]{:S(2)}) collective-permute-start(bf16[128,3200]{1,0:T(8,128)(2,1)S(1)} %collective-permute-done.7.refs_9_), channel_id=1, source_target_pairs={{0,16},{16,0},{1,17},{17,1},{2,18},{18,2},{3,19},{19,3},{4,20},{20... | collective-permute-start | bytes 2457608 | tf_op jit(solution)/shard_map/ppermute | solution.py:371
  64.7 5.7 %collective-permute-start.9 = (bf16[128,3200]{1,0:T(8,128)(2,1)}, bf16[128,3200]{1,0:T(8,128)(2,1)}, u32[]{:S(2)}, u32[]{:S(2)}) collective-permute-start(bf16[128,3200]{1,0:T(8,128)(2,1)} %collective-permute-done.6.refs_8_), channel_id=1, source_target_pairs={{0,16},{16,0},{1,17},{17,1},{2,18},{18,2},{3,19},{19,3},{4,20},{20... | collective-permute-start | bytes 2457608 | tf_op jit(solution)/shard_map/ppermute | solution.py:371
  70.4 1.9 %collective-permute-start.11 = (bf16[128,3200]{1,0:T(8,128)(2,1)}, bf16[128,3200]{1,0:T(8,128)(2,1)}, u32[]{:S(2)}, u32[]{:S(2)}) collective-permute-start(bf16[128,3200]{1,0:T(8,128)(2,1)} %collective-permute-done.4.refs_10_), channel_id=1, source_target_pairs={{0,16},{16,0},{1,17},{17,1},{2,18},{18,2},{3,19},{19,3},{4,20},{20... | collective-permute-start | bytes 2457608 | tf_op jit(solution)/shard_map/ppermute | solution.py:371
  72.6 2.3 %collective-permute-done.11.refs_14_ = bf16[128,3200]{1,0:T(8,128)(2,1)} collective-permute-done((bf16[128,3200]{1,0:T(8,128)(2,1)}, bf16[128,3200]{1,0:T(8,128)(2,1)}, u32[]{:S(2)}, u32[]{:S(2)}) %collective-permute-start.11) | collective-permute-done | bytes 819232 | tf_op jit(solution)/shard_map/ppermute | solution.py:371
  75.0 8.8 %forward.1 = (bf16[384,1024]{1,0:T(8,128)(2,1)}, bf16[384,1024]{1,0:T(8,128)(2,1)}, bf16[384,1024]{1,0:T(8,128)(2,1)}, bf16[128,1024]{1,0:T(8,128)(2,1)S(1)}, f3...) custom-call(s32[4]{0:T(128)S(1)} %pad_add_fusion.refs_0_, ...), custom_call_target="tpu_custom_call" | custom-call | flops 8999999488 | bytes 27000000 | tf_op jit(solution)/shard_map/forward/pallas_call | solution.py:446
  83.8 7.3 %all_to_all.20 = bf16[4,112,128]{2,1,0:T(8,128)(2,1)S(1)} all-to-all(bf16[4,112,128]{2,1,0:T(8,128)(2,1)S(1)} %reshape.43), channel_id=1, replica_groups={{0,32,64,96},{128,160,192,224},{256,288,320,352},{384,416,448,480},{16,..., dimensions={0} | all-to-all | bytes 229376 | tf_op jit(solution)/shard_map/all_to_all | solution.py:395
  91.3 9.3 %all_to_all.21.refs_0_ = bf16[16,112,128]{2,1,0:T(8,128)(2,1)S(1)} all-to-all(bf16[16,112,128]{2,1,0:T(8,128)(2,1)S(1)} %bitcast.22), channel_id=1, replica_groups={{0,128,256,384},{32,160,288,416},{64,192,320,448},{96,224,352,480},{16,..., dimensions={0} | all-to-all | bytes 917504 | tf_op jit(solution)/shard_map/all_to_all | solution.py:395
  100.5 4.9 %collective-permute-start.12 = (bf16[16,112,128]{2,1,0:T(8,128)(2,1)S(1)}, bf16[16,112,128]{2,1,0:T(8,128)(2,1)S(1)}, u32[]{:S(2)}, u32[]{:S(2)}) collective-permute-start(bf16[16,112,128]{2,1,0:T(8,128)(2,1)S(1)} %all_to_all.21.refs_0_), channel_id=1, source_target_pairs={{0,16},{16,0},{1,17},{17,1},{2,18},{18,2},{3,19},{19,3},{4,20},{20... | collective-permute-start | bytes 1376264 | tf_op jit(solution)/shard_map/ppermute | solution.py:371
  106.8 2.0 %crps.1 = (bf16[1024,128]{1,0:T(8,128)(2,1)}, bf16[192,128]{1,0:T(8,128)(2,1)S(1)}) custom-call(bf16[16,112,128]{2,1,0:T(8,128)(2,1)S(1)} %all_to_all.21.refs_0_, bf16[16,112,128]{2,1,0:T(8,128)(2,1)S(1)} %collective-permute-done.12.refs_1_, bf16[112,128]{1,0:T(8,128)(2,1)S(1)} %get-tuple-element.25.refs_2_, bf16[112,128]{1,0:T(8,128)(2,1)S(1)} %pad.9.refs_3_, ...), custom_call_target="tpu_custom_call" | custom-call | flops 3000000000 | bytes 9000000 | tf_op jit(solution)/shard_map/crps/pallas_call | solution.py:480
  108.8 4.7 %all-to-all-start.2 = ((bf16[32,32,128]{2,1,0:T(8,128)(2,1)}), bf16[32,32,128]{2,1,0:T(8,128)(2,1)S(1)}, u32[]{:S(2)}, u32[]{:S(2)}) async-start(bf16[32,32,128]{2,1,0:T(8,128)(2,1)} %bitcast.9), calls=%async_computation.2 | async-start | bytes 524288 | tf_op jit(solution)/shard_map/all_to_all | solution.py:507
  113.6 6.0 %collective-permute-start.13 = (bf16[192,128]{1,0:T(8,128)(2,1)S(1)}, bf16[192,128]{1,0:T(8,128)(2,1)S(1)}, u32[]{:S(2)}, u32[]{:S(2)}) collective-permute-start(bf16[192,128]{1,0:T(8,128)(2,1)S(1)} %get-tuple-element.31.refs_2_), channel_id=1, source_target_pairs={{0,15},{1,2},{2,1},{3,4},{4,3},{5,6},{6,5},{7,8},{8,7},{9,10},{10,... | collective-permute-start | bytes 147464 | tf_op jit(solution)/shard_map/ppermute | solution.py:349
  119.6 1.9 %collective-permute-start.14 = (bf16[192,128]{1,0:T(8,128)(2,1)S(1)}, bf16[192,128]{1,0:T(8,128)(2,1)S(1)}, u32[]{:S(2)}, u32[]{:S(2)}) collective-permute-start(bf16[192,128]{1,0:T(8,128)(2,1)S(1)} %get-tuple-element.31.refs_2_), channel_id=1, source_target_pairs={{0,1},{1,0},{2,3},{3,2},{4,5},{5,4},{6,7},{7,6},{8,9},{9,8},{10,11... | collective-permute-start | bytes 147464 | tf_op jit(solution)/shard_map/ppermute | solution.py:349
  121.5 3.5 %all-to-all-done.2.refs_0_ = bf16[32,32,128]{2,1,0:T(8,128)(2,1)S(1)} async-done(((bf16[32,32,128]{2,1,0:T(8,128)(2,1)}), bf16[32,32,128]{2,1,0:T(8,128)(2,1)S(1)}, u32[]{:S(2)}, u32[]{:S(2)}) %all-to-all-start.2) | async-done | bytes 262176 | tf_op jit(solution)/shard_map/all_to_all | solution.py:507
  125.8 5.5 %all-to-all-start.3 = ((bf16[16,32,128]{2,1,0:T(8,128)(2,1)}), bf16[16,32,128]{2,1,0:T(8,128)(2,1)S(1)}, u32[]{:S(2)}, u32[]{:S(2)}) async-start(bf16[16,32,128]{2,1,0:T(8,128)(2,1)} %middle.1), calls=%async_computation.3 | async-start | bytes 262144 | tf_op jit(solution)/shard_map/all_to_all | solution.py:518
  131.4 10.7 %backward.1 = bf16[1,128,1024]{2,1,0:T(8,128)(2,1)} custom-call(s32[4]{0:T(128)S(1)} %pad_add_fusion.refs_0_, bf16[192,128]{1,0:T(8,128)(2,1)S(1)} %collective-permute-done.13.refs_1_, bf16[192,128]{1,0:T(8,128)(2,1)S(1)} %get-tuple-element.31.refs_2_, bf16[192,128]{1,0:T(8,128)(2,1)S(1)} %collective-permute-done.14.refs_3_, ...), custom_call_target="tpu_custom_call" | custom-call | flops 12000000000 | bytes 36000000 | tf_op jit(solution)/shard_map/backward/pallas_call | solution.py:530
  (51 shorter events, 11.4 us)
Async XLA Ops:
  0.6 25.3 %copy-start.9 = (bf16[32,1024]{1,0:T(8,128)(2,1)S(1)}, bf16[32,1024]{1,0:T(8,128)(2,1)}, u32[]{:S(2)}) copy-start(bf16[32,1024]{1,0:T(8,128)(2,1)} %param.13) | copy-start | bytes 196612
  0.7 25.3 %copy-start.8 = (bf16[32,1024]{1,0:T(8,128)(2,1)S(1)}, bf16[32,1024]{1,0:T(8,128)(2,1)}, u32[]{:S(2)}) copy-start(bf16[32,1024]{1,0:T(8,128)(2,1)} %param.14) | copy-start | bytes 196612
  0.7 25.2 %copy-start.7 = (bf16[32,1024]{1,0:T(8,128)(2,1)S(1)}, bf16[32,1024]{1,0:T(8,128)(2,1)}, u32[]{:S(2)}) copy-start(bf16[32,1024]{1,0:T(8,128)(2,1)} %param.15) | copy-start | bytes 196612
  2.6 69.8 %copy-start.6 = (bf16[1024,100]{0,1:T(8,128)(2,1)S(1)}, bf16[1024,100]{0,1:T(8,128)(2,1)}, u32[]{:S(2)}) copy-start(bf16[1024,100]{0,1:T(8,128)(2,1)} %param.17) | copy-start | bytes 614404
  3.6 21.0 %collective-permute-start = (bf16[32,3200]{1,0:T(8,128)(2,1)S(1)}, bf16[32,3200]{1,0:T(8,128)(2,1)S(1)}, u32[]{:S(2)}, u32[]{:S(2)}) collective-permute-start(bf16[32,3200]{1,0:T(8,128)(2,1)S(1)} %pad_maximum_fusion.1), channel_id=1, source_target_pairs={{0,128},{16,48},{1,129},{17,49},{2,130},{18,50},{3,131},{19,51},{4... | collective-permute-start | bytes 614408 | tf_op jit(solution)/shard_map/ppermute | solution.py:371
  8.4 16.2 %collective-permute-start.1 = (bf16[32,3200]{1,0:T(8,128)(2,1)S(1)}, bf16[32,3200]{1,0:T(8,128)(2,1)S(1)}, u32[]{:S(2)}, u32[]{:S(2)}) collective-permute-start(bf16[32,3200]{1,0:T(8,128)(2,1)S(1)} %pad_maximum_fusion.1), channel_id=1, source_target_pairs={{0,384},{16,120},{1,385},{17,121},{2,386},{18,122},{3,387},{19,123... | collective-permute-start | bytes 614408 | tf_op jit(solution)/shard_map/ppermute | solution.py:371
  17.0 8.9 %collective-permute-start.2 = (bf16[32,3200]{1,0:T(8,128)(2,1)S(1)}, bf16[32,3200]{1,0:T(8,128)(2,1)S(1)}, u32[]{:S(2)}, u32[]{:S(2)}) collective-permute-start(bf16[32,3200]{1,0:T(8,128)(2,1)S(1)} %pad_maximum_fusion.1), channel_id=1, source_target_pairs={{0,256},{16,80},{1,257},{17,81},{2,258},{18,82},{3,259},{19,83},{4... | collective-permute-start | bytes 614408 | tf_op jit(solution)/shard_map/ppermute | solution.py:371
  20.1 54.8 %copy-start.1 = (bf16[128,1024]{1,0:T(8,128)(2,1)S(1)}, bf16[128,1024]{1,0:T(8,128)(2,1)}, u32[]{:S(2)}) copy-start(bf16[128,1024]{1,0:T(8,128)(2,1)} %refs_5_.3) | copy-start | bytes 786436
  20.1 54.8 %copy-start.2 = (bf16[1,128,1024]{2,1,0:T(8,128)(2,1)S(1)}, bf16[1,128,1024]{2,1,0:T(8,128)(2,1)}, u32[]{:S(2)}) copy-start(bf16[1,128,1024]{2,1,0:T(8,128)(2,1)} %refs_4_.3) | copy-start | bytes 786436
  21.4 10.7 %collective-permute-start.3 = (bf16[128,1024]{1,0:T(8,128)(2,1)S(1)}, bf16[128,1024]{1,0:T(8,128)(2,1)S(1)}, u32[]{:S(2)}, u32[]{:S(2)}) collective-permute-start(bf16[128,1024]{1,0:T(8,128)(2,1)S(1)} %multiply_convert_fusion.refs_2_), channel_id=1, source_target_pairs={{0,1},{1,0},{2,3},{3,2},{4,5},{5,4},{6,7},{7,6},{8,9},{9,8},{10,11... | collective-permute-start | bytes 786440 | tf_op jit(solution)/shard_map/ppermute | solution.py:349
  26.0 22.1 %collective-permute-start.7 = (bf16[128,3200]{1,0:T(8,128)(2,1)S(1)}, bf16[128,3200]{1,0:T(8,128)(2,1)S(1)}, u32[]{:S(2)}, u32[]{:S(2)}) collective-permute-start(bf16[128,3200]{1,0:T(8,128)(2,1)S(1)} %pad_maximum_fusion.refs_7_), channel_id=1, source_target_pairs={{0,104},{16,400},{1,105},{17,401},{2,106},{18,402},{3,107},{19,403... | collective-permute-start | bytes 2457608 | tf_op jit(solution)/shard_map/ppermute | solution.py:371
  30.1 34.6 %collective-permute-start.6 = (bf16[128,3200]{1,0:T(8,128)(2,1)S(1)}, bf16[128,3200]{1,0:T(8,128)(2,1)}, u32[]{:S(2)}, u32[]{:S(2)}) collective-permute-start(bf16[128,3200]{1,0:T(8,128)(2,1)S(1)} %pad_maximum_fusion.refs_7_), channel_id=1, source_target_pairs={{0,32},{16,144},{1,33},{17,145},{2,34},{18,146},{3,35},{19,147},{4... | collective-permute-start | bytes 2457608 | tf_op jit(solution)/shard_map/ppermute | solution.py:371
  32.0 38.3 %collective-permute-start.4 = (bf16[128,3200]{1,0:T(8,128)(2,1)S(1)}, bf16[128,3200]{1,0:T(8,128)(2,1)}, u32[]{:S(2)}, u32[]{:S(2)}) collective-permute-start(bf16[128,3200]{1,0:T(8,128)(2,1)S(1)} %pad_maximum_fusion.refs_7_), channel_id=1, source_target_pairs={{0,64},{16,272},{1,65},{17,273},{2,66},{18,274},{3,67},{19,275},{4... | collective-permute-start | bytes 2457608 | tf_op jit(solution)/shard_map/ppermute | solution.py:371
  35.7 34.7 %collective-permute-start.5 = (bf16[128,1024]{1,0:T(8,128)(2,1)S(1)}, bf16[128,1024]{1,0:T(8,128)(2,1)S(1)}, u32[]{:S(2)}, u32[]{:S(2)}) collective-permute-start(bf16[128,1024]{1,0:T(8,128)(2,1)S(1)} %multiply_convert_fusion.refs_2_), channel_id=1, source_target_pairs={{0,15},{1,2},{2,1},{3,4},{4,3},{5,6},{6,5},{7,8},{8,7},{9,10},{10,... | collective-permute-start | bytes 786440 | tf_op jit(solution)/shard_map/ppermute | solution.py:349
  43.2 29.3 %collective-permute-start.8 = (bf16[128,3200]{1,0:T(8,128)(2,1)S(1)}, bf16[128,3200]{1,0:T(8,128)(2,1)}, u32[]{:S(2)}, u32[]{:S(2)}) collective-permute-start(bf16[128,3200]{1,0:T(8,128)(2,1)S(1)} %pad_maximum_fusion.refs_7_), channel_id=1, source_target_pairs={{0,16},{16,0},{1,17},{17,1},{2,18},{18,2},{3,19},{19,3},{4,20},{20... | collective-permute-start | bytes 2457608 | tf_op jit(solution)/shard_map/ppermute | solution.py:371
  48.1 24.4 %collective-permute-start.10 = (bf16[128,3200]{1,0:T(8,128)(2,1)S(1)}, bf16[128,3200]{1,0:T(8,128)(2,1)}, u32[]{:S(2)}, u32[]{:S(2)}) collective-permute-start(bf16[128,3200]{1,0:T(8,128)(2,1)S(1)} %collective-permute-done.7.refs_9_), channel_id=1, source_target_pairs={{0,16},{16,0},{1,17},{17,1},{2,18},{18,2},{3,19},{19,3},{4,20},{20... | collective-permute-start | bytes 2457608 | tf_op jit(solution)/shard_map/ppermute | solution.py:371
  64.7 8.0 %collective-permute-start.9 = (bf16[128,3200]{1,0:T(8,128)(2,1)}, bf16[128,3200]{1,0:T(8,128)(2,1)}, u32[]{:S(2)}, u32[]{:S(2)}) collective-permute-start(bf16[128,3200]{1,0:T(8,128)(2,1)} %collective-permute-done.6.refs_8_), channel_id=1, source_target_pairs={{0,16},{16,0},{1,17},{17,1},{2,18},{18,2},{3,19},{19,3},{4,20},{20... | collective-permute-start | bytes 2457608 | tf_op jit(solution)/shard_map/ppermute | solution.py:371
  70.4 4.6 %collective-permute-start.11 = (bf16[128,3200]{1,0:T(8,128)(2,1)}, bf16[128,3200]{1,0:T(8,128)(2,1)}, u32[]{:S(2)}, u32[]{:S(2)}) collective-permute-start(bf16[128,3200]{1,0:T(8,128)(2,1)} %collective-permute-done.4.refs_10_), channel_id=1, source_target_pairs={{0,16},{16,0},{1,17},{17,1},{2,18},{18,2},{3,19},{19,3},{4,20},{20... | collective-permute-start | bytes 2457608 | tf_op jit(solution)/shard_map/ppermute | solution.py:371
  83.8 23.0 %copy-start.4 = (f32[128]{0:T(128)S(1)}, f32[128]{0:T(128)}, u32[]{:S(2)}) copy-start(f32[128]{0:T(128)} %param.19) | copy-start | bytes 1540
  100.5 6.3 %collective-permute-start.12 = (bf16[16,112,128]{2,1,0:T(8,128)(2,1)S(1)}, bf16[16,112,128]{2,1,0:T(8,128)(2,1)S(1)}, u32[]{:S(2)}, u32[]{:S(2)}) collective-permute-start(bf16[16,112,128]{2,1,0:T(8,128)(2,1)S(1)} %all_to_all.21.refs_0_), channel_id=1, source_target_pairs={{0,16},{16,0},{1,17},{17,1},{2,18},{18,2},{3,19},{19,3},{4,20},{20... | collective-permute-start | bytes 1376264 | tf_op jit(solution)/shard_map/ppermute | solution.py:371
  108.8 16.3 %all-to-all-start.2 = ((bf16[32,32,128]{2,1,0:T(8,128)(2,1)}), bf16[32,32,128]{2,1,0:T(8,128)(2,1)S(1)}, u32[]{:S(2)}, u32[]{:S(2)}) async-start(bf16[32,32,128]{2,1,0:T(8,128)(2,1)} %bitcast.9), calls=%async_computation.2 | async-start | bytes 524288 | tf_op jit(solution)/shard_map/all_to_all | solution.py:507
  113.6 17.8 %collective-permute-start.13 = (bf16[192,128]{1,0:T(8,128)(2,1)S(1)}, bf16[192,128]{1,0:T(8,128)(2,1)S(1)}, u32[]{:S(2)}, u32[]{:S(2)}) collective-permute-start(bf16[192,128]{1,0:T(8,128)(2,1)S(1)} %get-tuple-element.31.refs_2_), channel_id=1, source_target_pairs={{0,15},{1,2},{2,1},{3,4},{4,3},{5,6},{6,5},{7,8},{8,7},{9,10},{10,... | collective-permute-start | bytes 147464 | tf_op jit(solution)/shard_map/ppermute | solution.py:349
  119.6 11.7 %collective-permute-start.14 = (bf16[192,128]{1,0:T(8,128)(2,1)S(1)}, bf16[192,128]{1,0:T(8,128)(2,1)S(1)}, u32[]{:S(2)}, u32[]{:S(2)}) collective-permute-start(bf16[192,128]{1,0:T(8,128)(2,1)S(1)} %get-tuple-element.31.refs_2_), channel_id=1, source_target_pairs={{0,1},{1,0},{2,3},{3,2},{4,5},{5,4},{6,7},{7,6},{8,9},{9,8},{10,11... | collective-permute-start | bytes 147464 | tf_op jit(solution)/shard_map/ppermute | solution.py:349
  125.8 16.9 %all-to-all-start.3 = ((bf16[16,32,128]{2,1,0:T(8,128)(2,1)}), bf16[16,32,128]{2,1,0:T(8,128)(2,1)S(1)}, u32[]{:S(2)}, u32[]{:S(2)}) async-start(bf16[16,32,128]{2,1,0:T(8,128)(2,1)} %middle.1), calls=%async_computation.3 | async-start | bytes 262144 | tf_op jit(solution)/shard_map/all_to_all | solution.py:518
  (4 other events, 63.2 us)

commit v12 on v10

--- a/solution.py
+++ b/solution.py
@@ -372,13 +372,13 @@
 
 
 def ring(value, along, before=()):
-    out = [value]
-    for hop in (1, -1, -2):
-        if hop == -2 and before:
+    blocks = {0: value}
+    for hop in (-2, 1, -1):
+        if hop == -1 and before:
             value, *before = lax.optimization_barrier((value, *before))
         moves = [(hop, 0, 0) if axis == 0 else (0, hop, 0) for axis in along]
-        out.append(permute(value, moves))
-    return out + list(before)
+        blocks[hop] = permute(value, moves)
+    return [blocks[0], blocks[1], blocks[-1], blocks[-2], *before]
 
 
 def swapped(value):

time: 143 us -> 141 us (0.986)
  starting transfers between devices: 77.4 us -> 83.9 us
  waiting for transfers between devices: 14.2 us -> 8.46 us
  blocking collectives: 20.2 us -> 17.9 us
    ppermute x11, starting transfers between devices: 43.8 us -> 52.2 us  [permute(): return lax.ppermute(value, ('ens', 'node'), pairs)]
    ppermute x11, waiting for transfers between devices: 10.4 us -> 4.44 us  [permute(): return lax.ppermute(value, ('ens', 'node'), pairs)]
    all_to_all x2, blocking collectives: 20.2 us -> 17.9 us  [everyone(): lax.all_to_all(spread, 'ens', 0, 0, tiled=True, axis_index_groups=groups)]
  transfers between devices with their start and end apart: 17 -> 17, of which waited for: 6 -> 7; matrix products, arithmetic and copies ran while one was open for 2% -> 2% of each run, Pallas kernels for 8% -> 8%
where the time goes in v12:
time: 141 us; the launch traced here: 140 us
  starting transfers between devices  83.9 us (60%)
  Pallas kernels  23.1 us (16%)
  blocking collectives  17.9 us (13%)
  waiting for transfers between devices  8.46 us (6%)
  other arithmetic  3.52 us (2%)
    ppermute x11, starting transfers between devices, permute(): return lax.ppermute(value, ('ens', 'node'), pairs)  52.2 us
    ppermute x4, starting transfers between devices, halos(): lax.ppermute(value, 'node', [(n, (n + (1 if n % 2 == odd else -1)) % coun...  19.9 us
    all_to_all x2, blocking collectives, everyone(): lax.all_to_all(spread, 'ens', 0, 0, tiled=True, axis_index_groups=groups)  17.9 us
    pallas_call x1, Pallas kernels, per_device(): pl.pallas_call(lambda *refs: backward_kernel(scale, *refs), in_specs=[in_...  10.7 us
    pallas_call x1, Pallas kernels, per_device(): pl.pallas_call(lambda *refs: forward_kernel(scale, *refs), in_specs=[in_s...  8.83 us
    all_to_all x1, starting transfers between devices, per_device(): parts = lax.all_to_all(spread, 'node', 0, 0, tiled=True)  7.18 us
    all_to_all x1, starting transfers between devices, per_device(): lax.all_to_all(gram.reshape(members, rows, LANES), 'ens', 0, 0, tiled=True)  4.59 us
    ppermute x11, waiting for transfers between devices, permute(): return lax.ppermute(value, ('ens', 'node'), pairs)  4.44 us
  transfers between devices with their start and end apart: 17, of which 7 were waited for; matrix products, arithmetic and copies ran while one was open for 2% of the time, Pallas kernels for 8%

profile of v12, /device:TPU:1, one launch (start us, length us, event | category | flops | bytes accessed | tf_op | source)
XLA Modules:
  0.0 140.1 jit_solution(16373667303597323273)
XLA Ops:
  3.6 4.8 %collective-permute-start = (bf16[32,3200]{1,0:T(8,128)(2,1)S(1)}, bf16[32,3200]{1,0:T(8,128)(2,1)S(1)}, u32[]{:S(2)}, u32[]{:S(2)}) collective-permute-start(bf16[32,3200]{1,0:T(8,128)(2,1)S(1)} %pad_maximum_fusion.1), channel_id=1, source_target_pairs={{0,128},{16,48},{1,129},{17,49},{2,130},{18,50},{3,131},{19,51},{4... | collective-permute-start | bytes 614408 | tf_op jit(solution)/shard_map/ppermute | solution.py:371
  8.4 8.6 %collective-permute-start.1 = (bf16[32,3200]{1,0:T(8,128)(2,1)S(1)}, bf16[32,3200]{1,0:T(8,128)(2,1)S(1)}, u32[]{:S(2)}, u32[]{:S(2)}) collective-permute-start(bf16[32,3200]{1,0:T(8,128)(2,1)S(1)} %pad_maximum_fusion.1), channel_id=1, source_target_pairs={{0,384},{16,120},{1,385},{17,121},{2,386},{18,122},{3,387},{19,123... | collective-permute-start | bytes 614408 | tf_op jit(solution)/shard_map/ppermute | solution.py:371
  17.0 1.9 %collective-permute-start.2 = (bf16[32,3200]{1,0:T(8,128)(2,1)S(1)}, bf16[32,3200]{1,0:T(8,128)(2,1)S(1)}, u32[]{:S(2)}, u32[]{:S(2)}) collective-permute-start(bf16[32,3200]{1,0:T(8,128)(2,1)S(1)} %pad_maximum_fusion.1), channel_id=1, source_target_pairs={{0,256},{16,80},{1,257},{17,81},{2,258},{18,82},{3,259},{19,83},{4... | collective-permute-start | bytes 614408 | tf_op jit(solution)/shard_map/ppermute | solution.py:371
  21.4 8.3 %collective-permute-start.3 = (bf16[128,1024]{1,0:T(8,128)(2,1)S(1)}, bf16[128,1024]{1,0:T(8,128)(2,1)S(1)}, u32[]{:S(2)}, u32[]{:S(2)}) collective-permute-start(bf16[128,1024]{1,0:T(8,128)(2,1)S(1)} %multiply_convert_fusion.refs_2_), channel_id=1, source_target_pairs={{0,15},{1,2},{2,1},{3,4},{4,3},{5,6},{6,5},{7,8},{8,7},{9,10},{10,... | collective-permute-start | bytes 786440 | tf_op jit(solution)/shard_map/ppermute | solution.py:349
  29.7 1.9 %collective-permute-start.4 = (bf16[128,1024]{1,0:T(8,128)(2,1)S(1)}, bf16[128,1024]{1,0:T(8,128)(2,1)S(1)}, u32[]{:S(2)}, u32[]{:S(2)}) collective-permute-start(bf16[128,1024]{1,0:T(8,128)(2,1)S(1)} %multiply_convert_fusion.refs_2_), channel_id=1, source_target_pairs={{0,1},{1,0},{2,3},{3,2},{4,5},{5,4},{6,7},{7,6},{8,9},{9,8},{10,11... | collective-permute-start | bytes 786440 | tf_op jit(solution)/shard_map/ppermute | solution.py:349
  31.8 4.7 %collective-permute-start.7 = (bf16[128,3200]{1,0:T(8,128)(2,1)S(1)}, bf16[128,3200]{1,0:T(8,128)(2,1)S(1)}, u32[]{:S(2)}, u32[]{:S(2)}) collective-permute-start(bf16[128,3200]{1,0:T(8,128)(2,1)S(1)} %pad_maximum_fusion.refs_7_), channel_id=1, source_target_pairs={{0,64},{16,272},{1,65},{17,273},{2,66},{18,274},{3,67},{19,275},{4... | collective-permute-start | bytes 2457608 | tf_op jit(solution)/shard_map/ppermute | solution.py:371
  36.4 2.2 %collective-permute-start.5 = (bf16[128,3200]{1,0:T(8,128)(2,1)S(1)}, bf16[128,3200]{1,0:T(8,128)(2,1)}, u32[]{:S(2)}, u32[]{:S(2)}) collective-permute-start(bf16[128,3200]{1,0:T(8,128)(2,1)S(1)} %pad_maximum_fusion.refs_7_), channel_id=1, source_target_pairs={{0,32},{16,144},{1,33},{17,145},{2,34},{18,146},{3,35},{19,147},{4... | collective-permute-start | bytes 2457608 | tf_op jit(solution)/shard_map/ppermute | solution.py:371
  40.1 6.9 %collective-permute-start.6 = (bf16[128,3200]{1,0:T(8,128)(2,1)S(1)}, bf16[128,3200]{1,0:T(8,128)(2,1)}, u32[]{:S(2)}, u32[]{:S(2)}) collective-permute-start(bf16[128,3200]{1,0:T(8,128)(2,1)S(1)} %pad_maximum_fusion.refs_7_), channel_id=1, source_target_pairs={{0,104},{16,400},{1,105},{17,401},{2,106},{18,402},{3,107},{19,403... | collective-permute-start | bytes 2457608 | tf_op jit(solution)/shard_map/ppermute | solution.py:371
  47.1 2.7 %collective-permute-start.8 = (bf16[128,3200]{1,0:T(8,128)(2,1)S(1)}, bf16[128,3200]{1,0:T(8,128)(2,1)}, u32[]{:S(2)}, u32[]{:S(2)}) collective-permute-start(bf16[128,3200]{1,0:T(8,128)(2,1)S(1)} %pad_maximum_fusion.refs_7_), channel_id=1, source_target_pairs={{0,16},{16,0},{1,17},{17,1},{2,18},{18,2},{3,19},{19,3},{4,20},{20... | collective-permute-start | bytes 2457608 | tf_op jit(solution)/shard_map/ppermute | solution.py:371
  49.8 5.1 %collective-permute-start.11 = (bf16[128,3200]{1,0:T(8,128)(2,1)S(1)}, bf16[128,3200]{1,0:T(8,128)(2,1)}, u32[]{:S(2)}, u32[]{:S(2)}) collective-permute-start(bf16[128,3200]{1,0:T(8,128)(2,1)S(1)} %collective-permute-done.7.refs_10_), channel_id=1, source_target_pairs={{0,16},{16,0},{1,17},{17,1},{2,18},{18,2},{3,19},{19,3},{4,20},{20... | collective-permute-start | bytes 2457608 | tf_op jit(solution)/shard_map/ppermute | solution.py:371
  55.5 8.2 %collective-permute-start.9 = (bf16[128,3200]{1,0:T(8,128)(2,1)}, bf16[128,3200]{1,0:T(8,128)(2,1)}, u32[]{:S(2)}, u32[]{:S(2)}) collective-permute-start(bf16[128,3200]{1,0:T(8,128)(2,1)} %collective-permute-done.5.refs_8_), channel_id=1, source_target_pairs={{0,16},{16,0},{1,17},{17,1},{2,18},{18,2},{3,19},{19,3},{4,20},{20... | collective-permute-start | bytes 2457608 | tf_op jit(solution)/shard_map/ppermute | solution.py:371
  63.7 1.9 %collective-permute-start.10 = (bf16[128,3200]{1,0:T(8,128)(2,1)}, bf16[128,3200]{1,0:T(8,128)(2,1)}, u32[]{:S(2)}, u32[]{:S(2)}) collective-permute-start(bf16[128,3200]{1,0:T(8,128)(2,1)} %collective-permute-done.6.refs_9_), channel_id=1, source_target_pairs={{0,16},{16,0},{1,17},{17,1},{2,18},{18,2},{3,19},{19,3},{4,20},{20... | collective-permute-start | bytes 2457608 | tf_op jit(solution)/shard_map/ppermute | solution.py:371
  66.0 2.3 %collective-permute-done.10.refs_13_ = bf16[128,3200]{1,0:T(8,128)(2,1)} collective-permute-done((bf16[128,3200]{1,0:T(8,128)(2,1)}, bf16[128,3200]{1,0:T(8,128)(2,1)}, u32[]{:S(2)}, u32[]{:S(2)}) %collective-permute-start.10) | collective-permute-done | bytes 819232 | tf_op jit(solution)/shard_map/ppermute | solution.py:371
  68.3 8.8 %forward.1 = (bf16[384,1024]{1,0:T(8,128)(2,1)}, bf16[384,1024]{1,0:T(8,128)(2,1)}, bf16[384,1024]{1,0:T(8,128)(2,1)}, bf16[128,1024]{1,0:T(8,128)(2,1)S(1)}, f3...) custom-call(s32[4]{0:T(128)S(1)} %pad_add_fusion.refs_0_, ...), custom_call_target="tpu_custom_call" | custom-call | flops 8999999488 | bytes 27000000 | tf_op jit(solution)/shard_map/forward/pallas_call | solution.py:445
  77.2 8.1 %all_to_all.20 = bf16[4,112,128]{2,1,0:T(8,128)(2,1)S(1)} all-to-all(bf16[4,112,128]{2,1,0:T(8,128)(2,1)S(1)} %reshape.43), channel_id=1, replica_groups={{0,32,64,96},{128,160,192,224},{256,288,320,352},{384,416,448,480},{16,..., dimensions={0} | all-to-all | bytes 229376 | tf_op jit(solution)/shard_map/all_to_all | solution.py:395
  85.4 9.8 %all_to_all.21.refs_0_ = bf16[16,112,128]{2,1,0:T(8,128)(2,1)S(1)} all-to-all(bf16[16,112,128]{2,1,0:T(8,128)(2,1)S(1)} %bitcast.22), channel_id=1, replica_groups={{0,128,256,384},{32,160,288,416},{64,192,320,448},{96,224,352,480},{16,..., dimensions={0} | all-to-all | bytes 917504 | tf_op jit(solution)/shard_map/all_to_all | solution.py:395
  95.1 5.1 %collective-permute-start.12 = (bf16[16,112,128]{2,1,0:T(8,128)(2,1)S(1)}, bf16[16,112,128]{2,1,0:T(8,128)(2,1)S(1)}, u32[]{:S(2)}, u32[]{:S(2)}) collective-permute-start(bf16[16,112,128]{2,1,0:T(8,128)(2,1)S(1)} %all_to_all.21.refs_0_), channel_id=1, source_target_pairs={{0,16},{16,0},{1,17},{17,1},{2,18},{18,2},{3,19},{19,3},{4,20},{20... | collective-permute-start | bytes 1376264 | tf_op jit(solution)/shard_map/ppermute | solution.py:371
  101.7 2.0 %crps.1 = (bf16[1024,128]{1,0:T(8,128)(2,1)}, bf16[192,128]{1,0:T(8,128)(2,1)S(1)}) custom-call(bf16[16,112,128]{2,1,0:T(8,128)(2,1)S(1)} %all_to_all.21.refs_0_, bf16[16,112,128]{2,1,0:T(8,128)(2,1)S(1)} %collective-permute-done.12.refs_1_, bf16[112,128]{1,0:T(8,128)(2,1)S(1)} %get-tuple-element.23.refs_2_, bf16[112,128]{1,0:T(8,128)(2,1)S(1)} %pad.9.refs_3_, ...), custom_call_target="tpu_custom_call" | custom-call | flops 3000000000 | bytes 9000000 | tf_op jit(solution)/shard_map/crps/pallas_call | solution.py:479
  103.6 4.6 %all-to-all-start.2 = ((bf16[32,32,128]{2,1,0:T(8,128)(2,1)}), bf16[32,32,128]{2,1,0:T(8,128)(2,1)S(1)}, u32[]{:S(2)}, u32[]{:S(2)}) async-start(bf16[32,32,128]{2,1,0:T(8,128)(2,1)} %bitcast.9), calls=%async_computation.2 | async-start | bytes 524288 | tf_op jit(solution)/shard_map/all_to_all | solution.py:506
  108.3 7.7 %collective-permute-start.13 = (bf16[192,128]{1,0:T(8,128)(2,1)S(1)}, bf16[192,128]{1,0:T(8,128)(2,1)S(1)}, u32[]{:S(2)}, u32[]{:S(2)}) collective-permute-start(bf16[192,128]{1,0:T(8,128)(2,1)S(1)} %get-tuple-element.29.refs_2_), channel_id=1, source_target_pairs={{0,15},{1,2},{2,1},{3,4},{4,3},{5,6},{6,5},{7,8},{8,7},{9,10},{10,... | collective-permute-start | bytes 147464 | tf_op jit(solution)/shard_map/ppermute | solution.py:349
  116.1 1.9 %collective-permute-start.14 = (bf16[192,128]{1,0:T(8,128)(2,1)S(1)}, bf16[192,128]{1,0:T(8,128)(2,1)S(1)}, u32[]{:S(2)}, u32[]{:S(2)}) collective-permute-start(bf16[192,128]{1,0:T(8,128)(2,1)S(1)} %get-tuple-element.29.refs_2_), channel_id=1, source_target_pairs={{0,1},{1,0},{2,3},{3,2},{4,5},{5,4},{6,7},{7,6},{8,9},{9,8},{10,11... | collective-permute-start | bytes 147464 | tf_op jit(solution)/shard_map/ppermute | solution.py:349
  118.0 1.8 %all-to-all-done.2.refs_0_ = bf16[32,32,128]{2,1,0:T(8,128)(2,1)S(1)} async-done(((bf16[32,32,128]{2,1,0:T(8,128)(2,1)}), bf16[32,32,128]{2,1,0:T(8,128)(2,1)S(1)}, u32[]{:S(2)}, u32[]{:S(2)}) %all-to-all-start.2) | async-done | bytes 262176 | tf_op jit(solution)/shard_map/all_to_all | solution.py:506
  120.6 7.2 %all-to-all-start.3 = ((bf16[16,32,128]{2,1,0:T(8,128)(2,1)}), bf16[16,32,128]{2,1,0:T(8,128)(2,1)S(1)}, u32[]{:S(2)}, u32[]{:S(2)}) async-start(bf16[16,32,128]{2,1,0:T(8,128)(2,1)} %middle.1), calls=%async_computation.3 | async-start | bytes 262144 | tf_op jit(solution)/shard_map/all_to_all | solution.py:517
  127.8 10.7 %backward.1 = bf16[1,128,1024]{2,1,0:T(8,128)(2,1)} custom-call(s32[4]{0:T(128)S(1)} %pad_add_fusion.refs_0_, bf16[192,128]{1,0:T(8,128)(2,1)S(1)} %collective-permute-done.13.refs_1_, bf16[192,128]{1,0:T(8,128)(2,1)S(1)} %get-tuple-element.29.refs_2_, bf16[192,128]{1,0:T(8,128)(2,1)S(1)} %collective-permute-done.14.refs_3_, ...), custom_call_target="tpu_custom_call" | custom-call | flops 12000000000 | bytes 36000000 | tf_op jit(solution)/shard_map/backward/pallas_call | solution.py:529
  (51 shorter events, 11.7 us)
Async XLA Ops:
  0.6 31.0 %copy-start.9 = (bf16[32,1024]{1,0:T(8,128)(2,1)S(1)}, bf16[32,1024]{1,0:T(8,128)(2,1)}, u32[]{:S(2)}) copy-start(bf16[32,1024]{1,0:T(8,128)(2,1)} %param.13) | copy-start | bytes 196612
  0.7 31.0 %copy-start.8 = (bf16[32,1024]{1,0:T(8,128)(2,1)S(1)}, bf16[32,1024]{1,0:T(8,128)(2,1)}, u32[]{:S(2)}) copy-start(bf16[32,1024]{1,0:T(8,128)(2,1)} %param.14) | copy-start | bytes 196612
  0.7 31.0 %copy-start.7 = (bf16[32,1024]{1,0:T(8,128)(2,1)S(1)}, bf16[32,1024]{1,0:T(8,128)(2,1)}, u32[]{:S(2)}) copy-start(bf16[32,1024]{1,0:T(8,128)(2,1)} %param.15) | copy-start | bytes 196612
  2.6 63.1 %copy-start.6 = (bf16[1024,100]{0,1:T(8,128)(2,1)S(1)}, bf16[1024,100]{0,1:T(8,128)(2,1)}, u32[]{:S(2)}) copy-start(bf16[1024,100]{0,1:T(8,128)(2,1)} %param.17) | copy-start | bytes 614404
  3.6 28.1 %collective-permute-start = (bf16[32,3200]{1,0:T(8,128)(2,1)S(1)}, bf16[32,3200]{1,0:T(8,128)(2,1)S(1)}, u32[]{:S(2)}, u32[]{:S(2)}) collective-permute-start(bf16[32,3200]{1,0:T(8,128)(2,1)S(1)} %pad_maximum_fusion.1), channel_id=1, source_target_pairs={{0,128},{16,48},{1,129},{17,49},{2,130},{18,50},{3,131},{19,51},{4... | collective-permute-start | bytes 614408 | tf_op jit(solution)/shard_map/ppermute | solution.py:371
  8.4 23.2 %collective-permute-start.1 = (bf16[32,3200]{1,0:T(8,128)(2,1)S(1)}, bf16[32,3200]{1,0:T(8,128)(2,1)S(1)}, u32[]{:S(2)}, u32[]{:S(2)}) collective-permute-start(bf16[32,3200]{1,0:T(8,128)(2,1)S(1)} %pad_maximum_fusion.1), channel_id=1, source_target_pairs={{0,384},{16,120},{1,385},{17,121},{2,386},{18,122},{3,387},{19,123... | collective-permute-start | bytes 614408 | tf_op jit(solution)/shard_map/ppermute | solution.py:371
  17.0 14.6 %collective-permute-start.2 = (bf16[32,3200]{1,0:T(8,128)(2,1)S(1)}, bf16[32,3200]{1,0:T(8,128)(2,1)S(1)}, u32[]{:S(2)}, u32[]{:S(2)}) collective-permute-start(bf16[32,3200]{1,0:T(8,128)(2,1)S(1)} %pad_maximum_fusion.1), channel_id=1, source_target_pairs={{0,256},{16,80},{1,257},{17,81},{2,258},{18,82},{3,259},{19,83},{4... | collective-permute-start | bytes 614408 | tf_op jit(solution)/shard_map/ppermute | solution.py:371
  20.1 48.2 %copy-start.1 = (bf16[128,1024]{1,0:T(8,128)(2,1)S(1)}, bf16[128,1024]{1,0:T(8,128)(2,1)}, u32[]{:S(2)}) copy-start(bf16[128,1024]{1,0:T(8,128)(2,1)} %refs_5_.3) | copy-start | bytes 786436
  20.1 48.2 %copy-start.2 = (bf16[1,128,1024]{2,1,0:T(8,128)(2,1)S(1)}, bf16[1,128,1024]{2,1,0:T(8,128)(2,1)}, u32[]{:S(2)}) copy-start(bf16[1,128,1024]{2,1,0:T(8,128)(2,1)} %refs_4_.3) | copy-start | bytes 786436
  21.4 18.8 %collective-permute-start.3 = (bf16[128,1024]{1,0:T(8,128)(2,1)S(1)}, bf16[128,1024]{1,0:T(8,128)(2,1)S(1)}, u32[]{:S(2)}, u32[]{:S(2)}) collective-permute-start(bf16[128,1024]{1,0:T(8,128)(2,1)S(1)} %multiply_convert_fusion.refs_2_), channel_id=1, source_target_pairs={{0,15},{1,2},{2,1},{3,4},{4,3},{5,6},{6,5},{7,8},{8,7},{9,10},{10,... | collective-permute-start | bytes 786440 | tf_op jit(solution)/shard_map/ppermute | solution.py:349
  29.7 10.4 %collective-permute-start.4 = (bf16[128,1024]{1,0:T(8,128)(2,1)S(1)}, bf16[128,1024]{1,0:T(8,128)(2,1)S(1)}, u32[]{:S(2)}, u32[]{:S(2)}) collective-permute-start(bf16[128,1024]{1,0:T(8,128)(2,1)S(1)} %multiply_convert_fusion.refs_2_), channel_id=1, source_target_pairs={{0,1},{1,0},{2,3},{3,2},{4,5},{5,4},{6,7},{7,6},{8,9},{9,8},{10,11... | collective-permute-start | bytes 786440 | tf_op jit(solution)/shard_map/ppermute | solution.py:349
  31.8 18.0 %collective-permute-start.7 = (bf16[128,3200]{1,0:T(8,128)(2,1)S(1)}, bf16[128,3200]{1,0:T(8,128)(2,1)S(1)}, u32[]{:S(2)}, u32[]{:S(2)}) collective-permute-start(bf16[128,3200]{1,0:T(8,128)(2,1)S(1)} %pad_maximum_fusion.refs_7_), channel_id=1, source_target_pairs={{0,64},{16,272},{1,65},{17,273},{2,66},{18,274},{3,67},{19,275},{4... | collective-permute-start | bytes 2457608 | tf_op jit(solution)/shard_map/ppermute | solution.py:371
  36.4 19.1 %collective-permute-start.5 = (bf16[128,3200]{1,0:T(8,128)(2,1)S(1)}, bf16[128,3200]{1,0:T(8,128)(2,1)}, u32[]{:S(2)}, u32[]{:S(2)}) collective-permute-start(bf16[128,3200]{1,0:T(8,128)(2,1)S(1)} %pad_maximum_fusion.refs_7_), channel_id=1, source_target_pairs={{0,32},{16,144},{1,33},{17,145},{2,34},{18,146},{3,35},{19,147},{4... | collective-permute-start | bytes 2457608 | tf_op jit(solution)/shard_map/ppermute | solution.py:371
  40.1 23.6 %collective-permute-start.6 = (bf16[128,3200]{1,0:T(8,128)(2,1)S(1)}, bf16[128,3200]{1,0:T(8,128)(2,1)}, u32[]{:S(2)}, u32[]{:S(2)}) collective-permute-start(bf16[128,3200]{1,0:T(8,128)(2,1)S(1)} %pad_maximum_fusion.refs_7_), channel_id=1, source_target_pairs={{0,104},{16,400},{1,105},{17,401},{2,106},{18,402},{3,107},{19,403... | collective-permute-start | bytes 2457608 | tf_op jit(solution)/shard_map/ppermute | solution.py:371
  47.1 18.8 %collective-permute-start.8 = (bf16[128,3200]{1,0:T(8,128)(2,1)S(1)}, bf16[128,3200]{1,0:T(8,128)(2,1)}, u32[]{:S(2)}, u32[]{:S(2)}) collective-permute-start(bf16[128,3200]{1,0:T(8,128)(2,1)S(1)} %pad_maximum_fusion.refs_7_), channel_id=1, source_target_pairs={{0,16},{16,0},{1,17},{17,1},{2,18},{18,2},{3,19},{19,3},{4,20},{20... | collective-permute-start | bytes 2457608 | tf_op jit(solution)/shard_map/ppermute | solution.py:371
  49.8 16.1 %collective-permute-start.11 = (bf16[128,3200]{1,0:T(8,128)(2,1)S(1)}, bf16[128,3200]{1,0:T(8,128)(2,1)}, u32[]{:S(2)}, u32[]{:S(2)}) collective-permute-start(bf16[128,3200]{1,0:T(8,128)(2,1)S(1)} %collective-permute-done.7.refs_10_), channel_id=1, source_target_pairs={{0,16},{16,0},{1,17},{17,1},{2,18},{18,2},{3,19},{19,3},{4,20},{20... | collective-permute-start | bytes 2457608 | tf_op jit(solution)/shard_map/ppermute | solution.py:371
  55.5 10.5 %collective-permute-start.9 = (bf16[128,3200]{1,0:T(8,128)(2,1)}, bf16[128,3200]{1,0:T(8,128)(2,1)}, u32[]{:S(2)}, u32[]{:S(2)}) collective-permute-start(bf16[128,3200]{1,0:T(8,128)(2,1)} %collective-permute-done.5.refs_8_), channel_id=1, source_target_pairs={{0,16},{16,0},{1,17},{17,1},{2,18},{18,2},{3,19},{19,3},{4,20},{20... | collective-permute-start | bytes 2457608 | tf_op jit(solution)/shard_map/ppermute | solution.py:371
  63.7 4.6 %collective-permute-start.10 = (bf16[128,3200]{1,0:T(8,128)(2,1)}, bf16[128,3200]{1,0:T(8,128)(2,1)}, u32[]{:S(2)}, u32[]{:S(2)}) collective-permute-start(bf16[128,3200]{1,0:T(8,128)(2,1)} %collective-permute-done.6.refs_9_), channel_id=1, source_target_pairs={{0,16},{16,0},{1,17},{17,1},{2,18},{18,2},{3,19},{19,3},{4,20},{20... | collective-permute-start | bytes 2457608 | tf_op jit(solution)/shard_map/ppermute | solution.py:371
  77.1 24.5 %copy-start.4 = (f32[128]{0:T(128)S(1)}, f32[128]{0:T(128)}, u32[]{:S(2)}) copy-start(f32[128]{0:T(128)} %param.19) | copy-start | bytes 1540
  95.1 6.5 %collective-permute-start.12 = (bf16[16,112,128]{2,1,0:T(8,128)(2,1)S(1)}, bf16[16,112,128]{2,1,0:T(8,128)(2,1)S(1)}, u32[]{:S(2)}, u32[]{:S(2)}) collective-permute-start(bf16[16,112,128]{2,1,0:T(8,128)(2,1)S(1)} %all_to_all.21.refs_0_), channel_id=1, source_target_pairs={{0,16},{16,0},{1,17},{17,1},{2,18},{18,2},{3,19},{19,3},{4,20},{20... | collective-permute-start | bytes 1376264 | tf_op jit(solution)/shard_map/ppermute | solution.py:371
  103.6 16.2 %all-to-all-start.2 = ((bf16[32,32,128]{2,1,0:T(8,128)(2,1)}), bf16[32,32,128]{2,1,0:T(8,128)(2,1)S(1)}, u32[]{:S(2)}, u32[]{:S(2)}) async-start(bf16[32,32,128]{2,1,0:T(8,128)(2,1)} %bitcast.9), calls=%async_computation.2 | async-start | bytes 524288 | tf_op jit(solution)/shard_map/all_to_all | solution.py:506
  108.3 19.4 %collective-permute-start.13 = (bf16[192,128]{1,0:T(8,128)(2,1)S(1)}, bf16[192,128]{1,0:T(8,128)(2,1)S(1)}, u32[]{:S(2)}, u32[]{:S(2)}) collective-permute-start(bf16[192,128]{1,0:T(8,128)(2,1)S(1)} %get-tuple-element.29.refs_2_), channel_id=1, source_target_pairs={{0,15},{1,2},{2,1},{3,4},{4,3},{5,6},{6,5},{7,8},{8,7},{9,10},{10,... | collective-permute-start | bytes 147464 | tf_op jit(solution)/shard_map/ppermute | solution.py:349
  116.1 11.7 %collective-permute-start.14 = (bf16[192,128]{1,0:T(8,128)(2,1)S(1)}, bf16[192,128]{1,0:T(8,128)(2,1)S(1)}, u32[]{:S(2)}, u32[]{:S(2)}) collective-permute-start(bf16[192,128]{1,0:T(8,128)(2,1)S(1)} %get-tuple-element.29.refs_2_), channel_id=1, source_target_pairs={{0,1},{1,0},{2,3},{3,2},{4,5},{5,4},{6,7},{7,6},{8,9},{9,8},{10,11... | collective-permute-start | bytes 147464 | tf_op jit(solution)/shard_map/ppermute | solution.py:349
  120.6 18.6 %all-to-all-start.3 = ((bf16[16,32,128]{2,1,0:T(8,128)(2,1)}), bf16[16,32,128]{2,1,0:T(8,128)(2,1)S(1)}, u32[]{:S(2)}, u32[]{:S(2)}) async-start(bf16[16,32,128]{2,1,0:T(8,128)(2,1)} %middle.1), calls=%async_computation.3 | async-start | bytes 262144 | tf_op jit(solution)/shard_map/all_to_all | solution.py:517
  (4 other events, 68.0 us)

commit v13 on v12

--- a/solution.py
+++ b/solution.py
@@ -64,6 +64,38 @@
         out.append(piece)
         value = value - piece.astype(f32)
     return out
+
+
+def norm_kernel(hidden_in, forcing_in, gain, normed, inverse_rms, hidden, forcing, load):
+    loads = [
+        pltpu.make_async_copy(hidden_in, hidden, load.at[0]),
+        pltpu.make_async_copy(forcing_in, forcing, load.at[1]),
+    ]
+    for copy in loads:
+        copy.start()
+    for copy in loads:
+        copy.wait()
+    xfield = hidden[0].astype(f32) + forcing[...].astype(f32)
+    inverse = lax.rsqrt(jnp.mean(xfield * xfield, -1, keepdims=True) + EPS_NORM)
+    normed[...] = (xfield * inverse * gain[...]).astype(b16)
+    inverse_rms[...] = inverse
+
+
+def pack_kernel(w_query, w_key, w_value, w_out_in, decode_t, packed, w_out, load):
+    width = w_out.shape[1]
+    loads = [pltpu.make_async_copy(w_out_in, w_out, load.at[0])]
+    for index, part in enumerate((w_query, w_key, w_value)):
+        cols = packed.at[:, index * width : (index + 1) * width]
+        loads.append(pltpu.make_async_copy(part, cols, load.at[index + 1]))
+    for copy in loads:
+        copy.start()
+    loads[0].wait()
+    variables = decode_t.shape[0]
+    packed[:, 3 * width : 3 * width + variables] = nt(w_out[...], decode_t[...]).astype(b16)
+    blank = jnp.zeros((w_out.shape[0], LANES - variables), b16)
+    packed[:, 3 * width + variables :] = blank
+    for copy in loads[1:]:
+        copy.wait()
 
 
 def forward_kernel(scale, place, near, own, far, hidden, forcing, decode_t, *refs):
@@ -419,28 +451,48 @@
             flops=us * 10**9, transcendentals=0, bytes_accessed=us * 3 * 10**6
         )
     decode_t = jnp.pad(w_decode.T, ((0, LANES - variables), (0, 0)))
-    mixed = nt(w_out, decode_t).astype(b16)
     position = lax.axis_index("ens")
     core = position % 2
     parity = lax.axis_index("node") % 2
     place = jnp.stack([position // (2 * SIDE), position // 2 % SIDE, core, parity])
     place = place.astype(jnp.int32)
-    packed = jnp.concatenate([w_query, w_key, w_value, mixed], 1)
-    xfield = hidden[0].astype(f32) + forcing.astype(f32)
-    inverse_rms = lax.rsqrt(jnp.mean(xfield * xfield, -1, keepdims=True) + EPS_NORM)
-    normed = (xfield * inverse_rms * norm_gain).astype(b16)
+    in_smem = pl.BlockSpec(memory_space=pltpu.SMEM)
+    in_vmem = pl.BlockSpec(memory_space=pltpu.VMEM)
+    in_hbm = pl.BlockSpec(memory_space=pltpu.HBM)
+    packed_width = 3 * width + LANES
+
+    def held(value):
+        return pltpu.with_memory_space_constraint(value, pltpu.HBM)
+
+    packed = pl.pallas_call(
+        pack_kernel,
+        in_specs=[in_hbm] * 4 + [in_vmem],
+        out_specs=in_vmem,
+        out_shape=shape((rows, packed_width), b16),
+        scratch_shapes=[pltpu.VMEM((rows, width), b16), pltpu.SemaphoreType.DMA((4,))],
+        compiler_params=params(8),
+        cost_estimate=cost(1),
+        name="pack",
+    )(held(w_query), held(w_key), held(w_value), held(w_out), w_decode.T)
+    normed, inverse_rms = pl.pallas_call(
+        norm_kernel,
+        in_specs=[in_hbm, in_hbm, in_vmem],
+        out_specs=[in_vmem] * 2,
+        out_shape=[shape((node_rows, width), b16), shape((node_rows, 1), f32)],
+        scratch_shapes=[
+            pltpu.VMEM((1, node_rows, width), b16),
+            pltpu.VMEM((node_rows, width), b16),
+            pltpu.SemaphoreType.DMA((2,)),
+        ],
+        compiler_params=params(8),
+        cost_estimate=cost(1),
+        name="norm",
+    )(held(hidden), held(forcing), norm_gain[None])
     near, far = halos(normed)
     row = ring(packed, (0, 1))
     *mine, near, far = ring(jnp.concatenate(row, 0), (1, 0), (near, far))
     pieces = mine + [swapped(piece) for piece in mine]
 
-    packed_width = 3 * width + LANES
-    in_smem = pl.BlockSpec(memory_space=pltpu.SMEM)
-    in_vmem = pl.BlockSpec(memory_space=pltpu.VMEM)
-    in_hbm = pl.BlockSpec(memory_space=pltpu.HBM)
-
-    def held(value):
-        return pltpu.with_memory_space_constraint(value, pltpu.HBM)
 
     queries, keys, values, attended, lse, pred, mixed, full = pl.pallas_call(
         lambda *refs: forward_kernel(scale, *refs),

time: 141 us -> 142 us (level)
  local copies, waits for them, and re-layouts: 1.07 us -> 5.33 us
  other arithmetic: 3.52 us -> 0.14 us
  Pallas kernels: 23.1 us -> 25.2 us
    unnamed x22 -> x32, local copies, waits for them, and re-layouts: 0.86 us -> 5.23 us
    pallas_call x0 -> x2, Pallas kernels: none -> 2.31 us  [the longest x1 1.22 us: per_device(): pl.pallas_call(norm_kernel, in_specs=[in_hbm, in_hbm, in_vmem], out_specs...]
  transfers between devices with their start and end apart: 17 -> 17, of which waited for: 7 -> 6; matrix products, arithmetic and copies ran while one was open for 2% -> 0% of each run, Pallas kernels for 8% -> 9%
where the time goes in v13:
time: 142 us; the launch traced here: 141 us
  starting transfers between devices  82.7 us (58%)
  Pallas kernels  25.2 us (18%)
  blocking collectives  17.9 us (13%)
  waiting for transfers between devices  8.32 us (6%)
  local copies, waits for them, and re-layouts  5.33 us (4%)
    ppermute x11, starting transfers between devices, permute(): return lax.ppermute(value, ('ens', 'node'), pairs)  50.8 us
    ppermute x4, starting transfers between devices, halos(): lax.ppermute(value, 'node', [(n, (n + (1 if n % 2 == odd else -1)) % coun...  20.1 us
    all_to_all x2, blocking collectives, everyone(): lax.all_to_all(spread, 'ens', 0, 0, tiled=True, axis_index_groups=groups)  17.9 us
    pallas_call x1, Pallas kernels, per_device(): pl.pallas_call(lambda *refs: backward_kernel(scale, *refs), in_specs=[in_...  10.7 us
    pallas_call x1, Pallas kernels, per_device(): pl.pallas_call(lambda *refs: forward_kernel(scale, *refs), in_specs=[in_s...  8.6 us
    all_to_all x1, starting transfers between devices, per_device(): parts = lax.all_to_all(spread, 'node', 0, 0, tiled=True)  7.18 us
    unnamed x32, local copies, waits for them, and re-layouts  5.23 us
    all_to_all x1, starting transfers between devices, per_device(): lax.all_to_all(gram.reshape(members, rows, LANES), 'ens', 0, 0, tiled=True)  4.6 us
  transfers between devices with their start and end apart: 17, of which 6 were waited for; matrix products, arithmetic and copies ran while one was open for 0% of the time, Pallas kernels for 9%

profile of v13, /device:TPU:1, one launch (start us, length us, event | category | flops | bytes accessed | tf_op | source)
XLA Modules:
  0.0 140.7 jit_solution(3570176689077109051)
XLA Ops:
  2.7 4.8 %collective-permute-start = (bf16[32,3200]{1,0:T(8,128)(2,1)S(1)}, bf16[32,3200]{1,0:T(8,128)(2,1)S(1)}, u32[]{:S(2)}, u32[]{:S(2)}) collective-permute-start(bf16[32,3200]{1,0:T(8,128)(2,1)S(1)} %pack.1), channel_id=1, source_target_pairs={{0,128},{16,48},{1,129},{17,49},{2,130},{18,50},{3,131},{19,51},{4... | collective-permute-start | bytes 614408 | tf_op jit(solution)/shard_map/ppermute | solution.py:403
  7.5 8.6 %collective-permute-start.1 = (bf16[32,3200]{1,0:T(8,128)(2,1)S(1)}, bf16[32,3200]{1,0:T(8,128)(2,1)S(1)}, u32[]{:S(2)}, u32[]{:S(2)}) collective-permute-start(bf16[32,3200]{1,0:T(8,128)(2,1)S(1)} %pack.1), channel_id=1, source_target_pairs={{0,384},{16,120},{1,385},{17,121},{2,386},{18,122},{3,387},{19,123... | collective-permute-start | bytes 614408 | tf_op jit(solution)/shard_map/ppermute | solution.py:403
  16.1 1.9 %collective-permute-start.2 = (bf16[32,3200]{1,0:T(8,128)(2,1)S(1)}, bf16[32,3200]{1,0:T(8,128)(2,1)S(1)}, u32[]{:S(2)}, u32[]{:S(2)}) collective-permute-start(bf16[32,3200]{1,0:T(8,128)(2,1)S(1)} %pack.1), channel_id=1, source_target_pairs={{0,256},{16,80},{1,257},{17,81},{2,258},{18,82},{3,259},{19,83},{4... | collective-permute-start | bytes 614408 | tf_op jit(solution)/shard_map/ppermute | solution.py:403
  19.3 8.5 %collective-permute-start.3 = (bf16[128,1024]{1,0:T(8,128)(2,1)S(1)}, bf16[128,1024]{1,0:T(8,128)(2,1)S(1)}, u32[]{:S(2)}, u32[]{:S(2)}) collective-permute-start(bf16[128,1024]{1,0:T(8,128)(2,1)S(1)} %get-tuple-element.22.refs_2_), channel_id=1, source_target_pairs={{0,15},{1,2},{2,1},{3,4},{4,3},{5,6},{6,5},{7,8},{8,7},{9,10},{10,... | collective-permute-start | bytes 786440 | tf_op jit(solution)/shard_map/ppermute | solution.py:381
  27.8 1.9 %collective-permute-start.4 = (bf16[128,1024]{1,0:T(8,128)(2,1)S(1)}, bf16[128,1024]{1,0:T(8,128)(2,1)S(1)}, u32[]{:S(2)}, u32[]{:S(2)}) collective-permute-start(bf16[128,1024]{1,0:T(8,128)(2,1)S(1)} %get-tuple-element.22.refs_2_), channel_id=1, source_target_pairs={{0,1},{1,0},{2,3},{3,2},{4,5},{5,4},{6,7},{7,6},{8,9},{9,8},{10,11... | collective-permute-start | bytes 786440 | tf_op jit(solution)/shard_map/ppermute | solution.py:381
  29.8 4.7 %collective-permute-start.7 = (bf16[128,3200]{1,0:T(8,128)(2,1)S(1)}, bf16[128,3200]{1,0:T(8,128)(2,1)S(1)}, u32[]{:S(2)}, u32[]{:S(2)}) collective-permute-start(bf16[128,3200]{1,0:T(8,128)(2,1)S(1)} %pad_maximum_fusion.refs_7_), channel_id=1, source_target_pairs={{0,64},{16,272},{1,65},{17,273},{2,66},{18,274},{3,67},{19,275},{4... | collective-permute-start | bytes 2457608 | tf_op jit(solution)/shard_map/ppermute | solution.py:403
  34.5 2.2 %collective-permute-start.5 = (bf16[128,3200]{1,0:T(8,128)(2,1)S(1)}, bf16[128,3200]{1,0:T(8,128)(2,1)S(1)}, u32[]{:S(2)}, u32[]{:S(2)}) collective-permute-start(bf16[128,3200]{1,0:T(8,128)(2,1)S(1)} %pad_maximum_fusion.refs_7_), channel_id=1, source_target_pairs={{0,32},{16,144},{1,33},{17,145},{2,34},{18,146},{3,35},{19,147},{4... | collective-permute-start | bytes 2457608 | tf_op jit(solution)/shard_map/ppermute | solution.py:403
  39.6 6.9 %collective-permute-start.6 = (bf16[128,3200]{1,0:T(8,128)(2,1)S(1)}, bf16[128,3200]{1,0:T(8,128)(2,1)}, u32[]{:S(2)}, u32[]{:S(2)}) collective-permute-start(bf16[128,3200]{1,0:T(8,128)(2,1)S(1)} %pad_maximum_fusion.refs_7_), channel_id=1, source_target_pairs={{0,104},{16,400},{1,105},{17,401},{2,106},{18,402},{3,107},{19,403... | collective-permute-start | bytes 2457608 | tf_op jit(solution)/shard_map/ppermute | solution.py:403
  46.5 2.7 %collective-permute-start.8 = (bf16[128,3200]{1,0:T(8,128)(2,1)S(1)}, bf16[128,3200]{1,0:T(8,128)(2,1)}, u32[]{:S(2)}, u32[]{:S(2)}) collective-permute-start(bf16[128,3200]{1,0:T(8,128)(2,1)S(1)} %pad_maximum_fusion.refs_7_), channel_id=1, source_target_pairs={{0,16},{16,0},{1,17},{17,1},{2,18},{18,2},{3,19},{19,3},{4,20},{20... | collective-permute-start | bytes 2457608 | tf_op jit(solution)/shard_map/ppermute | solution.py:403
  49.3 3.7 %collective-permute-start.11 = (bf16[128,3200]{1,0:T(8,128)(2,1)S(1)}, bf16[128,3200]{1,0:T(8,128)(2,1)}, u32[]{:S(2)}, u32[]{:S(2)}) collective-permute-start(bf16[128,3200]{1,0:T(8,128)(2,1)S(1)} %collective-permute-done.7.refs_10_), channel_id=1, source_target_pairs={{0,16},{16,0},{1,17},{17,1},{2,18},{18,2},{3,19},{19,3},{4,20},{20... | collective-permute-start | bytes 2457608 | tf_op jit(solution)/shard_map/ppermute | solution.py:403
  53.5 8.2 %collective-permute-start.9 = (bf16[128,3200]{1,0:T(8,128)(2,1)S(1)}, bf16[128,3200]{1,0:T(8,128)(2,1)}, u32[]{:S(2)}, u32[]{:S(2)}) collective-permute-start(bf16[128,3200]{1,0:T(8,128)(2,1)S(1)} %collective-permute-done.5.refs_8_), channel_id=1, source_target_pairs={{0,16},{16,0},{1,17},{17,1},{2,18},{18,2},{3,19},{19,3},{4,20},{20... | collective-permute-start | bytes 2457608 | tf_op jit(solution)/shard_map/ppermute | solution.py:403
  61.7 1.9 %collective-permute-start.10 = (bf16[128,3200]{1,0:T(8,128)(2,1)}, bf16[128,3200]{1,0:T(8,128)(2,1)}, u32[]{:S(2)}, u32[]{:S(2)}) collective-permute-start(bf16[128,3200]{1,0:T(8,128)(2,1)} %collective-permute-done.6.refs_9_), channel_id=1, source_target_pairs={{0,16},{16,0},{1,17},{17,1},{2,18},{18,2},{3,19},{19,3},{4,20},{20... | collective-permute-start | bytes 2457608 | tf_op jit(solution)/shard_map/ppermute | solution.py:403
  63.8 2.4 %collective-permute-done.10.refs_13_ = bf16[128,3200]{1,0:T(8,128)(2,1)} collective-permute-done((bf16[128,3200]{1,0:T(8,128)(2,1)}, bf16[128,3200]{1,0:T(8,128)(2,1)}, u32[]{:S(2)}, u32[]{:S(2)}) %collective-permute-start.10) | collective-permute-done | bytes 819232 | tf_op jit(solution)/shard_map/ppermute | solution.py:403
  69.1 8.6 %forward.1 = (bf16[384,1024]{1,0:T(8,128)(2,1)}, bf16[384,1024]{1,0:T(8,128)(2,1)}, bf16[384,1024]{1,0:T(8,128)(2,1)}, bf16[128,1024]{1,0:T(8,128)(2,1)S(1)}, f3...) custom-call(s32[4]{0:T(128)S(1)} %pad_add_fusion.refs_0_, ...), custom_call_target="tpu_custom_call" | custom-call | flops 8999999488 | bytes 27000000 | tf_op jit(solution)/shard_map/forward/pallas_call | solution.py:497
  77.8 8.1 %all_to_all.20 = bf16[4,112,128]{2,1,0:T(8,128)(2,1)S(1)} all-to-all(bf16[4,112,128]{2,1,0:T(8,128)(2,1)S(1)} %reshape.19), channel_id=1, replica_groups={{0,32,64,96},{128,160,192,224},{256,288,320,352},{384,416,448,480},{16,..., dimensions={0} | all-to-all | bytes 229376 | tf_op jit(solution)/shard_map/all_to_all | solution.py:427
  86.0 9.8 %all_to_all.21.refs_0_ = bf16[16,112,128]{2,1,0:T(8,128)(2,1)S(1)} all-to-all(bf16[16,112,128]{2,1,0:T(8,128)(2,1)S(1)} %bitcast.16), channel_id=1, replica_groups={{0,128,256,384},{32,160,288,416},{64,192,320,448},{96,224,352,480},{16,..., dimensions={0} | all-to-all | bytes 917504 | tf_op jit(solution)/shard_map/all_to_all | solution.py:427
  95.8 5.1 %collective-permute-start.12 = (bf16[16,112,128]{2,1,0:T(8,128)(2,1)S(1)}, bf16[16,112,128]{2,1,0:T(8,128)(2,1)S(1)}, u32[]{:S(2)}, u32[]{:S(2)}) collective-permute-start(bf16[16,112,128]{2,1,0:T(8,128)(2,1)S(1)} %all_to_all.21.refs_0_), channel_id=1, source_target_pairs={{0,16},{16,0},{1,17},{17,1},{2,18},{18,2},{3,19},{19,3},{4,20},{20... | collective-permute-start | bytes 1376264 | tf_op jit(solution)/shard_map/ppermute | solution.py:403
  102.3 1.9 %crps.1 = (bf16[1024,128]{1,0:T(8,128)(2,1)}, bf16[192,128]{1,0:T(8,128)(2,1)S(1)}) custom-call(bf16[16,112,128]{2,1,0:T(8,128)(2,1)S(1)} %all_to_all.21.refs_0_, bf16[16,112,128]{2,1,0:T(8,128)(2,1)S(1)} %collective-permute-done.12.refs_1_, bf16[112,128]{1,0:T(8,128)(2,1)S(1)} %get-tuple-element.26.refs_2_, bf16[112,128]{1,0:T(8,128)(2,1)S(1)} %pad.9.refs_3_, ...), custom_call_target="tpu_custom_call" | custom-call | flops 3000000000 | bytes 9000000 | tf_op jit(solution)/shard_map/crps/pallas_call | solution.py:531
  104.3 4.6 %all-to-all-start.2 = ((bf16[32,32,128]{2,1,0:T(8,128)(2,1)}), bf16[32,32,128]{2,1,0:T(8,128)(2,1)S(1)}, u32[]{:S(2)}, u32[]{:S(2)}) async-start(bf16[32,32,128]{2,1,0:T(8,128)(2,1)} %bitcast.8), calls=%async_computation.2 | async-start | bytes 524288 | tf_op jit(solution)/shard_map/all_to_all | solution.py:558
  108.9 7.8 %collective-permute-start.13 = (bf16[192,128]{1,0:T(8,128)(2,1)S(1)}, bf16[192,128]{1,0:T(8,128)(2,1)S(1)}, u32[]{:S(2)}, u32[]{:S(2)}) collective-permute-start(bf16[192,128]{1,0:T(8,128)(2,1)S(1)} %get-tuple-element.32.refs_2_), channel_id=1, source_target_pairs={{0,15},{1,2},{2,1},{3,4},{4,3},{5,6},{6,5},{7,8},{8,7},{9,10},{10,... | collective-permute-start | bytes 147464 | tf_op jit(solution)/shard_map/ppermute | solution.py:381
  116.7 1.9 %collective-permute-start.14 = (bf16[192,128]{1,0:T(8,128)(2,1)S(1)}, bf16[192,128]{1,0:T(8,128)(2,1)S(1)}, u32[]{:S(2)}, u32[]{:S(2)}) collective-permute-start(bf16[192,128]{1,0:T(8,128)(2,1)S(1)} %get-tuple-element.32.refs_2_), channel_id=1, source_target_pairs={{0,1},{1,0},{2,3},{3,2},{4,5},{5,4},{6,7},{7,6},{8,9},{9,8},{10,11... | collective-permute-start | bytes 147464 | tf_op jit(solution)/shard_map/ppermute | solution.py:381
  118.6 1.8 %all-to-all-done.2.refs_0_ = bf16[32,32,128]{2,1,0:T(8,128)(2,1)S(1)} async-done(((bf16[32,32,128]{2,1,0:T(8,128)(2,1)}), bf16[32,32,128]{2,1,0:T(8,128)(2,1)S(1)}, u32[]{:S(2)}, u32[]{:S(2)}) %all-to-all-start.2) | async-done | bytes 262176 | tf_op jit(solution)/shard_map/all_to_all | solution.py:558
  121.2 7.2 %all-to-all-start.3 = ((bf16[16,32,128]{2,1,0:T(8,128)(2,1)}), bf16[16,32,128]{2,1,0:T(8,128)(2,1)S(1)}, u32[]{:S(2)}, u32[]{:S(2)}) async-start(bf16[16,32,128]{2,1,0:T(8,128)(2,1)} %middle.1), calls=%async_computation.3 | async-start | bytes 262144 | tf_op jit(solution)/shard_map/all_to_all | solution.py:569
  128.4 10.7 %backward.1 = bf16[1,128,1024]{2,1,0:T(8,128)(2,1)} custom-call(s32[4]{0:T(128)S(1)} %pad_add_fusion.refs_0_, bf16[192,128]{1,0:T(8,128)(2,1)S(1)} %collective-permute-done.13.refs_1_, bf16[192,128]{1,0:T(8,128)(2,1)S(1)} %get-tuple-element.32.refs_2_, bf16[192,128]{1,0:T(8,128)(2,1)S(1)} %collective-permute-done.14.refs_3_, ...), custom_call_target="tpu_custom_call" | custom-call | flops 12000000000 | bytes 36000000 | tf_op jit(solution)/shard_map/backward/pallas_call | solution.py:581
  (57 shorter events, 13.5 us)
Async XLA Ops:
  2.7 27.0 %collective-permute-start = (bf16[32,3200]{1,0:T(8,128)(2,1)S(1)}, bf16[32,3200]{1,0:T(8,128)(2,1)S(1)}, u32[]{:S(2)}, u32[]{:S(2)}) collective-permute-start(bf16[32,3200]{1,0:T(8,128)(2,1)S(1)} %pack.1), channel_id=1, source_target_pairs={{0,128},{16,48},{1,129},{17,49},{2,130},{18,50},{3,131},{19,51},{4... | collective-permute-start | bytes 614408 | tf_op jit(solution)/shard_map/ppermute | solution.py:403
  7.5 22.2 %collective-permute-start.1 = (bf16[32,3200]{1,0:T(8,128)(2,1)S(1)}, bf16[32,3200]{1,0:T(8,128)(2,1)S(1)}, u32[]{:S(2)}, u32[]{:S(2)}) collective-permute-start(bf16[32,3200]{1,0:T(8,128)(2,1)S(1)} %pack.1), channel_id=1, source_target_pairs={{0,384},{16,120},{1,385},{17,121},{2,386},{18,122},{3,387},{19,123... | collective-permute-start | bytes 614408 | tf_op jit(solution)/shard_map/ppermute | solution.py:403
  16.1 13.6 %collective-permute-start.2 = (bf16[32,3200]{1,0:T(8,128)(2,1)S(1)}, bf16[32,3200]{1,0:T(8,128)(2,1)S(1)}, u32[]{:S(2)}, u32[]{:S(2)}) collective-permute-start(bf16[32,3200]{1,0:T(8,128)(2,1)S(1)} %pack.1), channel_id=1, source_target_pairs={{0,256},{16,80},{1,257},{17,81},{2,258},{18,82},{3,259},{19,83},{4... | collective-permute-start | bytes 614408 | tf_op jit(solution)/shard_map/ppermute | solution.py:403
  19.3 42.4 %copy-start.4 = (bf16[128,1024]{1,0:T(8,128)(2,1)}, bf16[128,1024]{1,0:T(8,128)(2,1)S(1)}, u32[]{:S(2)}) copy-start(bf16[128,1024]{1,0:T(8,128)(2,1)S(1)} %get-tuple-element.22.refs_2_) | copy-start | bytes 786436
  19.3 44.4 %copy-start.1 = (bf16[1024,100]{0,1:T(8,128)(2,1)S(1)}, bf16[1024,100]{0,1:T(8,128)(2,1)}, u32[]{:S(2)}) copy-start(bf16[1024,100]{0,1:T(8,128)(2,1)} %param.17) | copy-start | bytes 614404
  19.3 47.0 %copy-start.2 = (bf16[1,128,1024]{2,1,0:T(8,128)(2,1)S(1)}, bf16[1,128,1024]{2,1,0:T(8,128)(2,1)}, u32[]{:S(2)}) copy-start(bf16[1,128,1024]{2,1,0:T(8,128)(2,1)} %refs_4_.3) | copy-start | bytes 786436
  19.3 47.0 %copy-start.3 = (bf16[128,1024]{1,0:T(8,128)(2,1)S(1)}, bf16[128,1024]{1,0:T(8,128)(2,1)}, u32[]{:S(2)}) copy-start(bf16[128,1024]{1,0:T(8,128)(2,1)} %refs_5_.3) | copy-start | bytes 786436
  19.3 18.9 %collective-permute-start.3 = (bf16[128,1024]{1,0:T(8,128)(2,1)S(1)}, bf16[128,1024]{1,0:T(8,128)(2,1)S(1)}, u32[]{:S(2)}, u32[]{:S(2)}) collective-permute-start(bf16[128,1024]{1,0:T(8,128)(2,1)S(1)} %get-tuple-element.22.refs_2_), channel_id=1, source_target_pairs={{0,15},{1,2},{2,1},{3,4},{4,3},{5,6},{6,5},{7,8},{8,7},{9,10},{10,... | collective-permute-start | bytes 786440 | tf_op jit(solution)/shard_map/ppermute | solution.py:381
  27.8 11.1 %collective-permute-start.4 = (bf16[128,1024]{1,0:T(8,128)(2,1)S(1)}, bf16[128,1024]{1,0:T(8,128)(2,1)S(1)}, u32[]{:S(2)}, u32[]{:S(2)}) collective-permute-start(bf16[128,1024]{1,0:T(8,128)(2,1)S(1)} %get-tuple-element.22.refs_2_), channel_id=1, source_target_pairs={{0,1},{1,0},{2,3},{3,2},{4,5},{5,4},{6,7},{7,6},{8,9},{9,8},{10,11... | collective-permute-start | bytes 786440 | tf_op jit(solution)/shard_map/ppermute | solution.py:381
  29.8 19.5 %collective-permute-start.7 = (bf16[128,3200]{1,0:T(8,128)(2,1)S(1)}, bf16[128,3200]{1,0:T(8,128)(2,1)S(1)}, u32[]{:S(2)}, u32[]{:S(2)}) collective-permute-start(bf16[128,3200]{1,0:T(8,128)(2,1)S(1)} %pad_maximum_fusion.refs_7_), channel_id=1, source_target_pairs={{0,64},{16,272},{1,65},{17,273},{2,66},{18,274},{3,67},{19,275},{4... | collective-permute-start | bytes 2457608 | tf_op jit(solution)/shard_map/ppermute | solution.py:403
  34.5 19.0 %collective-permute-start.5 = (bf16[128,3200]{1,0:T(8,128)(2,1)S(1)}, bf16[128,3200]{1,0:T(8,128)(2,1)S(1)}, u32[]{:S(2)}, u32[]{:S(2)}) collective-permute-start(bf16[128,3200]{1,0:T(8,128)(2,1)S(1)} %pad_maximum_fusion.refs_7_), channel_id=1, source_target_pairs={{0,32},{16,144},{1,33},{17,145},{2,34},{18,146},{3,35},{19,147},{4... | collective-permute-start | bytes 2457608 | tf_op jit(solution)/shard_map/ppermute | solution.py:403
  39.6 22.1 %collective-permute-start.6 = (bf16[128,3200]{1,0:T(8,128)(2,1)S(1)}, bf16[128,3200]{1,0:T(8,128)(2,1)}, u32[]{:S(2)}, u32[]{:S(2)}) collective-permute-start(bf16[128,3200]{1,0:T(8,128)(2,1)S(1)} %pad_maximum_fusion.refs_7_), channel_id=1, source_target_pairs={{0,104},{16,400},{1,105},{17,401},{2,106},{18,402},{3,107},{19,403... | collective-permute-start | bytes 2457608 | tf_op jit(solution)/shard_map/ppermute | solution.py:403
  46.5 17.3 %collective-permute-start.8 = (bf16[128,3200]{1,0:T(8,128)(2,1)S(1)}, bf16[128,3200]{1,0:T(8,128)(2,1)}, u32[]{:S(2)}, u32[]{:S(2)}) collective-permute-start(bf16[128,3200]{1,0:T(8,128)(2,1)S(1)} %pad_maximum_fusion.refs_7_), channel_id=1, source_target_pairs={{0,16},{16,0},{1,17},{17,1},{2,18},{18,2},{3,19},{19,3},{4,20},{20... | collective-permute-start | bytes 2457608 | tf_op jit(solution)/shard_map/ppermute | solution.py:403
  49.3 14.6 %collective-permute-start.11 = (bf16[128,3200]{1,0:T(8,128)(2,1)S(1)}, bf16[128,3200]{1,0:T(8,128)(2,1)}, u32[]{:S(2)}, u32[]{:S(2)}) collective-permute-start(bf16[128,3200]{1,0:T(8,128)(2,1)S(1)} %collective-permute-done.7.refs_10_), channel_id=1, source_target_pairs={{0,16},{16,0},{1,17},{17,1},{2,18},{18,2},{3,19},{19,3},{4,20},{20... | collective-permute-start | bytes 2457608 | tf_op jit(solution)/shard_map/ppermute | solution.py:403
  53.5 10.4 %collective-permute-start.9 = (bf16[128,3200]{1,0:T(8,128)(2,1)S(1)}, bf16[128,3200]{1,0:T(8,128)(2,1)}, u32[]{:S(2)}, u32[]{:S(2)}) collective-permute-start(bf16[128,3200]{1,0:T(8,128)(2,1)S(1)} %collective-permute-done.5.refs_8_), channel_id=1, source_target_pairs={{0,16},{16,0},{1,17},{17,1},{2,18},{18,2},{3,19},{19,3},{4,20},{20... | collective-permute-start | bytes 2457608 | tf_op jit(solution)/shard_map/ppermute | solution.py:403
  61.7 4.6 %collective-permute-start.10 = (bf16[128,3200]{1,0:T(8,128)(2,1)}, bf16[128,3200]{1,0:T(8,128)(2,1)}, u32[]{:S(2)}, u32[]{:S(2)}) collective-permute-start(bf16[128,3200]{1,0:T(8,128)(2,1)} %collective-permute-done.6.refs_9_), channel_id=1, source_target_pairs={{0,16},{16,0},{1,17},{17,1},{2,18},{18,2},{3,19},{19,3},{4,20},{20... | collective-permute-start | bytes 2457608 | tf_op jit(solution)/shard_map/ppermute | solution.py:403
  77.8 26.5 %copy-start.13 = (bf16[1024,128]{1,0:T(8,128)(2,1)}, bf16[1024,128]{1,0:T(8,128)(2,1)S(1)}, u32[]{:S(2)}) copy-start(bf16[1024,128]{1,0:T(8,128)(2,1)S(1)} %get-tuple-element.28.refs_6_.refs_9_) | copy-start | bytes 786436
  77.8 24.5 %copy-start.11 = (f32[128]{0:T(128)S(1)}, f32[128]{0:T(128)}, u32[]{:S(2)}) copy-start(f32[128]{0:T(128)} %param.19) | copy-start | bytes 1540
  77.8 24.5 %copy-start.12 = (f32[128,1024]{1,0:T(8,128)S(1)}, f32[128,1024]{1,0:T(8,128)}, u32[]{:S(2)}) copy-start(f32[128,1024]{1,0:T(8,128)} %get-tuple-element.29.refs_7_.refs_13_) | copy-start | bytes 1572868
  95.8 6.5 %collective-permute-start.12 = (bf16[16,112,128]{2,1,0:T(8,128)(2,1)S(1)}, bf16[16,112,128]{2,1,0:T(8,128)(2,1)S(1)}, u32[]{:S(2)}, u32[]{:S(2)}) collective-permute-start(bf16[16,112,128]{2,1,0:T(8,128)(2,1)S(1)} %all_to_all.21.refs_0_), channel_id=1, source_target_pairs={{0,16},{16,0},{1,17},{17,1},{2,18},{18,2},{3,19},{19,3},{4,20},{20... | collective-permute-start | bytes 1376264 | tf_op jit(solution)/shard_map/ppermute | solution.py:403
  104.3 16.2 %all-to-all-start.2 = ((bf16[32,32,128]{2,1,0:T(8,128)(2,1)}), bf16[32,32,128]{2,1,0:T(8,128)(2,1)S(1)}, u32[]{:S(2)}, u32[]{:S(2)}) async-start(bf16[32,32,128]{2,1,0:T(8,128)(2,1)} %bitcast.8), calls=%async_computation.2 | async-start | bytes 524288 | tf_op jit(solution)/shard_map/all_to_all | solution.py:558
  108.9 19.5 %collective-permute-start.13 = (bf16[192,128]{1,0:T(8,128)(2,1)S(1)}, bf16[192,128]{1,0:T(8,128)(2,1)S(1)}, u32[]{:S(2)}, u32[]{:S(2)}) collective-permute-start(bf16[192,128]{1,0:T(8,128)(2,1)S(1)} %get-tuple-element.32.refs_2_), channel_id=1, source_target_pairs={{0,15},{1,2},{2,1},{3,4},{4,3},{5,6},{6,5},{7,8},{8,7},{9,10},{10,... | collective-permute-start | bytes 147464 | tf_op jit(solution)/shard_map/ppermute | solution.py:381
  116.7 11.7 %collective-permute-start.14 = (bf16[192,128]{1,0:T(8,128)(2,1)S(1)}, bf16[192,128]{1,0:T(8,128)(2,1)S(1)}, u32[]{:S(2)}, u32[]{:S(2)}) collective-permute-start(bf16[192,128]{1,0:T(8,128)(2,1)S(1)} %get-tuple-element.32.refs_2_), channel_id=1, source_target_pairs={{0,1},{1,0},{2,3},{3,2},{4,5},{5,4},{6,7},{7,6},{8,9},{9,8},{10,11... | collective-permute-start | bytes 147464 | tf_op jit(solution)/shard_map/ppermute | solution.py:381
  121.2 18.6 %all-to-all-start.3 = ((bf16[16,32,128]{2,1,0:T(8,128)(2,1)}), bf16[16,32,128]{2,1,0:T(8,128)(2,1)S(1)}, u32[]{:S(2)}, u32[]{:S(2)}) async-start(bf16[16,32,128]{2,1,0:T(8,128)(2,1)} %middle.1), calls=%async_computation.3 | async-start | bytes 262144 | tf_op jit(solution)/shard_map/all_to_all | solution.py:569
  (9 other events, 64.3 us)
